TPU v7x, 32 devices: a whole 2x2x4 slice. The times are simulated.
32 devices in a mesh: groups: 2 (over y), adapter: 4 (over z), tensor: 2 (over x), replica: 2 (over core).
Axes of the slice: x: 2, y: 2, z: 4, core: 2. Of those that a mesh axis runs over, the one named last changes fastest.
Arguments:
- hidden_state_rows: bfloat16 [8192, 8192], P(('groups', 'adapter', 'replica'), 'tensor'), parts along dimension 0, may hold values from -6 to 6
- value_matrix: bfloat16 [8192, 1024], P('tensor', 'replica'), may hold values from -0.0625 to 0.0625
- adapter_down_weight: bfloat16 [4, 8192, 64], P('adapter', 'tensor'), may hold values from -0.0625 to 0.0625
- adapter_up_weight: bfloat16 [4, 64, 1024], P('adapter', None, 'tensor'), may hold values from -0.75 to 0.75
- adapter_index_rows: int32 [8192, 1], P(('groups', 'adapter', 'replica')), parts along dimension 0, may hold values from 0 to 3; in each aligned block of 512 rows (0 to 511, 512 to 1023, ...) at most 256 rows name the same one
Outputs:
- values: bfloat16 [8192, 1024], P(('groups', 'adapter', 'replica'), 'tensor'), parts along dimension 0
There are 2 independent parts, one for each index of `groups`. A program takes and returns all parts, laid end to end along the dimension named above; an argument that names none is the same for every part. Nothing has to cross between parts.
Inputs may be any that keep to these rules, and one draw needn't show every extreme that they name: `adapter_index_rows`: among the rows of one device (aligned blocks of 512 rows) no adapter is named by more than 256 rows; some adapter is named by exactly 256 rows of some device.
All inputs are finite; a program needn't handle non-finite values.
Results may differ from a plain program's by a relative error of at most 0.007.
Values may be sent and summed in bfloat16 or wider, within the bound.
No kernel may reach another device: no remote copies, remote signals or barrier semaphores. Data moves between devices by JAX's collectives and lax.ppermute only.
A program may use at most 128 MiB of HBM per device.

v0:
```python
import jax
import jax.numpy as jnp
from jax import lax
from jax.sharding import PartitionSpec as P


def shards(
    hidden_state_rows, value_matrix, adapter_down_weight, adapter_up_weight, adapter_index_rows
):
    adapter_indices = adapter_index_rows[:, 0]
    base_terms = jnp.dot(
        hidden_state_rows,
        lax.all_gather(value_matrix, "replica", axis=1, tiled=True),
        preferred_element_type=jnp.float32,
    )
    base_output = lax.psum_scatter(base_terms, "tensor", scatter_dimension=1, tiled=True)
    partial_output = lax.all_gather(adapter_down_weight, "adapter", axis=0, tiled=True)
    count = partial_output.shape[0]
    prod = jnp.einsum(
        "rd,kdq->rkq", hidden_state_rows, partial_output, preferred_element_type=jnp.float32
    )
    match = (adapter_indices[:, None] == jnp.arange(count, dtype=jnp.int32)[None, :]).astype(
        jnp.float32
    )
    low = jnp.sum(prod * match[:, :, None], axis=1)
    low = lax.psum(low, "tensor")
    lowrank_state = low.astype(jnp.bfloat16)
    partial_output = lax.all_gather(adapter_up_weight, "adapter", axis=0, tiled=True)
    count = partial_output.shape[0]
    match = (adapter_indices[:, None] == jnp.arange(count, dtype=jnp.int32)[None, :]).astype(
        jnp.bfloat16
    )
    masked_state = lowrank_state[:, None, :] * match[:, :, None]
    adapter_output_rows = jnp.einsum(
        "ypl,pls->ys", masked_state, partial_output, preferred_element_type=jnp.float32
    ).astype(jnp.bfloat16)
    return (base_output + adapter_output_rows.astype(jnp.float32)).astype(jnp.bfloat16)


def solution(mesh):
    return jax.shard_map(
        shards,
        mesh=mesh,
        in_specs=(
            P(("groups", "adapter", "replica"), "tensor"),
            P("tensor", "replica"),
            P("adapter", "tensor", None),
            P("adapter", None, "tensor"),
            P(("groups", "adapter", "replica"), None),
        ),
        out_specs=P(("groups", "adapter", "replica"), "tensor"),
        check_vma=False,
    )
```

profile of v0, /device:TPU:0, one launch (start us, length us, event | category | flops | bytes accessed | tf_op | source)
XLA Modules:
  0.0 128.1 jit_solution(7575635170928311747)
XLA Ops:
  6.5 0.0 all-gather.3.cloned.1.call-start
  6.5 0.7 all-gather.3.cloned.1.call-update
  7.3 0.0 all-gather.5.cloned.1.call-start
  7.3 0.7 all-gather.5.cloned.1.call-update
  8.0 0.0 copy-start
  8.0 0.0 copy-start.1
  8.0 0.0 reduce-scatter.2.cloned.1.call-start
  8.1 23.4 %all-gather.3.cloned.1.call-done = bf16[4096,1024]{1,0:T(8,128)(2,1)} async-done(((bf16[4096,512]{1,0:T(8,128)(2,1)}), bf16[4096,1024]{1,0:T(8,128)(2,1)}) %all-gather.3.cloned.1.call-update) | async-done | bytes 8388624 | tf_op jit(solution)/shard_map/all_gather | solution.py:13
  31.5 10.5 %fusion.9 = f32[512,1024]{1,0:T(8,128)} fusion(bf16[512,4096]{1,0:T(8,128)(2,1)} %param.5, bf16[4096,1024]{1,0:T(8,128)(2,1)} %all-gather.3.cloned.1.call-done), kind=kOutput, calls=%fused_computation.12 | convolution fusion | flops 4294967296 | bytes 14680064 | tf_op jit(solution)/shard_map/dot_general | solution.py:11
  41.9 0.0 reduce-scatter.2.cloned.1.call-update
  42.0 0.0 copy-done
  42.0 16.8 %all_gather.11 = bf16[4,64,512]{2,1,0:T(8,128)(2,1)S(1)} all-gather(bf16[1,64,512]{2,1,0:T(8,128)(2,1)S(1)} %copy-done), channel_id=1, replica_groups=mesh['groups'=2,'adapter'=4,'tensor'=2,'replica'=2] {'adapter'}, dimensions={0}, use_global_device_ids=true | all-gather | bytes 327680 | tf_op jit(solution)/shard_map/all_gather | solution.py:28
  58.7 0.0 copy-done.1
  58.8 25.6 %all-gather.5.cloned.1.call-done = bf16[4,4096,64]{1,2,0:T(8,128)(2,1)} async-done(((bf16[1,4096,64]{1,2,0:T(8,128)(2,1)}), bf16[4,4096,64]{1,2,0:T(8,128)(2,1)}) %all-gather.5.cloned.1.call-update) | async-done | bytes 2097168 | tf_op jit(solution)/shard_map/all_gather | solution.py:17
  84.3 4.1 %fusion.10 = f32[512,256]{0,1:S(1)} fusion(bf16[512,4096]{1,0:T(8,128)(2,1)} %param.5, bf16[4096,256]{0,1:T(8,128)(2,1)} %bitcast.22), kind=kOutput, calls=%fused_computation.13 | convolution fusion | flops 1073741824 | bytes 6815744
  88.5 0.1 multiply_reduce_fusion
  88.6 12.8 %all-reduce.1 = bf16[512,64]{0,1:T(8,128)(2,1)S(1)} all-reduce(f32[512,64]{0,1:T(8,128)S(1)} %multiply_reduce_fusion), channel_id=1, replica_groups=mesh['groups'=2,'adapter'=4,'tensor'=2,'replica'=2] {'tensor'}, use_global_device_ids=true, to_apply=%region_2.0 | all-reduce | flops 32768 | bytes 196608 | tf_op jit(solution)/shard_map/psum | solution.py:26
  101.4 17.8 %reduce-scatter.2.cloned.1.call-done = f32[512,512]{1,0:T(8,128)} async-done(((f32[512,1024]{1,0:T(8,128)}), f32[512,512]{1,0:T(8,128)}) %reduce-scatter.2.cloned.1.call-update) | async-done | bytes 1048592 | tf_op jit(solution)/shard_map/reduce_scatter | solution.py:16
  119.3 2.4 %fusion.3 = bf16[512,512]{1,0:T(8,128)(2,1)} fusion(f32[512,512]{1,0:T(8,128)} %reduce-scatter.2.cloned.1.call-done, bf16[4,64,512]{2,1,0:T(8,128)(2,1)S(1)} %all_gather.11, bf16[512,4]{0,1:T(4,128)(2,1)S(1)} %get-tuple-element.6, bf16[512,64]{0,1:T(8,128)(2,1)S(1)} %all-reduce.1), kind=kOutput, calls=%fused_computation.4 | convolution fusion | flops 135397376 | bytes 1904640 | tf_op jit(solution)/shard_map/ypl,pls->ys/dot_general | solution.py:34
  (1 shorter events, 0.0 us)
Async XLA Ops:
  6.5 25.0 %all-gather.3.cloned.1.call-start = ((), (), s32[]{:S(2)}) async-start(), calls=%async_computation.1 | async-start | bytes 12582912 | tf_op jit(solution)/shard_map/all_gather | solution.py:13
  7.3 77.1 %all-gather.5.cloned.1.call-start = ((), (), s32[]{:S(2)}) async-start(), calls=%async_computation.3 | async-start | bytes 2621440 | tf_op jit(solution)/shard_map/all_gather | solution.py:17
  8.0 34.0 %copy-start = (bf16[1,64,512]{2,1,0:T(8,128)(2,1)S(1)}, bf16[1,64,512]{2,1,0:T(8,128)(2,1)}, u32[]{:S(2)}) copy-start(bf16[1,64,512]{2,1,0:T(8,128)(2,1)} %param.8) | copy-start | bytes 196612
  8.0 50.7 %copy-start.1 = (s32[512,1]{0,1:T(1,128)S(1)}, s32[512,1]{0,1:T(1,128)}, u32[]{:S(2)}) copy-start(s32[512,1]{0,1:T(1,128)} %param.9) | copy-start | bytes 6148
  8.0 111.2 %reduce-scatter.2.cloned.1.call-start = ((), (), s32[]{:S(2)}) async-start(), calls=%async_computation.2 | async-start | bytes 3145728 | tf_op jit(solution)/shard_map/reduce_scatter | solution.py:16
Sparse Core Ops, SparseCore 0:
  8.9 22.5 all-gather.2
  33.1 51.2 all-gather.4
  86.6 32.6 reduce-scatter.1
where the time goes:
time: 128 us
  waiting for transfers between devices  68.3 us (53%)
  blocking collectives  29.6 us (23%)
  matrix products  17 us (13%)
  between operations  13.2 us (10%)
    all_gather x1, waiting for transfers between devices, shards(): lax.all_gather(adapter_down_weight, 'adapter', axis=0, tiled=True)  25.6 us
    all_gather x1, waiting for transfers between devices, shards(): lax.all_gather(value_matrix, 'replica', axis=1, tiled=True)  23.4 us
    reduce_scatter x1, waiting for transfers between devices, shards(): lax.psum_scatter(base_terms, 'tensor', scatter_dimension=1, tiled=True)  17.8 us
    all_gather x1, blocking collectives, shards(): lax.all_gather(adapter_up_weight, 'adapter', axis=0, tiled=True)  16.8 us
    psum x1, blocking collectives, shards(): low = lax.psum(low, 'tensor')  12.8 us
    dot_general x1, matrix products, shards(): jnp.dot(hidden_state_rows, lax.all_gather(value_matrix, 'replica', axis=1...  10.5 us
    unnamed x1, matrix products  4.15 us
  transfers between devices with their start and end apart: 3, of which 3 were waited for; matrix products, arithmetic and copies ran while one was open for 11% of the time, Pallas kernels for 0%

commit v1 on v0

v1 whole, which is shorter than its diff:
```python
import jax
import jax.numpy as jnp
from jax import lax
from jax.sharding import PartitionSpec as P

F32 = jnp.float32
BF16 = jnp.bfloat16


def shift(x, axis, size, by):
    return lax.ppermute(x, axis, [(i, (i + by) % size) for i in range(size)])


def build(mesh):
    groups, adapters = mesh.shape["groups"], mesh.shape["adapter"]
    tensors, replicas = mesh.shape["tensor"], mesh.shape["replica"]

    def others(x, axis, size):
        return [shift(x, axis, size, by) for by in range(1, size)]

    def shards(x, v, d, u, idx):
        g, a = lax.axis_index("groups"), lax.axis_index("adapter")
        t, r = lax.axis_index("tensor"), lax.axis_index("replica")
        rank, wide = d.shape[2], d.shape[1]
        cols, width = u.shape[2], v.shape[1]
        per = width // cols if width >= cols else 1

        held = [v] + others(v, "replica", replicas)

        own = jnp.concatenate([d[0].T, u[0]], axis=1)
        share = rank // (groups * replicas)
        mine = lax.dynamic_slice_in_dim(own, (g * replicas + r) * share, share, 0)
        down, up = [d[0].T], [u[0]]
        for by in range(1, adapters):
            part = shift(mine, "adapter", adapters, by)
            parts = jnp.concatenate([part] + others(part, "groups", groups), axis=0)
            parts = jnp.concatenate([parts] + others(parts, "replica", replicas), axis=0)
            down.append(parts[:, :wide])
            up.append(parts[:, wide:])

        local = jnp.zeros((x.shape[0], cols), F32)
        for h in range(replicas):
            terms = jnp.dot(x, held[h], preferred_element_type=F32)
            half = lax.rem(r - h + replicas, replicas)
            first = half * per
            here = (t >= first) & (t < first + per)
            block = lax.dynamic_slice_in_dim(terms, jnp.clip(t - first, 0, per - 1) * cols, cols, 1)
            local = local + jnp.where(here, block, 0.0)
            for by in range(1, tensors):
                pairs = [
                    (ti * replicas + ri, (ti + by) % tensors * replicas + ri)
                    for ti in range(tensors)
                    for ri in range(replicas)
                    if ((ti + by) % tensors) // per == (ri - h) % replicas
                ]
                if not pairs:
                    continue
                to = lax.rem(t + by, tensors)
                block = lax.dynamic_slice_in_dim(
                    terms, jnp.clip(to - first, 0, per - 1) * cols, cols, 1
                ).astype(BF16)
                local = local + lax.ppermute(block, ("tensor", "replica"), pairs).astype(F32)

        owner = lax.rem(a - jnp.arange(adapters, dtype=jnp.int32) + adapters, adapters)
        match = idx == owner[None, :]
        prod = jnp.einsum(
            "rd,qd->rq", x, jnp.concatenate(down, axis=0), preferred_element_type=F32
        ).reshape(x.shape[0], adapters, rank)
        low = jnp.sum(jnp.where(match[:, :, None], prod, 0.0), axis=1)
        sent = low.astype(BF16)
        low = low + sum(o.astype(F32) for o in others(sent, "tensor", tensors))
        low = low.astype(BF16)
        spread = jnp.where(match[:, :, None], low[:, None, :], 0).reshape(x.shape[0], adapters * rank)
        lora = jnp.dot(spread, jnp.concatenate(up, axis=0), preferred_element_type=F32).astype(BF16)
        return (local + lora.astype(F32)).astype(BF16)

    return shards


def solution(mesh):
    return jax.shard_map(
        build(mesh),
        mesh=mesh,
        in_specs=(
            P(("groups", "adapter", "replica"), "tensor"),
            P("tensor", "replica"),
            P("adapter", "tensor", None),
            P("adapter", None, "tensor"),
            P(("groups", "adapter", "replica"), None),
        ),
        out_specs=P(("groups", "adapter", "replica"), "tensor"),
        check_vma=False,
    )
```

time: 128 us -> 51.8 us (0.40)
  waiting for transfers between devices: 68.3 us -> 6.86 us
  blocking collectives: 29.6 us -> 0 us
  starting transfers between devices: 0.08 us -> 24.6 us
  between operations: 13.2 us -> 0.24 us
  other arithmetic: 0.06 us -> 2.01 us
  local copies, waits for them, and re-layouts: 0.01 us -> 1.93 us
  matrix products: 17 us -> 15.6 us
    all_gather x2 -> x0, waiting for transfers between devices: 49 us -> none  [the longest x1 25.6 us: shards(): lax.all_gather(adapter_down_weight, 'adapter', axis=0, tiled=True)]
    ppermute x0 -> x13, starting transfers between devices: none -> 24.6 us  [the longest x11 20.1 us: shift(): return lax.ppermute(x, axis, [(i, (i + by) % size) for i in range(size)])]
    reduce_scatter x1 -> x0, waiting for transfers between devices: 17.8 us -> none  [shards(): lax.psum_scatter(base_terms, 'tensor', scatter_dimension=1, tiled=True)]
    all_gather x1 -> x0, blocking collectives: 16.8 us -> none  [shards(): lax.all_gather(adapter_up_weight, 'adapter', axis=0, tiled=True)]
    psum x1 -> x0, blocking collectives: 12.8 us -> none  [shards(): low = lax.psum(low, 'tensor')]
    ppermute x0 -> x13, waiting for transfers between devices: none -> 6.86 us  [the longest x2 4.44 us: shards(): lax.ppermute(block, ('tensor', 'replica'), pairs).astype(F32)]
    unnamed x1 -> x0, matrix products: 4.15 us -> none
    dot_general x2 -> x4, matrix products: 12.8 us -> 15.6 us  [the longest x2 11.9 us: shards(): terms = jnp.dot(x, held[h], preferred_element_type=F32)]
  transfers between devices with their start and end apart: 3 -> 13, of which waited for: 3 -> 3; matrix products, arithmetic and copies ran while one was open for 11% -> 30% of each run, Pallas kernels for 0% -> 0%
where the time goes in v1:
time: 51.8 us; the launch traced here: 51.2 us
  starting transfers between devices  24.6 us (47%)
  matrix products  15.6 us (30%)
  waiting for transfers between devices  6.86 us (13%)
  other arithmetic  2.01 us (4%)
  local copies, waits for them, and re-layouts  1.93 us (4%)
    ppermute x11, starting transfers between devices, shift(): return lax.ppermute(x, axis, [(i, (i + by) % size) for i in range(size)])  20.1 us
    dot_general x2, matrix products, shards(): terms = jnp.dot(x, held[h], preferred_element_type=F32)  11.9 us
    ppermute x2, starting transfers between devices, shards(): lax.ppermute(block, ('tensor', 'replica'), pairs).astype(F32)  4.46 us
    ppermute x2, waiting for transfers between devices, shards(): lax.ppermute(block, ('tensor', 'replica'), pairs).astype(F32)  4.44 us
    dot_general x1, matrix products, shards(): jnp.dot(spread, jnp.concatenate(up, axis=0), preferred_element_type=F32)  2.42 us
    ppermute x11, waiting for transfers between devices, shift(): return lax.ppermute(x, axis, [(i, (i + by) % size) for i in range(size)])  2.42 us
    dot_general x1, matrix products, shards(): jnp.einsum('rd,qd->rq', x, jnp.concatenate(down, axis=0), preferred_eleme...  1.28 us
  transfers between devices with their start and end apart: 13, of which 3 were waited for; matrix products, arithmetic and copies ran while one was open for 30% of the time, Pallas kernels for 0%

profile of v1, /device:TPU:0, one launch (start us, length us, event | category | flops | bytes accessed | tf_op | source)
XLA Modules:
  0.0 51.2 jit_solution(13669247781882294183)
XLA Ops:
  0.0 0.9 %fusion.18 = bf16[16,4608]{1,0:T(8,128)(2,1)S(1)} fusion(s32[]{:T(128)S(6)} %select_n.37, bf16[64,4096]{1,0:T(8,128)(2,1)} %bitcast.16, bf16[64,512]{1,0:T(8,128)(2,1)} %bitcast.19), kind=kLoop, calls=%fused_computation.25 | loop fusion | flops 294912 | bytes 737284 | tf_op jit(solution)/shard_map/concatenate | solution.py:30
  0.9 0.0 copy-start.3
  0.9 3.1 %collective-permute-start.3 = (bf16[16,4608]{1,0:T(8,128)(2,1)S(1)}, bf16[16,4608]{1,0:T(8,128)(2,1)S(1)}, u32[]{:S(2)}, u32[]{:S(2)}) collective-permute-start(bf16[16,4608]{1,0:T(8,128)(2,1)S(1)} %fusion.18), channel_id=1, source_target_pairs={{0,4},{4,8},{8,12},{12,0},{1,5},{5,9},{9,13},{13,1},{2,6},{6,10},{... | collective-permute-start | bytes 442376 | tf_op jit(solution)/shard_map/ppermute | solution.py:11
  4.0 2.6 %collective-permute-start.6 = (bf16[16,4608]{1,0:T(8,128)(2,1)S(1)}, bf16[16,4608]{1,0:T(8,128)(2,1)S(1)}, u32[]{:S(2)}, u32[]{:S(2)}) collective-permute-start(bf16[16,4608]{1,0:T(8,128)(2,1)S(1)} %fusion.18), channel_id=1, source_target_pairs={{0,8},{4,12},{8,0},{12,4},{1,9},{5,13},{9,1},{13,5},{2,10},{6,14},... | collective-permute-start | bytes 442376 | tf_op jit(solution)/shard_map/ppermute | solution.py:11
  6.6 1.3 %collective-permute-start.9 = (bf16[16,4608]{1,0:T(8,128)(2,1)S(1)}, bf16[16,4608]{1,0:T(8,128)(2,1)S(1)}, u32[]{:S(2)}, u32[]{:S(2)}) collective-permute-start(bf16[16,4608]{1,0:T(8,128)(2,1)S(1)} %fusion.18), channel_id=1, source_target_pairs={{0,12},{4,0},{8,4},{12,8},{1,13},{5,1},{9,5},{13,9},{2,14},{6,2},{... | collective-permute-start | bytes 442376 | tf_op jit(solution)/shard_map/ppermute | solution.py:11
  7.9 0.0 collective-permute-start.1
  8.0 6.6 %fusion.23 = (bf16[512,512]{1,0:T(8,128)(2,1)}, f32[512,512]{1,0:T(8,128)S(1)}) fusion(bf16[512,4096]{1,0:T(8,128)(2,1)} %param.5, bf16[4096,512]{1,0:T(8,128)(2,1)} %param.6), kind=kOutput, calls=%fused_computation.43 | convolution fusion | flops 2147745792 | bytes 9961472 | tf_op jit(solution)/shard_map/dot_general | solution.py:43
  14.5 1.3 %collective-permute-start = (bf16[512,512]{1,0:T(8,128)(2,1)}, bf16[512,512]{1,0:T(8,128)(2,1)}, u32[]{:S(2)}, u32[]{:S(2)}) collective-permute-start(bf16[512,512]{1,0:T(8,128)(2,1)} %get-tuple-element.7), channel_id=1, source_target_pairs={{1,3},{2,0},{5,7},{6,4},{9,11},{10,8},{13,15},{14,12},{17,19},{18,... | collective-permute-start | bytes 1572872 | tf_op jit(solution)/shard_map/ppermute | solution.py:62
  15.8 0.0 copy-done.3
  15.8 0.1 broadcast_compare_fusion
  15.9 0.0 copy-start.1
  15.9 0.0 copy-start.4
  15.9 0.0 collective-permute-done.3
  15.9 1.6 %collective-permute-start.4 = (bf16[16,4608]{1,0:T(8,128)(2,1)S(1)}, bf16[16,4608]{1,0:T(8,128)(2,1)S(1)}, u32[]{:S(2)}, u32[]{:S(2)}) collective-permute-start(bf16[16,4608]{1,0:T(8,128)(2,1)S(1)} %collective-permute-done.3), channel_id=1, source_target_pairs={{0,16},{16,0},{1,17},{17,1},{2,18},{18,2},{3,19},{19,3},{4,20},{20... | collective-permute-start | bytes 442376 | tf_op jit(solution)/shard_map/ppermute | solution.py:11
  17.5 0.0 collective-permute-done.6
  17.5 0.6 %collective-permute-start.7 = (bf16[16,4608]{1,0:T(8,128)(2,1)S(1)}, bf16[16,4608]{1,0:T(8,128)(2,1)S(1)}, u32[]{:S(2)}, u32[]{:S(2)}) collective-permute-start(bf16[16,4608]{1,0:T(8,128)(2,1)S(1)} %collective-permute-done.6), channel_id=1, source_target_pairs={{0,16},{16,0},{1,17},{17,1},{2,18},{18,2},{3,19},{19,3},{4,20},{20... | collective-permute-start | bytes 442376 | tf_op jit(solution)/shard_map/ppermute | solution.py:11
  18.1 0.0 collective-permute-done.9
  18.1 1.6 %collective-permute-start.10 = (bf16[16,4608]{1,0:T(8,128)(2,1)S(1)}, bf16[16,4608]{1,0:T(8,128)(2,1)S(1)}, u32[]{:S(2)}, u32[]{:S(2)}) collective-permute-start(bf16[16,4608]{1,0:T(8,128)(2,1)S(1)} %collective-permute-done.9), channel_id=1, source_target_pairs={{0,16},{16,0},{1,17},{17,1},{2,18},{18,2},{3,19},{19,3},{4,20},{20... | collective-permute-start | bytes 442376 | tf_op jit(solution)/shard_map/ppermute | solution.py:11
  19.7 1.4 %collective-permute-done.4 = bf16[16,4608]{1,0:T(8,128)(2,1)S(1)} collective-permute-done((bf16[16,4608]{1,0:T(8,128)(2,1)S(1)}, bf16[16,4608]{1,0:T(8,128)(2,1)S(1)}, u32[]{:S(2)}, u32[]{:S(2)}) %collective-permute-start.4) | collective-permute-done | bytes 147488 | tf_op jit(solution)/shard_map/ppermute | solution.py:11
  21.2 4.0 %collective-permute-start.5 = (bf16[32,4608]{1,0:T(8,128)(2,1)S(1)}, bf16[32,4608]{1,0:T(8,128)(2,1)S(1)}, u32[]{:S(2)}, u32[]{:S(2)}) collective-permute-start(bf16[32,4608]{1,0:T(8,128)(2,1)S(1)} %pad_maximum_fusion), channel_id=1, source_target_pairs={{0,1},{1,0},{2,3},{3,2},{4,5},{5,4},{6,7},{7,6},{8,9},{9,8},{10,11... | collective-permute-start | bytes 884744 | tf_op jit(solution)/shard_map/ppermute | solution.py:11
  25.1 0.0 collective-permute-done.7
  25.1 2.3 %collective-permute-start.8 = (bf16[32,4608]{1,0:T(8,128)(2,1)S(1)}, bf16[32,4608]{1,0:T(8,128)(2,1)S(1)}, u32[]{:S(2)}, u32[]{:S(2)}) collective-permute-start(bf16[32,4608]{1,0:T(8,128)(2,1)S(1)} %pad_maximum_fusion.1), channel_id=1, source_target_pairs={{0,1},{1,0},{2,3},{3,2},{4,5},{5,4},{6,7},{7,6},{8,9},{9,8},{10,11... | collective-permute-start | bytes 884744 | tf_op jit(solution)/shard_map/ppermute | solution.py:11
  27.4 0.0 collective-permute-done.10
  27.4 1.6 %collective-permute-start.11 = (bf16[32,4608]{1,0:T(8,128)(2,1)S(1)}, bf16[32,4608]{1,0:T(8,128)(2,1)S(1)}, u32[]{:S(2)}, u32[]{:S(2)}) collective-permute-start(bf16[32,4608]{1,0:T(8,128)(2,1)S(1)} %pad_maximum_fusion.2), channel_id=1, source_target_pairs={{0,1},{1,0},{2,3},{3,2},{4,5},{5,4},{6,7},{7,6},{8,9},{9,8},{10,11... | collective-permute-start | bytes 884744 | tf_op jit(solution)/shard_map/ppermute | solution.py:11
  29.0 0.0 collective-permute-done.5
  29.1 0.0 collective-permute-done.8
  29.2 1.0 %collective-permute-done.11 = bf16[32,4608]{1,0:T(8,128)(2,1)S(1)} collective-permute-done((bf16[32,4608]{1,0:T(8,128)(2,1)S(1)}, bf16[32,4608]{1,0:T(8,128)(2,1)S(1)}, u32[]{:S(2)}, u32[]{:S(2)}) %collective-permute-start.11) | collective-permute-done | bytes 294944 | tf_op jit(solution)/shard_map/ppermute | solution.py:11
  30.2 0.0 copy-start
  30.2 0.8 %copy-done = bf16[64,4608]{1,0:T(8,128)(2,1)} copy-done((bf16[64,4608]{1,0:T(8,128)(2,1)}, bf16[64,4608]{1,0:T(8,128)(2,1)S(1)}, u32[]{:S(2)}) %copy-start) | copy-done | bytes 589848
  31.1 0.0 copy-done.1
  31.1 0.0 copy-done.4
  31.1 1.3 %fusion = f32[256,512]{1,0:T(8,128)S(1)} fusion(bf16[512,4096]{1,0:T(8,128)(2,1)S(1)} %copy-done.4, bf16[64,4096]{1,0:T(8,128)(2,1)S(1)} %slice.26, bf16[64,4096]{1,0:T(8,128)(2,1)S(1)} %slice.25, bf16[64,4096]{1,0:T(8,128)(2,1)S(1)} %slice.24, bf16[64,4096]{1,0:T(8,128)(2,1)S(1)} %bitcast.17), kind=kOutput, calls=%fused_computation | convolution fusion | flops 1082130432 | bytes 6815744 | tf_op jit(solution)/shard_map/rd,qd->rq/dot_general | solution.py:66
  32.4 0.1 select_reduce_fusion
  32.5 0.0 copy-start.2
  32.5 1.6 %collective-permute-start.12 = (bf16[512,64]{0,1:T(8,128)(2,1)S(1)}, bf16[512,64]{0,1:T(8,128)(2,1)}, u32[]{:S(2)}, u32[]{:S(2)}) collective-permute-start(bf16[512,64]{0,1:T(8,128)(2,1)S(1)} %convert_element_type.36), channel_id=1, source_target_pairs={{0,2},{2,0},{1,3},{3,1},{4,6},{6,4},{5,7},{7,5},{8,10},{10,8},{9,1... | collective-permute-start | bytes 196616 | tf_op jit(solution)/shard_map/ppermute | solution.py:11
  34.1 0.0 collective-permute-done.1
  34.1 5.3 %fusion.22 = (bf16[512,512]{1,0:T(8,128)(2,1)}, f32[512,512]{1,0:T(8,128)S(1)}) fusion(bf16[512,4096]{1,0:T(8,128)(2,1)S(1)} %copy-done.4, bf16[4096,512]{1,0:T(8,128)(2,1)} %collective-permute-done.1), kind=kOutput, calls=%fused_computation.42 | convolution fusion | flops 2147745792 | bytes 9961472 | tf_op jit(solution)/shard_map/dot_general | solution.py:43
  39.4 3.2 %collective-permute-start.2 = (bf16[512,512]{1,0:T(8,128)(2,1)}, bf16[512,512]{1,0:T(8,128)(2,1)}, u32[]{:S(2)}, u32[]{:S(2)}) collective-permute-start(bf16[512,512]{1,0:T(8,128)(2,1)} %get-tuple-element.5), channel_id=1, source_target_pairs={{0,2},{3,1},{4,6},{7,5},{8,10},{11,9},{12,14},{15,13},{16,18},{19,... | collective-permute-start | bytes 1572872 | tf_op jit(solution)/shard_map/ppermute | solution.py:62
  42.6 0.8 %slice.29 = bf16[64,512]{1,0:T(8,128)(2,1)S(1)} slice(bf16[64,4608]{1,0:T(8,128)(2,1)} %copy-done), slice={[0:64], [4096:4608]} | slice | bytes 131072 | tf_op jit(solution)/shard_map/slice | solution.py:39
  43.4 0.0 collective-permute-done.12
  43.4 0.9 %add_convert_fusion.1 = bf16[512,64]{0,1:T(8,128)(2,1)S(1)} fusion(f32[512,64]{0,1:T(8,128)S(1)} %select_reduce_fusion, bf16[512,64]{0,1:T(8,128)(2,1)} %collective-permute-done.12), kind=kLoop, calls=%fused_computation.26 | loop fusion | flops 98304 | bytes 262144 | tf_op jit(solution)/shard_map/convert_element_type | solution.py:72
  44.3 0.0 collective-permute-done
  44.3 4.4 %collective-permute-done.2 = bf16[512,512]{1,0:T(8,128)(2,1)} collective-permute-done((bf16[512,512]{1,0:T(8,128)(2,1)}, bf16[512,512]{1,0:T(8,128)(2,1)}, u32[]{:S(2)}, u32[]{:S(2)}) %collective-permute-start.2) | collective-permute-done | bytes 524320 | tf_op jit(solution)/shard_map/ppermute | solution.py:62
  48.8 0.0 copy-done.2
  48.8 2.4 %add_convert_fusion = bf16[512,512]{1,0:T(8,128)(2,1)} fusion(bf16[512,512]{1,0:T(8,128)(2,1)} %collective-permute-done.2, f32[512,512]{1,0:T(8,128)S(1)} %get-tuple-element.6, bf16[512,512]{1,0:T(8,128)(2,1)} %collective-permute-done, f32[512,512]{1,0:T(8,128)S(1)} %get-tuple-element.8, pred[]{:T(512)S(6)} %and.19, pred[]{:T(512)S(6)} %and.18, ...), kind=kOutput, calls=%fused_computation.10 | convolution fusion | flops 138149888 | bytes 4194306 | tf_op jit(solution)/shard_map/dot_general | solution.py:74
  (20 shorter events, 0.4 us)
Async XLA Ops:
  0.9 14.9 %copy-start.3 = (s32[512,1]{0,1:T(1,128)S(1)}, s32[512,1]{0,1:T(1,128)}, u32[]{:S(2)}) copy-start(s32[512,1]{0,1:T(1,128)} %param.9) | copy-start | bytes 6148
  0.9 15.0 %collective-permute-start.3 = (bf16[16,4608]{1,0:T(8,128)(2,1)S(1)}, bf16[16,4608]{1,0:T(8,128)(2,1)S(1)}, u32[]{:S(2)}, u32[]{:S(2)}) collective-permute-start(bf16[16,4608]{1,0:T(8,128)(2,1)S(1)} %fusion.18), channel_id=1, source_target_pairs={{0,4},{4,8},{8,12},{12,0},{1,5},{5,9},{9,13},{13,1},{2,6},{6,10},{... | collective-permute-start | bytes 442376 | tf_op jit(solution)/shard_map/ppermute | solution.py:11
  4.0 13.5 %collective-permute-start.6 = (bf16[16,4608]{1,0:T(8,128)(2,1)S(1)}, bf16[16,4608]{1,0:T(8,128)(2,1)S(1)}, u32[]{:S(2)}, u32[]{:S(2)}) collective-permute-start(bf16[16,4608]{1,0:T(8,128)(2,1)S(1)} %fusion.18), channel_id=1, source_target_pairs={{0,8},{4,12},{8,0},{12,4},{1,9},{5,13},{9,1},{13,5},{2,10},{6,14},... | collective-permute-start | bytes 442376 | tf_op jit(solution)/shard_map/ppermute | solution.py:11
  6.6 11.5 %collective-permute-start.9 = (bf16[16,4608]{1,0:T(8,128)(2,1)S(1)}, bf16[16,4608]{1,0:T(8,128)(2,1)S(1)}, u32[]{:S(2)}, u32[]{:S(2)}) collective-permute-start(bf16[16,4608]{1,0:T(8,128)(2,1)S(1)} %fusion.18), channel_id=1, source_target_pairs={{0,12},{4,0},{8,4},{12,8},{1,13},{5,1},{9,5},{13,9},{2,14},{6,2},{... | collective-permute-start | bytes 442376 | tf_op jit(solution)/shard_map/ppermute | solution.py:11
  7.9 26.1 %collective-permute-start.1 = (bf16[4096,512]{1,0:T(8,128)(2,1)}, bf16[4096,512]{1,0:T(8,128)(2,1)}, u32[]{:S(2)}, u32[]{:S(2)}) collective-permute-start(bf16[4096,512]{1,0:T(8,128)(2,1)} %param.6), channel_id=1, source_target_pairs={{0,1},{1,0},{2,3},{3,2},{4,5},{5,4},{6,7},{7,6},{8,9},{9,8},{10,11... | collective-permute-start | bytes 12582920 | tf_op jit(solution)/shard_map/ppermute | solution.py:11
  14.5 29.8 %collective-permute-start = (bf16[512,512]{1,0:T(8,128)(2,1)}, bf16[512,512]{1,0:T(8,128)(2,1)}, u32[]{:S(2)}, u32[]{:S(2)}) collective-permute-start(bf16[512,512]{1,0:T(8,128)(2,1)} %get-tuple-element.7), channel_id=1, source_target_pairs={{1,3},{2,0},{5,7},{6,4},{9,11},{10,8},{13,15},{14,12},{17,19},{18,... | collective-permute-start | bytes 1572872 | tf_op jit(solution)/shard_map/ppermute | solution.py:62
  15.9 15.2 %copy-start.1 = (bf16[1,4096,64]{1,2,0:T(8,128)(2,1)S(1)}, bf16[1,4096,64]{1,2,0:T(8,128)(2,1)}, u32[]{:S(2)}) copy-start(bf16[1,4096,64]{1,2,0:T(8,128)(2,1)} %param.7) | copy-start | bytes 1572868
  15.9 15.2 %copy-start.4 = (bf16[512,4096]{1,0:T(8,128)(2,1)S(1)}, bf16[512,4096]{1,0:T(8,128)(2,1)}, u32[]{:S(2)}) copy-start(bf16[512,4096]{1,0:T(8,128)(2,1)} %param.5) | copy-start | bytes 12582916
  15.9 5.2 %collective-permute-start.4 = (bf16[16,4608]{1,0:T(8,128)(2,1)S(1)}, bf16[16,4608]{1,0:T(8,128)(2,1)S(1)}, u32[]{:S(2)}, u32[]{:S(2)}) collective-permute-start(bf16[16,4608]{1,0:T(8,128)(2,1)S(1)} %collective-permute-done.3), channel_id=1, source_target_pairs={{0,16},{16,0},{1,17},{17,1},{2,18},{18,2},{3,19},{19,3},{4,20},{20... | collective-permute-start | bytes 442376 | tf_op jit(solution)/shard_map/ppermute | solution.py:11
  17.5 7.6 %collective-permute-start.7 = (bf16[16,4608]{1,0:T(8,128)(2,1)S(1)}, bf16[16,4608]{1,0:T(8,128)(2,1)S(1)}, u32[]{:S(2)}, u32[]{:S(2)}) collective-permute-start(bf16[16,4608]{1,0:T(8,128)(2,1)S(1)} %collective-permute-done.6), channel_id=1, source_target_pairs={{0,16},{16,0},{1,17},{17,1},{2,18},{18,2},{3,19},{19,3},{4,20},{20... | collective-permute-start | bytes 442376 | tf_op jit(solution)/shard_map/ppermute | solution.py:11
  18.1 9.3 %collective-permute-start.10 = (bf16[16,4608]{1,0:T(8,128)(2,1)S(1)}, bf16[16,4608]{1,0:T(8,128)(2,1)S(1)}, u32[]{:S(2)}, u32[]{:S(2)}) collective-permute-start(bf16[16,4608]{1,0:T(8,128)(2,1)S(1)} %collective-permute-done.9), channel_id=1, source_target_pairs={{0,16},{16,0},{1,17},{17,1},{2,18},{18,2},{3,19},{19,3},{4,20},{20... | collective-permute-start | bytes 442376 | tf_op jit(solution)/shard_map/ppermute | solution.py:11
  21.2 7.9 %collective-permute-start.5 = (bf16[32,4608]{1,0:T(8,128)(2,1)S(1)}, bf16[32,4608]{1,0:T(8,128)(2,1)S(1)}, u32[]{:S(2)}, u32[]{:S(2)}) collective-permute-start(bf16[32,4608]{1,0:T(8,128)(2,1)S(1)} %pad_maximum_fusion), channel_id=1, source_target_pairs={{0,1},{1,0},{2,3},{3,2},{4,5},{5,4},{6,7},{7,6},{8,9},{9,8},{10,11... | collective-permute-start | bytes 884744 | tf_op jit(solution)/shard_map/ppermute | solution.py:11
  25.1 4.0 %collective-permute-start.8 = (bf16[32,4608]{1,0:T(8,128)(2,1)S(1)}, bf16[32,4608]{1,0:T(8,128)(2,1)S(1)}, u32[]{:S(2)}, u32[]{:S(2)}) collective-permute-start(bf16[32,4608]{1,0:T(8,128)(2,1)S(1)} %pad_maximum_fusion.1), channel_id=1, source_target_pairs={{0,1},{1,0},{2,3},{3,2},{4,5},{5,4},{6,7},{7,6},{8,9},{9,8},{10,11... | collective-permute-start | bytes 884744 | tf_op jit(solution)/shard_map/ppermute | solution.py:11
  27.4 2.8 %collective-permute-start.11 = (bf16[32,4608]{1,0:T(8,128)(2,1)S(1)}, bf16[32,4608]{1,0:T(8,128)(2,1)S(1)}, u32[]{:S(2)}, u32[]{:S(2)}) collective-permute-start(bf16[32,4608]{1,0:T(8,128)(2,1)S(1)} %pad_maximum_fusion.2), channel_id=1, source_target_pairs={{0,1},{1,0},{2,3},{3,2},{4,5},{5,4},{6,7},{7,6},{8,9},{9,8},{10,11... | collective-permute-start | bytes 884744 | tf_op jit(solution)/shard_map/ppermute | solution.py:11
  30.2 0.8 %copy-start = (bf16[64,4608]{1,0:T(8,128)(2,1)}, bf16[64,4608]{1,0:T(8,128)(2,1)S(1)}, u32[]{:S(2)}) copy-start(bf16[64,4608]{1,0:T(8,128)(2,1)S(1)} %constant_dynamic-update-slice_fusion.6) | copy-start | bytes 1769476
  32.5 16.3 %copy-start.2 = (bf16[1,64,512]{2,1,0:T(8,128)(2,1)S(1)}, bf16[1,64,512]{2,1,0:T(8,128)(2,1)}, u32[]{:S(2)}) copy-start(bf16[1,64,512]{2,1,0:T(8,128)(2,1)} %param.8) | copy-start | bytes 196612
  32.5 11.0 %collective-permute-start.12 = (bf16[512,64]{0,1:T(8,128)(2,1)S(1)}, bf16[512,64]{0,1:T(8,128)(2,1)}, u32[]{:S(2)}, u32[]{:S(2)}) collective-permute-start(bf16[512,64]{0,1:T(8,128)(2,1)S(1)} %convert_element_type.36), channel_id=1, source_target_pairs={{0,2},{2,0},{1,3},{3,1},{4,6},{6,4},{5,7},{7,5},{8,10},{10,8},{9,1... | collective-permute-start | bytes 196616 | tf_op jit(solution)/shard_map/ppermute | solution.py:11
  39.4 9.4 %collective-permute-start.2 = (bf16[512,512]{1,0:T(8,128)(2,1)}, bf16[512,512]{1,0:T(8,128)(2,1)}, u32[]{:S(2)}, u32[]{:S(2)}) collective-permute-start(bf16[512,512]{1,0:T(8,128)(2,1)} %get-tuple-element.5), channel_id=1, source_target_pairs={{0,2},{3,1},{4,6},{7,5},{8,10},{11,9},{12,14},{15,13},{16,18},{19,... | collective-permute-start | bytes 1572872 | tf_op jit(solution)/shard_map/ppermute | solution.py:62

commit v2 on v1

v2 whole, which is shorter than its diff:
```python
import functools

import jax
import jax.numpy as jnp
from jax import lax
from jax.experimental import pallas as pl
from jax.experimental.pallas import tpu as pltpu
from jax.sharding import PartitionSpec as P

F32 = jnp.float32
BF16 = jnp.bfloat16
VMEM = pl.BlockSpec(memory_space=pltpu.VMEM)
SMEM = pl.BlockSpec(memory_space=pltpu.SMEM)
BATCH = 4


def call(kernel, outs, args, scratch=(), flops=0, limit=16, specs=None):
    size = sum(a.size * a.dtype.itemsize for a in args)
    return pl.pallas_call(
        kernel,
        out_shape=outs,
        in_specs=specs or [VMEM] * len(args),
        out_specs=jax.tree.map(lambda _: VMEM, outs),
        scratch_shapes=scratch,
        compiler_params=pltpu.CompilerParams(vmem_limit_bytes=limit << 20),
        cost_estimate=pl.CostEstimate(flops=flops, bytes_accessed=size, transcendentals=0),
    )(*args)


def base_kernel(x_ref, v_ref, o_ref):
    o_ref[...] = jnp.dot(x_ref[...], v_ref[...], preferred_element_type=F32).astype(BF16)


def base_terms(x, v):
    out = jax.ShapeDtypeStruct((x.shape[0], v.shape[1]), BF16)
    return call(base_kernel, out, (x, v), flops=2 * x.size * v.shape[1])


def fill(scratch, group, lanes):
    row = 0
    for parts in group:
        for part in parts:
            scratch[row : row + part.shape[0], :] = part[:, lanes]
            row += part.shape[0]
    return row


def down_kernel(layout, wide, owner_ref, idx_ref, x_ref, *refs):
    parts, (low_ref, sent_ref, scratch) = refs[:-3], refs[-3:]
    groups, at = [], 0
    for count in layout:
        groups.append(parts[at : at + count])
        at += count
    rank = low_ref.shape[0]
    low = jnp.zeros(low_ref.shape, F32)
    for first in range(0, len(groups), BATCH):
        group = groups[first : first + BATCH]
        rows = fill(scratch, group, slice(0, wide))
        prod = lax.dot_general(
            scratch[:rows, :], x_ref[...], (((1,), (1,)), ((), ())), preferred_element_type=F32
        )
        for k in range(len(group)):
            match = idx_ref[...] == owner_ref[first + k]
            low = low + jnp.where(match, prod[k * rank : (k + 1) * rank, :], 0.0)
    low_ref[...] = low
    sent_ref[...] = low.astype(BF16)


def last_kernel(layout, wide, owner_ref, here_ref, idx_ref, low_ref, *refs):
    counts, refs = layout, list(refs)
    take = lambda n: [refs.pop(0) for _ in range(n)]
    lows, parts = take(counts[0]), take(sum(counts[1]))
    blocks, recvs = take(counts[2]), take(counts[3])
    out_ref, up, spread = refs
    groups, at = [], 0
    for count in counts[1]:
        groups.append(parts[at : at + count])
        at += count
    rank, cols = low_ref.shape[0], out_ref.shape[1]
    low = low_ref[...]
    for other in lows:
        low = low + other[...].astype(F32)
    low = low.astype(BF16).astype(F32)
    lora = jnp.zeros(out_ref.shape, F32)
    for first in range(0, len(groups), BATCH):
        group = groups[first : first + BATCH]
        row = 0
        for k, members in enumerate(group):
            match = idx_ref[...] == owner_ref[first + k]
            spread[k * rank : (k + 1) * rank, :] = jnp.where(match, low, 0.0).astype(BF16)
            for part in members:
                begin = part.shape[1] - cols
                up[row : row + part.shape[0], :] = part[:, begin : begin + cols]
                row += part.shape[0]
        lora = lora + lax.dot_general(
            spread[:row, :], up[:row, :], (((0,), (0,)), ((), ())), preferred_element_type=F32
        )
    total = lora.astype(BF16).astype(F32)
    for recv in recvs:
        total = total + recv[...].astype(F32)
    for h, block in enumerate(blocks):
        total = total + jnp.where(here_ref[h] == 1, block[...].astype(F32), 0.0)
    out_ref[...] = total.astype(BF16)


def shift(x, axis, size, by):
    return lax.ppermute(x, axis, [(i, (i + by) % size) for i in range(size)])


def after(x, *others):
    return lax.optimization_barrier((x, *others))[0]


def build(mesh):
    groups, adapters = mesh.shape["groups"], mesh.shape["adapter"]
    tensors, replicas = mesh.shape["tensor"], mesh.shape["replica"]

    def others(x, axis, size):
        return [shift(x, axis, size, by) for by in range(1, size)]

    def shards(x, v, d, u, idx):
        g, a = lax.axis_index("groups"), lax.axis_index("adapter")
        t, r = lax.axis_index("tensor"), lax.axis_index("replica")
        tokens, rank, wide = x.shape[0], d.shape[2], d.shape[1]
        cols, width = u.shape[2], v.shape[1]
        per = width // cols
        row = idx.reshape(1, tokens)
        owner = lax.rem(a - jnp.arange(adapters, dtype=jnp.int32) + adapters, adapters)

        held = [v] + others(v, "replica", replicas)

        down = d[0].T
        own = jnp.concatenate([down, u[0]], axis=1)
        share = rank // (groups * replicas)
        mine = lax.dynamic_slice_in_dim(own, (g * replicas + r) * share, share, 0)
        first = [shift(mine, "adapter", adapters, by) for by in range(1, adapters)]

        blocks, recvs, here = [], [], []
        for h in range(replicas):
            terms = base_terms(x, held[h])
            half = lax.rem(r - h + replicas, replicas)
            begin = half * per

            def cut(n):
                if per == 1:
                    return terms
                at = jnp.clip(n - begin, 0, per - 1) * cols
                return lax.dynamic_slice_in_dim(terms, at, cols, 1)

            blocks.append(cut(t))
            here.append(((t >= begin) & (t < begin + per)).astype(jnp.int32))
            for by in range(1, tensors):
                pairs = [
                    (ti * replicas + ri, (ti + by) % tensors * replicas + ri)
                    for ti in range(tensors)
                    for ri in range(replicas)
                    if ((ti + by) % tensors) // per == (ri - h) % replicas
                ]
                if pairs:
                    block = cut(lax.rem(t + by, tensors))
                    recvs.append(lax.ppermute(block, ("tensor", "replica"), pairs))

        parts = []
        for part in first:
            members = [part] + others(part, "groups", groups)
            both = jnp.concatenate(members, axis=0) if groups > 1 else part
            members += others(both, "replica", replicas)
            parts.append(members)

        layout = [1] + [len(members) for members in parts]
        refs = [ref for members in parts for ref in members]
        low, sent = call(
            functools.partial(down_kernel, layout, wide),
            (jax.ShapeDtypeStruct((rank, tokens), F32), jax.ShapeDtypeStruct((rank, tokens), BF16)),
            (owner, row, x, down, *refs),
            scratch=[pltpu.VMEM((min(BATCH, adapters) * rank, wide), BF16)],
            flops=2 * x.size * rank * adapters,
            specs=[SMEM] + [VMEM] * (3 + len(refs)),
        )
        lows = others(sent, "tensor", tensors)
        return call(
            functools.partial(last_kernel, (len(lows), layout, len(blocks), len(recvs)), wide),
            jax.ShapeDtypeStruct((tokens, cols), BF16),
            (owner, jnp.stack(here), row, low, *lows, u[0], *refs, *blocks, *recvs),
            scratch=[
                pltpu.VMEM((min(BATCH, adapters) * rank, cols), BF16),
                pltpu.VMEM((min(BATCH, adapters) * rank, tokens), BF16),
            ],
            flops=2 * tokens * rank * adapters * cols,
            specs=[SMEM] * 2 + [VMEM] * (3 + len(lows) + len(refs) + len(blocks) + len(recvs)),
        )

    return shards


def solution(mesh):
    return jax.shard_map(
        build(mesh),
        mesh=mesh,
        in_specs=(
            P(("groups", "adapter", "replica"), "tensor"),
            P("tensor", "replica"),
            P("adapter", "tensor", None),
            P("adapter", None, "tensor"),
            P(("groups", "adapter", "replica"), None),
        ),
        out_specs=P(("groups", "adapter", "replica"), "tensor"),
        check_vma=False,
    )
```

time: 51.8 us -> 54.6 us (1.054)
  the two profiles are of different devices: /device:TPU:0 before, /device:TPU:24 now
where the time goes in v2:
time: 54.6 us; the launch traced here: 54.2 us
  starting transfers between devices  18.1 us (33%)
  waiting for transfers between devices  15 us (27%)
  Pallas kernels  11.2 us (21%)
  local copies, waits for them, and re-layouts  6.58 us (12%)
  other arithmetic  3.22 us (6%)
    ppermute x11, waiting for transfers between devices, shift(): return lax.ppermute(x, axis, [(i, (i + by) % size) for i in range(size)])  15 us
    ppermute x11, starting transfers between devices, shift(): return lax.ppermute(x, axis, [(i, (i + by) % size) for i in range(size)])  13.6 us
    pallas_call x4, Pallas kernels, call(): pl.pallas_call(kernel, out_shape=outs, in_specs=specs or [VMEM] * len(arg...  11.2 us
    unnamed x12, local copies, waits for them, and re-layouts  6.58 us
    ppermute x2, starting transfers between devices, shards(): recvs.append(lax.ppermute(block, ('tensor', 'replica'), pairs))  4.47 us
    concatenate x3, other arithmetic, shards(): both = jnp.concatenate(members, axis=0) if groups > 1 else part  2.22 us
  transfers between devices with their start and end apart: 13, of which 4 were waited for; matrix products, arithmetic and copies ran while one was open for 6% of the time, Pallas kernels for 16%

profile of v2, /device:TPU:24, one launch (start us, length us, event | category | flops | bytes accessed | tf_op | source)
XLA Modules:
  0.0 54.2 jit_solution(4735335650907019684)
XLA Ops:
  0.0 0.0 collective-permute-start.10
  0.0 0.9 %fusion = bf16[16,4608]{1,0:T(8,128)(2,1)S(1)} fusion(s32[]{:T(128)S(6)} %select_n.3, bf16[64,4096]{1,0:T(8,128)(2,1)} %bitcast.7, bf16[64,512]{1,0:T(8,128)(2,1)} %bitcast.9), kind=kLoop, calls=%fused_computation.5 | loop fusion | flops 294912 | bytes 737284 | tf_op jit(solution)/shard_map/concatenate | solution.py:133
  0.9 0.4 collective-permute-start.3
  1.3 0.2 collective-permute-start.6
  1.5 3.6 %collective-permute-start = (bf16[16,4608]{1,0:T(8,128)(2,1)S(1)}, bf16[16,4608]{1,0:T(8,128)(2,1)S(1)}, u32[]{:S(2)}, u32[]{:S(2)}) collective-permute-start(bf16[16,4608]{1,0:T(8,128)(2,1)S(1)} %fusion), channel_id=1, source_target_pairs={{0,4},{4,8},{8,12},{12,0},{1,5},{5,9},{9,13},{13,1},{2,6},{6,10},{... | collective-permute-start | bytes 442376 | tf_op jit(solution)/shard_map/ppermute | solution.py:107
  5.2 9.3 %collective-permute-done.3.refs_4_.refs_5_ = bf16[16,4608]{1,0:T(8,128)(2,1)S(1)} collective-permute-done((bf16[16,4608]{1,0:T(8,128)(2,1)S(1)}, bf16[16,4608]{1,0:T(8,128)(2,1)S(1)}, u32[]{:S(2)}, u32[]{:S(2)}) %collective-permute-start.3) | collective-permute-done | bytes 147488 | tf_op jit(solution)/shard_map/ppermute | solution.py:107
  14.5 1.5 %collective-permute-start.4 = (bf16[16,4608]{1,0:T(8,128)(2,1)S(1)}, bf16[16,4608]{1,0:T(8,128)(2,1)S(1)}, u32[]{:S(2)}, u32[]{:S(2)}) collective-permute-start(bf16[16,4608]{1,0:T(8,128)(2,1)S(1)} %collective-permute-done.3.refs_4_.refs_5_), channel_id=1, source_target_pairs={{0,16},{16,0},{1,17},{17,1},{2,18},{18,2},{3,19},{19,3},{4,20},{20... | collective-permute-start | bytes 442376 | tf_op jit(solution)/shard_map/ppermute | solution.py:107
  16.0 0.0 copy-start
  16.0 2.2 %copy-done = bf16[512,4096]{1,0:T(8,128)(2,1)S(1)} copy-done((bf16[512,4096]{1,0:T(8,128)(2,1)S(1)}, bf16[512,4096]{1,0:T(8,128)(2,1)}, u32[]{:S(2)}) %copy-start) | copy-done | bytes 4194328
  18.2 0.0 copy-start.2
  18.2 2.2 %copy-done.2 = bf16[4096,512]{1,0:T(8,128)(2,1)S(1)} copy-done((bf16[4096,512]{1,0:T(8,128)(2,1)S(1)}, bf16[4096,512]{1,0:T(8,128)(2,1)}, u32[]{:S(2)}) %copy-start.2) | copy-done | bytes 4194328
  20.4 2.3 %shard_map.56.refs_11_ = bf16[512,512]{1,0:T(8,128)(2,1)S(1)} custom-call(bf16[512,4096]{1,0:T(8,128)(2,1)S(1)} %copy-done, bf16[4096,512]{1,0:T(8,128)(2,1)S(1)} %copy-done.2), custom_call_target="tpu_custom_call" | custom-call | flops 2147483648 | bytes 8388608 | tf_op jit(solution)/shard_map/pallas_call | solution.py:19
  22.7 1.3 %collective-permute-start.11 = (bf16[512,512]{1,0:T(8,128)(2,1)S(1)}, bf16[512,512]{1,0:T(8,128)(2,1)}, u32[]{:S(2)}, u32[]{:S(2)}) collective-permute-start(bf16[512,512]{1,0:T(8,128)(2,1)S(1)} %shard_map.56.refs_11_), channel_id=1, source_target_pairs={{1,3},{2,0},{5,7},{6,4},{9,11},{10,8},{13,15},{14,12},{17,19},{18,... | collective-permute-start | bytes 1572872 | tf_op jit(solution)/shard_map/ppermute | solution.py:161
  24.0 0.0 collective-permute-done.6.refs_7_.refs_8_
  24.0 0.6 %collective-permute-start.7 = (bf16[16,4608]{1,0:T(8,128)(2,1)S(1)}, bf16[16,4608]{1,0:T(8,128)(2,1)S(1)}, u32[]{:S(2)}, u32[]{:S(2)}) collective-permute-start(bf16[16,4608]{1,0:T(8,128)(2,1)S(1)} %collective-permute-done.6.refs_7_.refs_8_), channel_id=1, source_target_pairs={{0,16},{16,0},{1,17},{17,1},{2,18},{18,2},{3,19},{19,3},{4,20},{20... | collective-permute-start | bytes 442376 | tf_op jit(solution)/shard_map/ppermute | solution.py:107
  24.6 0.0 collective-permute-done.refs_1_.refs_2_
  24.6 1.5 %collective-permute-start.1 = (bf16[16,4608]{1,0:T(8,128)(2,1)S(1)}, bf16[16,4608]{1,0:T(8,128)(2,1)S(1)}, u32[]{:S(2)}, u32[]{:S(2)}) collective-permute-start(bf16[16,4608]{1,0:T(8,128)(2,1)S(1)} %collective-permute-done.refs_1_.refs_2_), channel_id=1, source_target_pairs={{0,16},{16,0},{1,17},{17,1},{2,18},{18,2},{3,19},{19,3},{4,20},{20... | collective-permute-start | bytes 442376 | tf_op jit(solution)/shard_map/ppermute | solution.py:107
  26.1 0.0 collective-permute-done.4.refs_5_.refs_6_
  26.1 0.7 %pad_maximum_fusion.1 = bf16[32,4608]{1,0:T(8,128)(2,1)} fusion(bf16[16,4608]{1,0:T(8,128)(2,1)S(1)} %collective-permute-done.4.refs_5_.refs_6_, bf16[16,4608]{1,0:T(8,128)(2,1)S(1)} %collective-permute-done.3.refs_4_.refs_5_), kind=kLoop, calls=%fused_computation.3 | loop fusion | flops 589824 | bytes 589824 | tf_op jit(solution)/shard_map/concatenate | solution.py:166
  26.8 1.7 %collective-permute-start.5 = (bf16[32,4608]{1,0:T(8,128)(2,1)}, bf16[32,4608]{1,0:T(8,128)(2,1)S(1)}, u32[]{:S(2)}, u32[]{:S(2)}) collective-permute-start(bf16[32,4608]{1,0:T(8,128)(2,1)} %pad_maximum_fusion.1), channel_id=1, source_target_pairs={{0,1},{1,0},{2,3},{3,2},{4,5},{5,4},{6,7},{7,6},{8,9},{9,8},{10,11... | collective-permute-start | bytes 884744 | tf_op jit(solution)/shard_map/ppermute | solution.py:107
  28.6 0.9 %collective-permute-done.7.refs_8_.refs_9_ = bf16[16,4608]{1,0:T(8,128)(2,1)S(1)} collective-permute-done((bf16[16,4608]{1,0:T(8,128)(2,1)S(1)}, bf16[16,4608]{1,0:T(8,128)(2,1)S(1)}, u32[]{:S(2)}, u32[]{:S(2)}) %collective-permute-start.7) | collective-permute-done | bytes 147488 | tf_op jit(solution)/shard_map/ppermute | solution.py:107
  29.4 0.7 %pad_maximum_fusion.2 = bf16[32,4608]{1,0:T(8,128)(2,1)} fusion(bf16[16,4608]{1,0:T(8,128)(2,1)S(1)} %collective-permute-done.7.refs_8_.refs_9_, bf16[16,4608]{1,0:T(8,128)(2,1)S(1)} %collective-permute-done.6.refs_7_.refs_8_), kind=kLoop, calls=%fused_computation.4 | loop fusion | flops 589824 | bytes 589824 | tf_op jit(solution)/shard_map/concatenate | solution.py:166
  30.2 0.0 copy-start.3
  30.2 0.0 copy-start.5
  30.2 2.9 %collective-permute-start.8 = (bf16[32,4608]{1,0:T(8,128)(2,1)}, bf16[32,4608]{1,0:T(8,128)(2,1)S(1)}, u32[]{:S(2)}, u32[]{:S(2)}) collective-permute-start(bf16[32,4608]{1,0:T(8,128)(2,1)} %pad_maximum_fusion.2), channel_id=1, source_target_pairs={{0,1},{1,0},{2,3},{3,2},{4,5},{5,4},{6,7},{7,6},{8,9},{9,8},{10,11... | collective-permute-start | bytes 884744 | tf_op jit(solution)/shard_map/ppermute | solution.py:107
  33.1 0.0 collective-permute-done.10.v_ref
  33.1 4.5 %shard_map.57.refs_12_ = bf16[512,512]{1,0:T(8,128)(2,1)S(1)} custom-call(bf16[512,4096]{1,0:T(8,128)(2,1)S(1)} %copy-done, bf16[4096,512]{1,0:T(8,128)(2,1)} %collective-permute-done.10.v_ref), custom_call_target="tpu_custom_call" | custom-call | flops 2147483648 | bytes 8388608 | tf_op jit(solution)/shard_map/pallas_call | solution.py:19
  37.6 0.0 copy-start.4
  37.6 3.2 %collective-permute-start.12 = (bf16[512,512]{1,0:T(8,128)(2,1)S(1)}, bf16[512,512]{1,0:T(8,128)(2,1)}, u32[]{:S(2)}, u32[]{:S(2)}) collective-permute-start(bf16[512,512]{1,0:T(8,128)(2,1)S(1)} %shard_map.57.refs_12_), channel_id=1, source_target_pairs={{0,2},{3,1},{4,6},{7,5},{8,10},{11,9},{12,14},{15,13},{16,18},{19,... | collective-permute-start | bytes 1572872 | tf_op jit(solution)/shard_map/ppermute | solution.py:161
  40.8 0.0 collective-permute-done.1.refs_2_.refs_3_
  40.8 0.7 %pad_maximum_fusion = bf16[32,4608]{1,0:T(8,128)(2,1)} fusion(bf16[16,4608]{1,0:T(8,128)(2,1)S(1)} %collective-permute-done.1.refs_2_.refs_3_, bf16[16,4608]{1,0:T(8,128)(2,1)S(1)} %collective-permute-done.refs_1_.refs_2_), kind=kLoop, calls=%fused_computation.2 | loop fusion | flops 589824 | bytes 589824 | tf_op jit(solution)/shard_map/concatenate | solution.py:166
  41.5 0.0 collective-permute-start.2
  41.5 0.0 collective-permute-done.5.refs_6_.refs_7_
  41.5 0.0 collective-permute-done.8.refs_9_.refs_10_
  41.6 1.8 %collective-permute-done.2.refs_3_.refs_4_ = bf16[32,4608]{1,0:T(8,128)(2,1)S(1)} collective-permute-done((bf16[32,4608]{1,0:T(8,128)(2,1)}, bf16[32,4608]{1,0:T(8,128)(2,1)S(1)}, u32[]{:S(2)}, u32[]{:S(2)}) %collective-permute-start.2) | collective-permute-done | bytes 294944 | tf_op jit(solution)/shard_map/ppermute | solution.py:107
  43.3 0.0 copy-done.3
  43.3 0.0 copy-done.5
  43.3 0.0 copy-start.1
  43.3 2.2 %copy-done.1 = bf16[512,4096]{1,0:T(8,128)(2,1)S(1)} copy-done((bf16[512,4096]{1,0:T(8,128)(2,1)S(1)}, bf16[512,4096]{1,0:T(8,128)(2,1)}, u32[]{:S(2)}) %copy-start.1) | copy-done | bytes 4194328
  45.5 1.8 %shard_map.55 = (f32[64,512]{1,0:T(8,128)S(1)}, bf16[64,512]{1,0:T(8,128)(2,1)S(1)}) custom-call(s32[4]{0:T(128)S(1)} %compare_select_fusion.owner_ref, s32[1,512]{1,0:T(1,128)S(1)} %bitcast.11, bf16[512,4096]{1,0:T(8,128)(2,1)S(1)} %copy-done.1, bf16[64,4096]{1,0:T(8,128)(2,1)S(1)} %bitcast.8, bf16[16,4608]{1,0:T(8,128)(2,1)S(1)} %collective-permute-done.refs_1_.refs_2_, ...), custom_call_target="tpu_custom_call" | custom-call | flops 1073741824 | bytes 6490128 | tf_op jit(solution)/shard_map/pallas_call | solution.py:19
  47.3 1.2 %collective-permute-start.9 = (bf16[64,512]{1,0:T(8,128)(2,1)S(1)}, bf16[64,512]{1,0:T(8,128)(2,1)S(1)}, u32[]{:S(2)}, u32[]{:S(2)}) collective-permute-start(bf16[64,512]{1,0:T(8,128)(2,1)S(1)} %get-tuple-element.8), channel_id=1, source_target_pairs={{0,2},{2,0},{1,3},{3,1},{4,6},{6,4},{5,7},{7,5},{8,10},{10,8},{9,1... | collective-permute-start | bytes 196616 | tf_op jit(solution)/shard_map/ppermute | solution.py:107
  48.5 0.1 add_convert_fusion.here_ref
  48.6 0.0 collective-permute-done.11.refs_13_
  48.6 3.1 %collective-permute-done.9.refs_0_ = bf16[64,512]{1,0:T(8,128)(2,1)S(1)} collective-permute-done((bf16[64,512]{1,0:T(8,128)(2,1)S(1)}, bf16[64,512]{1,0:T(8,128)(2,1)S(1)}, u32[]{:S(2)}, u32[]{:S(2)}) %collective-permute-start.9) | collective-permute-done | bytes 65568 | tf_op jit(solution)/shard_map/ppermute | solution.py:107
  51.7 0.0 collective-permute-done.12.refs_14_
  51.7 0.0 copy-done.4
  51.7 2.6 %shard_map.58 = bf16[512,512]{1,0:T(8,128)(2,1)} custom-call(s32[4]{0:T(128)S(1)} %compare_select_fusion.owner_ref, s32[2]{0:T(128)S(1)} %add_convert_fusion.here_ref, s32[1,512]{1,0:T(1,128)S(1)} %bitcast.12, f32[64,512]{1,0:T(8,128)S(1)} %get-tuple-element.7.low_ref, bf16[64,512]{1,0:T(8,128)(2,1)S(1)} %collective-permute-done.9.refs_0_, ...), custom_call_target="tpu_custom_call" | custom-call | flops 134217728 | bytes 4130840 | tf_op jit(solution)/shard_map/pallas_call | solution.py:19
  (1 shorter events, 0.0 us)
Async XLA Ops:
  0.0 33.1 %collective-permute-start.10 = (bf16[4096,512]{1,0:T(8,128)(2,1)}, bf16[4096,512]{1,0:T(8,128)(2,1)}, u32[]{:S(2)}, u32[]{:S(2)}) collective-permute-start(bf16[4096,512]{1,0:T(8,128)(2,1)} %v_ref.1), channel_id=1, source_target_pairs={{0,1},{1,0},{2,3},{3,2},{4,5},{5,4},{6,7},{7,6},{8,9},{9,8},{10,11... | collective-permute-start | bytes 12582920 | tf_op jit(solution)/shard_map/ppermute | solution.py:107
  0.9 13.5 %collective-permute-start.3 = (bf16[16,4608]{1,0:T(8,128)(2,1)S(1)}, bf16[16,4608]{1,0:T(8,128)(2,1)S(1)}, u32[]{:S(2)}, u32[]{:S(2)}) collective-permute-start(bf16[16,4608]{1,0:T(8,128)(2,1)S(1)} %fusion), channel_id=1, source_target_pairs={{0,8},{4,12},{8,0},{12,4},{1,9},{5,13},{9,1},{13,5},{2,10},{6,14},... | collective-permute-start | bytes 442376 | tf_op jit(solution)/shard_map/ppermute | solution.py:107
  1.3 22.7 %collective-permute-start.6 = (bf16[16,4608]{1,0:T(8,128)(2,1)S(1)}, bf16[16,4608]{1,0:T(8,128)(2,1)S(1)}, u32[]{:S(2)}, u32[]{:S(2)}) collective-permute-start(bf16[16,4608]{1,0:T(8,128)(2,1)S(1)} %fusion), channel_id=1, source_target_pairs={{0,12},{4,0},{8,4},{12,8},{1,13},{5,1},{9,5},{13,9},{2,14},{6,2},{... | collective-permute-start | bytes 442376 | tf_op jit(solution)/shard_map/ppermute | solution.py:107
  1.5 23.1 %collective-permute-start = (bf16[16,4608]{1,0:T(8,128)(2,1)S(1)}, bf16[16,4608]{1,0:T(8,128)(2,1)S(1)}, u32[]{:S(2)}, u32[]{:S(2)}) collective-permute-start(bf16[16,4608]{1,0:T(8,128)(2,1)S(1)} %fusion), channel_id=1, source_target_pairs={{0,4},{4,8},{8,12},{12,0},{1,5},{5,9},{9,13},{13,1},{2,6},{6,10},{... | collective-permute-start | bytes 442376 | tf_op jit(solution)/shard_map/ppermute | solution.py:107
  14.5 11.6 %collective-permute-start.4 = (bf16[16,4608]{1,0:T(8,128)(2,1)S(1)}, bf16[16,4608]{1,0:T(8,128)(2,1)S(1)}, u32[]{:S(2)}, u32[]{:S(2)}) collective-permute-start(bf16[16,4608]{1,0:T(8,128)(2,1)S(1)} %collective-permute-done.3.refs_4_.refs_5_), channel_id=1, source_target_pairs={{0,16},{16,0},{1,17},{17,1},{2,18},{18,2},{3,19},{19,3},{4,20},{20... | collective-permute-start | bytes 442376 | tf_op jit(solution)/shard_map/ppermute | solution.py:107
  16.0 2.2 %copy-start = (bf16[512,4096]{1,0:T(8,128)(2,1)S(1)}, bf16[512,4096]{1,0:T(8,128)(2,1)}, u32[]{:S(2)}) copy-start(bf16[512,4096]{1,0:T(8,128)(2,1)} %x_ref.5) | copy-start | bytes 12582916
  18.2 2.2 %copy-start.2 = (bf16[4096,512]{1,0:T(8,128)(2,1)S(1)}, bf16[4096,512]{1,0:T(8,128)(2,1)}, u32[]{:S(2)}) copy-start(bf16[4096,512]{1,0:T(8,128)(2,1)} %v_ref.1) | copy-start | bytes 12582916
  22.7 25.9 %collective-permute-start.11 = (bf16[512,512]{1,0:T(8,128)(2,1)S(1)}, bf16[512,512]{1,0:T(8,128)(2,1)}, u32[]{:S(2)}, u32[]{:S(2)}) collective-permute-start(bf16[512,512]{1,0:T(8,128)(2,1)S(1)} %shard_map.56.refs_11_), channel_id=1, source_target_pairs={{1,3},{2,0},{5,7},{6,4},{9,11},{10,8},{13,15},{14,12},{17,19},{18,... | collective-permute-start | bytes 1572872 | tf_op jit(solution)/shard_map/ppermute | solution.py:161
  24.0 5.4 %collective-permute-start.7 = (bf16[16,4608]{1,0:T(8,128)(2,1)S(1)}, bf16[16,4608]{1,0:T(8,128)(2,1)S(1)}, u32[]{:S(2)}, u32[]{:S(2)}) collective-permute-start(bf16[16,4608]{1,0:T(8,128)(2,1)S(1)} %collective-permute-done.6.refs_7_.refs_8_), channel_id=1, source_target_pairs={{0,16},{16,0},{1,17},{17,1},{2,18},{18,2},{3,19},{19,3},{4,20},{20... | collective-permute-start | bytes 442376 | tf_op jit(solution)/shard_map/ppermute | solution.py:107
  24.6 16.2 %collective-permute-start.1 = (bf16[16,4608]{1,0:T(8,128)(2,1)S(1)}, bf16[16,4608]{1,0:T(8,128)(2,1)S(1)}, u32[]{:S(2)}, u32[]{:S(2)}) collective-permute-start(bf16[16,4608]{1,0:T(8,128)(2,1)S(1)} %collective-permute-done.refs_1_.refs_2_), channel_id=1, source_target_pairs={{0,16},{16,0},{1,17},{17,1},{2,18},{18,2},{3,19},{19,3},{4,20},{20... | collective-permute-start | bytes 442376 | tf_op jit(solution)/shard_map/ppermute | solution.py:107
  26.8 14.7 %collective-permute-start.5 = (bf16[32,4608]{1,0:T(8,128)(2,1)}, bf16[32,4608]{1,0:T(8,128)(2,1)S(1)}, u32[]{:S(2)}, u32[]{:S(2)}) collective-permute-start(bf16[32,4608]{1,0:T(8,128)(2,1)} %pad_maximum_fusion.1), channel_id=1, source_target_pairs={{0,1},{1,0},{2,3},{3,2},{4,5},{5,4},{6,7},{7,6},{8,9},{9,8},{10,11... | collective-permute-start | bytes 884744 | tf_op jit(solution)/shard_map/ppermute | solution.py:107
  30.2 13.1 %copy-start.3 = (bf16[1,4096,64]{1,2,0:T(8,128)(2,1)S(1)}, bf16[1,4096,64]{1,2,0:T(8,128)(2,1)}, u32[]{:S(2)}) copy-start(bf16[1,4096,64]{1,2,0:T(8,128)(2,1)} %param.7) | copy-start | bytes 1572868
  30.2 13.2 %copy-start.5 = (s32[512,1]{0,1:T(1,128)S(1)}, s32[512,1]{0,1:T(1,128)}, u32[]{:S(2)}) copy-start(s32[512,1]{0,1:T(1,128)} %param.9) | copy-start | bytes 6148
  30.2 11.4 %collective-permute-start.8 = (bf16[32,4608]{1,0:T(8,128)(2,1)}, bf16[32,4608]{1,0:T(8,128)(2,1)S(1)}, u32[]{:S(2)}, u32[]{:S(2)}) collective-permute-start(bf16[32,4608]{1,0:T(8,128)(2,1)} %pad_maximum_fusion.2), channel_id=1, source_target_pairs={{0,1},{1,0},{2,3},{3,2},{4,5},{5,4},{6,7},{7,6},{8,9},{9,8},{10,11... | collective-permute-start | bytes 884744 | tf_op jit(solution)/shard_map/ppermute | solution.py:107
  37.6 14.1 %copy-start.4 = (bf16[1,64,512]{2,1,0:T(8,128)(2,1)S(1)}, bf16[1,64,512]{2,1,0:T(8,128)(2,1)}, u32[]{:S(2)}) copy-start(bf16[1,64,512]{2,1,0:T(8,128)(2,1)} %param.8) | copy-start | bytes 196612
  37.6 14.1 %collective-permute-start.12 = (bf16[512,512]{1,0:T(8,128)(2,1)S(1)}, bf16[512,512]{1,0:T(8,128)(2,1)}, u32[]{:S(2)}, u32[]{:S(2)}) collective-permute-start(bf16[512,512]{1,0:T(8,128)(2,1)S(1)} %shard_map.57.refs_12_), channel_id=1, source_target_pairs={{0,2},{3,1},{4,6},{7,5},{8,10},{11,9},{12,14},{15,13},{16,18},{19,... | collective-permute-start | bytes 1572872 | tf_op jit(solution)/shard_map/ppermute | solution.py:161
  41.5 1.8 %collective-permute-start.2 = (bf16[32,4608]{1,0:T(8,128)(2,1)}, bf16[32,4608]{1,0:T(8,128)(2,1)S(1)}, u32[]{:S(2)}, u32[]{:S(2)}) collective-permute-start(bf16[32,4608]{1,0:T(8,128)(2,1)} %pad_maximum_fusion), channel_id=1, source_target_pairs={{0,1},{1,0},{2,3},{3,2},{4,5},{5,4},{6,7},{7,6},{8,9},{9,8},{10,11... | collective-permute-start | bytes 884744 | tf_op jit(solution)/shard_map/ppermute | solution.py:107
  43.3 2.2 %copy-start.1 = (bf16[512,4096]{1,0:T(8,128)(2,1)S(1)}, bf16[512,4096]{1,0:T(8,128)(2,1)}, u32[]{:S(2)}) copy-start(bf16[512,4096]{1,0:T(8,128)(2,1)} %x_ref.5) | copy-start | bytes 12582916
  47.3 4.3 %collective-permute-start.9 = (bf16[64,512]{1,0:T(8,128)(2,1)S(1)}, bf16[64,512]{1,0:T(8,128)(2,1)S(1)}, u32[]{:S(2)}, u32[]{:S(2)}) collective-permute-start(bf16[64,512]{1,0:T(8,128)(2,1)S(1)} %get-tuple-element.8), channel_id=1, source_target_pairs={{0,2},{2,0},{1,3},{3,1},{4,6},{6,4},{5,7},{7,5},{8,10},{10,8},{9,1... | collective-permute-start | bytes 196616 | tf_op jit(solution)/shard_map/ppermute | solution.py:107

commit v3 on v0

v3 whole, which is shorter than its diff:
```python
import functools

import jax
import jax.numpy as jnp
from jax import lax
from jax.experimental import pallas as pl
from jax.experimental.pallas import tpu as pltpu
from jax.sharding import PartitionSpec as P

F32 = jnp.float32
BF16 = jnp.bfloat16
VMEM = pl.BlockSpec(memory_space=pltpu.VMEM)
SMEM = pl.BlockSpec(memory_space=pltpu.SMEM)
HBM = pl.BlockSpec(memory_space=pltpu.HBM)
WHOLE = 58
CHUNKS = 4
BATCH = 4


def call(kernel, outs, args, scratch=(), flops=0, limit=16, specs=None):
    size = sum(a.size * a.dtype.itemsize for a in args)
    return pl.pallas_call(
        kernel,
        out_shape=outs,
        in_specs=specs or [VMEM] * len(args),
        out_specs=jax.tree.map(lambda _: VMEM, outs),
        scratch_shapes=scratch,
        compiler_params=pltpu.CompilerParams(vmem_limit_bytes=limit << 20),
        cost_estimate=pl.CostEstimate(flops=flops, bytes_accessed=size, transcendentals=0),
    )(*args)


def chunks(refs, buffers, sems):
    copies = []
    for k in range(CHUNKS):
        copies.append([])
        for n, (ref, buffer) in enumerate(zip(refs, buffers)):
            copy = pltpu.make_async_copy(ref(k), buffer.at[k], sems.at[n, k])
            copy.start()
            copies[-1].append(copy)
    return copies


def part(ref, axis):
    size = ref.shape[axis] // CHUNKS
    if axis == 0:
        return lambda k: ref.at[pl.ds(k * size, size)]
    return lambda k: ref.at[:, pl.ds(k * size, size)]


def base_kernel(x_ref, v_ref, o_ref, x_buf, v_buf, acc, sems):
    copies = chunks((part(x_ref, 1), part(v_ref, 0)), (x_buf, v_buf), sems)
    for k in range(CHUNKS):
        for copy in copies[k]:
            copy.wait()
        prod = jnp.dot(x_buf[k], v_buf[k], preferred_element_type=F32)
        if k > 0:
            prod = prod + acc[...]
        if k < CHUNKS - 1:
            acc[...] = prod
        else:
            o_ref[...] = prod.astype(BF16)


def base_terms(x, v):
    rows, wide, width = x.shape[0], x.shape[1], v.shape[1]
    return call(
        base_kernel,
        jax.ShapeDtypeStruct((rows, width), BF16),
        (x, v),
        scratch=[
            pltpu.VMEM((CHUNKS, rows, wide // CHUNKS), BF16),
            pltpu.VMEM((CHUNKS, wide // CHUNKS, width), BF16),
            pltpu.VMEM((rows, width), F32),
            pltpu.SemaphoreType.DMA((2, CHUNKS)),
        ],
        flops=2 * x.size * width,
        limit=WHOLE,
        specs=[HBM] * 2,
    )


def fill(scratch, refs, pieces, lanes):
    row = 0
    for which, begin, rows in pieces:
        scratch[row : row + rows, :] = refs[which][begin : begin + rows, lanes]
        row += rows


def down_kernel(layout, owner_ref, idx_ref, x_ref, own_ref, *refs):
    parts, (low_ref, sent_ref, up_ref, scratch, x_buf, acc, sems) = refs[:-7], refs[-7:]
    rank, wide, cols = low_ref.shape[0], x_ref.shape[1], own_ref.shape[1]
    copies = chunks((part(x_ref, 1),), (x_buf,), sems)
    up_ref[:rank, :] = own_ref[...]
    pieces = [p for pieces in layout[1:] for p in pieces]
    fill(up_ref.at[rank:], parts, pieces, slice(wide, wide + cols))
    low = jnp.zeros(low_ref.shape, F32)
    for first in range(0, len(layout), BATCH):
        group = layout[first : first + BATCH]
        rows = len(group) * rank
        for k in range(CHUNKS):
            lanes = slice(k * wide // CHUNKS, (k + 1) * wide // CHUNKS)
            fill(scratch.at[k], parts, [p for pieces in group for p in pieces], lanes)
            if first == 0:
                copies[k][0].wait()
            prod = lax.dot_general(
                scratch[k, :rows, :],
                x_buf[k],
                (((1,), (1,)), ((), ())),
                preferred_element_type=F32,
            )
            if k > 0:
                prod = prod + acc[:rows, :]
            if k < CHUNKS - 1:
                acc[:rows, :] = prod
        for k in range(len(group)):
            match = idx_ref[...] == owner_ref[first + k]
            low = low + jnp.where(match, prod[k * rank : (k + 1) * rank, :], 0.0)
    low_ref[...] = low
    sent_ref[...] = low.astype(BF16)


def last_kernel(blocks, owner_ref, flag_ref, idx_ref, low_ref, up_ref, *refs):
    terms, others, (out_ref, spread) = refs[:blocks], refs[blocks:-2], refs[-2:]
    rank = low_ref.shape[0]
    low = low_ref[...]
    for other in others:
        low = low + other[...].astype(F32)
    low = low.astype(BF16).astype(F32)
    for k in range(up_ref.shape[0] // rank):
        match = idx_ref[...] == owner_ref[k]
        spread[k * rank : (k + 1) * rank, :] = jnp.where(match, low, 0.0).astype(BF16)
    lora = lax.dot_general(
        spread[...], up_ref[...], (((0,), (0,)), ((), ())), preferred_element_type=F32
    )
    total = lora.astype(BF16).astype(F32)
    for n, term in enumerate(terms):
        total = total + jnp.where(flag_ref[n] == 1, term[...].astype(F32), 0.0)
    out_ref[...] = total.astype(BF16)


def after(x, *others):
    return lax.optimization_barrier((x, *others))[0]


def build(mesh):
    groups, adapters = mesh.shape["groups"], mesh.shape["adapter"]
    tensors, replicas = mesh.shape["tensor"], mesh.shape["replica"]

    def shift(x, axis, by):
        size = mesh.shape[axis]
        return lax.ppermute(x, axis, [(i, (i + by) % size) for i in range(size)])

    def others(x, axis):
        return [shift(x, axis, by) for by in range(1, mesh.shape[axis])]

    def flip(x, bit):
        return lax.ppermute(x, "adapter", [(i, i ^ bit) for i in range(adapters)])

    def base_pairs(h, by):
        pairs = {}
        for ti in range(tensors):
            for ri in range(replicas):
                to = (ti + by) % tensors
                if to // per_half == (ri - h) % replicas:
                    pairs[ti * replicas + ri] = to * replicas + ri
        free = set(range(tensors * replicas)) - set(pairs.values())
        for source in range(tensors * replicas):
            if source not in pairs:
                chip = source // replicas
                near = [n for n in sorted(free) if n // replicas == chip] or sorted(free)
                pairs[source] = near[0]
                free.remove(near[0])
        return sorted(pairs.items())

    per_half = max(1, tensors // replicas)

    def shards(x, v, d, u, idx):
        g, a = lax.axis_index("groups"), lax.axis_index("adapter")
        t, r = lax.axis_index("tensor"), lax.axis_index("replica")
        tokens, rank, wide = x.shape[0], d.shape[2], d.shape[1]
        cols = u.shape[2]
        row = idx.reshape(1, tokens)

        held = [v] + others(v, "replica")

        down = d[0].T
        own = jnp.concatenate([down, u[0]], axis=1)
        share = rank // (groups * replicas)
        mine = lax.dynamic_slice_in_dim(own, (g * replicas + r) * share, share, 0)
        bits = [1 << n for n in reversed(range((adapters - 1).bit_length()))]
        pieces, direct = {}, []
        for bit in bits:
            direct.append((bit, flip(mine, bit)))

        blocks, here, recvs, real = [], [], [], []

        def base(h):
            terms = base_terms(x, held[h])
            half = lax.rem(r - h + replicas, replicas)
            begin = half * per_half

            def cut(n):
                if per_half == 1:
                    return terms
                at = jnp.clip(n - begin, 0, per_half - 1) * cols
                return lax.dynamic_slice_in_dim(terms, at, cols, 1)

            blocks.append(cut(t))
            here.append((t >= begin) & (t < begin + per_half))
            for by in range(1, tensors):
                block = cut(lax.rem(t + by, tensors))
                if h == 0 and direct:
                    block = after(block, *[piece for _, piece in direct])
                recvs.append(lax.ppermute(block, ("tensor", "replica"), base_pairs(h, by)))
                real.append(here[-1])
            return terms

        x = after(x, mine)
        terms = base(0)
        for bit, piece in direct:
            pieces[bit] = after(piece, terms)
            for prior in [p for p in pieces if p > bit and not p & bit]:
                pieces[prior | bit] = flip(pieces[prior], bit)
        early = list(recvs)
        order = [p for p in sorted(pieces, key=lambda p: (bin(p).count("1"), p))]
        for h in range(1, replicas):
            terms = base(h)
        arrays, layout = [], [[(0, 0, rank)]]

        def keep(array):
            arrays.append(array)
            return len(arrays)

        near, places = [], []
        for p in order:
            piece = after(pieces[p], terms) if p == order[-1] else pieces[p]
            layout.append([])
            members = [piece] + others(piece, "groups")
            last = members.pop() if p == order[-1] and groups > 1 else None
            for member in members:
                layout[-1].append((keep(member), 0, share))
                places.append((len(layout) - 1, len(near)))
                near.append(member)
        if replicas > 1:
            for other in others(jnp.concatenate(list(lax.optimization_barrier((terms, *near, *early)))[1 : len(near) + 1], axis=0), "replica"):
                which = keep(other)
                for k, at in places:
                    layout[k].append((which, at * share, share))
        if last is not None:
            for member in [last] + others(last, "replica"):
                layout[-1].append((keep(member), 0, share))

        owner = jnp.stack([a] + [lax.bitwise_xor(a, jnp.int32(p)) for p in order])
        low, sent, every = call(
            functools.partial(down_kernel, layout),
            (jax.ShapeDtypeStruct((rank, tokens), F32), jax.ShapeDtypeStruct((rank, tokens), BF16),
                jax.ShapeDtypeStruct((adapters * rank, cols), BF16)),
            (owner, row, after(x, *recvs), u[0], down, *arrays),
            scratch=[
                pltpu.VMEM((CHUNKS, min(BATCH, adapters) * rank, wide // CHUNKS), BF16),
                pltpu.VMEM((CHUNKS, tokens, wide // CHUNKS), BF16),
                pltpu.VMEM((min(BATCH, adapters) * rank, tokens), F32),
                pltpu.SemaphoreType.DMA((1, CHUNKS)),
            ],
            flops=2 * x.size * rank * adapters,
            limit=WHOLE,
            specs=[SMEM, VMEM, HBM] + [VMEM] * (2 + len(arrays)),
        )
        lows = others(sent, "tensor")
        flags = jnp.stack(here + real).astype(jnp.int32)
        terms = blocks + recvs
        return call(
            functools.partial(last_kernel, len(terms)),
            jax.ShapeDtypeStruct((tokens, cols), BF16),
            (owner, flags, row, low, every, *terms, *lows),
            scratch=[pltpu.VMEM((adapters * rank, tokens), BF16)],
            flops=2 * tokens * rank * adapters * cols,
            specs=[SMEM] * 2 + [VMEM] * (3 + len(terms) + len(lows)),
        )

    return shards


def solution(mesh):
    return jax.shard_map(
        build(mesh),
        mesh=mesh,
        in_specs=(
            P(("groups", "adapter", "replica"), "tensor"),
            P("tensor", "replica"),
            P("adapter", "tensor", None),
            P("adapter", None, "tensor"),
            P(("groups", "adapter", "replica"), None),
        ),
        out_specs=P(("groups", "adapter", "replica"), "tensor"),
        check_vma=False,
    )
```

time: 128 us -> 50.8 us (0.40)
  waiting for transfers between devices: 68.3 us -> 11.2 us
  blocking collectives: 29.6 us -> 0 us
  Pallas kernels: 0 us -> 17.4 us
  matrix products: 17 us -> 0 us
  starting transfers between devices: 0.08 us -> 14.2 us
  between operations: 13.2 us -> 0.16 us
  local copies, waits for them, and re-layouts: 0.01 us -> 6.11 us
  other arithmetic: 0.06 us -> 1.59 us
    all_gather x2 -> x0, waiting for transfers between devices: 49 us -> none  [the longest x1 25.6 us: shards(): lax.all_gather(adapter_down_weight, 'adapter', axis=0, tiled=True)]
    reduce_scatter x1 -> x0, waiting for transfers between devices: 17.8 us -> none  [shards(): lax.psum_scatter(base_terms, 'tensor', scatter_dimension=1, tiled=True)]
    pallas_call x0 -> x4, Pallas kernels: none -> 17.4 us  [call(): pl.pallas_call(kernel, out_shape=outs, in_specs=specs or [VMEM] * len(arg...]
    all_gather x1 -> x0, blocking collectives: 16.8 us -> none  [shards(): lax.all_gather(adapter_up_weight, 'adapter', axis=0, tiled=True)]
    ppermute x0 -> x12, starting transfers between devices: none -> 14.2 us  [the longest x3 6.71 us: flip(): return lax.ppermute(x, 'adapter', [(i, i ^ bit) for i in range(adapters)])]
    psum x1 -> x0, blocking collectives: 12.8 us -> none  [shards(): low = lax.psum(low, 'tensor')]
    dot_general x2 -> x0, matrix products: 12.8 us -> none  [the longest x1 10.5 us: shards(): jnp.dot(hidden_state_rows, lax.all_gather(value_matrix, 'replica', axis=1...]
    ppermute x0 -> x12, waiting for transfers between devices: none -> 11.2 us  [the longest x7 8.56 us: shift(): return lax.ppermute(x, axis, [(i, (i + by) % size) for i in range(size)])]
  transfers between devices with their start and end apart: 3 -> 12, of which waited for: 3 -> 6; matrix products, arithmetic and copies ran while one was open for 11% -> 3% of each run, Pallas kernels for 0% -> 20%
where the time goes in v3:
time: 50.8 us; the launch traced here: 50.6 us
  Pallas kernels  17.4 us (34%)
  starting transfers between devices  14.2 us (28%)
  waiting for transfers between devices  11.2 us (22%)
  local copies, waits for them, and re-layouts  6.11 us (12%)
  other arithmetic  1.59 us (3%)
    pallas_call x4, Pallas kernels, call(): pl.pallas_call(kernel, out_shape=outs, in_specs=specs or [VMEM] * len(arg...  17.4 us
    ppermute x7, waiting for transfers between devices, shift(): return lax.ppermute(x, axis, [(i, (i + by) % size) for i in range(size)])  8.56 us
    ppermute x3, starting transfers between devices, flip(): return lax.ppermute(x, 'adapter', [(i, i ^ bit) for i in range(adapters)])  6.71 us
    ppermute x7, starting transfers between devices, shift(): return lax.ppermute(x, axis, [(i, (i + by) % size) for i in range(size)])  6.46 us
    unnamed x32, local copies, waits for them, and re-layouts  5.46 us
    ppermute x3, waiting for transfers between devices, flip(): return lax.ppermute(x, 'adapter', [(i, i ^ bit) for i in range(adapters)])  1.4 us
    ppermute x2, waiting for transfers between devices, base(): recvs.append(lax.ppermute(block, ('tensor', 'replica'), base_pairs(h, by)))  1.21 us
    ppermute x2, starting transfers between devices, base(): recvs.append(lax.ppermute(block, ('tensor', 'replica'), base_pairs(h, by)))  1.07 us
  transfers between devices with their start and end apart: 12, of which 6 were waited for; matrix products, arithmetic and copies ran while one was open for 3% of the time, Pallas kernels for 20%

profile of v3, /device:TPU:0, one launch (start us, length us, event | category | flops | bytes accessed | tf_op | source)
XLA Modules:
  0.0 50.6 jit_solution(1245227699031418143)
XLA Ops:
  0.0 0.5 collective-permute-start.3
  0.5 0.9 %fusion = bf16[16,4608]{1,0:T(8,128)(2,1)S(1)} fusion(s32[]{:T(128)S(6)} %select_n.3, bf16[64,4096]{1,0:T(8,128)(2,1)} %bitcast.13, bf16[64,512]{1,0:T(8,128)(2,1)} %bitcast.15), kind=kLoop, calls=%fused_computation.2 | loop fusion | flops 294912 | bytes 737284 | tf_op jit(solution)/shard_map/concatenate | solution.py:188
  1.4 3.7 %collective-permute-start = (bf16[16,4608]{1,0:T(8,128)(2,1)S(1)}, bf16[16,4608]{1,0:T(8,128)(2,1)S(1)}, u32[]{:S(2)}, u32[]{:S(2)}) collective-permute-start(bf16[16,4608]{1,0:T(8,128)(2,1)S(1)} %fusion), channel_id=1, source_target_pairs={{0,8},{4,12},{8,0},{12,4},{1,9},{5,13},{9,1},{13,5},{2,10},{6,14},... | collective-permute-start | bytes 442376 | tf_op jit(solution)/shard_map/ppermute | solution.py:158
  5.0 1.6 %collective-permute-start.1 = (bf16[16,4608]{1,0:T(8,128)(2,1)S(1)}, bf16[16,4608]{1,0:T(8,128)(2,1)S(1)}, u32[]{:S(2)}, u32[]{:S(2)}) collective-permute-start(bf16[16,4608]{1,0:T(8,128)(2,1)S(1)} %fusion), channel_id=1, source_target_pairs={{0,4},{4,0},{8,12},{12,8},{1,5},{5,1},{9,13},{13,9},{2,6},{6,2},{1... | collective-permute-start | bytes 442376 | tf_op jit(solution)/shard_map/ppermute | solution.py:158
  6.6 5.0 %shard_map.55.refs_0_ = bf16[512,512]{1,0:T(8,128)(2,1)} custom-call(bf16[512,4096]{1,0:T(8,128)(2,1)} %x_ref.2, bf16[4096,512]{1,0:T(8,128)(2,1)} %v_ref.1), custom_call_target="tpu_custom_call" | custom-call | flops 2147483648 | bytes 8388608 | tf_op jit(solution)/shard_map/pallas_call | solution.py:22
  11.6 1.2 %collective-permute-done.refs_3_ = bf16[16,4608]{1,0:T(8,128)(2,1)S(1)} collective-permute-done((bf16[16,4608]{1,0:T(8,128)(2,1)S(1)}, bf16[16,4608]{1,0:T(8,128)(2,1)S(1)}, u32[]{:S(2)}, u32[]{:S(2)}) %collective-permute-start) | collective-permute-done | bytes 147488 | tf_op jit(solution)/shard_map/ppermute | solution.py:158
  12.8 0.2 collective-permute-done.1.refs_1_
  13.0 0.0 collective-permute-start.2
  13.0 1.5 %collective-permute-start.7 = (bf16[16,4608]{1,0:T(8,128)(2,1)S(1)}, bf16[16,4608]{1,0:T(8,128)(2,1)S(1)}, u32[]{:S(2)}, u32[]{:S(2)}) collective-permute-start(bf16[16,4608]{1,0:T(8,128)(2,1)S(1)} %collective-permute-done.refs_3_), channel_id=1, source_target_pairs={{0,4},{4,0},{8,12},{12,8},{1,5},{5,1},{9,13},{13,9},{2,6},{6,2},{1... | collective-permute-start | bytes 442376 | tf_op jit(solution)/shard_map/ppermute | solution.py:158
  14.5 1.5 %collective-permute-start.6 = (bf16[16,4608]{1,0:T(8,128)(2,1)S(1)}, bf16[16,4608]{1,0:T(8,128)(2,1)S(1)}, u32[]{:S(2)}, u32[]{:S(2)}) collective-permute-start(bf16[16,4608]{1,0:T(8,128)(2,1)S(1)} %collective-permute-done.refs_3_), channel_id=1, source_target_pairs={{0,16},{16,0},{1,17},{17,1},{2,18},{18,2},{3,19},{19,3},{4,20},{20... | collective-permute-start | bytes 442376 | tf_op jit(solution)/shard_map/ppermute | solution.py:152
  16.0 0.5 %collective-permute-start.5 = (bf16[16,4608]{1,0:T(8,128)(2,1)S(1)}, bf16[16,4608]{1,0:T(8,128)(2,1)S(1)}, u32[]{:S(2)}, u32[]{:S(2)}) collective-permute-start(bf16[16,4608]{1,0:T(8,128)(2,1)S(1)} %collective-permute-done.1.refs_1_), channel_id=1, source_target_pairs={{0,16},{16,0},{1,17},{17,1},{2,18},{18,2},{3,19},{19,3},{4,20},{20... | collective-permute-start | bytes 442376 | tf_op jit(solution)/shard_map/ppermute | solution.py:152
  16.5 0.0 collective-permute-done.3.v_ref
  16.5 5.0 %shard_map.56.refs_1_ = bf16[512,512]{1,0:T(8,128)(2,1)} custom-call(bf16[512,4096]{1,0:T(8,128)(2,1)} %x_ref.2, bf16[4096,512]{1,0:T(8,128)(2,1)} %collective-permute-done.3.v_ref), custom_call_target="tpu_custom_call" | custom-call | flops 2147483648 | bytes 8388608 | tf_op jit(solution)/shard_map/pallas_call | solution.py:22
  21.5 0.0 copy-start
  21.6 0.0 copy-start.1
  21.6 0.0 copy-start.4
  21.6 0.0 collective-permute-done.7.refs_5_
  21.6 0.0 copy-start.9
  21.6 0.0 collective-permute-done.6.refs_4_
  21.6 0.0 copy-start.10
  21.6 2.4 %collective-permute-done.5.refs_2_ = bf16[16,4608]{1,0:T(8,128)(2,1)S(1)} collective-permute-done((bf16[16,4608]{1,0:T(8,128)(2,1)S(1)}, bf16[16,4608]{1,0:T(8,128)(2,1)S(1)}, u32[]{:S(2)}, u32[]{:S(2)}) %collective-permute-start.5) | collective-permute-done | bytes 147488 | tf_op jit(solution)/shard_map/ppermute | solution.py:152
  24.1 0.0 collective-permute-done.2.refs_2_
  24.1 0.0 copy-done.8
  24.1 0.7 %constant_dynamic-update-slice_fusion.4 = bf16[80,4608]{1,0:T(8,128)(2,1)} fusion(bf16[16,4608]{1,0:T(8,128)(2,1)S(1)} %collective-permute-done.1.refs_1_), kind=kLoop, calls=%fused_computation.7 | loop fusion | bytes 294912
  24.8 0.7 %constant_dynamic-update-slice_fusion.3 = bf16[80,4608]{1,0:T(8,128)(2,1)} fusion(bf16[80,4608]{1,0:T(8,128)(2,1)} %constant_dynamic-update-slice_fusion.4, bf16[16,4608]{1,0:T(8,128)(2,1)S(1)} %collective-permute-done.5.refs_2_), kind=kLoop, calls=%fused_computation.6 | loop fusion | bytes 294912
  25.4 0.0 copy-done.7
  25.4 0.7 %constant_dynamic-update-slice_fusion.2 = bf16[80,4608]{1,0:T(8,128)(2,1)} fusion(bf16[80,4608]{1,0:T(8,128)(2,1)} %constant_dynamic-update-slice_fusion.3, bf16[16,4608]{1,0:T(8,128)(2,1)S(1)} %collective-permute-done.refs_3_), kind=kLoop, calls=%fused_computation.5 | loop fusion | bytes 294912
  26.1 0.7 %constant_dynamic-update-slice_fusion.1 = bf16[80,4608]{1,0:T(8,128)(2,1)} fusion(bf16[80,4608]{1,0:T(8,128)(2,1)} %constant_dynamic-update-slice_fusion.2, bf16[16,4608]{1,0:T(8,128)(2,1)S(1)} %collective-permute-done.6.refs_4_), kind=kLoop, calls=%fused_computation.4 | loop fusion | bytes 294912
  26.8 0.7 %constant_dynamic-update-slice_fusion = bf16[80,4608]{1,0:T(8,128)(2,1)} fusion(bf16[80,4608]{1,0:T(8,128)(2,1)} %constant_dynamic-update-slice_fusion.1, bf16[16,4608]{1,0:T(8,128)(2,1)S(1)} %collective-permute-done.7.refs_5_), kind=kLoop, calls=%fused_computation.3 | loop fusion | bytes 294912 | tf_op jit(solution)/shard_map/concatenate | solution.py:246
  27.4 0.0 collective-permute-start.8
  27.4 1.1 %collective-permute-start.4 = (bf16[512,512]{1,0:T(8,128)(2,1)}, bf16[512,512]{1,0:T(8,128)(2,1)S(1)}, u32[]{:S(2)}, u32[]{:S(2)}) collective-permute-start(bf16[512,512]{1,0:T(8,128)(2,1)} %shard_map.56.refs_1_), channel_id=1, source_target_pairs={{0,2},{1,0},{2,3},{3,1},{4,6},{5,4},{6,7},{7,5},{8,10},{9,8},{10,1... | collective-permute-start | bytes 1572872 | tf_op jit(solution)/shard_map/ppermute | solution.py:215
  28.5 1.5 %collective-permute-start.9 = (bf16[16,4608]{1,0:T(8,128)(2,1)S(1)}, bf16[16,4608]{1,0:T(8,128)(2,1)S(1)}, u32[]{:S(2)}, u32[]{:S(2)}) collective-permute-start(bf16[16,4608]{1,0:T(8,128)(2,1)S(1)} %collective-permute-done.7.refs_5_), channel_id=1, source_target_pairs={{0,16},{16,0},{1,17},{17,1},{2,18},{18,2},{3,19},{19,3},{4,20},{20... | collective-permute-start | bytes 442376 | tf_op jit(solution)/shard_map/ppermute | solution.py:152
  30.0 3.7 %collective-permute-done.9.refs_7_ = bf16[16,4608]{1,0:T(8,128)(2,1)S(1)} collective-permute-done((bf16[16,4608]{1,0:T(8,128)(2,1)S(1)}, bf16[16,4608]{1,0:T(8,128)(2,1)S(1)}, u32[]{:S(2)}, u32[]{:S(2)}) %collective-permute-start.9) | collective-permute-done | bytes 147488 | tf_op jit(solution)/shard_map/ppermute | solution.py:152
  33.7 0.0 collective-permute-start.10
  33.7 0.6 %pad_add_fusion.owner_ref = s32[4]{0:T(128)} fusion(s32[1]{0:T(128)} %bitcast.3, s32[1]{0:T(128)} %bitcast.2, s32[1]{0:T(128)} %bitcast.1, s32[1]{0:T(128)} %bitcast), kind=kLoop, calls=%fused_computation.9 | loop fusion | flops 12 | bytes 32 | tf_op jit(solution)/shard_map/stack | solution.py:254
  34.3 1.2 %collective-permute-done.4.refs_3_ = bf16[512,512]{1,0:T(8,128)(2,1)S(1)} collective-permute-done((bf16[512,512]{1,0:T(8,128)(2,1)}, bf16[512,512]{1,0:T(8,128)(2,1)S(1)}, u32[]{:S(2)}, u32[]{:S(2)}) %collective-permute-start.4) | collective-permute-done | bytes 524320 | tf_op jit(solution)/shard_map/ppermute | solution.py:215
  35.5 0.0 collective-permute-done.10.refs_8_
  35.5 0.0 collective-permute-done.8.refs_6_
  35.6 0.6 %copy-done.13 = bf16[16,4608]{1,0:T(8,128)(2,1)} copy-done((bf16[16,4608]{1,0:T(8,128)(2,1)}, bf16[16,4608]{1,0:T(8,128)(2,1)S(1)}, u32[]{:S(2)}) %copy-start.13) | copy-done | bytes 147480
  36.2 0.3 copy-done.6
  36.4 5.4 %shard_map.57 = (f32[64,512]{1,0:T(8,128)}, bf16[64,512]{1,0:T(8,128)(2,1)}, bf16[256,512]{1,0:T(8,128)(2,1)}) custom-call(s32[4]{0:T(128)} %pad_add_fusion.owner_ref, s32[1,512]{1,0:T(1,128)} %bitcast.11, bf16[512,4096]{1,0:T(8,128)(2,1)} %x_ref.2, bf16[64,512]{1,0:T(8,128)(2,1)} %bitcast.16, bf16[64,4096]{1,0:T(8,128)(2,1)} %bitcast.14, ...), custom_call_target="tpu_custom_call" | custom-call | flops 1073741824 | bytes 6555664 | tf_op jit(solution)/shard_map/pallas_call | solution.py:22
  41.9 2.4 %collective-permute-start.11 = (bf16[64,512]{1,0:T(8,128)(2,1)}, bf16[64,512]{1,0:T(8,128)(2,1)S(1)}, u32[]{:S(2)}, u32[]{:S(2)}) collective-permute-start(bf16[64,512]{1,0:T(8,128)(2,1)} %get-tuple-element.32), channel_id=1, source_target_pairs={{0,2},{2,0},{1,3},{3,1},{4,6},{6,4},{5,7},{7,5},{8,10},{10,8},{9,1... | collective-permute-start | bytes 196616 | tf_op jit(solution)/shard_map/ppermute | solution.py:152
  44.3 0.1 add_convert_fusion.flag_ref
  44.4 2.4 %collective-permute-done.11.refs_4_ = bf16[64,512]{1,0:T(8,128)(2,1)S(1)} collective-permute-done((bf16[64,512]{1,0:T(8,128)(2,1)}, bf16[64,512]{1,0:T(8,128)(2,1)S(1)}, u32[]{:S(2)}, u32[]{:S(2)}) %collective-permute-start.11) | collective-permute-done | bytes 65568 | tf_op jit(solution)/shard_map/ppermute | solution.py:152
  46.8 0.0 copy-done
  46.8 0.9 %copy-done.2 = bf16[256,512]{1,0:T(8,128)(2,1)S(1)} copy-done((bf16[256,512]{1,0:T(8,128)(2,1)S(1)}, bf16[256,512]{1,0:T(8,128)(2,1)}, u32[]{:S(2)}) %copy-start.2) | copy-done | bytes 262168
  47.8 0.9 %copy-done.3 = f32[64,512]{1,0:T(8,128)S(1)} copy-done((f32[64,512]{1,0:T(8,128)S(1)}, f32[64,512]{1,0:T(8,128)}, u32[]{:S(2)}) %copy-start.3) | copy-done | bytes 131096
  48.7 2.0 %shard_map.58 = bf16[512,512]{1,0:T(8,128)(2,1)} custom-call(s32[4]{0:T(128)S(1)} %copy-done.5, s32[4]{0:T(128)S(1)} %add_convert_fusion.flag_ref, s32[1,512]{1,0:T(1,128)S(1)} %bitcast.12, f32[64,512]{1,0:T(8,128)S(1)} %copy-done.3, bf16[256,512]{1,0:T(8,128)(2,1)S(1)} %copy-done.2, bf16[512,512]{1,0:T(8,128)(2,1)S(1)} %copy-done, ...), custom_call_target="tpu_custom_call" | custom-call | flops 134217728 | bytes 2557984 | tf_op jit(solution)/shard_map/pallas_call | solution.py:22
  (16 shorter events, 0.0 us)
Async XLA Ops:
  0.0 16.5 %collective-permute-start.3 = (bf16[4096,512]{1,0:T(8,128)(2,1)}, bf16[4096,512]{1,0:T(8,128)(2,1)}, u32[]{:S(2)}, u32[]{:S(2)}) collective-permute-start(bf16[4096,512]{1,0:T(8,128)(2,1)} %v_ref.1), channel_id=1, source_target_pairs={{0,1},{1,0},{2,3},{3,2},{4,5},{5,4},{6,7},{7,6},{8,9},{9,8},{10,11... | collective-permute-start | bytes 12582920 | tf_op jit(solution)/shard_map/ppermute | solution.py:152
  1.4 11.4 %collective-permute-start = (bf16[16,4608]{1,0:T(8,128)(2,1)S(1)}, bf16[16,4608]{1,0:T(8,128)(2,1)S(1)}, u32[]{:S(2)}, u32[]{:S(2)}) collective-permute-start(bf16[16,4608]{1,0:T(8,128)(2,1)S(1)} %fusion), channel_id=1, source_target_pairs={{0,8},{4,12},{8,0},{12,4},{1,9},{5,13},{9,1},{13,5},{2,10},{6,14},... | collective-permute-start | bytes 442376 | tf_op jit(solution)/shard_map/ppermute | solution.py:158
  5.0 8.0 %collective-permute-start.1 = (bf16[16,4608]{1,0:T(8,128)(2,1)S(1)}, bf16[16,4608]{1,0:T(8,128)(2,1)S(1)}, u32[]{:S(2)}, u32[]{:S(2)}) collective-permute-start(bf16[16,4608]{1,0:T(8,128)(2,1)S(1)} %fusion), channel_id=1, source_target_pairs={{0,4},{4,0},{8,12},{12,8},{1,5},{5,1},{9,13},{13,9},{2,6},{6,2},{1... | collective-permute-start | bytes 442376 | tf_op jit(solution)/shard_map/ppermute | solution.py:158
  12.8 12.6 %copy-start.7 = (bf16[16,4608]{1,0:T(8,128)(2,1)}, bf16[16,4608]{1,0:T(8,128)(2,1)S(1)}, u32[]{:S(2)}) copy-start(bf16[16,4608]{1,0:T(8,128)(2,1)S(1)} %collective-permute-done.refs_3_) | copy-start | bytes 442372
  13.0 11.1 %copy-start.8 = (bf16[16,4608]{1,0:T(8,128)(2,1)}, bf16[16,4608]{1,0:T(8,128)(2,1)S(1)}, u32[]{:S(2)}) copy-start(bf16[16,4608]{1,0:T(8,128)(2,1)S(1)} %collective-permute-done.1.refs_1_) | copy-start | bytes 442372
  13.0 11.1 %collective-permute-start.2 = (bf16[512,512]{1,0:T(8,128)(2,1)}, bf16[512,512]{1,0:T(8,128)(2,1)S(1)}, u32[]{:S(2)}, u32[]{:S(2)}) collective-permute-start(bf16[512,512]{1,0:T(8,128)(2,1)} %shard_map.55.refs_0_), channel_id=1, source_target_pairs={{0,1},{1,3},{2,0},{3,2},{4,5},{5,7},{6,4},{7,6},{8,9},{9,11},{10,8... | collective-permute-start | bytes 1572872 | tf_op jit(solution)/shard_map/ppermute | solution.py:215
  13.0 8.6 %collective-permute-start.7 = (bf16[16,4608]{1,0:T(8,128)(2,1)S(1)}, bf16[16,4608]{1,0:T(8,128)(2,1)S(1)}, u32[]{:S(2)}, u32[]{:S(2)}) collective-permute-start(bf16[16,4608]{1,0:T(8,128)(2,1)S(1)} %collective-permute-done.refs_3_), channel_id=1, source_target_pairs={{0,4},{4,0},{8,12},{12,8},{1,5},{5,1},{9,13},{13,9},{2,6},{6,2},{1... | collective-permute-start | bytes 442376 | tf_op jit(solution)/shard_map/ppermute | solution.py:158
  14.5 7.1 %collective-permute-start.6 = (bf16[16,4608]{1,0:T(8,128)(2,1)S(1)}, bf16[16,4608]{1,0:T(8,128)(2,1)S(1)}, u32[]{:S(2)}, u32[]{:S(2)}) collective-permute-start(bf16[16,4608]{1,0:T(8,128)(2,1)S(1)} %collective-permute-done.refs_3_), channel_id=1, source_target_pairs={{0,16},{16,0},{1,17},{17,1},{2,18},{18,2},{3,19},{19,3},{4,20},{20... | collective-permute-start | bytes 442376 | tf_op jit(solution)/shard_map/ppermute | solution.py:152
  16.0 8.0 %collective-permute-start.5 = (bf16[16,4608]{1,0:T(8,128)(2,1)S(1)}, bf16[16,4608]{1,0:T(8,128)(2,1)S(1)}, u32[]{:S(2)}, u32[]{:S(2)}) collective-permute-start(bf16[16,4608]{1,0:T(8,128)(2,1)S(1)} %collective-permute-done.1.refs_1_), channel_id=1, source_target_pairs={{0,16},{16,0},{1,17},{17,1},{2,18},{18,2},{3,19},{19,3},{4,20},{20... | collective-permute-start | bytes 442376 | tf_op jit(solution)/shard_map/ppermute | solution.py:152
  21.5 25.3 %copy-start = (bf16[512,512]{1,0:T(8,128)(2,1)S(1)}, bf16[512,512]{1,0:T(8,128)(2,1)}, u32[]{:S(2)}) copy-start(bf16[512,512]{1,0:T(8,128)(2,1)} %shard_map.55.refs_0_) | copy-start | bytes 1572868
  21.6 25.2 %copy-start.1 = (bf16[512,512]{1,0:T(8,128)(2,1)S(1)}, bf16[512,512]{1,0:T(8,128)(2,1)}, u32[]{:S(2)}) copy-start(bf16[512,512]{1,0:T(8,128)(2,1)} %shard_map.56.refs_1_) | copy-start | bytes 1572868
  21.6 25.2 %copy-start.4 = (s32[512,1]{0,1:T(1,128)S(1)}, s32[512,1]{0,1:T(1,128)}, u32[]{:S(2)}) copy-start(s32[512,1]{0,1:T(1,128)} %param.9) | copy-start | bytes 6148
  21.6 13.9 %copy-start.9 = (bf16[16,4608]{1,0:T(8,128)(2,1)}, bf16[16,4608]{1,0:T(8,128)(2,1)S(1)}, u32[]{:S(2)}) copy-start(bf16[16,4608]{1,0:T(8,128)(2,1)S(1)} %collective-permute-done.7.refs_5_) | copy-start | bytes 442372
  21.6 13.9 %copy-start.10 = (bf16[16,4608]{1,0:T(8,128)(2,1)}, bf16[16,4608]{1,0:T(8,128)(2,1)S(1)}, u32[]{:S(2)}) copy-start(bf16[16,4608]{1,0:T(8,128)(2,1)S(1)} %collective-permute-done.6.refs_4_) | copy-start | bytes 442372
  24.1 3.4 %copy-start.11 = (bf16[16,4608]{1,0:T(8,128)(2,1)}, bf16[16,4608]{1,0:T(8,128)(2,1)S(1)}, u32[]{:S(2)}) copy-start(bf16[16,4608]{1,0:T(8,128)(2,1)S(1)} %collective-permute-done.5.refs_2_) | copy-start | bytes 442372
  27.4 8.1 %collective-permute-start.8 = (bf16[80,4608]{1,0:T(8,128)(2,1)}, bf16[80,4608]{1,0:T(8,128)(2,1)S(1)}, u32[]{:S(2)}, u32[]{:S(2)}) collective-permute-start(bf16[80,4608]{1,0:T(8,128)(2,1)} %constant_dynamic-update-slice_fusion), channel_id=1, source_target_pairs={{0,1},{1,0},{2,3},{3,2},{4,5},{5,4},{6,7},{7,6},{8,9},{9,8},{10,11... | collective-permute-start | bytes 2211848 | tf_op jit(solution)/shard_map/ppermute | solution.py:152
  27.4 8.1 %collective-permute-start.4 = (bf16[512,512]{1,0:T(8,128)(2,1)}, bf16[512,512]{1,0:T(8,128)(2,1)S(1)}, u32[]{:S(2)}, u32[]{:S(2)}) collective-permute-start(bf16[512,512]{1,0:T(8,128)(2,1)} %shard_map.56.refs_1_), channel_id=1, source_target_pairs={{0,2},{1,0},{2,3},{3,1},{4,6},{5,4},{6,7},{7,5},{8,10},{9,8},{10,1... | collective-permute-start | bytes 1572872 | tf_op jit(solution)/shard_map/ppermute | solution.py:215
  28.5 5.2 %collective-permute-start.9 = (bf16[16,4608]{1,0:T(8,128)(2,1)S(1)}, bf16[16,4608]{1,0:T(8,128)(2,1)S(1)}, u32[]{:S(2)}, u32[]{:S(2)}) collective-permute-start(bf16[16,4608]{1,0:T(8,128)(2,1)S(1)} %collective-permute-done.7.refs_5_), channel_id=1, source_target_pairs={{0,16},{16,0},{1,17},{17,1},{2,18},{18,2},{3,19},{19,3},{4,20},{20... | collective-permute-start | bytes 442376 | tf_op jit(solution)/shard_map/ppermute | solution.py:152
  33.7 1.9 %copy-start.12 = (bf16[16,4608]{1,0:T(8,128)(2,1)}, bf16[16,4608]{1,0:T(8,128)(2,1)S(1)}, u32[]{:S(2)}) copy-start(bf16[16,4608]{1,0:T(8,128)(2,1)S(1)} %collective-permute-done.9.refs_7_) | copy-start | bytes 442372
  33.7 1.8 %collective-permute-start.10 = (bf16[16,4608]{1,0:T(8,128)(2,1)S(1)}, bf16[16,4608]{1,0:T(8,128)(2,1)S(1)}, u32[]{:S(2)}, u32[]{:S(2)}) collective-permute-start(bf16[16,4608]{1,0:T(8,128)(2,1)S(1)} %collective-permute-done.9.refs_7_), channel_id=1, source_target_pairs={{0,1},{1,0},{2,3},{3,2},{4,5},{5,4},{6,7},{7,6},{8,9},{9,8},{10,11... | collective-permute-start | bytes 442376 | tf_op jit(solution)/shard_map/ppermute | solution.py:152
  34.3 12.5 %copy-start.5 = (s32[4]{0:T(128)S(1)}, s32[4]{0:T(128)}, u32[]{:S(2)}) copy-start(s32[4]{0:T(128)} %pad_add_fusion.owner_ref) | copy-start | bytes 52
  35.5 0.7 %copy-start.13 = (bf16[16,4608]{1,0:T(8,128)(2,1)}, bf16[16,4608]{1,0:T(8,128)(2,1)S(1)}, u32[]{:S(2)}) copy-start(bf16[16,4608]{1,0:T(8,128)(2,1)S(1)} %collective-permute-done.10.refs_8_) | copy-start | bytes 442372
  35.5 0.9 %copy-start.6 = (bf16[80,4608]{1,0:T(8,128)(2,1)}, bf16[80,4608]{1,0:T(8,128)(2,1)S(1)}, u32[]{:S(2)}) copy-start(bf16[80,4608]{1,0:T(8,128)(2,1)S(1)} %collective-permute-done.8.refs_6_) | copy-start | bytes 2211844
  41.9 4.9 %collective-permute-start.11 = (bf16[64,512]{1,0:T(8,128)(2,1)}, bf16[64,512]{1,0:T(8,128)(2,1)S(1)}, u32[]{:S(2)}, u32[]{:S(2)}) collective-permute-start(bf16[64,512]{1,0:T(8,128)(2,1)} %get-tuple-element.32), channel_id=1, source_target_pairs={{0,2},{2,0},{1,3},{3,1},{4,6},{6,4},{5,7},{7,5},{8,10},{10,8},{9,1... | collective-permute-start | bytes 196616 | tf_op jit(solution)/shard_map/ppermute | solution.py:152
  46.8 1.0 %copy-start.2 = (bf16[256,512]{1,0:T(8,128)(2,1)S(1)}, bf16[256,512]{1,0:T(8,128)(2,1)}, u32[]{:S(2)}) copy-start(bf16[256,512]{1,0:T(8,128)(2,1)} %get-tuple-element.31.up_ref) | copy-start | bytes 786436
  47.8 0.9 %copy-start.3 = (f32[64,512]{1,0:T(8,128)S(1)}, f32[64,512]{1,0:T(8,128)}, u32[]{:S(2)}) copy-start(f32[64,512]{1,0:T(8,128)} %get-tuple-element.30.low_ref) | copy-start | bytes 393220

commit v4 on v3

v4 whole, which is shorter than its diff:
```python
import functools

import jax
import jax.numpy as jnp
from jax import lax
from jax.experimental import pallas as pl
from jax.experimental.pallas import tpu as pltpu
from jax.sharding import PartitionSpec as P

F32 = jnp.float32
BF16 = jnp.bfloat16
VMEM = pl.BlockSpec(memory_space=pltpu.VMEM)
SMEM = pl.BlockSpec(memory_space=pltpu.SMEM)
HBM = pl.BlockSpec(memory_space=pltpu.HBM)
CHUNKS = 4
BATCH = 4


def call(kernel, outs, args, scratch=(), flops=0, limit=16, specs=None):
    size = sum(a.size * a.dtype.itemsize for a in args)
    return pl.pallas_call(
        kernel,
        out_shape=outs,
        in_specs=specs or [VMEM] * len(args),
        out_specs=jax.tree.map(lambda _: VMEM, outs),
        scratch_shapes=scratch,
        compiler_params=pltpu.CompilerParams(vmem_limit_bytes=limit << 20),
        cost_estimate=pl.CostEstimate(flops=flops, bytes_accessed=size, transcendentals=0),
    )(*args)


def chunks(refs, buffers, sems):
    copies = []
    for k in range(CHUNKS):
        copies.append([])
        for n, (ref, buffer) in enumerate(zip(refs, buffers)):
            copy = pltpu.make_async_copy(ref(k), buffer.at[k], sems.at[n, k])
            copy.start()
            copies[-1].append(copy)
    return copies


def part(ref, axis):
    size = ref.shape[axis] // CHUNKS
    if axis == 0:
        return lambda k: ref.at[pl.ds(k * size, size)]
    return lambda k: ref.at[:, pl.ds(k * size, size)]


def add_chunk(k, prod, acc, out_ref):
    if k > 0:
        prod = prod + acc[...]
    if k < CHUNKS - 1:
        acc[...] = prod
    else:
        out_ref[...] = prod.astype(BF16)


def first_kernel(x_ref, v_ref, o_ref, x_out, v_buf, acc, sems):
    copies = chunks((part(x_ref, 1), part(v_ref, 0)), (x_out, v_buf), sems)
    for k in range(CHUNKS):
        for copy in copies[k]:
            copy.wait()
        add_chunk(k, jnp.dot(x_out[k], v_buf[k], preferred_element_type=F32), acc, o_ref)


def first_terms(x, v):
    rows, wide, width = x.shape[0], x.shape[1], v.shape[1]
    cut = (CHUNKS, rows, wide // CHUNKS)
    return call(
        first_kernel,
        (jax.ShapeDtypeStruct((rows, width), BF16), jax.ShapeDtypeStruct(cut, BF16)),
        (x, v),
        scratch=[
            pltpu.VMEM((CHUNKS, wide // CHUNKS, width), BF16),
            pltpu.VMEM((rows, width), F32),
            pltpu.SemaphoreType.DMA((2, CHUNKS)),
        ],
        flops=2 * x.size * width,
        limit=48,
        specs=[HBM] * 2,
    )


def next_kernel(x_ref, v_ref, o_ref, acc):
    size = x_ref.shape[2]
    for k in range(CHUNKS):
        prod = jnp.dot(x_ref[k], v_ref[k * size : (k + 1) * size, :], preferred_element_type=F32)
        add_chunk(k, prod, acc, o_ref)


def next_terms(x, v):
    rows, width = x.shape[1], v.shape[1]
    return call(
        next_kernel,
        jax.ShapeDtypeStruct((rows, width), BF16),
        (x, v),
        scratch=[pltpu.VMEM((rows, width), F32)],
        flops=2 * x.size * width,
    )


def fill(scratch, refs, pieces, lanes):
    row = 0
    for which, begin, rows in pieces:
        scratch[row : row + rows, :] = refs[which][begin : begin + rows, lanes]
        row += rows


def down_kernel(layout, info_ref, idx_ref, x_ref, own_ref, *refs):
    parts, (low_ref, sent_ref, up_ref, scratch) = refs[:-4], refs[-4:]
    rank, size, cols = low_ref.shape[0], x_ref.shape[2], own_ref.shape[1]
    up_ref[:rank, :] = own_ref[...]
    pieces = [p for pieces in layout[1:] for p in pieces]
    fill(up_ref.at[rank:], parts, pieces, slice(CHUNKS * size, CHUNKS * size + cols))
    low = jnp.zeros(low_ref.shape, F32)
    for first in range(0, len(layout), BATCH):
        group = layout[first : first + BATCH]
        prod = 0.0
        for k in range(CHUNKS):
            lanes = slice(k * size, (k + 1) * size)
            fill(scratch.at[k], parts, [p for pieces in group for p in pieces], lanes)
            prod += lax.dot_general(
                scratch[k, : len(group) * rank, :],
                x_ref[k],
                (((1,), (1,)), ((), ())),
                preferred_element_type=F32,
            )
        for k in range(len(group)):
            match = idx_ref[...] == info_ref[first + k]
            low = low + jnp.where(match, prod[k * rank : (k + 1) * rank, :], 0.0)
    low_ref[...] = low
    sent_ref[...] = low.astype(BF16)


def last_kernel(blocks, info_ref, idx_ref, low_ref, up_ref, *refs):
    terms, others, (out_ref, spread) = refs[:blocks], refs[blocks:-2], refs[-2:]
    rank = low_ref.shape[0]
    low = low_ref[...]
    for other in others:
        low = low + other[...].astype(F32)
    low = low.astype(BF16).astype(F32)
    adapters = up_ref.shape[0] // rank
    for k in range(adapters):
        match = idx_ref[...] == info_ref[k]
        spread[k * rank : (k + 1) * rank, :] = jnp.where(match, low, 0.0).astype(BF16)
    lora = lax.dot_general(
        spread[...], up_ref[...], (((0,), (0,)), ((), ())), preferred_element_type=F32
    )
    total = lora.astype(BF16).astype(F32)
    for n, term in enumerate(terms):
        total = total + jnp.where(info_ref[adapters + n] == 1, term[...].astype(F32), 0.0)
    out_ref[...] = total.astype(BF16)


def after(x, *others):
    return lax.optimization_barrier((x, *others))[0]


def build(mesh):
    groups, adapters = mesh.shape["groups"], mesh.shape["adapter"]
    tensors, replicas = mesh.shape["tensor"], mesh.shape["replica"]

    def shift(x, axis, by):
        size = mesh.shape[axis]
        return lax.ppermute(x, axis, [(i, (i + by) % size) for i in range(size)])

    def others(x, axis):
        return [shift(x, axis, by) for by in range(1, mesh.shape[axis])]

    def flip(x, bit):
        return lax.ppermute(x, "adapter", [(i, i ^ bit) for i in range(adapters)])

    def base_pairs(h, by):
        pairs = {}
        for ti in range(tensors):
            for ri in range(replicas):
                to = (ti + by) % tensors
                if to // per_half == (ri - h) % replicas:
                    pairs[ti * replicas + ri] = to * replicas + ri
        free = set(range(tensors * replicas)) - set(pairs.values())
        for source in range(tensors * replicas):
            if source not in pairs:
                chip = source // replicas
                near = [n for n in sorted(free) if n // replicas == chip] or sorted(free)
                pairs[source] = near[0]
                free.remove(near[0])
        return sorted(pairs.items())

    per_half = max(1, tensors // replicas)

    def shards(x, v, d, u, idx):
        g, a = lax.axis_index("groups"), lax.axis_index("adapter")
        t, r = lax.axis_index("tensor"), lax.axis_index("replica")
        tokens, rank, wide = x.shape[0], d.shape[2], d.shape[1]
        cols = u.shape[2]
        row = idx.reshape(1, tokens)

        held = [v] + others(v, "replica")

        down = d[0].T
        own = jnp.concatenate([down, u[0]], axis=1)
        share = rank // (groups * replicas)
        mine = lax.dynamic_slice_in_dim(own, (g * replicas + r) * share, share, 0)
        bits = [1 << n for n in reversed(range((adapters - 1).bit_length()))]
        pieces = {}
        direct = [(bit, flip(mine, bit)) for bit in bits]

        blocks, recvs = [], []

        def base(h):
            terms, cuts = first_terms(x, v) if h == 0 else (next_terms(xs, held[h]), None)
            half = lax.rem(r - h + replicas, replicas)
            begin = half * per_half

            def cut(n):
                if per_half == 1:
                    return terms
                at = jnp.clip(n - begin, 0, per_half - 1) * cols
                return lax.dynamic_slice_in_dim(terms, at, cols, 1)

            blocks.append(cut(t))
            for by in range(1, tensors):
                block = after(cut(lax.rem(t + by, tensors)), *[piece for _, piece in direct])
                recvs.append(lax.ppermute(block, ("tensor", "replica"), base_pairs(h, by)))
            return terms, cuts

        order = sorted(range(1, adapters), key=lambda p: (bin(p).count("1"), p))
        halves = [lax.rem(r - h + replicas, replicas) * per_half for h in range(replicas)]
        here = [((t >= n) & (t < n + per_half)).astype(jnp.int32) for n in halves]
        info = [a] + [lax.bitwise_xor(a, jnp.int32(p)) for p in order]
        info = jnp.stack(info + here + [f for f in here for _ in range(1, tensors)])
        xs = None
        x, info = lax.optimization_barrier((x, info, mine))[:2]
        done = []
        for h in range(replicas):
            terms, cuts = base(h)
            done.append(terms)
            xs = cuts if h == 0 else xs
        for bit, piece in direct:
            pieces[bit] = after(piece, done[0])
            for prior in [p for p in pieces if p > bit and not p & bit]:
                pieces[prior | bit] = flip(pieces[prior], bit)
        arrays, layout = [], [[(0, 0, rank)]]

        def keep(array):
            arrays.append(array)
            return len(arrays)

        for p in order:
            layout.append([])
            piece = pieces[p]
            for member in [piece] + others(piece, "groups"):
                for array in [member] + others(member, "replica"):
                    layout[-1].append((keep(array), 0, share))

        low, sent, every = call(
            functools.partial(down_kernel, layout),
            (jax.ShapeDtypeStruct((rank, tokens), F32), jax.ShapeDtypeStruct((rank, tokens), BF16),
                jax.ShapeDtypeStruct((adapters * rank, cols), BF16)),
            (info, row, after(xs, *recvs), u[0], down, *arrays),
            scratch=[
                pltpu.VMEM((CHUNKS, min(BATCH, adapters) * rank, wide // CHUNKS), BF16),
            ],
            flops=2 * x.size * rank * adapters,
            specs=[SMEM] + [VMEM] * (4 + len(arrays)),
        )
        lows = others(sent, "tensor")
        terms = blocks + recvs
        return call(
            functools.partial(last_kernel, len(terms)),
            jax.ShapeDtypeStruct((tokens, cols), BF16),
            (info, row, low, every, *terms, *lows),
            scratch=[pltpu.VMEM((adapters * rank, tokens), BF16)],
            flops=2 * tokens * rank * adapters * cols,
            specs=[SMEM] + [VMEM] * (3 + len(terms) + len(lows)),
        )

    return shards


def solution(mesh):
    return jax.shard_map(
        build(mesh),
        mesh=mesh,
        in_specs=(
            P(("groups", "adapter", "replica"), "tensor"),
            P("tensor", "replica"),
            P("adapter", "tensor", None),
            P("adapter", None, "tensor"),
            P(("groups", "adapter", "replica"), None),
        ),
        out_specs=P(("groups", "adapter", "replica"), "tensor"),
        check_vma=False,
    )
```

time: 50.8 us -> 42.5 us (0.84)
  local copies, waits for them, and re-layouts: 6.11 us -> 0.1 us
  Pallas kernels: 17.4 us -> 12.6 us
  waiting for transfers between devices: 11.2 us -> 13.5 us
  starting transfers between devices: 14.2 us -> 15.2 us
  other arithmetic: 1.59 us -> 0.92 us
    unnamed x32 -> x6, local copies, waits for them, and re-layouts: 5.46 us -> 0.02 us
    pallas_call x4, Pallas kernels: 17.4 us -> 12.6 us  [call(): pl.pallas_call(kernel, out_shape=outs, in_specs=specs or [VMEM] * len(arg...]
    ppermute x3, waiting for transfers between devices: 1.4 us -> 3.74 us  [flip(): return lax.ppermute(x, 'adapter', [(i, i ^ bit) for i in range(adapters)])]
    ppermute x7 -> x11, waiting for transfers between devices: 8.56 us -> 9.8 us  [shift(): return lax.ppermute(x, axis, [(i, (i + by) % size) for i in range(size)])]
    ppermute x2, waiting for transfers between devices: 1.21 us -> 0.01 us  [base(): recvs.append(lax.ppermute(block, ('tensor', 'replica'), base_pairs(h, by)))]
    ppermute x2, starting transfers between devices: 1.07 us -> 2.03 us  [base(): recvs.append(lax.ppermute(block, ('tensor', 'replica'), base_pairs(h, by)))]
    concatenate x1 -> x0, local copies, waits for them, and re-layouts: 0.66 us -> none  [shards(): jnp.concatenate(list(lax.optimization_barrier((terms, *near, *early)))[1:...]
    another operation x1 -> x0, other arithmetic: 0.6 us -> none  [shards(): owner = jnp.stack([a] + [lax.bitwise_xor(a, jnp.int32(p)) for p in order])]
  transfers between devices with their start and end apart: 12 -> 16, of which waited for: 6 -> 10; matrix products, arithmetic and copies ran while one was open for 3% -> 2% of each run, Pallas kernels for 20% -> 21%
where the time goes in v4:
time: 42.5 us; the launch traced here: 42.4 us
  starting transfers between devices  15.2 us (36%)
  waiting for transfers between devices  13.5 us (32%)
  Pallas kernels  12.6 us (30%)
  other arithmetic  0.92 us (2%)
    pallas_call x4, Pallas kernels, call(): pl.pallas_call(kernel, out_shape=outs, in_specs=specs or [VMEM] * len(arg...  12.6 us
    ppermute x11, waiting for transfers between devices, shift(): return lax.ppermute(x, axis, [(i, (i + by) % size) for i in range(size)])  9.8 us
    ppermute x3, starting transfers between devices, flip(): return lax.ppermute(x, 'adapter', [(i, i ^ bit) for i in range(adapters)])  6.71 us
    ppermute x11, starting transfers between devices, shift(): return lax.ppermute(x, axis, [(i, (i + by) % size) for i in range(size)])  6.42 us
    ppermute x3, waiting for transfers between devices, flip(): return lax.ppermute(x, 'adapter', [(i, i ^ bit) for i in range(adapters)])  3.74 us
    ppermute x2, starting transfers between devices, base(): recvs.append(lax.ppermute(block, ('tensor', 'replica'), base_pairs(h, by)))  2.03 us
    concatenate x1, other arithmetic, shards(): own = jnp.concatenate([down, u[0]], axis=1)  0.92 us
  transfers between devices with their start and end apart: 16, of which 10 were waited for; matrix products, arithmetic and copies ran while one was open for 2% of the time, Pallas kernels for 21%

profile of v4, /device:TPU:0, one launch (start us, length us, event | category | flops | bytes accessed | tf_op | source)
XLA Modules:
  0.0 42.4 jit_solution(6425563233311436271)
XLA Ops:
  0.0 0.5 %collective-permute-start.3 = (bf16[4096,512]{1,0:T(8,128)(2,1)}, bf16[4096,512]{1,0:T(8,128)(2,1)}, u32[]{:S(2)}, u32[]{:S(2)}) collective-permute-start(bf16[4096,512]{1,0:T(8,128)(2,1)} %v_ref.1), channel_id=1, source_target_pairs={{0,1},{1,0},{2,3},{3,2},{4,5},{5,4},{6,7},{7,6},{8,9},{9,8},{10,11... | collective-permute-start | bytes 12582920 | tf_op jit(solution)/shard_map/ppermute | solution.py:166
  0.5 0.9 %fusion = bf16[16,4608]{1,0:T(8,128)(2,1)S(1)} fusion(s32[]{:T(128)S(6)} %select_n.3, bf16[64,4096]{1,0:T(8,128)(2,1)} %bitcast.11, bf16[64,512]{1,0:T(8,128)(2,1)} %bitcast.13), kind=kLoop, calls=%fused_computation.2 | loop fusion | flops 294912 | bytes 737284 | tf_op jit(solution)/shard_map/concatenate | solution.py:202
  1.4 3.7 %collective-permute-start = (bf16[16,4608]{1,0:T(8,128)(2,1)S(1)}, bf16[16,4608]{1,0:T(8,128)(2,1)S(1)}, u32[]{:S(2)}, u32[]{:S(2)}) collective-permute-start(bf16[16,4608]{1,0:T(8,128)(2,1)S(1)} %fusion), channel_id=1, source_target_pairs={{0,8},{4,12},{8,0},{12,4},{1,9},{5,13},{9,1},{13,5},{2,10},{6,14},... | collective-permute-start | bytes 442376 | tf_op jit(solution)/shard_map/ppermute | solution.py:172
  5.0 1.6 %collective-permute-start.1 = (bf16[16,4608]{1,0:T(8,128)(2,1)S(1)}, bf16[16,4608]{1,0:T(8,128)(2,1)S(1)}, u32[]{:S(2)}, u32[]{:S(2)}) collective-permute-start(bf16[16,4608]{1,0:T(8,128)(2,1)S(1)} %fusion), channel_id=1, source_target_pairs={{0,4},{4,0},{8,12},{12,8},{1,5},{5,1},{9,13},{13,9},{2,6},{6,2},{1... | collective-permute-start | bytes 442376 | tf_op jit(solution)/shard_map/ppermute | solution.py:172
  6.6 0.1 stack.37.info_ref
  6.7 4.2 %shard_map.55 = (bf16[512,512]{1,0:T(8,128)(2,1)S(1)}, bf16[4,512,1024]{2,1,0:T(8,128)(2,1)S(1)}) custom-call(bf16[512,4096]{1,0:T(8,128)(2,1)} %x_ref, bf16[4096,512]{1,0:T(8,128)(2,1)} %v_ref.1), custom_call_target="tpu_custom_call" | custom-call | flops 2147483648 | bytes 8388608 | tf_op jit(solution)/shard_map/pallas_call | solution.py:21
  10.9 1.9 %collective-permute-done.refs_5_ = bf16[16,4608]{1,0:T(8,128)(2,1)S(1)} collective-permute-done((bf16[16,4608]{1,0:T(8,128)(2,1)S(1)}, bf16[16,4608]{1,0:T(8,128)(2,1)S(1)}, u32[]{:S(2)}, u32[]{:S(2)}) %collective-permute-start) | collective-permute-done | bytes 147488 | tf_op jit(solution)/shard_map/ppermute | solution.py:172
  12.8 0.2 collective-permute-done.1.refs_1_
  13.0 0.0 collective-permute-start.2
  13.0 0.0 collective-permute-done.3.v_ref
  13.0 0.0 copy-start
  13.0 0.0 copy-start.1
  13.0 0.0 copy-start.2
  13.0 4.6 %shard_map.56.refs_1_ = bf16[512,512]{1,0:T(8,128)(2,1)S(1)} custom-call(bf16[4,512,1024]{2,1,0:T(8,128)(2,1)S(1)} %get-tuple-element.23.x_ref, bf16[4096,512]{1,0:T(8,128)(2,1)} %collective-permute-done.3.v_ref), custom_call_target="tpu_custom_call" | custom-call | flops 2147483648 | bytes 8388608 | tf_op jit(solution)/shard_map/pallas_call | solution.py:21
  17.6 2.0 %collective-permute-start.4 = (bf16[512,512]{1,0:T(8,128)(2,1)S(1)}, bf16[512,512]{1,0:T(8,128)(2,1)S(1)}, u32[]{:S(2)}, u32[]{:S(2)}) collective-permute-start(bf16[512,512]{1,0:T(8,128)(2,1)S(1)} %shard_map.56.refs_1_), channel_id=1, source_target_pairs={{0,2},{1,0},{2,3},{3,1},{4,6},{5,4},{6,7},{7,5},{8,10},{9,8},{10,1... | collective-permute-start | bytes 1572872 | tf_op jit(solution)/shard_map/ppermute | solution.py:225
  19.6 1.5 %collective-permute-start.11 = (bf16[16,4608]{1,0:T(8,128)(2,1)S(1)}, bf16[16,4608]{1,0:T(8,128)(2,1)S(1)}, u32[]{:S(2)}, u32[]{:S(2)}) collective-permute-start(bf16[16,4608]{1,0:T(8,128)(2,1)S(1)} %collective-permute-done.refs_5_), channel_id=1, source_target_pairs={{0,4},{4,0},{8,12},{12,8},{1,5},{5,1},{9,13},{13,9},{2,6},{6,2},{1... | collective-permute-start | bytes 442376 | tf_op jit(solution)/shard_map/ppermute | solution.py:172
  21.1 1.5 %collective-permute-start.9 = (bf16[16,4608]{1,0:T(8,128)(2,1)S(1)}, bf16[16,4608]{1,0:T(8,128)(2,1)S(1)}, u32[]{:S(2)}, u32[]{:S(2)}) collective-permute-start(bf16[16,4608]{1,0:T(8,128)(2,1)S(1)} %collective-permute-done.refs_5_), channel_id=1, source_target_pairs={{0,16},{16,0},{1,17},{17,1},{2,18},{18,2},{3,19},{19,3},{4,20},{20... | collective-permute-start | bytes 442376 | tf_op jit(solution)/shard_map/ppermute | solution.py:166
  22.6 0.5 %collective-permute-start.6 = (bf16[16,4608]{1,0:T(8,128)(2,1)S(1)}, bf16[16,4608]{1,0:T(8,128)(2,1)S(1)}, u32[]{:S(2)}, u32[]{:S(2)}) collective-permute-start(bf16[16,4608]{1,0:T(8,128)(2,1)S(1)} %collective-permute-done.1.refs_1_), channel_id=1, source_target_pairs={{0,16},{16,0},{1,17},{17,1},{2,18},{18,2},{3,19},{19,3},{4,20},{20... | collective-permute-start | bytes 442376 | tf_op jit(solution)/shard_map/ppermute | solution.py:166
  23.1 1.6 %collective-permute-done.11.refs_9_ = bf16[16,4608]{1,0:T(8,128)(2,1)S(1)} collective-permute-done((bf16[16,4608]{1,0:T(8,128)(2,1)S(1)}, bf16[16,4608]{1,0:T(8,128)(2,1)S(1)}, u32[]{:S(2)}, u32[]{:S(2)}) %collective-permute-start.11) | collective-permute-done | bytes 147488 | tf_op jit(solution)/shard_map/ppermute | solution.py:172
  24.8 0.0 collective-permute-start.5
  24.8 2.4 %collective-permute-done.9.refs_7_ = bf16[16,4608]{1,0:T(8,128)(2,1)S(1)} collective-permute-done((bf16[16,4608]{1,0:T(8,128)(2,1)S(1)}, bf16[16,4608]{1,0:T(8,128)(2,1)S(1)}, u32[]{:S(2)}, u32[]{:S(2)}) %collective-permute-start.9) | collective-permute-done | bytes 147488 | tf_op jit(solution)/shard_map/ppermute | solution.py:166
  27.2 1.5 %collective-permute-start.13 = (bf16[16,4608]{1,0:T(8,128)(2,1)S(1)}, bf16[16,4608]{1,0:T(8,128)(2,1)S(1)}, u32[]{:S(2)}, u32[]{:S(2)}) collective-permute-start(bf16[16,4608]{1,0:T(8,128)(2,1)S(1)} %collective-permute-done.11.refs_9_), channel_id=1, source_target_pairs={{0,16},{16,0},{1,17},{17,1},{2,18},{18,2},{3,19},{19,3},{4,20},{20... | collective-permute-start | bytes 442376 | tf_op jit(solution)/shard_map/ppermute | solution.py:166
  28.7 0.8 %collective-permute-done.6.refs_3_ = bf16[16,4608]{1,0:T(8,128)(2,1)S(1)} collective-permute-done((bf16[16,4608]{1,0:T(8,128)(2,1)S(1)}, bf16[16,4608]{1,0:T(8,128)(2,1)S(1)}, u32[]{:S(2)}, u32[]{:S(2)}) %collective-permute-start.6) | collective-permute-done | bytes 147488 | tf_op jit(solution)/shard_map/ppermute | solution.py:166
  29.5 0.0 collective-permute-start.8
  29.5 0.0 collective-permute-done.5.refs_2_
  29.5 0.5 %collective-permute-start.12 = (bf16[16,4608]{1,0:T(8,128)(2,1)S(1)}, bf16[16,4608]{1,0:T(8,128)(2,1)S(1)}, u32[]{:S(2)}, u32[]{:S(2)}) collective-permute-start(bf16[16,4608]{1,0:T(8,128)(2,1)S(1)} %collective-permute-done.11.refs_9_), channel_id=1, source_target_pairs={{0,1},{1,0},{2,3},{3,2},{4,5},{5,4},{6,7},{7,6},{8,9},{9,8},{10,11... | collective-permute-start | bytes 442376 | tf_op jit(solution)/shard_map/ppermute | solution.py:166
  30.0 2.3 %collective-permute-done.13.refs_11_ = bf16[16,4608]{1,0:T(8,128)(2,1)S(1)} collective-permute-done((bf16[16,4608]{1,0:T(8,128)(2,1)S(1)}, bf16[16,4608]{1,0:T(8,128)(2,1)S(1)}, u32[]{:S(2)}, u32[]{:S(2)}) %collective-permute-start.13) | collective-permute-done | bytes 147488 | tf_op jit(solution)/shard_map/ppermute | solution.py:166
  32.3 0.0 collective-permute-start.10
  32.3 0.0 collective-permute-done.2.refs_2_
  32.3 0.5 %collective-permute-start.7 = (bf16[16,4608]{1,0:T(8,128)(2,1)S(1)}, bf16[16,4608]{1,0:T(8,128)(2,1)S(1)}, u32[]{:S(2)}, u32[]{:S(2)}) collective-permute-start(bf16[16,4608]{1,0:T(8,128)(2,1)S(1)} %collective-permute-done.6.refs_3_), channel_id=1, source_target_pairs={{0,1},{1,0},{2,3},{3,2},{4,5},{5,4},{6,7},{7,6},{8,9},{9,8},{10,11... | collective-permute-start | bytes 442376 | tf_op jit(solution)/shard_map/ppermute | solution.py:166
  32.8 0.0 collective-permute-done.4.refs_3_
  32.8 0.1 collective-permute-start.14
  32.9 0.0 collective-permute-done.8.refs_6_
  32.9 0.8 %collective-permute-done.10.refs_8_ = bf16[16,4608]{1,0:T(8,128)(2,1)S(1)} collective-permute-done((bf16[16,4608]{1,0:T(8,128)(2,1)S(1)}, bf16[16,4608]{1,0:T(8,128)(2,1)S(1)}, u32[]{:S(2)}, u32[]{:S(2)}) %collective-permute-start.10) | collective-permute-done | bytes 147488 | tf_op jit(solution)/shard_map/ppermute | solution.py:166
  33.7 0.0 collective-permute-done.12.refs_10_
  33.7 0.2 collective-permute-done.7.refs_4_
  33.9 0.3 collective-permute-done.14.refs_12_
  34.2 0.0 copy-done
  34.2 0.0 copy-done.1
  34.2 0.0 copy-done.2
  34.2 1.8 %shard_map.57 = (f32[64,512]{1,0:T(8,128)S(1)}, bf16[64,512]{1,0:T(8,128)(2,1)S(1)}, bf16[256,512]{1,0:T(8,128)(2,1)S(1)}) custom-call(s32[8]{0:T(128)S(1)} %stack.37.info_ref, s32[1,512]{1,0:T(1,128)S(1)} %bitcast.15, bf16[4,512,1024]{2,1,0:T(8,128)(2,1)S(1)} %get-tuple-element.23.x_ref, bf16[64,512]{1,0:T(8,128)(2,1)S(1)} %bitcast.14, ...), custom_call_target="tpu_custom_call" | custom-call | flops 1073741824 | bytes 6555680 | tf_op jit(solution)/shard_map/pallas_call | solution.py:21
  36.1 1.3 %collective-permute-start.15 = (bf16[64,512]{1,0:T(8,128)(2,1)S(1)}, bf16[64,512]{1,0:T(8,128)(2,1)S(1)}, u32[]{:S(2)}, u32[]{:S(2)}) collective-permute-start(bf16[64,512]{1,0:T(8,128)(2,1)S(1)} %get-tuple-element.28), channel_id=1, source_target_pairs={{0,2},{2,0},{1,3},{3,1},{4,6},{6,4},{5,7},{7,5},{8,10},{10,8},{9,1... | collective-permute-start | bytes 196616 | tf_op jit(solution)/shard_map/ppermute | solution.py:166
  37.4 3.0 %collective-permute-done.15.refs_4_ = bf16[64,512]{1,0:T(8,128)(2,1)S(1)} collective-permute-done((bf16[64,512]{1,0:T(8,128)(2,1)S(1)}, bf16[64,512]{1,0:T(8,128)(2,1)S(1)}, u32[]{:S(2)}, u32[]{:S(2)}) %collective-permute-start.15) | collective-permute-done | bytes 65568 | tf_op jit(solution)/shard_map/ppermute | solution.py:166
  40.4 2.0 %shard_map.58 = bf16[512,512]{1,0:T(8,128)(2,1)} custom-call(s32[8]{0:T(128)S(1)} %stack.37.info_ref, s32[1,512]{1,0:T(1,128)S(1)} %bitcast.16, f32[64,512]{1,0:T(8,128)S(1)} %get-tuple-element.26.low_ref, bf16[256,512]{1,0:T(8,128)(2,1)S(1)} %get-tuple-element.27.up_ref, bf16[512,512]{1,0:T(8,128)(2,1)S(1)} %get-tuple-element.21.refs_0_, ...), custom_call_target="tpu_custom_call" | custom-call | flops 134217728 | bytes 2557984 | tf_op jit(solution)/shard_map/pallas_call | solution.py:21
Async XLA Ops:
  0.0 13.0 %collective-permute-start.3 = (bf16[4096,512]{1,0:T(8,128)(2,1)}, bf16[4096,512]{1,0:T(8,128)(2,1)}, u32[]{:S(2)}, u32[]{:S(2)}) collective-permute-start(bf16[4096,512]{1,0:T(8,128)(2,1)} %v_ref.1), channel_id=1, source_target_pairs={{0,1},{1,0},{2,3},{3,2},{4,5},{5,4},{6,7},{7,6},{8,9},{9,8},{10,11... | collective-permute-start | bytes 12582920 | tf_op jit(solution)/shard_map/ppermute | solution.py:166
  1.4 11.4 %collective-permute-start = (bf16[16,4608]{1,0:T(8,128)(2,1)S(1)}, bf16[16,4608]{1,0:T(8,128)(2,1)S(1)}, u32[]{:S(2)}, u32[]{:S(2)}) collective-permute-start(bf16[16,4608]{1,0:T(8,128)(2,1)S(1)} %fusion), channel_id=1, source_target_pairs={{0,8},{4,12},{8,0},{12,4},{1,9},{5,13},{9,1},{13,5},{2,10},{6,14},... | collective-permute-start | bytes 442376 | tf_op jit(solution)/shard_map/ppermute | solution.py:172
  5.0 8.0 %collective-permute-start.1 = (bf16[16,4608]{1,0:T(8,128)(2,1)S(1)}, bf16[16,4608]{1,0:T(8,128)(2,1)S(1)}, u32[]{:S(2)}, u32[]{:S(2)}) collective-permute-start(bf16[16,4608]{1,0:T(8,128)(2,1)S(1)} %fusion), channel_id=1, source_target_pairs={{0,4},{4,0},{8,12},{12,8},{1,5},{5,1},{9,13},{13,9},{2,6},{6,2},{1... | collective-permute-start | bytes 442376 | tf_op jit(solution)/shard_map/ppermute | solution.py:172
  13.0 19.3 %collective-permute-start.2 = (bf16[512,512]{1,0:T(8,128)(2,1)S(1)}, bf16[512,512]{1,0:T(8,128)(2,1)S(1)}, u32[]{:S(2)}, u32[]{:S(2)}) collective-permute-start(bf16[512,512]{1,0:T(8,128)(2,1)S(1)} %get-tuple-element.21.refs_0_), channel_id=1, source_target_pairs={{0,1},{1,3},{2,0},{3,2},{4,5},{5,7},{6,4},{7,6},{8,9},{9,11},{10,8... | collective-permute-start | bytes 1572872 | tf_op jit(solution)/shard_map/ppermute | solution.py:225
  13.0 21.2 %copy-start = (bf16[1,4096,64]{1,2,0:T(8,128)(2,1)S(1)}, bf16[1,4096,64]{1,2,0:T(8,128)(2,1)}, u32[]{:S(2)}) copy-start(bf16[1,4096,64]{1,2,0:T(8,128)(2,1)} %param.7) | copy-start | bytes 1572868
  13.0 21.2 %copy-start.1 = (bf16[1,64,512]{2,1,0:T(8,128)(2,1)S(1)}, bf16[1,64,512]{2,1,0:T(8,128)(2,1)}, u32[]{:S(2)}) copy-start(bf16[1,64,512]{2,1,0:T(8,128)(2,1)} %param.8) | copy-start | bytes 196612
  13.0 21.2 %copy-start.2 = (s32[512,1]{0,1:T(1,128)S(1)}, s32[512,1]{0,1:T(1,128)}, u32[]{:S(2)}) copy-start(s32[512,1]{0,1:T(1,128)} %param.9) | copy-start | bytes 6148
  17.6 15.2 %collective-permute-start.4 = (bf16[512,512]{1,0:T(8,128)(2,1)S(1)}, bf16[512,512]{1,0:T(8,128)(2,1)S(1)}, u32[]{:S(2)}, u32[]{:S(2)}) collective-permute-start(bf16[512,512]{1,0:T(8,128)(2,1)S(1)} %shard_map.56.refs_1_), channel_id=1, source_target_pairs={{0,2},{1,0},{2,3},{3,1},{4,6},{5,4},{6,7},{7,5},{8,10},{9,8},{10,1... | collective-permute-start | bytes 1572872 | tf_op jit(solution)/shard_map/ppermute | solution.py:225
  19.6 5.1 %collective-permute-start.11 = (bf16[16,4608]{1,0:T(8,128)(2,1)S(1)}, bf16[16,4608]{1,0:T(8,128)(2,1)S(1)}, u32[]{:S(2)}, u32[]{:S(2)}) collective-permute-start(bf16[16,4608]{1,0:T(8,128)(2,1)S(1)} %collective-permute-done.refs_5_), channel_id=1, source_target_pairs={{0,4},{4,0},{8,12},{12,8},{1,5},{5,1},{9,13},{13,9},{2,6},{6,2},{1... | collective-permute-start | bytes 442376 | tf_op jit(solution)/shard_map/ppermute | solution.py:172
  21.1 6.0 %collective-permute-start.9 = (bf16[16,4608]{1,0:T(8,128)(2,1)S(1)}, bf16[16,4608]{1,0:T(8,128)(2,1)S(1)}, u32[]{:S(2)}, u32[]{:S(2)}) collective-permute-start(bf16[16,4608]{1,0:T(8,128)(2,1)S(1)} %collective-permute-done.refs_5_), channel_id=1, source_target_pairs={{0,16},{16,0},{1,17},{17,1},{2,18},{18,2},{3,19},{19,3},{4,20},{20... | collective-permute-start | bytes 442376 | tf_op jit(solution)/shard_map/ppermute | solution.py:166
  22.6 6.9 %collective-permute-start.6 = (bf16[16,4608]{1,0:T(8,128)(2,1)S(1)}, bf16[16,4608]{1,0:T(8,128)(2,1)S(1)}, u32[]{:S(2)}, u32[]{:S(2)}) collective-permute-start(bf16[16,4608]{1,0:T(8,128)(2,1)S(1)} %collective-permute-done.1.refs_1_), channel_id=1, source_target_pairs={{0,16},{16,0},{1,17},{17,1},{2,18},{18,2},{3,19},{19,3},{4,20},{20... | collective-permute-start | bytes 442376 | tf_op jit(solution)/shard_map/ppermute | solution.py:166
  24.8 4.8 %collective-permute-start.5 = (bf16[16,4608]{1,0:T(8,128)(2,1)S(1)}, bf16[16,4608]{1,0:T(8,128)(2,1)S(1)}, u32[]{:S(2)}, u32[]{:S(2)}) collective-permute-start(bf16[16,4608]{1,0:T(8,128)(2,1)S(1)} %collective-permute-done.1.refs_1_), channel_id=1, source_target_pairs={{0,1},{1,0},{2,3},{3,2},{4,5},{5,4},{6,7},{7,6},{8,9},{9,8},{10,11... | collective-permute-start | bytes 442376 | tf_op jit(solution)/shard_map/ppermute | solution.py:166
  27.2 5.1 %collective-permute-start.13 = (bf16[16,4608]{1,0:T(8,128)(2,1)S(1)}, bf16[16,4608]{1,0:T(8,128)(2,1)S(1)}, u32[]{:S(2)}, u32[]{:S(2)}) collective-permute-start(bf16[16,4608]{1,0:T(8,128)(2,1)S(1)} %collective-permute-done.11.refs_9_), channel_id=1, source_target_pairs={{0,16},{16,0},{1,17},{17,1},{2,18},{18,2},{3,19},{19,3},{4,20},{20... | collective-permute-start | bytes 442376 | tf_op jit(solution)/shard_map/ppermute | solution.py:166
  29.5 3.4 %collective-permute-start.8 = (bf16[16,4608]{1,0:T(8,128)(2,1)S(1)}, bf16[16,4608]{1,0:T(8,128)(2,1)S(1)}, u32[]{:S(2)}, u32[]{:S(2)}) collective-permute-start(bf16[16,4608]{1,0:T(8,128)(2,1)S(1)} %collective-permute-done.refs_5_), channel_id=1, source_target_pairs={{0,1},{1,0},{2,3},{3,2},{4,5},{5,4},{6,7},{7,6},{8,9},{9,8},{10,11... | collective-permute-start | bytes 442376 | tf_op jit(solution)/shard_map/ppermute | solution.py:166
  29.5 4.1 %collective-permute-start.12 = (bf16[16,4608]{1,0:T(8,128)(2,1)S(1)}, bf16[16,4608]{1,0:T(8,128)(2,1)S(1)}, u32[]{:S(2)}, u32[]{:S(2)}) collective-permute-start(bf16[16,4608]{1,0:T(8,128)(2,1)S(1)} %collective-permute-done.11.refs_9_), channel_id=1, source_target_pairs={{0,1},{1,0},{2,3},{3,2},{4,5},{5,4},{6,7},{7,6},{8,9},{9,8},{10,11... | collective-permute-start | bytes 442376 | tf_op jit(solution)/shard_map/ppermute | solution.py:166
  32.3 1.4 %collective-permute-start.10 = (bf16[16,4608]{1,0:T(8,128)(2,1)S(1)}, bf16[16,4608]{1,0:T(8,128)(2,1)S(1)}, u32[]{:S(2)}, u32[]{:S(2)}) collective-permute-start(bf16[16,4608]{1,0:T(8,128)(2,1)S(1)} %collective-permute-done.9.refs_7_), channel_id=1, source_target_pairs={{0,1},{1,0},{2,3},{3,2},{4,5},{5,4},{6,7},{7,6},{8,9},{9,8},{10,11... | collective-permute-start | bytes 442376 | tf_op jit(solution)/shard_map/ppermute | solution.py:166
  32.3 1.6 %collective-permute-start.7 = (bf16[16,4608]{1,0:T(8,128)(2,1)S(1)}, bf16[16,4608]{1,0:T(8,128)(2,1)S(1)}, u32[]{:S(2)}, u32[]{:S(2)}) collective-permute-start(bf16[16,4608]{1,0:T(8,128)(2,1)S(1)} %collective-permute-done.6.refs_3_), channel_id=1, source_target_pairs={{0,1},{1,0},{2,3},{3,2},{4,5},{5,4},{6,7},{7,6},{8,9},{9,8},{10,11... | collective-permute-start | bytes 442376 | tf_op jit(solution)/shard_map/ppermute | solution.py:166
  32.8 1.4 %collective-permute-start.14 = (bf16[16,4608]{1,0:T(8,128)(2,1)S(1)}, bf16[16,4608]{1,0:T(8,128)(2,1)S(1)}, u32[]{:S(2)}, u32[]{:S(2)}) collective-permute-start(bf16[16,4608]{1,0:T(8,128)(2,1)S(1)} %collective-permute-done.13.refs_11_), channel_id=1, source_target_pairs={{0,1},{1,0},{2,3},{3,2},{4,5},{5,4},{6,7},{7,6},{8,9},{9,8},{10,11... | collective-permute-start | bytes 442376 | tf_op jit(solution)/shard_map/ppermute | solution.py:166
  36.1 4.3 %collective-permute-start.15 = (bf16[64,512]{1,0:T(8,128)(2,1)S(1)}, bf16[64,512]{1,0:T(8,128)(2,1)S(1)}, u32[]{:S(2)}, u32[]{:S(2)}) collective-permute-start(bf16[64,512]{1,0:T(8,128)(2,1)S(1)} %get-tuple-element.28), channel_id=1, source_target_pairs={{0,2},{2,0},{1,3},{3,1},{4,6},{6,4},{5,7},{7,5},{8,10},{10,8},{9,1... | collective-permute-start | bytes 196616 | tf_op jit(solution)/shard_map/ppermute | solution.py:166

commit v5 on v4

--- a/solution.py
+++ b/solution.py
@@ -45,6 +45,19 @@
     if axis == 0:
         return lambda k: ref.at[pl.ds(k * size, size)]
     return lambda k: ref.at[:, pl.ds(k * size, size)]
+
+
+def share_kernel(info_ref, down_ref, up_ref, out_ref, sems):
+    share, wide = out_ref.shape[0], down_ref.shape[1]
+    rows = pl.ds(pl.multiple_of(info_ref[0] * share, share), share)
+    copies = [
+        pltpu.make_async_copy(down_ref.at[rows], out_ref.at[:, :wide], sems.at[0]),
+        pltpu.make_async_copy(up_ref.at[rows], out_ref.at[:, wide:], sems.at[1]),
+    ]
+    for copy in copies:
+        copy.start()
+    for copy in copies:
+        copy.wait()
 
 
 def add_chunk(k, prod, acc, out_ref):
@@ -82,21 +95,27 @@
     )
 
 
-def next_kernel(x_ref, v_ref, o_ref, acc):
-    size = x_ref.shape[2]
+def next_kernel(x_ref, v_ref, o_ref, v_buf, acc, sems):
+    copies = chunks((part(v_ref, 0),), (v_buf,), sems)
     for k in range(CHUNKS):
-        prod = jnp.dot(x_ref[k], v_ref[k * size : (k + 1) * size, :], preferred_element_type=F32)
-        add_chunk(k, prod, acc, o_ref)
+        copies[k][0].wait()
+        add_chunk(k, jnp.dot(x_ref[k], v_buf[k], preferred_element_type=F32), acc, o_ref)
 
 
 def next_terms(x, v):
-    rows, width = x.shape[1], v.shape[1]
+    rows, wide, width = x.shape[1], v.shape[0], v.shape[1]
     return call(
         next_kernel,
         jax.ShapeDtypeStruct((rows, width), BF16),
         (x, v),
-        scratch=[pltpu.VMEM((rows, width), F32)],
+        scratch=[
+            pltpu.VMEM((CHUNKS, wide // CHUNKS, width), BF16),
+            pltpu.VMEM((rows, width), F32),
+            pltpu.SemaphoreType.DMA((1, CHUNKS)),
+        ],
         flops=2 * x.size * width,
+        limit=48,
+        specs=[VMEM, HBM],
     )
 
 
@@ -127,30 +146,34 @@
                 preferred_element_type=F32,
             )
         for k in range(len(group)):
-            match = idx_ref[...] == info_ref[first + k]
+            match = idx_ref[...] == info_ref[1 + first + k]
             low = low + jnp.where(match, prod[k * rank : (k + 1) * rank, :], 0.0)
     low_ref[...] = low
     sent_ref[...] = low.astype(BF16)
 
 
-def last_kernel(blocks, info_ref, idx_ref, low_ref, up_ref, *refs):
-    terms, others, (out_ref, spread) = refs[:blocks], refs[blocks:-2], refs[-2:]
+def sum_kernel(adapters, info_ref, *refs):
+    terms, out_ref = refs[:-1], refs[-1]
+    total = jnp.zeros(out_ref.shape, F32)
+    for n, term in enumerate(terms):
+        total = total + jnp.where(info_ref[1 + adapters + n] == 1, term[...].astype(F32), 0.0)
+    out_ref[...] = total
+
+
+def last_kernel(info_ref, idx_ref, base_ref, up_ref, low_ref, *refs):
+    others, (out_ref, spread) = refs[:-2], refs[-2:]
     rank = low_ref.shape[0]
     low = low_ref[...]
     for other in others:
         low = low + other[...].astype(F32)
     low = low.astype(BF16).astype(F32)
-    adapters = up_ref.shape[0] // rank
-    for k in range(adapters):
-        match = idx_ref[...] == info_ref[k]
+    for k in range(up_ref.shape[0] // rank):
+        match = idx_ref[...] == info_ref[1 + k]
         spread[k * rank : (k + 1) * rank, :] = jnp.where(match, low, 0.0).astype(BF16)
     lora = lax.dot_general(
         spread[...], up_ref[...], (((0,), (0,)), ((), ())), preferred_element_type=F32
     )
-    total = lora.astype(BF16).astype(F32)
-    for n, term in enumerate(terms):
-        total = total + jnp.where(info_ref[adapters + n] == 1, term[...].astype(F32), 0.0)
-    out_ref[...] = total.astype(BF16)
+    out_ref[...] = (base_ref[...] + lora.astype(BF16).astype(F32)).astype(BF16)
 
 
 def after(x, *others):
@@ -167,9 +190,6 @@
 
     def others(x, axis):
         return [shift(x, axis, by) for by in range(1, mesh.shape[axis])]
-
-    def flip(x, bit):
-        return lax.ppermute(x, "adapter", [(i, i ^ bit) for i in range(adapters)])
 
     def base_pairs(h, by):
         pairs = {}
@@ -196,19 +216,29 @@
         cols = u.shape[2]
         row = idx.reshape(1, tokens)
 
+        order = [n * sign for n in range(1, adapters // 2 + 1) for sign in (1, -1)][: adapters - 1]
+        halves = [lax.rem(r - h + replicas, replicas) * per_half for h in range(replicas)]
+        here = [((t >= n) & (t < n + per_half)).astype(jnp.int32) for n in halves]
+        info = [g * replicas + r, a] + [lax.rem(a - p + adapters, adapters) for p in order]
+        info = jnp.stack(info + here + [f for f in here for _ in range(1, tensors)])
+
         held = [v] + others(v, "replica")
 
         down = d[0].T
-        own = jnp.concatenate([down, u[0]], axis=1)
         share = rank // (groups * replicas)
-        mine = lax.dynamic_slice_in_dim(own, (g * replicas + r) * share, share, 0)
-        bits = [1 << n for n in reversed(range((adapters - 1).bit_length()))]
-        pieces = {}
-        direct = [(bit, flip(mine, bit)) for bit in bits]
+        mine = call(
+            share_kernel,
+            jax.ShapeDtypeStruct((share, wide + cols), BF16),
+            (info, down, u[0]),
+            scratch=[pltpu.SemaphoreType.DMA((2,))],
+            limit=61,
+            specs=[SMEM, HBM, HBM],
+        )
+        pieces = {1: shift(mine, "adapter", 1)} if adapters > 1 else {}
 
         blocks, recvs = [], []
 
-        def base(h):
+        def base(h, gate):
             terms, cuts = first_terms(x, v) if h == 0 else (next_terms(xs, held[h]), None)
             half = lax.rem(r - h + replicas, replicas)
             begin = half * per_half
@@ -221,26 +251,19 @@
 
             blocks.append(cut(t))
             for by in range(1, tensors):
-                block = after(cut(lax.rem(t + by, tensors)), *[piece for _, piece in direct])
+                block = after(cut(lax.rem(t + by, tensors)), *gate)
                 recvs.append(lax.ppermute(block, ("tensor", "replica"), base_pairs(h, by)))
             return terms, cuts
 
-        order = sorted(range(1, adapters), key=lambda p: (bin(p).count("1"), p))
-        halves = [lax.rem(r - h + replicas, replicas) * per_half for h in range(replicas)]
-        here = [((t >= n) & (t < n + per_half)).astype(jnp.int32) for n in halves]
-        info = [a] + [lax.bitwise_xor(a, jnp.int32(p)) for p in order]
-        info = jnp.stack(info + here + [f for f in here for _ in range(1, tensors)])
         xs = None
-        x, info = lax.optimization_barrier((x, info, mine))[:2]
-        done = []
-        for h in range(replicas):
-            terms, cuts = base(h)
-            done.append(terms)
-            xs = cuts if h == 0 else xs
-        for bit, piece in direct:
-            pieces[bit] = after(piece, done[0])
-            for prior in [p for p in pieces if p > bit and not p & bit]:
-                pieces[prior | bit] = flip(pieces[prior], bit)
+        x = after(x, mine)
+        first, xs = base(0, [])
+        for p in order[1:]:
+            sign = 1 if p > 0 else -1
+            behind = after(mine, first) if p == -1 else pieces[p - sign]
+            pieces[p] = shift(behind, "adapter", sign)
+        for h in range(1, replicas):
+            base(h, [])
         arrays, layout = [], [[(0, 0, rank)]]
 
         def keep(array):
@@ -258,7 +281,7 @@
             functools.partial(down_kernel, layout),
             (jax.ShapeDtypeStruct((rank, tokens), F32), jax.ShapeDtypeStruct((rank, tokens), BF16),
                 jax.ShapeDtypeStruct((adapters * rank, cols), BF16)),
-            (info, row, after(xs, *recvs), u[0], down, *arrays),
+            (info, row, after(xs, *recvs[: tensors - 1]), u[0], down, *arrays),
             scratch=[
                 pltpu.VMEM((CHUNKS, min(BATCH, adapters) * rank, wide // CHUNKS), BF16),
             ],
@@ -267,13 +290,20 @@
         )
         lows = others(sent, "tensor")
         terms = blocks + recvs
+        total = call(
+            functools.partial(sum_kernel, adapters),
+            jax.ShapeDtypeStruct((tokens, cols), F32),
+            (info, *terms),
+            flops=len(terms) * tokens * cols,
+            specs=[SMEM] + [VMEM] * len(terms),
+        )
         return call(
-            functools.partial(last_kernel, len(terms)),
+            last_kernel,
             jax.ShapeDtypeStruct((tokens, cols), BF16),
-            (info, row, low, every, *terms, *lows),
+            (info, row, total, every, low, *lows),
             scratch=[pltpu.VMEM((adapters * rank, tokens), BF16)],
             flops=2 * tokens * rank * adapters * cols,
-            specs=[SMEM] + [VMEM] * (3 + len(terms) + len(lows)),
+            specs=[SMEM] + [VMEM] * (4 + len(lows)),
         )
 
     return shards

time: 42.5 us -> 39 us (0.918)
  starting transfers between devices: 15.2 us -> 12.2 us
  waiting for transfers between devices: 13.5 us -> 11.2 us
  Pallas kernels: 12.6 us -> 14.7 us
  other arithmetic: 0.92 us -> 0 us
  local copies, waits for them, and re-layouts: 0.1 us -> 0.71 us
    ppermute x3 -> x0, starting transfers between devices: 6.71 us -> none  [flip(): return lax.ppermute(x, 'adapter', [(i, i ^ bit) for i in range(adapters)])]
    ppermute x11 -> x14, starting transfers between devices: 6.42 us -> 11.1 us  [shift(): return lax.ppermute(x, axis, [(i, (i + by) % size) for i in range(size)])]
    ppermute x3 -> x0, waiting for transfers between devices: 3.74 us -> none  [flip(): return lax.ppermute(x, 'adapter', [(i, i ^ bit) for i in range(adapters)])]
    pallas_call x4 -> x6, Pallas kernels: 12.6 us -> 14.7 us  [call(): pl.pallas_call(kernel, out_shape=outs, in_specs=specs or [VMEM] * len(arg...]
    ppermute x11 -> x14, waiting for transfers between devices: 9.8 us -> 11.2 us  [shift(): return lax.ppermute(x, axis, [(i, (i + by) % size) for i in range(size)])]
    ppermute x2, starting transfers between devices: 2.03 us -> 1.05 us  [base(): recvs.append(lax.ppermute(block, ('tensor', 'replica'), base_pairs(h, by)))]
    concatenate x1 -> x0, other arithmetic: 0.92 us -> none  [shards(): own = jnp.concatenate([down, u[0]], axis=1)]
    another operation x1, local copies, waits for them, and re-layouts: 0.08 us -> 0.69 us  [shards(): info = jnp.stack(info + here + [f for f in here for _ in range(1, tensors)])]
  transfers between devices with their start and end apart: 16 -> 16, of which waited for: 10 -> 6; matrix products, arithmetic and copies ran while one was open for 2% -> 2% of each run, Pallas kernels for 21% -> 33%
where the time goes in v5:
time: 39 us; the launch traced here: 38.9 us
  Pallas kernels  14.7 us (38%)
  starting transfers between devices  12.2 us (31%)
  waiting for transfers between devices  11.2 us (29%)
  local copies, waits for them, and re-layouts  0.71 us (2%)
    pallas_call x6, Pallas kernels, call(): pl.pallas_call(kernel, out_shape=outs, in_specs=specs or [VMEM] * len(arg...  14.7 us
    ppermute x14, waiting for transfers between devices, shift(): return lax.ppermute(x, axis, [(i, (i + by) % size) for i in range(size)])  11.2 us
    ppermute x14, starting transfers between devices, shift(): return lax.ppermute(x, axis, [(i, (i + by) % size) for i in range(size)])  11.1 us
    ppermute x2, starting transfers between devices, base(): recvs.append(lax.ppermute(block, ('tensor', 'replica'), base_pairs(h, by)))  1.05 us
  transfers between devices with their start and end apart: 16, of which 6 were waited for; matrix products, arithmetic and copies ran while one was open for 2% of the time, Pallas kernels for 33%

profile of v5, /device:TPU:0, one launch (start us, length us, event | category | flops | bytes accessed | tf_op | source)
XLA Modules:
  0.0 38.9 jit_solution(6255657814889571939)
XLA Ops:
  0.0 0.5 %collective-permute-start = (bf16[4096,512]{1,0:T(8,128)(2,1)}, bf16[4096,512]{1,0:T(8,128)(2,1)}, u32[]{:S(2)}, u32[]{:S(2)}) collective-permute-start(bf16[4096,512]{1,0:T(8,128)(2,1)} %v_ref.1), channel_id=1, source_target_pairs={{0,1},{1,0},{2,3},{3,2},{4,5},{5,4},{6,7},{7,6},{8,9},{9,8},{10,11... | collective-permute-start | bytes 12582920 | tf_op jit(solution)/shard_map/ppermute | solution.py:189
  0.5 0.7 %stack.41.info_ref = s32[9]{0:T(128)} concatenate(s32[1]{0:T(128)} %bitcast, s32[1]{0:T(128)} %bitcast.1, s32[1]{0:T(128)} %bitcast.2, s32[1]{0:T(128)} %bitcast.3, s32[1]{0:T(128)} %bitcast.4, s32[1]{0:T(128)} %bitcast.5, s32[1]{0:T(128)} %bitcast.6, s32[1]{0:T(128)} %bitcast.5, s32[1]{0:T(128)} %bitcast.6), dimensions={0} | concatenate | bytes 72 | tf_op jit(solution)/shard_map/stack | solution.py:223
  1.1 2.2 %shard_map.55 = bf16[16,4608]{1,0:T(8,128)(2,1)} custom-call(s32[9]{0:T(128)} %stack.41.info_ref, bf16[64,4096]{1,0:T(8,128)(2,1)} %bitcast.12, bf16[64,512]{1,0:T(8,128)(2,1)} %bitcast.14), custom_call_target="tpu_custom_call" | custom-call | bytes 589860 | tf_op jit(solution)/shard_map/pallas_call | solution.py:21
  3.4 0.0 copy-start.4
  3.4 2.6 %collective-permute-start.3 = (bf16[16,4608]{1,0:T(8,128)(2,1)}, bf16[16,4608]{1,0:T(8,128)(2,1)S(1)}, u32[]{:S(2)}, u32[]{:S(2)}) collective-permute-start(bf16[16,4608]{1,0:T(8,128)(2,1)} %shard_map.55), channel_id=1, source_target_pairs={{0,4},{4,8},{8,12},{12,0},{1,5},{5,9},{9,13},{13,1},{2,6},{6,10},{... | collective-permute-start | bytes 442376 | tf_op jit(solution)/shard_map/ppermute | solution.py:189
  6.0 4.2 %shard_map.56 = (bf16[512,512]{1,0:T(8,128)(2,1)S(1)}, bf16[4,512,1024]{2,1,0:T(8,128)(2,1)S(1)}) custom-call(bf16[512,4096]{1,0:T(8,128)(2,1)} %x_ref, bf16[4096,512]{1,0:T(8,128)(2,1)} %v_ref.1), custom_call_target="tpu_custom_call" | custom-call | flops 2147483648 | bytes 8388608 | tf_op jit(solution)/shard_map/pallas_call | solution.py:21
  10.2 0.2 collective-permute-start.1
  10.5 0.0 copy-done.4
  10.5 2.3 %collective-permute-start.7 = (bf16[16,4608]{1,0:T(8,128)(2,1)S(1)}, bf16[16,4608]{1,0:T(8,128)(2,1)S(1)}, u32[]{:S(2)}, u32[]{:S(2)}) collective-permute-start(bf16[16,4608]{1,0:T(8,128)(2,1)S(1)} %copy-done.4), channel_id=1, source_target_pairs={{0,12},{4,0},{8,4},{12,8},{1,13},{5,1},{9,5},{13,9},{2,14},{6,2},{... | collective-permute-start | bytes 442376 | tf_op jit(solution)/shard_map/ppermute | solution.py:189
  12.8 0.0 collective-permute-done.3.refs_1_
  12.8 0.9 %collective-permute-start.4 = (bf16[16,4608]{1,0:T(8,128)(2,1)S(1)}, bf16[16,4608]{1,0:T(8,128)(2,1)S(1)}, u32[]{:S(2)}, u32[]{:S(2)}) collective-permute-start(bf16[16,4608]{1,0:T(8,128)(2,1)S(1)} %collective-permute-done.3.refs_1_), channel_id=1, source_target_pairs={{0,1},{1,0},{2,3},{3,2},{4,5},{5,4},{6,7},{7,6},{8,9},{9,8},{10,11... | collective-permute-start | bytes 442376 | tf_op jit(solution)/shard_map/ppermute | solution.py:189
  13.7 1.5 %collective-permute-start.5 = (bf16[16,4608]{1,0:T(8,128)(2,1)S(1)}, bf16[16,4608]{1,0:T(8,128)(2,1)S(1)}, u32[]{:S(2)}, u32[]{:S(2)}) collective-permute-start(bf16[16,4608]{1,0:T(8,128)(2,1)S(1)} %collective-permute-done.3.refs_1_), channel_id=1, source_target_pairs={{0,16},{16,0},{1,17},{17,1},{2,18},{18,2},{3,19},{19,3},{4,20},{20... | collective-permute-start | bytes 442376 | tf_op jit(solution)/shard_map/ppermute | solution.py:189
  15.3 0.0 collective-permute-done.v_ref
  15.3 0.0 collective-permute-start.11
  15.3 0.0 copy-start.1
  15.3 0.0 copy-start.2
  15.3 0.0 copy-start.3
  15.3 3.8 %shard_map.57.refs_1_ = bf16[512,512]{1,0:T(8,128)(2,1)S(1)} custom-call(bf16[4,512,1024]{2,1,0:T(8,128)(2,1)S(1)} %get-tuple-element.16.x_ref, bf16[4096,512]{1,0:T(8,128)(2,1)} %collective-permute-done.v_ref), custom_call_target="tpu_custom_call" | custom-call | flops 2147483648 | bytes 8388608 | tf_op jit(solution)/shard_map/pallas_call | solution.py:21
  19.1 0.0 collective-permute-done.7.refs_5_
  19.1 0.8 %collective-permute-start.2 = (bf16[512,512]{1,0:T(8,128)(2,1)S(1)}, bf16[512,512]{1,0:T(8,128)(2,1)S(1)}, u32[]{:S(2)}, u32[]{:S(2)}) collective-permute-start(bf16[512,512]{1,0:T(8,128)(2,1)S(1)} %shard_map.57.refs_1_), channel_id=1, source_target_pairs={{0,2},{1,0},{2,3},{3,1},{4,6},{5,4},{6,7},{7,5},{8,10},{9,8},{10,1... | collective-permute-start | bytes 1572872 | tf_op jit(solution)/shard_map/ppermute | solution.py:255
  19.9 0.0 collective-permute-done.4.refs_2_
  19.9 0.0 collective-permute-start.8
  19.9 0.0 collective-permute-done.5.refs_3_
  19.9 1.1 %collective-permute-start.9 = (bf16[16,4608]{1,0:T(8,128)(2,1)S(1)}, bf16[16,4608]{1,0:T(8,128)(2,1)S(1)}, u32[]{:S(2)}, u32[]{:S(2)}) collective-permute-start(bf16[16,4608]{1,0:T(8,128)(2,1)S(1)} %collective-permute-done.7.refs_5_), channel_id=1, source_target_pairs={{0,16},{16,0},{1,17},{17,1},{2,18},{18,2},{3,19},{19,3},{4,20},{20... | collective-permute-start | bytes 442376 | tf_op jit(solution)/shard_map/ppermute | solution.py:189
  21.0 1.5 %collective-permute-done.11.refs_9_ = bf16[16,4608]{1,0:T(8,128)(2,1)S(1)} collective-permute-done((bf16[16,4608]{1,0:T(8,128)(2,1)S(1)}, bf16[16,4608]{1,0:T(8,128)(2,1)S(1)}, u32[]{:S(2)}, u32[]{:S(2)}) %collective-permute-start.11) | collective-permute-done | bytes 147488 | tf_op jit(solution)/shard_map/ppermute | solution.py:189
  22.5 1.4 %collective-permute-start.13 = (bf16[16,4608]{1,0:T(8,128)(2,1)S(1)}, bf16[16,4608]{1,0:T(8,128)(2,1)S(1)}, u32[]{:S(2)}, u32[]{:S(2)}) collective-permute-start(bf16[16,4608]{1,0:T(8,128)(2,1)S(1)} %collective-permute-done.11.refs_9_), channel_id=1, source_target_pairs={{0,16},{16,0},{1,17},{17,1},{2,18},{18,2},{3,19},{19,3},{4,20},{20... | collective-permute-start | bytes 442376 | tf_op jit(solution)/shard_map/ppermute | solution.py:189
  23.9 0.0 collective-permute-done.8.refs_6_
  23.9 0.0 collective-permute-start.12
  23.9 2.7 %collective-permute-done.9.refs_7_ = bf16[16,4608]{1,0:T(8,128)(2,1)S(1)} collective-permute-done((bf16[16,4608]{1,0:T(8,128)(2,1)S(1)}, bf16[16,4608]{1,0:T(8,128)(2,1)S(1)}, u32[]{:S(2)}, u32[]{:S(2)}) %collective-permute-start.9) | collective-permute-done | bytes 147488 | tf_op jit(solution)/shard_map/ppermute | solution.py:189
  26.7 0.0 collective-permute-start.6
  26.7 2.7 %collective-permute-done.13.refs_11_ = bf16[16,4608]{1,0:T(8,128)(2,1)S(1)} collective-permute-done((bf16[16,4608]{1,0:T(8,128)(2,1)S(1)}, bf16[16,4608]{1,0:T(8,128)(2,1)S(1)}, u32[]{:S(2)}, u32[]{:S(2)}) %collective-permute-start.13) | collective-permute-done | bytes 147488 | tf_op jit(solution)/shard_map/ppermute | solution.py:189
  29.4 0.0 collective-permute-start.10
  29.4 0.0 collective-permute-done.1.refs_2_
  29.4 0.5 %collective-permute-start.14 = (bf16[16,4608]{1,0:T(8,128)(2,1)S(1)}, bf16[16,4608]{1,0:T(8,128)(2,1)S(1)}, u32[]{:S(2)}, u32[]{:S(2)}) collective-permute-start(bf16[16,4608]{1,0:T(8,128)(2,1)S(1)} %collective-permute-done.13.refs_11_), channel_id=1, source_target_pairs={{0,1},{1,0},{2,3},{3,2},{4,5},{5,4},{6,7},{7,6},{8,9},{9,8},{10,11... | collective-permute-start | bytes 442376 | tf_op jit(solution)/shard_map/ppermute | solution.py:189
  29.9 0.0 collective-permute-done.6.refs_4_
  29.9 0.9 %collective-permute-done.10.refs_8_ = bf16[16,4608]{1,0:T(8,128)(2,1)S(1)} collective-permute-done((bf16[16,4608]{1,0:T(8,128)(2,1)S(1)}, bf16[16,4608]{1,0:T(8,128)(2,1)S(1)}, u32[]{:S(2)}, u32[]{:S(2)}) %collective-permute-start.10) | collective-permute-done | bytes 147488 | tf_op jit(solution)/shard_map/ppermute | solution.py:189
  30.7 0.0 collective-permute-done.12.refs_10_
  30.7 0.2 collective-permute-done.14.refs_12_
  31.0 0.0 copy-done
  31.0 0.0 copy-done.1
  31.0 0.0 copy-done.2
  31.0 0.0 copy-done.3
  31.0 1.8 %shard_map.59 = (f32[64,512]{1,0:T(8,128)S(1)}, bf16[64,512]{1,0:T(8,128)(2,1)S(1)}, bf16[256,512]{1,0:T(8,128)(2,1)S(1)}) custom-call(s32[9]{0:T(128)S(1)} %copy-done.2, s32[1,512]{1,0:T(1,128)S(1)} %bitcast.16, bf16[4,512,1024]{2,1,0:T(8,128)(2,1)S(1)} %get-tuple-element.16.x_ref, bf16[64,512]{1,0:T(8,128)(2,1)S(1)} %bitcast.15, ...), custom_call_target="tpu_custom_call" | custom-call | flops 1073741824 | bytes 6555684 | tf_op jit(solution)/shard_map/pallas_call | solution.py:21
  32.8 0.3 collective-permute-start.15
  33.1 0.0 collective-permute-done.2.refs_3_
  33.1 0.9 %shard_map.58.base_ref = f32[512,512]{1,0:T(8,128)S(1)} custom-call(s32[9]{0:T(128)S(1)} %copy-done.2, bf16[512,512]{1,0:T(8,128)(2,1)S(1)} %get-tuple-element.14.refs_0_, bf16[512,512]{1,0:T(8,128)(2,1)S(1)} %shard_map.57.refs_1_, bf16[512,512]{1,0:T(8,128)(2,1)S(1)} %collective-permute-done.1.refs_2_, bf16[512,512]{1,0:T(8,128)(2,1)S(1)} %collective-permute-done.2.refs_3_), custom_call_target="tpu_custom_call" | custom-call | flops 1048576 | bytes 2097188 | tf_op jit(solution)/shard_map/pallas_call | solution.py:21
  34.1 3.1 %collective-permute-done.15.refs_0_ = bf16[64,512]{1,0:T(8,128)(2,1)S(1)} collective-permute-done((bf16[64,512]{1,0:T(8,128)(2,1)S(1)}, bf16[64,512]{1,0:T(8,128)(2,1)S(1)}, u32[]{:S(2)}, u32[]{:S(2)}) %collective-permute-start.15) | collective-permute-done | bytes 65568 | tf_op jit(solution)/shard_map/ppermute | solution.py:189
  37.2 1.7 %shard_map.60 = bf16[512,512]{1,0:T(8,128)(2,1)} custom-call(s32[9]{0:T(128)S(1)} %copy-done.2, s32[1,512]{1,0:T(1,128)S(1)} %bitcast.17, f32[512,512]{1,0:T(8,128)S(1)} %shard_map.58.base_ref, bf16[256,512]{1,0:T(8,128)(2,1)S(1)} %get-tuple-element.18.up_ref, f32[64,512]{1,0:T(8,128)S(1)} %get-tuple-element.19.low_ref, ...), custom_call_target="tpu_custom_call" | custom-call | flops 134217728 | bytes 1509412 | tf_op jit(solution)/shard_map/pallas_call | solution.py:21
  (1 shorter events, 0.0 us)
Async XLA Ops:
  0.0 15.3 %collective-permute-start = (bf16[4096,512]{1,0:T(8,128)(2,1)}, bf16[4096,512]{1,0:T(8,128)(2,1)}, u32[]{:S(2)}, u32[]{:S(2)}) collective-permute-start(bf16[4096,512]{1,0:T(8,128)(2,1)} %v_ref.1), channel_id=1, source_target_pairs={{0,1},{1,0},{2,3},{3,2},{4,5},{5,4},{6,7},{7,6},{8,9},{9,8},{10,11... | collective-permute-start | bytes 12582920 | tf_op jit(solution)/shard_map/ppermute | solution.py:189
  3.4 7.1 %copy-start.4 = (bf16[16,4608]{1,0:T(8,128)(2,1)S(1)}, bf16[16,4608]{1,0:T(8,128)(2,1)}, u32[]{:S(2)}) copy-start(bf16[16,4608]{1,0:T(8,128)(2,1)} %shard_map.55) | copy-start | bytes 442372
  3.4 9.4 %collective-permute-start.3 = (bf16[16,4608]{1,0:T(8,128)(2,1)}, bf16[16,4608]{1,0:T(8,128)(2,1)S(1)}, u32[]{:S(2)}, u32[]{:S(2)}) collective-permute-start(bf16[16,4608]{1,0:T(8,128)(2,1)} %shard_map.55), channel_id=1, source_target_pairs={{0,4},{4,8},{8,12},{12,0},{1,5},{5,9},{9,13},{13,1},{2,6},{6,10},{... | collective-permute-start | bytes 442376 | tf_op jit(solution)/shard_map/ppermute | solution.py:189
  10.2 19.1 %collective-permute-start.1 = (bf16[512,512]{1,0:T(8,128)(2,1)S(1)}, bf16[512,512]{1,0:T(8,128)(2,1)S(1)}, u32[]{:S(2)}, u32[]{:S(2)}) collective-permute-start(bf16[512,512]{1,0:T(8,128)(2,1)S(1)} %get-tuple-element.14.refs_0_), channel_id=1, source_target_pairs={{0,1},{1,3},{2,0},{3,2},{4,5},{5,7},{6,4},{7,6},{8,9},{9,11},{10,8... | collective-permute-start | bytes 1572872 | tf_op jit(solution)/shard_map/ppermute | solution.py:255
  10.5 8.6 %collective-permute-start.7 = (bf16[16,4608]{1,0:T(8,128)(2,1)S(1)}, bf16[16,4608]{1,0:T(8,128)(2,1)S(1)}, u32[]{:S(2)}, u32[]{:S(2)}) collective-permute-start(bf16[16,4608]{1,0:T(8,128)(2,1)S(1)} %copy-done.4), channel_id=1, source_target_pairs={{0,12},{4,0},{8,4},{12,8},{1,13},{5,1},{9,5},{13,9},{2,14},{6,2},{... | collective-permute-start | bytes 442376 | tf_op jit(solution)/shard_map/ppermute | solution.py:189
  12.8 7.1 %collective-permute-start.4 = (bf16[16,4608]{1,0:T(8,128)(2,1)S(1)}, bf16[16,4608]{1,0:T(8,128)(2,1)S(1)}, u32[]{:S(2)}, u32[]{:S(2)}) collective-permute-start(bf16[16,4608]{1,0:T(8,128)(2,1)S(1)} %collective-permute-done.3.refs_1_), channel_id=1, source_target_pairs={{0,1},{1,0},{2,3},{3,2},{4,5},{5,4},{6,7},{7,6},{8,9},{9,8},{10,11... | collective-permute-start | bytes 442376 | tf_op jit(solution)/shard_map/ppermute | solution.py:189
  13.7 6.2 %collective-permute-start.5 = (bf16[16,4608]{1,0:T(8,128)(2,1)S(1)}, bf16[16,4608]{1,0:T(8,128)(2,1)S(1)}, u32[]{:S(2)}, u32[]{:S(2)}) collective-permute-start(bf16[16,4608]{1,0:T(8,128)(2,1)S(1)} %collective-permute-done.3.refs_1_), channel_id=1, source_target_pairs={{0,16},{16,0},{1,17},{17,1},{2,18},{18,2},{3,19},{19,3},{4,20},{20... | collective-permute-start | bytes 442376 | tf_op jit(solution)/shard_map/ppermute | solution.py:189
  15.3 7.3 %collective-permute-start.11 = (bf16[16,4608]{1,0:T(8,128)(2,1)S(1)}, bf16[16,4608]{1,0:T(8,128)(2,1)S(1)}, u32[]{:S(2)}, u32[]{:S(2)}) collective-permute-start(bf16[16,4608]{1,0:T(8,128)(2,1)S(1)} %collective-permute-done.3.refs_1_), channel_id=1, source_target_pairs={{0,4},{4,8},{8,12},{12,0},{1,5},{5,9},{9,13},{13,1},{2,6},{6,10},{... | collective-permute-start | bytes 442376 | tf_op jit(solution)/shard_map/ppermute | solution.py:189
  15.3 15.7 %copy-start = (bf16[1,4096,64]{1,2,0:T(8,128)(2,1)S(1)}, bf16[1,4096,64]{1,2,0:T(8,128)(2,1)}, u32[]{:S(2)}) copy-start(bf16[1,4096,64]{1,2,0:T(8,128)(2,1)} %param.7) | copy-start | bytes 1572868
  15.3 15.7 %copy-start.1 = (bf16[1,64,512]{2,1,0:T(8,128)(2,1)S(1)}, bf16[1,64,512]{2,1,0:T(8,128)(2,1)}, u32[]{:S(2)}) copy-start(bf16[1,64,512]{2,1,0:T(8,128)(2,1)} %param.8) | copy-start | bytes 196612
  15.3 15.7 %copy-start.2 = (s32[9]{0:T(128)S(1)}, s32[9]{0:T(128)}, u32[]{:S(2)}) copy-start(s32[9]{0:T(128)} %stack.41.info_ref) | copy-start | bytes 112
  15.3 15.7 %copy-start.3 = (s32[512,1]{0,1:T(1,128)S(1)}, s32[512,1]{0,1:T(1,128)}, u32[]{:S(2)}) copy-start(s32[512,1]{0,1:T(1,128)} %param.9) | copy-start | bytes 6148
  19.1 14.0 %collective-permute-start.2 = (bf16[512,512]{1,0:T(8,128)(2,1)S(1)}, bf16[512,512]{1,0:T(8,128)(2,1)S(1)}, u32[]{:S(2)}, u32[]{:S(2)}) collective-permute-start(bf16[512,512]{1,0:T(8,128)(2,1)S(1)} %shard_map.57.refs_1_), channel_id=1, source_target_pairs={{0,2},{1,0},{2,3},{3,1},{4,6},{5,4},{6,7},{7,5},{8,10},{9,8},{10,1... | collective-permute-start | bytes 1572872 | tf_op jit(solution)/shard_map/ppermute | solution.py:255
  19.9 4.0 %collective-permute-start.8 = (bf16[16,4608]{1,0:T(8,128)(2,1)S(1)}, bf16[16,4608]{1,0:T(8,128)(2,1)S(1)}, u32[]{:S(2)}, u32[]{:S(2)}) collective-permute-start(bf16[16,4608]{1,0:T(8,128)(2,1)S(1)} %collective-permute-done.7.refs_5_), channel_id=1, source_target_pairs={{0,1},{1,0},{2,3},{3,2},{4,5},{5,4},{6,7},{7,6},{8,9},{9,8},{10,11... | collective-permute-start | bytes 442376 | tf_op jit(solution)/shard_map/ppermute | solution.py:189
  19.9 6.7 %collective-permute-start.9 = (bf16[16,4608]{1,0:T(8,128)(2,1)S(1)}, bf16[16,4608]{1,0:T(8,128)(2,1)S(1)}, u32[]{:S(2)}, u32[]{:S(2)}) collective-permute-start(bf16[16,4608]{1,0:T(8,128)(2,1)S(1)} %collective-permute-done.7.refs_5_), channel_id=1, source_target_pairs={{0,16},{16,0},{1,17},{17,1},{2,18},{18,2},{3,19},{19,3},{4,20},{20... | collective-permute-start | bytes 442376 | tf_op jit(solution)/shard_map/ppermute | solution.py:189
  22.5 6.8 %collective-permute-start.13 = (bf16[16,4608]{1,0:T(8,128)(2,1)S(1)}, bf16[16,4608]{1,0:T(8,128)(2,1)S(1)}, u32[]{:S(2)}, u32[]{:S(2)}) collective-permute-start(bf16[16,4608]{1,0:T(8,128)(2,1)S(1)} %collective-permute-done.11.refs_9_), channel_id=1, source_target_pairs={{0,16},{16,0},{1,17},{17,1},{2,18},{18,2},{3,19},{19,3},{4,20},{20... | collective-permute-start | bytes 442376 | tf_op jit(solution)/shard_map/ppermute | solution.py:189
  23.9 6.8 %collective-permute-start.12 = (bf16[16,4608]{1,0:T(8,128)(2,1)S(1)}, bf16[16,4608]{1,0:T(8,128)(2,1)S(1)}, u32[]{:S(2)}, u32[]{:S(2)}) collective-permute-start(bf16[16,4608]{1,0:T(8,128)(2,1)S(1)} %collective-permute-done.11.refs_9_), channel_id=1, source_target_pairs={{0,1},{1,0},{2,3},{3,2},{4,5},{5,4},{6,7},{7,6},{8,9},{9,8},{10,11... | collective-permute-start | bytes 442376 | tf_op jit(solution)/shard_map/ppermute | solution.py:189
  26.7 3.2 %collective-permute-start.6 = (bf16[16,4608]{1,0:T(8,128)(2,1)S(1)}, bf16[16,4608]{1,0:T(8,128)(2,1)S(1)}, u32[]{:S(2)}, u32[]{:S(2)}) collective-permute-start(bf16[16,4608]{1,0:T(8,128)(2,1)S(1)} %collective-permute-done.5.refs_3_), channel_id=1, source_target_pairs={{0,1},{1,0},{2,3},{3,2},{4,5},{5,4},{6,7},{7,6},{8,9},{9,8},{10,11... | collective-permute-start | bytes 442376 | tf_op jit(solution)/shard_map/ppermute | solution.py:189
  29.4 1.4 %collective-permute-start.10 = (bf16[16,4608]{1,0:T(8,128)(2,1)S(1)}, bf16[16,4608]{1,0:T(8,128)(2,1)S(1)}, u32[]{:S(2)}, u32[]{:S(2)}) collective-permute-start(bf16[16,4608]{1,0:T(8,128)(2,1)S(1)} %collective-permute-done.9.refs_7_), channel_id=1, source_target_pairs={{0,1},{1,0},{2,3},{3,2},{4,5},{5,4},{6,7},{7,6},{8,9},{9,8},{10,11... | collective-permute-start | bytes 442376 | tf_op jit(solution)/shard_map/ppermute | solution.py:189
  29.4 1.6 %collective-permute-start.14 = (bf16[16,4608]{1,0:T(8,128)(2,1)S(1)}, bf16[16,4608]{1,0:T(8,128)(2,1)S(1)}, u32[]{:S(2)}, u32[]{:S(2)}) collective-permute-start(bf16[16,4608]{1,0:T(8,128)(2,1)S(1)} %collective-permute-done.13.refs_11_), channel_id=1, source_target_pairs={{0,1},{1,0},{2,3},{3,2},{4,5},{5,4},{6,7},{7,6},{8,9},{9,8},{10,11... | collective-permute-start | bytes 442376 | tf_op jit(solution)/shard_map/ppermute | solution.py:189
  32.8 4.4 %collective-permute-start.15 = (bf16[64,512]{1,0:T(8,128)(2,1)S(1)}, bf16[64,512]{1,0:T(8,128)(2,1)S(1)}, u32[]{:S(2)}, u32[]{:S(2)}) collective-permute-start(bf16[64,512]{1,0:T(8,128)(2,1)S(1)} %get-tuple-element.20), channel_id=1, source_target_pairs={{0,2},{2,0},{1,3},{3,1},{4,6},{6,4},{5,7},{7,5},{8,10},{10,8},{9,1... | collective-permute-start | bytes 196616 | tf_op jit(solution)/shard_map/ppermute | solution.py:189

commit v6 on v5

--- a/solution.py
+++ b/solution.py
@@ -47,17 +47,11 @@
     return lambda k: ref.at[:, pl.ds(k * size, size)]
 
 
-def share_kernel(info_ref, down_ref, up_ref, out_ref, sems):
-    share, wide = out_ref.shape[0], down_ref.shape[1]
-    rows = pl.ds(pl.multiple_of(info_ref[0] * share, share), share)
-    copies = [
-        pltpu.make_async_copy(down_ref.at[rows], out_ref.at[:, :wide], sems.at[0]),
-        pltpu.make_async_copy(up_ref.at[rows], out_ref.at[:, wide:], sems.at[1]),
-    ]
-    for copy in copies:
-        copy.start()
-    for copy in copies:
-        copy.wait()
+def pack_kernel(*refs):
+    row = 0
+    for ref in refs[:-1]:
+        refs[-1][row : row + ref.shape[0], :] = ref[...]
+        row += ref.shape[0]
 
 
 def add_chunk(k, prod, acc, out_ref):
@@ -146,7 +140,7 @@
                 preferred_element_type=F32,
             )
         for k in range(len(group)):
-            match = idx_ref[...] == info_ref[1 + first + k]
+            match = idx_ref[...] == info_ref[first + k]
             low = low + jnp.where(match, prod[k * rank : (k + 1) * rank, :], 0.0)
     low_ref[...] = low
     sent_ref[...] = low.astype(BF16)
@@ -156,7 +150,7 @@
     terms, out_ref = refs[:-1], refs[-1]
     total = jnp.zeros(out_ref.shape, F32)
     for n, term in enumerate(terms):
-        total = total + jnp.where(info_ref[1 + adapters + n] == 1, term[...].astype(F32), 0.0)
+        total = total + jnp.where(info_ref[adapters + n] == 1, term[...].astype(F32), 0.0)
     out_ref[...] = total
 
 
@@ -168,7 +162,7 @@
         low = low + other[...].astype(F32)
     low = low.astype(BF16).astype(F32)
     for k in range(up_ref.shape[0] // rank):
-        match = idx_ref[...] == info_ref[1 + k]
+        match = idx_ref[...] == info_ref[k]
         spread[k * rank : (k + 1) * rank, :] = jnp.where(match, low, 0.0).astype(BF16)
     lora = lax.dot_general(
         spread[...], up_ref[...], (((0,), (0,)), ((), ())), preferred_element_type=F32
@@ -219,21 +213,15 @@
         order = [n * sign for n in range(1, adapters // 2 + 1) for sign in (1, -1)][: adapters - 1]
         halves = [lax.rem(r - h + replicas, replicas) * per_half for h in range(replicas)]
         here = [((t >= n) & (t < n + per_half)).astype(jnp.int32) for n in halves]
-        info = [g * replicas + r, a] + [lax.rem(a - p + adapters, adapters) for p in order]
+        info = [a] + [lax.rem(a - p + adapters, adapters) for p in order]
         info = jnp.stack(info + here + [f for f in here for _ in range(1, tensors)])
 
         held = [v] + others(v, "replica")
 
         down = d[0].T
         share = rank // (groups * replicas)
-        mine = call(
-            share_kernel,
-            jax.ShapeDtypeStruct((share, wide + cols), BF16),
-            (info, down, u[0]),
-            scratch=[pltpu.SemaphoreType.DMA((2,))],
-            limit=61,
-            specs=[SMEM, HBM, HBM],
-        )
+        own = jnp.concatenate([down, u[0]], axis=1)
+        mine = lax.dynamic_slice_in_dim(own, (g * replicas + r) * share, share, 0)
         pieces = {1: shift(mine, "adapter", 1)} if adapters > 1 else {}
 
         blocks, recvs = [], []
@@ -256,37 +244,59 @@
             return terms, cuts
 
         xs = None
-        x = after(x, mine)
-        first, xs = base(0, [])
-        for p in order[1:]:
+        x, info = lax.optimization_barrier((x, info, mine))[:2]
+        near = [p for p in order if abs(p) == 1]
+        for p in near[1:]:
+            pieces[p] = shift(mine, "adapter", p)
+        first, xs = base(0, [pieces[n] for n in near])
+        for p, piece in zip(near, lax.optimization_barrier((*[pieces[p] for p in near], first))):
+            pieces[p] = piece
+        for p in order[len(near) :]:
             sign = 1 if p > 0 else -1
-            behind = after(mine, first) if p == -1 else pieces[p - sign]
-            pieces[p] = shift(behind, "adapter", sign)
+            pieces[p] = shift(pieces[p - sign], "adapter", sign)
         for h in range(1, replicas):
-            base(h, [])
-        arrays, layout = [], [[(0, 0, rank)]]
-
-        def keep(array):
-            arrays.append(array)
-            return len(arrays)
-
-        for p in order:
-            layout.append([])
-            piece = pieces[p]
-            for member in [piece] + others(piece, "groups"):
-                for array in [member] + others(member, "replica"):
-                    layout[-1].append((keep(array), 0, share))
+            base(h, [pieces[order[-1]]])
+        arrays, layout = [down], [[(0, 0, rank)]] + [[] for _ in order]
+
+        def keep(k, array, begin=0):
+            where = [n for n, other in enumerate(arrays) if other is array]
+            if not where:
+                arrays.append(array)
+            layout[k].append((where[0] if where else len(arrays) - 1, begin, share))
+
+        shares = [
+            (1 + n, member)
+            for n, p in enumerate(order)
+            for member in [pieces[p]] + others(pieces[p], "groups")
+        ]
+        for k, member in shares:
+            keep(k, member)
+        if replicas > 1:
+            (last, member), bundles = shares[-1], [shares[n : n + 2] for n in range(0, len(shares) - 1, 2)]
+            bundles[-1] = [s for s in bundles[-1] if s is not shares[-1]]
+            held_back = blocks
+            for bundle in bundles:
+                members = lax.optimization_barrier((*[array for _, array in bundle], *held_back))[: len(bundle)]
+                packed = members[0]
+                if len(bundle) > 1:
+                    shape = (share * len(bundle), wide + cols)
+                    packed = call(pack_kernel, jax.ShapeDtypeStruct(shape, BF16), tuple(members))
+                for other in others(packed, "replica"):
+                    for n, (k, _) in enumerate(bundle):
+                        keep(k, other, n * share)
+            for other in others(member, "replica"):
+                keep(last, other)
 
         low, sent, every = call(
             functools.partial(down_kernel, layout),
             (jax.ShapeDtypeStruct((rank, tokens), F32), jax.ShapeDtypeStruct((rank, tokens), BF16),
                 jax.ShapeDtypeStruct((adapters * rank, cols), BF16)),
-            (info, row, after(xs, *recvs[: tensors - 1]), u[0], down, *arrays),
+            (info, row, after(xs, *recvs[: tensors - 1]), u[0], *arrays),
             scratch=[
                 pltpu.VMEM((CHUNKS, min(BATCH, adapters) * rank, wide // CHUNKS), BF16),
             ],
             flops=2 * x.size * rank * adapters,
-            specs=[SMEM] + [VMEM] * (4 + len(arrays)),
+            specs=[SMEM] + [VMEM] * (3 + len(arrays)),
         )
         lows = others(sent, "tensor")
         terms = blocks + recvs

time: 39 us -> 37.5 us (0.962)
  Pallas kernels: 14.7 us -> 12.5 us
  starting transfers between devices: 12.2 us -> 13.3 us
  other arithmetic: 0 us -> 0.92 us
  waiting for transfers between devices: 11.2 us -> 10.5 us
  local copies, waits for them, and re-layouts: 0.71 us -> 0.1 us
    pallas_call x6 -> x7, Pallas kernels: 14.7 us -> 12.5 us  [call(): pl.pallas_call(kernel, out_shape=outs, in_specs=specs or [VMEM] * len(arg...]
    concatenate x0 -> x1, other arithmetic: none -> 0.92 us  [shards(): own = jnp.concatenate([down, u[0]], axis=1)]
    ppermute x14 -> x12, starting transfers between devices: 11.1 us -> 12 us  [shift(): return lax.ppermute(x, axis, [(i, (i + by) % size) for i in range(size)])]
    ppermute x14 -> x12, waiting for transfers between devices: 11.2 us -> 10.5 us  [shift(): return lax.ppermute(x, axis, [(i, (i + by) % size) for i in range(size)])]
    another operation x1, local copies, waits for them, and re-layouts: 0.69 us -> 0.08 us  [shards(): info = jnp.stack(info + here + [f for f in here for _ in range(1, tensors)])]
  transfers between devices with their start and end apart: 16 -> 14, of which waited for: 6 -> 7; matrix products, arithmetic and copies ran while one was open for 2% -> 3% of each run, Pallas kernels for 33% -> 29%
where the time goes in v6:
time: 37.5 us; the launch traced here: 37.3 us
  starting transfers between devices  13.3 us (35%)
  Pallas kernels  12.5 us (33%)
  waiting for transfers between devices  10.5 us (28%)
  other arithmetic  0.92 us (2%)
    pallas_call x7, Pallas kernels, call(): pl.pallas_call(kernel, out_shape=outs, in_specs=specs or [VMEM] * len(arg...  12.5 us
    ppermute x12, starting transfers between devices, shift(): return lax.ppermute(x, axis, [(i, (i + by) % size) for i in range(size)])  12 us
    ppermute x12, waiting for transfers between devices, shift(): return lax.ppermute(x, axis, [(i, (i + by) % size) for i in range(size)])  10.5 us
    ppermute x2, starting transfers between devices, base(): recvs.append(lax.ppermute(block, ('tensor', 'replica'), base_pairs(h, by)))  1.3 us
    concatenate x1, other arithmetic, shards(): own = jnp.concatenate([down, u[0]], axis=1)  0.92 us
  transfers between devices with their start and end apart: 14, of which 7 were waited for; matrix products, arithmetic and copies ran while one was open for 3% of the time, Pallas kernels for 29%

profile of v6, /device:TPU:0, one launch (start us, length us, event | category | flops | bytes accessed | tf_op | source)
XLA Modules:
  0.0 37.3 jit_solution(18003348447921658906)
XLA Ops:
  0.0 0.5 %collective-permute-start = (bf16[4096,512]{1,0:T(8,128)(2,1)}, bf16[4096,512]{1,0:T(8,128)(2,1)}, u32[]{:S(2)}, u32[]{:S(2)}) collective-permute-start(bf16[4096,512]{1,0:T(8,128)(2,1)} %v_ref.1), channel_id=1, source_target_pairs={{0,1},{1,0},{2,3},{3,2},{4,5},{5,4},{6,7},{7,6},{8,9},{9,8},{10,11... | collective-permute-start | bytes 12582920 | tf_op jit(solution)/shard_map/ppermute | solution.py:183
  0.5 0.9 %fusion = bf16[16,4608]{1,0:T(8,128)(2,1)S(1)} fusion(s32[]{:T(128)S(6)} %select_n.3, bf16[64,4096]{1,0:T(8,128)(2,1)} %bitcast.11, bf16[64,512]{1,0:T(8,128)(2,1)} %bitcast.13), kind=kLoop, calls=%fused_computation.2 | loop fusion | flops 294912 | bytes 737284 | tf_op jit(solution)/shard_map/concatenate | solution.py:223
  1.4 2.6 %collective-permute-start.1 = (bf16[16,4608]{1,0:T(8,128)(2,1)S(1)}, bf16[16,4608]{1,0:T(8,128)(2,1)S(1)}, u32[]{:S(2)}, u32[]{:S(2)}) collective-permute-start(bf16[16,4608]{1,0:T(8,128)(2,1)S(1)} %fusion), channel_id=1, source_target_pairs={{0,4},{4,8},{8,12},{12,0},{1,5},{5,9},{9,13},{13,1},{2,6},{6,10},{... | collective-permute-start | bytes 442376 | tf_op jit(solution)/shard_map/ppermute | solution.py:183
  4.0 2.1 %collective-permute-start.2 = (bf16[16,4608]{1,0:T(8,128)(2,1)S(1)}, bf16[16,4608]{1,0:T(8,128)(2,1)S(1)}, u32[]{:S(2)}, u32[]{:S(2)}) collective-permute-start(bf16[16,4608]{1,0:T(8,128)(2,1)S(1)} %fusion), channel_id=1, source_target_pairs={{0,12},{4,0},{8,4},{12,8},{1,13},{5,1},{9,5},{13,9},{2,14},{6,2},{... | collective-permute-start | bytes 442376 | tf_op jit(solution)/shard_map/ppermute | solution.py:183
  6.1 0.1 stack.37.info_ref
  6.2 4.2 %shard_map.55 = (bf16[512,512]{1,0:T(8,128)(2,1)S(1)}, bf16[4,512,1024]{2,1,0:T(8,128)(2,1)S(1)}) custom-call(bf16[512,4096]{1,0:T(8,128)(2,1)} %x_ref, bf16[4096,512]{1,0:T(8,128)(2,1)} %v_ref.1), custom_call_target="tpu_custom_call" | custom-call | flops 2147483648 | bytes 8388608 | tf_op jit(solution)/shard_map/pallas_call | solution.py:21
  10.4 0.4 %collective-permute-done.1.refs_0_.refs_1_ = bf16[16,4608]{1,0:T(8,128)(2,1)S(1)} collective-permute-done((bf16[16,4608]{1,0:T(8,128)(2,1)S(1)}, bf16[16,4608]{1,0:T(8,128)(2,1)S(1)}, u32[]{:S(2)}, u32[]{:S(2)}) %collective-permute-start.1) | collective-permute-done | bytes 147488 | tf_op jit(solution)/shard_map/ppermute | solution.py:183
  10.8 2.4 %collective-permute-done.2.refs_0_.refs_3_ = bf16[16,4608]{1,0:T(8,128)(2,1)S(1)} collective-permute-done((bf16[16,4608]{1,0:T(8,128)(2,1)S(1)}, bf16[16,4608]{1,0:T(8,128)(2,1)S(1)}, u32[]{:S(2)}, u32[]{:S(2)}) %collective-permute-start.2) | collective-permute-done | bytes 147488 | tf_op jit(solution)/shard_map/ppermute | solution.py:183
  13.1 0.0 collective-permute-start.3
  13.1 1.2 %collective-permute-start.4 = (bf16[16,4608]{1,0:T(8,128)(2,1)S(1)}, bf16[16,4608]{1,0:T(8,128)(2,1)S(1)}, u32[]{:S(2)}, u32[]{:S(2)}) collective-permute-start(bf16[16,4608]{1,0:T(8,128)(2,1)S(1)} %collective-permute-done.1.refs_0_.refs_1_), channel_id=1, source_target_pairs={{0,4},{4,8},{8,12},{12,0},{1,5},{5,9},{9,13},{13,1},{2,6},{6,10},{... | collective-permute-start | bytes 442376 | tf_op jit(solution)/shard_map/ppermute | solution.py:183
  14.3 1.5 %collective-permute-start.6 = (bf16[16,4608]{1,0:T(8,128)(2,1)S(1)}, bf16[16,4608]{1,0:T(8,128)(2,1)S(1)}, u32[]{:S(2)}, u32[]{:S(2)}) collective-permute-start(bf16[16,4608]{1,0:T(8,128)(2,1)S(1)} %collective-permute-done.1.refs_0_.refs_1_), channel_id=1, source_target_pairs={{0,16},{16,0},{1,17},{17,1},{2,18},{18,2},{3,19},{19,3},{4,20},{20... | collective-permute-start | bytes 442376 | tf_op jit(solution)/shard_map/ppermute | solution.py:183
  15.8 0.5 %collective-permute-start.7 = (bf16[16,4608]{1,0:T(8,128)(2,1)S(1)}, bf16[16,4608]{1,0:T(8,128)(2,1)S(1)}, u32[]{:S(2)}, u32[]{:S(2)}) collective-permute-start(bf16[16,4608]{1,0:T(8,128)(2,1)S(1)} %collective-permute-done.2.refs_0_.refs_3_), channel_id=1, source_target_pairs={{0,16},{16,0},{1,17},{17,1},{2,18},{18,2},{3,19},{19,3},{4,20},{20... | collective-permute-start | bytes 442376 | tf_op jit(solution)/shard_map/ppermute | solution.py:183
  16.3 0.0 collective-permute-done.v_ref
  16.3 0.0 copy-start
  16.3 0.0 copy-start.1
  16.3 0.0 copy-start.2
  16.4 3.8 %shard_map.56.refs_1_ = bf16[512,512]{1,0:T(8,128)(2,1)S(1)} custom-call(bf16[4,512,1024]{2,1,0:T(8,128)(2,1)S(1)} %get-tuple-element.29.x_ref, bf16[4096,512]{1,0:T(8,128)(2,1)} %collective-permute-done.v_ref), custom_call_target="tpu_custom_call" | custom-call | flops 2147483648 | bytes 8388608 | tf_op jit(solution)/shard_map/pallas_call | solution.py:21
  20.2 1.2 %collective-permute-done.4.refs_5_ = bf16[16,4608]{1,0:T(8,128)(2,1)S(1)} collective-permute-done((bf16[16,4608]{1,0:T(8,128)(2,1)S(1)}, bf16[16,4608]{1,0:T(8,128)(2,1)S(1)}, u32[]{:S(2)}, u32[]{:S(2)}) %collective-permute-start.4) | collective-permute-done | bytes 147488 | tf_op jit(solution)/shard_map/ppermute | solution.py:183
  21.4 1.3 %collective-permute-start.5 = (bf16[512,512]{1,0:T(8,128)(2,1)S(1)}, bf16[512,512]{1,0:T(8,128)(2,1)S(1)}, u32[]{:S(2)}, u32[]{:S(2)}) collective-permute-start(bf16[512,512]{1,0:T(8,128)(2,1)S(1)} %shard_map.56.refs_1_), channel_id=1, source_target_pairs={{0,2},{1,0},{2,3},{3,1},{4,6},{5,4},{6,7},{7,5},{8,10},{9,8},{10,1... | collective-permute-start | bytes 1572872 | tf_op jit(solution)/shard_map/ppermute | solution.py:243
  22.7 1.5 %collective-permute-start.8 = (bf16[16,4608]{1,0:T(8,128)(2,1)S(1)}, bf16[16,4608]{1,0:T(8,128)(2,1)S(1)}, u32[]{:S(2)}, u32[]{:S(2)}) collective-permute-start(bf16[16,4608]{1,0:T(8,128)(2,1)S(1)} %collective-permute-done.4.refs_5_), channel_id=1, source_target_pairs={{0,16},{16,0},{1,17},{17,1},{2,18},{18,2},{3,19},{19,3},{4,20},{20... | collective-permute-start | bytes 442376 | tf_op jit(solution)/shard_map/ppermute | solution.py:183
  24.2 0.0 collective-permute-done.6.refs_1_.refs_2_
  24.2 0.1 collective-permute-start.9
  24.3 0.0 collective-permute-done.7.refs_1_.refs_4_
  24.4 0.5 %collective-permute-start.10 = (bf16[32,4608]{1,0:T(8,128)(2,1)S(1)}, bf16[32,4608]{1,0:T(8,128)(2,1)S(1)}, u32[]{:S(2)}, u32[]{:S(2)}) collective-permute-start(bf16[32,4608]{1,0:T(8,128)(2,1)S(1)} %shard_map.59), channel_id=1, source_target_pairs={{0,1},{1,0},{2,3},{3,2},{4,5},{5,4},{6,7},{7,6},{8,9},{9,8},{10,11... | collective-permute-start | bytes 884744 | tf_op jit(solution)/shard_map/ppermute | solution.py:183
  24.9 2.9 %collective-permute-done.8.refs_6_ = bf16[16,4608]{1,0:T(8,128)(2,1)S(1)} collective-permute-done((bf16[16,4608]{1,0:T(8,128)(2,1)S(1)}, bf16[16,4608]{1,0:T(8,128)(2,1)S(1)}, u32[]{:S(2)}, u32[]{:S(2)}) %collective-permute-start.8) | collective-permute-done | bytes 147488 | tf_op jit(solution)/shard_map/ppermute | solution.py:183
  27.8 0.0 collective-permute-start.12
  27.8 0.0 collective-permute-done.3.refs_2_
  27.8 0.5 %collective-permute-start.11 = (bf16[16,4608]{1,0:T(8,128)(2,1)S(1)}, bf16[16,4608]{1,0:T(8,128)(2,1)S(1)}, u32[]{:S(2)}, u32[]{:S(2)}) collective-permute-start(bf16[16,4608]{1,0:T(8,128)(2,1)S(1)} %collective-permute-done.4.refs_5_), channel_id=1, source_target_pairs={{0,1},{1,0},{2,3},{3,2},{4,5},{5,4},{6,7},{7,6},{8,9},{9,8},{10,11... | collective-permute-start | bytes 442376 | tf_op jit(solution)/shard_map/ppermute | solution.py:183
  28.4 0.9 %collective-permute-done.12.refs_10_ = bf16[16,4608]{1,0:T(8,128)(2,1)S(1)} collective-permute-done((bf16[16,4608]{1,0:T(8,128)(2,1)S(1)}, bf16[16,4608]{1,0:T(8,128)(2,1)S(1)}, u32[]{:S(2)}, u32[]{:S(2)}) %collective-permute-start.12) | collective-permute-done | bytes 147488 | tf_op jit(solution)/shard_map/ppermute | solution.py:183
  29.2 0.2 collective-permute-done.11.refs_9_
  29.4 0.0 collective-permute-done.9.refs_7_
  29.4 0.0 collective-permute-done.10.refs_8_
  29.4 0.0 copy-done
  29.4 0.0 copy-done.1
  29.4 0.0 copy-done.2
  29.5 1.8 %shard_map.60 = (f32[64,512]{1,0:T(8,128)S(1)}, bf16[64,512]{1,0:T(8,128)(2,1)S(1)}, bf16[256,512]{1,0:T(8,128)(2,1)S(1)}) custom-call(s32[8]{0:T(128)S(1)} %stack.37.info_ref, s32[1,512]{1,0:T(1,128)S(1)} %bitcast.15, bf16[4,512,1024]{2,1,0:T(8,128)(2,1)S(1)} %get-tuple-element.29.x_ref, bf16[64,512]{1,0:T(8,128)(2,1)S(1)} %bitcast.14, ...), custom_call_target="tpu_custom_call" | custom-call | flops 1073741824 | bytes 6555680 | tf_op jit(solution)/shard_map/pallas_call | solution.py:21
  31.3 1.0 %collective-permute-start.13 = (bf16[64,512]{1,0:T(8,128)(2,1)S(1)}, bf16[64,512]{1,0:T(8,128)(2,1)S(1)}, u32[]{:S(2)}, u32[]{:S(2)}) collective-permute-start(bf16[64,512]{1,0:T(8,128)(2,1)S(1)} %get-tuple-element.38), channel_id=1, source_target_pairs={{0,2},{2,0},{1,3},{3,1},{4,6},{6,4},{5,7},{7,5},{8,10},{10,8},{9,1... | collective-permute-start | bytes 196616 | tf_op jit(solution)/shard_map/ppermute | solution.py:183
  32.3 0.0 collective-permute-done.5.refs_3_
  32.3 0.9 %shard_map.57.base_ref = f32[512,512]{1,0:T(8,128)S(1)} custom-call(s32[8]{0:T(128)S(1)} %stack.37.info_ref, bf16[512,512]{1,0:T(8,128)(2,1)S(1)} %get-tuple-element.26.refs_0_, bf16[512,512]{1,0:T(8,128)(2,1)S(1)} %shard_map.56.refs_1_, bf16[512,512]{1,0:T(8,128)(2,1)S(1)} %collective-permute-done.3.refs_2_, bf16[512,512]{1,0:T(8,128)(2,1)S(1)} %collective-permute-done.5.refs_3_), custom_call_target="tpu_custom_call" | custom-call | flops 1048576 | bytes 2097184 | tf_op jit(solution)/shard_map/pallas_call | solution.py:21
  33.2 2.5 %collective-permute-done.13.refs_0_ = bf16[64,512]{1,0:T(8,128)(2,1)S(1)} collective-permute-done((bf16[64,512]{1,0:T(8,128)(2,1)S(1)}, bf16[64,512]{1,0:T(8,128)(2,1)S(1)}, u32[]{:S(2)}, u32[]{:S(2)}) %collective-permute-start.13) | collective-permute-done | bytes 65568 | tf_op jit(solution)/shard_map/ppermute | solution.py:183
  35.7 1.7 %shard_map.61 = bf16[512,512]{1,0:T(8,128)(2,1)} custom-call(s32[8]{0:T(128)S(1)} %stack.37.info_ref, s32[1,512]{1,0:T(1,128)S(1)} %bitcast.16, f32[512,512]{1,0:T(8,128)S(1)} %shard_map.57.base_ref, bf16[256,512]{1,0:T(8,128)(2,1)S(1)} %get-tuple-element.36.up_ref, f32[64,512]{1,0:T(8,128)S(1)} %get-tuple-element.37.low_ref, ...), custom_call_target="tpu_custom_call" | custom-call | flops 134217728 | bytes 1509408 | tf_op jit(solution)/shard_map/pallas_call | solution.py:21
  (2 shorter events, 0.0 us)
Async XLA Ops:
  0.0 16.3 %collective-permute-start = (bf16[4096,512]{1,0:T(8,128)(2,1)}, bf16[4096,512]{1,0:T(8,128)(2,1)}, u32[]{:S(2)}, u32[]{:S(2)}) collective-permute-start(bf16[4096,512]{1,0:T(8,128)(2,1)} %v_ref.1), channel_id=1, source_target_pairs={{0,1},{1,0},{2,3},{3,2},{4,5},{5,4},{6,7},{7,6},{8,9},{9,8},{10,11... | collective-permute-start | bytes 12582920 | tf_op jit(solution)/shard_map/ppermute | solution.py:183
  1.4 9.4 %collective-permute-start.1 = (bf16[16,4608]{1,0:T(8,128)(2,1)S(1)}, bf16[16,4608]{1,0:T(8,128)(2,1)S(1)}, u32[]{:S(2)}, u32[]{:S(2)}) collective-permute-start(bf16[16,4608]{1,0:T(8,128)(2,1)S(1)} %fusion), channel_id=1, source_target_pairs={{0,4},{4,8},{8,12},{12,0},{1,5},{5,9},{9,13},{13,1},{2,6},{6,10},{... | collective-permute-start | bytes 442376 | tf_op jit(solution)/shard_map/ppermute | solution.py:183
  4.0 9.1 %collective-permute-start.2 = (bf16[16,4608]{1,0:T(8,128)(2,1)S(1)}, bf16[16,4608]{1,0:T(8,128)(2,1)S(1)}, u32[]{:S(2)}, u32[]{:S(2)}) collective-permute-start(bf16[16,4608]{1,0:T(8,128)(2,1)S(1)} %fusion), channel_id=1, source_target_pairs={{0,12},{4,0},{8,4},{12,8},{1,13},{5,1},{9,5},{13,9},{2,14},{6,2},{... | collective-permute-start | bytes 442376 | tf_op jit(solution)/shard_map/ppermute | solution.py:183
  13.1 14.7 %collective-permute-start.3 = (bf16[512,512]{1,0:T(8,128)(2,1)S(1)}, bf16[512,512]{1,0:T(8,128)(2,1)S(1)}, u32[]{:S(2)}, u32[]{:S(2)}) collective-permute-start(bf16[512,512]{1,0:T(8,128)(2,1)S(1)} %get-tuple-element.26.refs_0_), channel_id=1, source_target_pairs={{0,1},{1,3},{2,0},{3,2},{4,5},{5,7},{6,4},{7,6},{8,9},{9,11},{10,8... | collective-permute-start | bytes 1572872 | tf_op jit(solution)/shard_map/ppermute | solution.py:243
  13.1 8.2 %collective-permute-start.4 = (bf16[16,4608]{1,0:T(8,128)(2,1)S(1)}, bf16[16,4608]{1,0:T(8,128)(2,1)S(1)}, u32[]{:S(2)}, u32[]{:S(2)}) collective-permute-start(bf16[16,4608]{1,0:T(8,128)(2,1)S(1)} %collective-permute-done.1.refs_0_.refs_1_), channel_id=1, source_target_pairs={{0,4},{4,8},{8,12},{12,0},{1,5},{5,9},{9,13},{13,1},{2,6},{6,10},{... | collective-permute-start | bytes 442376 | tf_op jit(solution)/shard_map/ppermute | solution.py:183
  14.3 9.9 %collective-permute-start.6 = (bf16[16,4608]{1,0:T(8,128)(2,1)S(1)}, bf16[16,4608]{1,0:T(8,128)(2,1)S(1)}, u32[]{:S(2)}, u32[]{:S(2)}) collective-permute-start(bf16[16,4608]{1,0:T(8,128)(2,1)S(1)} %collective-permute-done.1.refs_0_.refs_1_), channel_id=1, source_target_pairs={{0,16},{16,0},{1,17},{17,1},{2,18},{18,2},{3,19},{19,3},{4,20},{20... | collective-permute-start | bytes 442376 | tf_op jit(solution)/shard_map/ppermute | solution.py:183
  15.8 8.5 %collective-permute-start.7 = (bf16[16,4608]{1,0:T(8,128)(2,1)S(1)}, bf16[16,4608]{1,0:T(8,128)(2,1)S(1)}, u32[]{:S(2)}, u32[]{:S(2)}) collective-permute-start(bf16[16,4608]{1,0:T(8,128)(2,1)S(1)} %collective-permute-done.2.refs_0_.refs_3_), channel_id=1, source_target_pairs={{0,16},{16,0},{1,17},{17,1},{2,18},{18,2},{3,19},{19,3},{4,20},{20... | collective-permute-start | bytes 442376 | tf_op jit(solution)/shard_map/ppermute | solution.py:183
  16.3 13.1 %copy-start = (bf16[1,4096,64]{1,2,0:T(8,128)(2,1)S(1)}, bf16[1,4096,64]{1,2,0:T(8,128)(2,1)}, u32[]{:S(2)}) copy-start(bf16[1,4096,64]{1,2,0:T(8,128)(2,1)} %param.7) | copy-start | bytes 1572868
  16.3 13.1 %copy-start.1 = (bf16[1,64,512]{2,1,0:T(8,128)(2,1)S(1)}, bf16[1,64,512]{2,1,0:T(8,128)(2,1)}, u32[]{:S(2)}) copy-start(bf16[1,64,512]{2,1,0:T(8,128)(2,1)} %param.8) | copy-start | bytes 196612
  16.3 13.1 %copy-start.2 = (s32[512,1]{0,1:T(1,128)S(1)}, s32[512,1]{0,1:T(1,128)}, u32[]{:S(2)}) copy-start(s32[512,1]{0,1:T(1,128)} %param.9) | copy-start | bytes 6148
  21.4 10.9 %collective-permute-start.5 = (bf16[512,512]{1,0:T(8,128)(2,1)S(1)}, bf16[512,512]{1,0:T(8,128)(2,1)S(1)}, u32[]{:S(2)}, u32[]{:S(2)}) collective-permute-start(bf16[512,512]{1,0:T(8,128)(2,1)S(1)} %shard_map.56.refs_1_), channel_id=1, source_target_pairs={{0,2},{1,0},{2,3},{3,1},{4,6},{5,4},{6,7},{7,5},{8,10},{9,8},{10,1... | collective-permute-start | bytes 1572872 | tf_op jit(solution)/shard_map/ppermute | solution.py:243
  22.7 5.1 %collective-permute-start.8 = (bf16[16,4608]{1,0:T(8,128)(2,1)S(1)}, bf16[16,4608]{1,0:T(8,128)(2,1)S(1)}, u32[]{:S(2)}, u32[]{:S(2)}) collective-permute-start(bf16[16,4608]{1,0:T(8,128)(2,1)S(1)} %collective-permute-done.4.refs_5_), channel_id=1, source_target_pairs={{0,16},{16,0},{1,17},{17,1},{2,18},{18,2},{3,19},{19,3},{4,20},{20... | collective-permute-start | bytes 442376 | tf_op jit(solution)/shard_map/ppermute | solution.py:183
  24.2 5.2 %collective-permute-start.9 = (bf16[32,4608]{1,0:T(8,128)(2,1)S(1)}, bf16[32,4608]{1,0:T(8,128)(2,1)S(1)}, u32[]{:S(2)}, u32[]{:S(2)}) collective-permute-start(bf16[32,4608]{1,0:T(8,128)(2,1)S(1)} %shard_map.58), channel_id=1, source_target_pairs={{0,1},{1,0},{2,3},{3,2},{4,5},{5,4},{6,7},{7,6},{8,9},{9,8},{10,11... | collective-permute-start | bytes 884744 | tf_op jit(solution)/shard_map/ppermute | solution.py:183
  24.4 5.1 %collective-permute-start.10 = (bf16[32,4608]{1,0:T(8,128)(2,1)S(1)}, bf16[32,4608]{1,0:T(8,128)(2,1)S(1)}, u32[]{:S(2)}, u32[]{:S(2)}) collective-permute-start(bf16[32,4608]{1,0:T(8,128)(2,1)S(1)} %shard_map.59), channel_id=1, source_target_pairs={{0,1},{1,0},{2,3},{3,2},{4,5},{5,4},{6,7},{7,6},{8,9},{9,8},{10,11... | collective-permute-start | bytes 884744 | tf_op jit(solution)/shard_map/ppermute | solution.py:183
  27.8 1.4 %collective-permute-start.12 = (bf16[16,4608]{1,0:T(8,128)(2,1)S(1)}, bf16[16,4608]{1,0:T(8,128)(2,1)S(1)}, u32[]{:S(2)}, u32[]{:S(2)}) collective-permute-start(bf16[16,4608]{1,0:T(8,128)(2,1)S(1)} %collective-permute-done.8.refs_6_), channel_id=1, source_target_pairs={{0,1},{1,0},{2,3},{3,2},{4,5},{5,4},{6,7},{7,6},{8,9},{9,8},{10,11... | collective-permute-start | bytes 442376 | tf_op jit(solution)/shard_map/ppermute | solution.py:183
  27.8 1.6 %collective-permute-start.11 = (bf16[16,4608]{1,0:T(8,128)(2,1)S(1)}, bf16[16,4608]{1,0:T(8,128)(2,1)S(1)}, u32[]{:S(2)}, u32[]{:S(2)}) collective-permute-start(bf16[16,4608]{1,0:T(8,128)(2,1)S(1)} %collective-permute-done.4.refs_5_), channel_id=1, source_target_pairs={{0,1},{1,0},{2,3},{3,2},{4,5},{5,4},{6,7},{7,6},{8,9},{9,8},{10,11... | collective-permute-start | bytes 442376 | tf_op jit(solution)/shard_map/ppermute | solution.py:183
  31.3 4.4 %collective-permute-start.13 = (bf16[64,512]{1,0:T(8,128)(2,1)S(1)}, bf16[64,512]{1,0:T(8,128)(2,1)S(1)}, u32[]{:S(2)}, u32[]{:S(2)}) collective-permute-start(bf16[64,512]{1,0:T(8,128)(2,1)S(1)} %get-tuple-element.38), channel_id=1, source_target_pairs={{0,2},{2,0},{1,3},{3,1},{4,6},{6,4},{5,7},{7,5},{8,10},{10,8},{9,1... | collective-permute-start | bytes 196616 | tf_op jit(solution)/shard_map/ppermute | solution.py:183

commit v7 on v6

--- a/solution.py
+++ b/solution.py
@@ -248,7 +248,7 @@
         near = [p for p in order if abs(p) == 1]
         for p in near[1:]:
             pieces[p] = shift(mine, "adapter", p)
-        first, xs = base(0, [pieces[n] for n in near])
+        first, xs = base(0, [])
         for p, piece in zip(near, lax.optimization_barrier((*[pieces[p] for p in near], first))):
             pieces[p] = piece
         for p in order[len(near) :]:
@@ -256,36 +256,27 @@
             pieces[p] = shift(pieces[p - sign], "adapter", sign)
         for h in range(1, replicas):
             base(h, [pieces[order[-1]]])
+
         arrays, layout = [down], [[(0, 0, rank)]] + [[] for _ in order]
 
-        def keep(k, array, begin=0):
-            where = [n for n, other in enumerate(arrays) if other is array]
-            if not where:
-                arrays.append(array)
-            layout[k].append((where[0] if where else len(arrays) - 1, begin, share))
-
-        shares = [
-            (1 + n, member)
-            for n, p in enumerate(order)
-            for member in [pieces[p]] + others(pieces[p], "groups")
-        ]
-        for k, member in shares:
-            keep(k, member)
-        if replicas > 1:
-            (last, member), bundles = shares[-1], [shares[n : n + 2] for n in range(0, len(shares) - 1, 2)]
-            bundles[-1] = [s for s in bundles[-1] if s is not shares[-1]]
-            held_back = blocks
-            for bundle in bundles:
-                members = lax.optimization_barrier((*[array for _, array in bundle], *held_back))[: len(bundle)]
-                packed = members[0]
-                if len(bundle) > 1:
-                    shape = (share * len(bundle), wide + cols)
-                    packed = call(pack_kernel, jax.ShapeDtypeStruct(shape, BF16), tuple(members))
-                for other in others(packed, "replica"):
-                    for n, (k, _) in enumerate(bundle):
-                        keep(k, other, n * share)
-            for other in others(member, "replica"):
-                keep(last, other)
+        def keep(array, pair):
+            arrays.append(array)
+            for n, p in enumerate(pair):
+                layout[1 + order.index(p)].append((len(arrays) - 1, n * share, share))
+
+        for n in range(0, len(order), 2):
+            pair = order[n : n + 2]
+            packed = pieces[pair[0]]
+            if len(pair) > 1:
+                packed = call(
+                    pack_kernel,
+                    jax.ShapeDtypeStruct((share * len(pair), wide + cols), BF16),
+                    tuple(pieces[p] for p in pair),
+                )
+            for member in [packed] + others(packed, "groups"):
+                keep(member, pair)
+                for other in others(member, "replica"):
+                    keep(other, pair)
 
         low, sent, every = call(
             functools.partial(down_kernel, layout),

time: 37.5 us -> 38 us (1.013)
  waiting for transfers between devices: 10.5 us -> 13 us
  starting transfers between devices: 13.3 us -> 11.2 us
    ppermute x12 -> x11, waiting for transfers between devices: 10.5 us -> 13 us  [shift(): return lax.ppermute(x, axis, [(i, (i + by) % size) for i in range(size)])]
    ppermute x12 -> x11, starting transfers between devices: 12 us -> 9.48 us  [shift(): return lax.ppermute(x, axis, [(i, (i + by) % size) for i in range(size)])]
    ppermute x2, starting transfers between devices: 1.3 us -> 1.73 us  [base(): recvs.append(lax.ppermute(block, ('tensor', 'replica'), base_pairs(h, by)))]
    pallas_call x7 -> x6, Pallas kernels: 12.5 us -> 12.5 us  [call(): pl.pallas_call(kernel, out_shape=outs, in_specs=specs or [VMEM] * len(arg...]
  transfers between devices with their start and end apart: 14 -> 13, of which waited for: 7 -> 7; matrix products, arithmetic and copies ran while one was open for 3% -> 3% of each run, Pallas kernels for 29% -> 29%
where the time goes in v7:
time: 38 us; the launch traced here: 37.8 us
  waiting for transfers between devices  13 us (34%)
  Pallas kernels  12.5 us (33%)
  starting transfers between devices  11.2 us (29%)
  other arithmetic  0.92 us (2%)
    ppermute x11, waiting for transfers between devices, shift(): return lax.ppermute(x, axis, [(i, (i + by) % size) for i in range(size)])  13 us
    pallas_call x6, Pallas kernels, call(): pl.pallas_call(kernel, out_shape=outs, in_specs=specs or [VMEM] * len(arg...  12.5 us
    ppermute x11, starting transfers between devices, shift(): return lax.ppermute(x, axis, [(i, (i + by) % size) for i in range(size)])  9.48 us
    ppermute x2, starting transfers between devices, base(): recvs.append(lax.ppermute(block, ('tensor', 'replica'), base_pairs(h, by)))  1.73 us
    concatenate x1, other arithmetic, shards(): own = jnp.concatenate([down, u[0]], axis=1)  0.92 us
  transfers between devices with their start and end apart: 13, of which 7 were waited for; matrix products, arithmetic and copies ran while one was open for 3% of the time, Pallas kernels for 29%

profile of v7, /device:TPU:0, one launch (start us, length us, event | category | flops | bytes accessed | tf_op | source)
XLA Modules:
  0.0 37.8 jit_solution(10062272976834485325)
XLA Ops:
  0.0 0.5 %collective-permute-start = (bf16[4096,512]{1,0:T(8,128)(2,1)}, bf16[4096,512]{1,0:T(8,128)(2,1)}, u32[]{:S(2)}, u32[]{:S(2)}) collective-permute-start(bf16[4096,512]{1,0:T(8,128)(2,1)} %v_ref.1), channel_id=1, source_target_pairs={{0,1},{1,0},{2,3},{3,2},{4,5},{5,4},{6,7},{7,6},{8,9},{9,8},{10,11... | collective-permute-start | bytes 12582920 | tf_op jit(solution)/shard_map/ppermute | solution.py:183
  0.5 0.9 %fusion = bf16[16,4608]{1,0:T(8,128)(2,1)S(1)} fusion(s32[]{:T(128)S(6)} %select_n.3, bf16[64,4096]{1,0:T(8,128)(2,1)} %bitcast.11, bf16[64,512]{1,0:T(8,128)(2,1)} %bitcast.13), kind=kLoop, calls=%fused_computation.2 | loop fusion | flops 294912 | bytes 737284 | tf_op jit(solution)/shard_map/concatenate | solution.py:223
  1.4 2.6 %collective-permute-start.2 = (bf16[16,4608]{1,0:T(8,128)(2,1)S(1)}, bf16[16,4608]{1,0:T(8,128)(2,1)S(1)}, u32[]{:S(2)}, u32[]{:S(2)}) collective-permute-start(bf16[16,4608]{1,0:T(8,128)(2,1)S(1)} %fusion), channel_id=1, source_target_pairs={{0,4},{4,8},{8,12},{12,0},{1,5},{5,9},{9,13},{13,1},{2,6},{6,10},{... | collective-permute-start | bytes 442376 | tf_op jit(solution)/shard_map/ppermute | solution.py:183
  4.0 2.1 %collective-permute-start.3 = (bf16[16,4608]{1,0:T(8,128)(2,1)S(1)}, bf16[16,4608]{1,0:T(8,128)(2,1)S(1)}, u32[]{:S(2)}, u32[]{:S(2)}) collective-permute-start(bf16[16,4608]{1,0:T(8,128)(2,1)S(1)} %fusion), channel_id=1, source_target_pairs={{0,12},{4,0},{8,4},{12,8},{1,13},{5,1},{9,5},{13,9},{2,14},{6,2},{... | collective-permute-start | bytes 442376 | tf_op jit(solution)/shard_map/ppermute | solution.py:183
  6.1 0.1 stack.37.info_ref
  6.2 4.2 %shard_map.55 = (bf16[512,512]{1,0:T(8,128)(2,1)S(1)}, bf16[4,512,1024]{2,1,0:T(8,128)(2,1)S(1)}) custom-call(bf16[512,4096]{1,0:T(8,128)(2,1)} %x_ref, bf16[4096,512]{1,0:T(8,128)(2,1)} %v_ref.1), custom_call_target="tpu_custom_call" | custom-call | flops 2147483648 | bytes 8388608 | tf_op jit(solution)/shard_map/pallas_call | solution.py:21
  10.4 0.2 collective-permute-start.1
  10.6 0.1 collective-permute-done.2.refs_0_
  10.8 2.4 %collective-permute-done.3.refs_1_ = bf16[16,4608]{1,0:T(8,128)(2,1)S(1)} collective-permute-done((bf16[16,4608]{1,0:T(8,128)(2,1)S(1)}, bf16[16,4608]{1,0:T(8,128)(2,1)S(1)}, u32[]{:S(2)}, u32[]{:S(2)}) %collective-permute-start.3) | collective-permute-done | bytes 147488 | tf_op jit(solution)/shard_map/ppermute | solution.py:183
  13.2 1.6 %collective-permute-start.7 = (bf16[32,4608]{1,0:T(8,128)(2,1)S(1)}, bf16[32,4608]{1,0:T(8,128)(2,1)S(1)}, u32[]{:S(2)}, u32[]{:S(2)}) collective-permute-start(bf16[32,4608]{1,0:T(8,128)(2,1)S(1)} %shard_map.58.refs_1_), channel_id=1, source_target_pairs={{0,16},{16,0},{1,17},{17,1},{2,18},{18,2},{3,19},{19,3},{4,20},{20... | collective-permute-start | bytes 884744 | tf_op jit(solution)/shard_map/ppermute | solution.py:183
  14.8 1.1 %collective-permute-start.4 = (bf16[16,4608]{1,0:T(8,128)(2,1)S(1)}, bf16[16,4608]{1,0:T(8,128)(2,1)S(1)}, u32[]{:S(2)}, u32[]{:S(2)}) collective-permute-start(bf16[16,4608]{1,0:T(8,128)(2,1)S(1)} %collective-permute-done.2.refs_0_), channel_id=1, source_target_pairs={{0,4},{4,8},{8,12},{12,0},{1,5},{5,9},{9,13},{13,1},{2,6},{6,10},{... | collective-permute-start | bytes 442376 | tf_op jit(solution)/shard_map/ppermute | solution.py:183
  15.9 0.0 collective-permute-done.v_ref
  15.9 0.0 copy-start
  15.9 0.0 copy-start.1
  15.9 0.0 copy-start.2
  15.9 3.8 %shard_map.56.refs_1_ = bf16[512,512]{1,0:T(8,128)(2,1)S(1)} custom-call(bf16[4,512,1024]{2,1,0:T(8,128)(2,1)S(1)} %get-tuple-element.22.x_ref, bf16[4096,512]{1,0:T(8,128)(2,1)} %collective-permute-done.v_ref), custom_call_target="tpu_custom_call" | custom-call | flops 2147483648 | bytes 8388608 | tf_op jit(solution)/shard_map/pallas_call | solution.py:21
  19.7 2.0 %collective-permute-done.4.refs_5_ = bf16[16,4608]{1,0:T(8,128)(2,1)S(1)} collective-permute-done((bf16[16,4608]{1,0:T(8,128)(2,1)S(1)}, bf16[16,4608]{1,0:T(8,128)(2,1)S(1)}, u32[]{:S(2)}, u32[]{:S(2)}) %collective-permute-start.4) | collective-permute-done | bytes 147488 | tf_op jit(solution)/shard_map/ppermute | solution.py:183
  21.7 1.5 %collective-permute-start.5 = (bf16[512,512]{1,0:T(8,128)(2,1)S(1)}, bf16[512,512]{1,0:T(8,128)(2,1)S(1)}, u32[]{:S(2)}, u32[]{:S(2)}) collective-permute-start(bf16[512,512]{1,0:T(8,128)(2,1)S(1)} %shard_map.56.refs_1_), channel_id=1, source_target_pairs={{0,2},{1,0},{2,3},{3,1},{4,6},{5,4},{6,7},{7,5},{8,10},{9,8},{10,1... | collective-permute-start | bytes 1572872 | tf_op jit(solution)/shard_map/ppermute | solution.py:243
  23.2 0.5 %collective-permute-start.10 = (bf16[16,4608]{1,0:T(8,128)(2,1)S(1)}, bf16[16,4608]{1,0:T(8,128)(2,1)S(1)}, u32[]{:S(2)}, u32[]{:S(2)}) collective-permute-start(bf16[16,4608]{1,0:T(8,128)(2,1)S(1)} %collective-permute-done.4.refs_5_), channel_id=1, source_target_pairs={{0,16},{16,0},{1,17},{17,1},{2,18},{18,2},{3,19},{19,3},{4,20},{20... | collective-permute-start | bytes 442376 | tf_op jit(solution)/shard_map/ppermute | solution.py:183
  23.7 0.0 collective-permute-start.6
  23.7 0.0 collective-permute-done.7.refs_3_
  23.7 0.5 %collective-permute-start.8 = (bf16[32,4608]{1,0:T(8,128)(2,1)S(1)}, bf16[32,4608]{1,0:T(8,128)(2,1)S(1)}, u32[]{:S(2)}, u32[]{:S(2)}) collective-permute-start(bf16[32,4608]{1,0:T(8,128)(2,1)S(1)} %collective-permute-done.7.refs_3_), channel_id=1, source_target_pairs={{0,1},{1,0},{2,3},{3,2},{4,5},{5,4},{6,7},{7,6},{8,9},{9,8},{10,11... | collective-permute-start | bytes 884744 | tf_op jit(solution)/shard_map/ppermute | solution.py:183
  24.2 4.1 %collective-permute-done.10.refs_7_ = bf16[16,4608]{1,0:T(8,128)(2,1)S(1)} collective-permute-done((bf16[16,4608]{1,0:T(8,128)(2,1)S(1)}, bf16[16,4608]{1,0:T(8,128)(2,1)S(1)}, u32[]{:S(2)}, u32[]{:S(2)}) %collective-permute-start.10) | collective-permute-done | bytes 147488 | tf_op jit(solution)/shard_map/ppermute | solution.py:183
  28.3 0.0 collective-permute-start.9
  28.3 0.0 collective-permute-done.1.refs_2_
  28.3 0.5 %collective-permute-start.11 = (bf16[16,4608]{1,0:T(8,128)(2,1)S(1)}, bf16[16,4608]{1,0:T(8,128)(2,1)S(1)}, u32[]{:S(2)}, u32[]{:S(2)}) collective-permute-start(bf16[16,4608]{1,0:T(8,128)(2,1)S(1)} %collective-permute-done.10.refs_7_), channel_id=1, source_target_pairs={{0,1},{1,0},{2,3},{3,2},{4,5},{5,4},{6,7},{7,6},{8,9},{9,8},{10,11... | collective-permute-start | bytes 442376 | tf_op jit(solution)/shard_map/ppermute | solution.py:183
  28.8 0.0 collective-permute-done.6.refs_2_
  28.8 0.9 %collective-permute-done.9.refs_6_ = bf16[16,4608]{1,0:T(8,128)(2,1)S(1)} collective-permute-done((bf16[16,4608]{1,0:T(8,128)(2,1)S(1)}, bf16[16,4608]{1,0:T(8,128)(2,1)S(1)}, u32[]{:S(2)}, u32[]{:S(2)}) %collective-permute-start.9) | collective-permute-done | bytes 147488 | tf_op jit(solution)/shard_map/ppermute | solution.py:183
  29.7 0.2 collective-permute-done.11.refs_8_
  29.9 0.0 collective-permute-done.8.refs_4_
  29.9 0.0 copy-done
  29.9 0.0 copy-done.1
  29.9 0.0 copy-done.2
  29.9 1.8 %shard_map.59 = (f32[64,512]{1,0:T(8,128)S(1)}, bf16[64,512]{1,0:T(8,128)(2,1)S(1)}, bf16[256,512]{1,0:T(8,128)(2,1)S(1)}) custom-call(s32[8]{0:T(128)S(1)} %stack.37.info_ref, s32[1,512]{1,0:T(1,128)S(1)} %bitcast.15, bf16[4,512,1024]{2,1,0:T(8,128)(2,1)S(1)} %get-tuple-element.22.x_ref, bf16[64,512]{1,0:T(8,128)(2,1)S(1)} %bitcast.14, ...), custom_call_target="tpu_custom_call" | custom-call | flops 1073741824 | bytes 6555680 | tf_op jit(solution)/shard_map/pallas_call | solution.py:21
  31.8 0.1 collective-permute-start.12
  31.9 0.0 collective-permute-done.5.refs_3_
  31.9 0.9 %shard_map.57.base_ref = f32[512,512]{1,0:T(8,128)S(1)} custom-call(s32[8]{0:T(128)S(1)} %stack.37.info_ref, bf16[512,512]{1,0:T(8,128)(2,1)S(1)} %get-tuple-element.18.refs_0_, bf16[512,512]{1,0:T(8,128)(2,1)S(1)} %shard_map.56.refs_1_, bf16[512,512]{1,0:T(8,128)(2,1)S(1)} %collective-permute-done.1.refs_2_, bf16[512,512]{1,0:T(8,128)(2,1)S(1)} %collective-permute-done.5.refs_3_), custom_call_target="tpu_custom_call" | custom-call | flops 1048576 | bytes 2097184 | tf_op jit(solution)/shard_map/pallas_call | solution.py:21
  32.8 3.4 %collective-permute-done.12.refs_0_ = bf16[64,512]{1,0:T(8,128)(2,1)S(1)} collective-permute-done((bf16[64,512]{1,0:T(8,128)(2,1)S(1)}, bf16[64,512]{1,0:T(8,128)(2,1)S(1)}, u32[]{:S(2)}, u32[]{:S(2)}) %collective-permute-start.12) | collective-permute-done | bytes 65568 | tf_op jit(solution)/shard_map/ppermute | solution.py:183
  36.2 1.7 %shard_map.60 = bf16[512,512]{1,0:T(8,128)(2,1)} custom-call(s32[8]{0:T(128)S(1)} %stack.37.info_ref, s32[1,512]{1,0:T(1,128)S(1)} %bitcast.16, f32[512,512]{1,0:T(8,128)S(1)} %shard_map.57.base_ref, bf16[256,512]{1,0:T(8,128)(2,1)S(1)} %get-tuple-element.24.up_ref, f32[64,512]{1,0:T(8,128)S(1)} %get-tuple-element.25.low_ref, ...), custom_call_target="tpu_custom_call" | custom-call | flops 134217728 | bytes 1509408 | tf_op jit(solution)/shard_map/pallas_call | solution.py:21
  (1 shorter events, 0.0 us)
Async XLA Ops:
  0.0 15.9 %collective-permute-start = (bf16[4096,512]{1,0:T(8,128)(2,1)}, bf16[4096,512]{1,0:T(8,128)(2,1)}, u32[]{:S(2)}, u32[]{:S(2)}) collective-permute-start(bf16[4096,512]{1,0:T(8,128)(2,1)} %v_ref.1), channel_id=1, source_target_pairs={{0,1},{1,0},{2,3},{3,2},{4,5},{5,4},{6,7},{7,6},{8,9},{9,8},{10,11... | collective-permute-start | bytes 12582920 | tf_op jit(solution)/shard_map/ppermute | solution.py:183
  1.4 9.4 %collective-permute-start.2 = (bf16[16,4608]{1,0:T(8,128)(2,1)S(1)}, bf16[16,4608]{1,0:T(8,128)(2,1)S(1)}, u32[]{:S(2)}, u32[]{:S(2)}) collective-permute-start(bf16[16,4608]{1,0:T(8,128)(2,1)S(1)} %fusion), channel_id=1, source_target_pairs={{0,4},{4,8},{8,12},{12,0},{1,5},{5,9},{9,13},{13,1},{2,6},{6,10},{... | collective-permute-start | bytes 442376 | tf_op jit(solution)/shard_map/ppermute | solution.py:183
  4.0 9.1 %collective-permute-start.3 = (bf16[16,4608]{1,0:T(8,128)(2,1)S(1)}, bf16[16,4608]{1,0:T(8,128)(2,1)S(1)}, u32[]{:S(2)}, u32[]{:S(2)}) collective-permute-start(bf16[16,4608]{1,0:T(8,128)(2,1)S(1)} %fusion), channel_id=1, source_target_pairs={{0,12},{4,0},{8,4},{12,8},{1,13},{5,1},{9,5},{13,9},{2,14},{6,2},{... | collective-permute-start | bytes 442376 | tf_op jit(solution)/shard_map/ppermute | solution.py:183
  10.4 17.9 %collective-permute-start.1 = (bf16[512,512]{1,0:T(8,128)(2,1)S(1)}, bf16[512,512]{1,0:T(8,128)(2,1)S(1)}, u32[]{:S(2)}, u32[]{:S(2)}) collective-permute-start(bf16[512,512]{1,0:T(8,128)(2,1)S(1)} %get-tuple-element.18.refs_0_), channel_id=1, source_target_pairs={{0,1},{1,3},{2,0},{3,2},{4,5},{5,7},{6,4},{7,6},{8,9},{9,11},{10,8... | collective-permute-start | bytes 1572872 | tf_op jit(solution)/shard_map/ppermute | solution.py:243
  13.2 10.5 %collective-permute-start.7 = (bf16[32,4608]{1,0:T(8,128)(2,1)S(1)}, bf16[32,4608]{1,0:T(8,128)(2,1)S(1)}, u32[]{:S(2)}, u32[]{:S(2)}) collective-permute-start(bf16[32,4608]{1,0:T(8,128)(2,1)S(1)} %shard_map.58.refs_1_), channel_id=1, source_target_pairs={{0,16},{16,0},{1,17},{17,1},{2,18},{18,2},{3,19},{19,3},{4,20},{20... | collective-permute-start | bytes 884744 | tf_op jit(solution)/shard_map/ppermute | solution.py:183
  14.8 6.9 %collective-permute-start.4 = (bf16[16,4608]{1,0:T(8,128)(2,1)S(1)}, bf16[16,4608]{1,0:T(8,128)(2,1)S(1)}, u32[]{:S(2)}, u32[]{:S(2)}) collective-permute-start(bf16[16,4608]{1,0:T(8,128)(2,1)S(1)} %collective-permute-done.2.refs_0_), channel_id=1, source_target_pairs={{0,4},{4,8},{8,12},{12,0},{1,5},{5,9},{9,13},{13,1},{2,6},{6,10},{... | collective-permute-start | bytes 442376 | tf_op jit(solution)/shard_map/ppermute | solution.py:183
  15.9 14.0 %copy-start = (bf16[1,4096,64]{1,2,0:T(8,128)(2,1)S(1)}, bf16[1,4096,64]{1,2,0:T(8,128)(2,1)}, u32[]{:S(2)}) copy-start(bf16[1,4096,64]{1,2,0:T(8,128)(2,1)} %param.7) | copy-start | bytes 1572868
  15.9 14.0 %copy-start.1 = (bf16[1,64,512]{2,1,0:T(8,128)(2,1)S(1)}, bf16[1,64,512]{2,1,0:T(8,128)(2,1)}, u32[]{:S(2)}) copy-start(bf16[1,64,512]{2,1,0:T(8,128)(2,1)} %param.8) | copy-start | bytes 196612
  15.9 14.0 %copy-start.2 = (s32[512,1]{0,1:T(1,128)S(1)}, s32[512,1]{0,1:T(1,128)}, u32[]{:S(2)}) copy-start(s32[512,1]{0,1:T(1,128)} %param.9) | copy-start | bytes 6148
  21.7 10.2 %collective-permute-start.5 = (bf16[512,512]{1,0:T(8,128)(2,1)S(1)}, bf16[512,512]{1,0:T(8,128)(2,1)S(1)}, u32[]{:S(2)}, u32[]{:S(2)}) collective-permute-start(bf16[512,512]{1,0:T(8,128)(2,1)S(1)} %shard_map.56.refs_1_), channel_id=1, source_target_pairs={{0,2},{1,0},{2,3},{3,1},{4,6},{5,4},{6,7},{7,5},{8,10},{9,8},{10,1... | collective-permute-start | bytes 1572872 | tf_op jit(solution)/shard_map/ppermute | solution.py:243
  23.2 5.1 %collective-permute-start.10 = (bf16[16,4608]{1,0:T(8,128)(2,1)S(1)}, bf16[16,4608]{1,0:T(8,128)(2,1)S(1)}, u32[]{:S(2)}, u32[]{:S(2)}) collective-permute-start(bf16[16,4608]{1,0:T(8,128)(2,1)S(1)} %collective-permute-done.4.refs_5_), channel_id=1, source_target_pairs={{0,16},{16,0},{1,17},{17,1},{2,18},{18,2},{3,19},{19,3},{4,20},{20... | collective-permute-start | bytes 442376 | tf_op jit(solution)/shard_map/ppermute | solution.py:183
  23.7 5.2 %collective-permute-start.6 = (bf16[32,4608]{1,0:T(8,128)(2,1)S(1)}, bf16[32,4608]{1,0:T(8,128)(2,1)S(1)}, u32[]{:S(2)}, u32[]{:S(2)}) collective-permute-start(bf16[32,4608]{1,0:T(8,128)(2,1)S(1)} %shard_map.58.refs_1_), channel_id=1, source_target_pairs={{0,1},{1,0},{2,3},{3,2},{4,5},{5,4},{6,7},{7,6},{8,9},{9,8},{10,11... | collective-permute-start | bytes 884744 | tf_op jit(solution)/shard_map/ppermute | solution.py:183
  23.7 6.2 %collective-permute-start.8 = (bf16[32,4608]{1,0:T(8,128)(2,1)S(1)}, bf16[32,4608]{1,0:T(8,128)(2,1)S(1)}, u32[]{:S(2)}, u32[]{:S(2)}) collective-permute-start(bf16[32,4608]{1,0:T(8,128)(2,1)S(1)} %collective-permute-done.7.refs_3_), channel_id=1, source_target_pairs={{0,1},{1,0},{2,3},{3,2},{4,5},{5,4},{6,7},{7,6},{8,9},{9,8},{10,11... | collective-permute-start | bytes 884744 | tf_op jit(solution)/shard_map/ppermute | solution.py:183
  28.3 1.4 %collective-permute-start.9 = (bf16[16,4608]{1,0:T(8,128)(2,1)S(1)}, bf16[16,4608]{1,0:T(8,128)(2,1)S(1)}, u32[]{:S(2)}, u32[]{:S(2)}) collective-permute-start(bf16[16,4608]{1,0:T(8,128)(2,1)S(1)} %collective-permute-done.4.refs_5_), channel_id=1, source_target_pairs={{0,1},{1,0},{2,3},{3,2},{4,5},{5,4},{6,7},{7,6},{8,9},{9,8},{10,11... | collective-permute-start | bytes 442376 | tf_op jit(solution)/shard_map/ppermute | solution.py:183
  28.3 1.6 %collective-permute-start.11 = (bf16[16,4608]{1,0:T(8,128)(2,1)S(1)}, bf16[16,4608]{1,0:T(8,128)(2,1)S(1)}, u32[]{:S(2)}, u32[]{:S(2)}) collective-permute-start(bf16[16,4608]{1,0:T(8,128)(2,1)S(1)} %collective-permute-done.10.refs_7_), channel_id=1, source_target_pairs={{0,1},{1,0},{2,3},{3,2},{4,5},{5,4},{6,7},{7,6},{8,9},{9,8},{10,11... | collective-permute-start | bytes 442376 | tf_op jit(solution)/shard_map/ppermute | solution.py:183
  31.8 4.4 %collective-permute-start.12 = (bf16[64,512]{1,0:T(8,128)(2,1)S(1)}, bf16[64,512]{1,0:T(8,128)(2,1)S(1)}, u32[]{:S(2)}, u32[]{:S(2)}) collective-permute-start(bf16[64,512]{1,0:T(8,128)(2,1)S(1)} %get-tuple-element.26), channel_id=1, source_target_pairs={{0,2},{2,0},{1,3},{3,1},{4,6},{6,4},{5,7},{7,5},{8,10},{10,8},{9,1... | collective-permute-start | bytes 196616 | tf_op jit(solution)/shard_map/ppermute | solution.py:183

commit v8 on v7

--- a/solution.py
+++ b/solution.py
@@ -185,6 +185,9 @@
     def others(x, axis):
         return [shift(x, axis, by) for by in range(1, mesh.shape[axis])]
 
+    def flip(x, bits):
+        return lax.ppermute(x, "adapter", [(i, i ^ bits) for i in range(adapters)])
+
     def base_pairs(h, by):
         pairs = {}
         for ti in range(tensors):
@@ -210,10 +213,10 @@
         cols = u.shape[2]
         row = idx.reshape(1, tokens)
 
-        order = [n * sign for n in range(1, adapters // 2 + 1) for sign in (1, -1)][: adapters - 1]
+        order = [*range(1, adapters, 2), *range(2, adapters, 2)]
         halves = [lax.rem(r - h + replicas, replicas) * per_half for h in range(replicas)]
         here = [((t >= n) & (t < n + per_half)).astype(jnp.int32) for n in halves]
-        info = [a] + [lax.rem(a - p + adapters, adapters) for p in order]
+        info = [a] + [lax.bitwise_xor(a, jnp.int32(p)) for p in order]
         info = jnp.stack(info + here + [f for f in here for _ in range(1, tensors)])
 
         held = [v] + others(v, "replica")
@@ -222,7 +225,8 @@
         share = rank // (groups * replicas)
         own = jnp.concatenate([down, u[0]], axis=1)
         mine = lax.dynamic_slice_in_dim(own, (g * replicas + r) * share, share, 0)
-        pieces = {1: shift(mine, "adapter", 1)} if adapters > 1 else {}
+        near = [p for p in order if p % 2]
+        pieces = {p: flip(mine, p) for p in near}
 
         blocks, recvs = [], []
 
@@ -245,17 +249,13 @@
 
         xs = None
         x, info = lax.optimization_barrier((x, info, mine))[:2]
-        near = [p for p in order if abs(p) == 1]
-        for p in near[1:]:
-            pieces[p] = shift(mine, "adapter", p)
         first, xs = base(0, [])
         for p, piece in zip(near, lax.optimization_barrier((*[pieces[p] for p in near], first))):
             pieces[p] = piece
         for p in order[len(near) :]:
-            sign = 1 if p > 0 else -1
-            pieces[p] = shift(pieces[p - sign], "adapter", sign)
+            pieces[p] = flip(pieces[p + 1], 1)
         for h in range(1, replicas):
-            base(h, [pieces[order[-1]]])
+            base(h, [])
 
         arrays, layout = [down], [[(0, 0, rank)]] + [[] for _ in order]
 

time: 38 us -> 36.3 us (0.955)
  waiting for transfers between devices: 13 us -> 11.5 us
    ppermute x0 -> x3, starting transfers between devices: none -> 5.69 us  [flip(): return lax.ppermute(x, 'adapter', [(i, i ^ bits) for i in range(adapters)])]
    ppermute x11 -> x8, starting transfers between devices: 9.48 us -> 3.85 us  [shift(): return lax.ppermute(x, axis, [(i, (i + by) % size) for i in range(size)])]
    ppermute x11 -> x8, waiting for transfers between devices: 13 us -> 8.36 us  [shift(): return lax.ppermute(x, axis, [(i, (i + by) % size) for i in range(size)])]
    ppermute x0 -> x3, waiting for transfers between devices: none -> 3.17 us  [flip(): return lax.ppermute(x, 'adapter', [(i, i ^ bits) for i in range(adapters)])]
  transfers between devices with their start and end apart: 13 -> 13, of which waited for: 7 -> 6; matrix products, arithmetic and copies ran while one was open for 3% -> 3% of each run, Pallas kernels for 29% -> 30%
where the time goes in v8:
time: 36.3 us; the launch traced here: 36.2 us
  Pallas kernels  12.5 us (34%)
  waiting for transfers between devices  11.5 us (32%)
  starting transfers between devices  11.1 us (31%)
  other arithmetic  0.92 us (3%)
    pallas_call x6, Pallas kernels, call(): pl.pallas_call(kernel, out_shape=outs, in_specs=specs or [VMEM] * len(arg...  12.5 us
    ppermute x8, waiting for transfers between devices, shift(): return lax.ppermute(x, axis, [(i, (i + by) % size) for i in range(size)])  8.36 us
    ppermute x3, starting transfers between devices, flip(): return lax.ppermute(x, 'adapter', [(i, i ^ bits) for i in range(adapters)])  5.69 us
    ppermute x8, starting transfers between devices, shift(): return lax.ppermute(x, axis, [(i, (i + by) % size) for i in range(size)])  3.85 us
    ppermute x3, waiting for transfers between devices, flip(): return lax.ppermute(x, 'adapter', [(i, i ^ bits) for i in range(adapters)])  3.17 us
    ppermute x2, starting transfers between devices, base(): recvs.append(lax.ppermute(block, ('tensor', 'replica'), base_pairs(h, by)))  1.53 us
    concatenate x1, other arithmetic, shards(): own = jnp.concatenate([down, u[0]], axis=1)  0.92 us
  transfers between devices with their start and end apart: 13, of which 6 were waited for; matrix products, arithmetic and copies ran while one was open for 3% of the time, Pallas kernels for 30%

profile of v8, /device:TPU:0, one launch (start us, length us, event | category | flops | bytes accessed | tf_op | source)
XLA Modules:
  0.0 36.2 jit_solution(16089224202781534262)
XLA Ops:
  0.0 0.5 %collective-permute-start = (bf16[4096,512]{1,0:T(8,128)(2,1)}, bf16[4096,512]{1,0:T(8,128)(2,1)}, u32[]{:S(2)}, u32[]{:S(2)}) collective-permute-start(bf16[4096,512]{1,0:T(8,128)(2,1)} %v_ref.1), channel_id=1, source_target_pairs={{0,1},{1,0},{2,3},{3,2},{4,5},{5,4},{6,7},{7,6},{8,9},{9,8},{10,11... | collective-permute-start | bytes 12582920 | tf_op jit(solution)/shard_map/ppermute | solution.py:183
  0.5 0.9 %fusion = bf16[16,4608]{1,0:T(8,128)(2,1)S(1)} fusion(s32[]{:T(128)S(6)} %select_n.3, bf16[64,4096]{1,0:T(8,128)(2,1)} %bitcast.11, bf16[64,512]{1,0:T(8,128)(2,1)} %bitcast.13), kind=kLoop, calls=%fused_computation.2 | loop fusion | flops 294912 | bytes 737284 | tf_op jit(solution)/shard_map/concatenate | solution.py:226
  1.4 2.6 %collective-permute-start.3 = (bf16[16,4608]{1,0:T(8,128)(2,1)S(1)}, bf16[16,4608]{1,0:T(8,128)(2,1)S(1)}, u32[]{:S(2)}, u32[]{:S(2)}) collective-permute-start(bf16[16,4608]{1,0:T(8,128)(2,1)S(1)} %fusion), channel_id=1, source_target_pairs={{0,4},{4,0},{8,12},{12,8},{1,5},{5,1},{9,13},{13,9},{2,6},{6,2},{1... | collective-permute-start | bytes 442376 | tf_op jit(solution)/shard_map/ppermute | solution.py:189
  4.0 2.5 %collective-permute-start.4 = (bf16[16,4608]{1,0:T(8,128)(2,1)S(1)}, bf16[16,4608]{1,0:T(8,128)(2,1)S(1)}, u32[]{:S(2)}, u32[]{:S(2)}) collective-permute-start(bf16[16,4608]{1,0:T(8,128)(2,1)S(1)} %fusion), channel_id=1, source_target_pairs={{0,12},{4,8},{8,4},{12,0},{1,13},{5,9},{9,5},{13,1},{2,14},{6,10},... | collective-permute-start | bytes 442376 | tf_op jit(solution)/shard_map/ppermute | solution.py:189
  6.5 0.1 stack.37.info_ref
  6.6 4.2 %shard_map.55 = (bf16[512,512]{1,0:T(8,128)(2,1)S(1)}, bf16[4,512,1024]{2,1,0:T(8,128)(2,1)S(1)}) custom-call(bf16[512,4096]{1,0:T(8,128)(2,1)} %x_ref, bf16[4096,512]{1,0:T(8,128)(2,1)} %v_ref.1), custom_call_target="tpu_custom_call" | custom-call | flops 2147483648 | bytes 8388608 | tf_op jit(solution)/shard_map/pallas_call | solution.py:21
  10.8 0.0 collective-permute-start.1
  10.8 0.0 collective-permute-done.3.refs_0_
  10.8 3.2 %collective-permute-done.4.refs_1_ = bf16[16,4608]{1,0:T(8,128)(2,1)S(1)} collective-permute-done((bf16[16,4608]{1,0:T(8,128)(2,1)S(1)}, bf16[16,4608]{1,0:T(8,128)(2,1)S(1)}, u32[]{:S(2)}, u32[]{:S(2)}) %collective-permute-start.4) | collective-permute-done | bytes 147488 | tf_op jit(solution)/shard_map/ppermute | solution.py:189
  14.0 1.6 %collective-permute-start.6 = (bf16[32,4608]{1,0:T(8,128)(2,1)S(1)}, bf16[32,4608]{1,0:T(8,128)(2,1)S(1)}, u32[]{:S(2)}, u32[]{:S(2)}) collective-permute-start(bf16[32,4608]{1,0:T(8,128)(2,1)S(1)} %shard_map.58.refs_1_), channel_id=1, source_target_pairs={{0,16},{16,0},{1,17},{17,1},{2,18},{18,2},{3,19},{19,3},{4,20},{20... | collective-permute-start | bytes 884744 | tf_op jit(solution)/shard_map/ppermute | solution.py:183
  15.6 0.6 %collective-permute-start.8 = (bf16[16,4608]{1,0:T(8,128)(2,1)S(1)}, bf16[16,4608]{1,0:T(8,128)(2,1)S(1)}, u32[]{:S(2)}, u32[]{:S(2)}) collective-permute-start(bf16[16,4608]{1,0:T(8,128)(2,1)S(1)} %collective-permute-done.4.refs_1_), channel_id=1, source_target_pairs={{0,4},{4,0},{8,12},{12,8},{1,5},{5,1},{9,13},{13,9},{2,6},{6,2},{1... | collective-permute-start | bytes 442376 | tf_op jit(solution)/shard_map/ppermute | solution.py:189
  16.2 0.0 collective-permute-done.v_ref
  16.2 0.0 copy-start
  16.2 0.0 copy-start.1
  16.2 0.0 copy-start.2
  16.2 3.8 %shard_map.56.refs_1_ = bf16[512,512]{1,0:T(8,128)(2,1)S(1)} custom-call(bf16[4,512,1024]{2,1,0:T(8,128)(2,1)S(1)} %get-tuple-element.19.x_ref, bf16[4096,512]{1,0:T(8,128)(2,1)} %collective-permute-done.v_ref), custom_call_target="tpu_custom_call" | custom-call | flops 2147483648 | bytes 8388608 | tf_op jit(solution)/shard_map/pallas_call | solution.py:21
  20.0 1.5 %collective-permute-start.2 = (bf16[512,512]{1,0:T(8,128)(2,1)S(1)}, bf16[512,512]{1,0:T(8,128)(2,1)S(1)}, u32[]{:S(2)}, u32[]{:S(2)}) collective-permute-start(bf16[512,512]{1,0:T(8,128)(2,1)S(1)} %shard_map.56.refs_1_), channel_id=1, source_target_pairs={{0,2},{1,0},{2,3},{3,1},{4,6},{5,4},{6,7},{7,5},{8,10},{9,8},{10,1... | collective-permute-start | bytes 1572872 | tf_op jit(solution)/shard_map/ppermute | solution.py:247
  21.5 0.0 collective-permute-done.8.refs_5_
  21.5 0.5 %collective-permute-start.10 = (bf16[16,4608]{1,0:T(8,128)(2,1)S(1)}, bf16[16,4608]{1,0:T(8,128)(2,1)S(1)}, u32[]{:S(2)}, u32[]{:S(2)}) collective-permute-start(bf16[16,4608]{1,0:T(8,128)(2,1)S(1)} %collective-permute-done.8.refs_5_), channel_id=1, source_target_pairs={{0,16},{16,0},{1,17},{17,1},{2,18},{18,2},{3,19},{19,3},{4,20},{20... | collective-permute-start | bytes 442376 | tf_op jit(solution)/shard_map/ppermute | solution.py:183
  22.0 0.0 collective-permute-start.5
  22.0 0.6 %collective-permute-done.6.refs_3_ = bf16[32,4608]{1,0:T(8,128)(2,1)S(1)} collective-permute-done((bf16[32,4608]{1,0:T(8,128)(2,1)S(1)}, bf16[32,4608]{1,0:T(8,128)(2,1)S(1)}, u32[]{:S(2)}, u32[]{:S(2)}) %collective-permute-start.6) | collective-permute-done | bytes 294944 | tf_op jit(solution)/shard_map/ppermute | solution.py:183
  22.7 0.0 collective-permute-start.7
  22.7 4.0 %collective-permute-done.10.refs_7_ = bf16[16,4608]{1,0:T(8,128)(2,1)S(1)} collective-permute-done((bf16[16,4608]{1,0:T(8,128)(2,1)S(1)}, bf16[16,4608]{1,0:T(8,128)(2,1)S(1)}, u32[]{:S(2)}, u32[]{:S(2)}) %collective-permute-start.10) | collective-permute-done | bytes 147488 | tf_op jit(solution)/shard_map/ppermute | solution.py:183
  26.7 0.0 collective-permute-start.9
  26.7 0.0 collective-permute-done.1.refs_2_
  26.7 0.5 %collective-permute-start.11 = (bf16[16,4608]{1,0:T(8,128)(2,1)S(1)}, bf16[16,4608]{1,0:T(8,128)(2,1)S(1)}, u32[]{:S(2)}, u32[]{:S(2)}) collective-permute-start(bf16[16,4608]{1,0:T(8,128)(2,1)S(1)} %collective-permute-done.10.refs_7_), channel_id=1, source_target_pairs={{0,1},{1,0},{2,3},{3,2},{4,5},{5,4},{6,7},{7,6},{8,9},{9,8},{10,11... | collective-permute-start | bytes 442376 | tf_op jit(solution)/shard_map/ppermute | solution.py:183
  27.2 0.0 collective-permute-done.5.refs_2_
  27.2 0.9 %collective-permute-done.9.refs_6_ = bf16[16,4608]{1,0:T(8,128)(2,1)S(1)} collective-permute-done((bf16[16,4608]{1,0:T(8,128)(2,1)S(1)}, bf16[16,4608]{1,0:T(8,128)(2,1)S(1)}, u32[]{:S(2)}, u32[]{:S(2)}) %collective-permute-start.9) | collective-permute-done | bytes 147488 | tf_op jit(solution)/shard_map/ppermute | solution.py:183
  28.0 0.2 collective-permute-done.11.refs_8_
  28.2 0.0 collective-permute-done.7.refs_4_
  28.2 0.0 copy-done
  28.2 0.0 copy-done.1
  28.2 0.0 copy-done.2
  28.3 1.8 %shard_map.59 = (f32[64,512]{1,0:T(8,128)S(1)}, bf16[64,512]{1,0:T(8,128)(2,1)S(1)}, bf16[256,512]{1,0:T(8,128)(2,1)S(1)}) custom-call(s32[8]{0:T(128)S(1)} %stack.37.info_ref, s32[1,512]{1,0:T(1,128)S(1)} %bitcast.15, bf16[4,512,1024]{2,1,0:T(8,128)(2,1)S(1)} %get-tuple-element.19.x_ref, bf16[64,512]{1,0:T(8,128)(2,1)S(1)} %bitcast.14, ...), custom_call_target="tpu_custom_call" | custom-call | flops 1073741824 | bytes 6555680 | tf_op jit(solution)/shard_map/pallas_call | solution.py:21
  30.1 0.8 %collective-permute-start.12 = (bf16[64,512]{1,0:T(8,128)(2,1)S(1)}, bf16[64,512]{1,0:T(8,128)(2,1)S(1)}, u32[]{:S(2)}, u32[]{:S(2)}) collective-permute-start(bf16[64,512]{1,0:T(8,128)(2,1)S(1)} %get-tuple-element.24), channel_id=1, source_target_pairs={{0,2},{2,0},{1,3},{3,1},{4,6},{6,4},{5,7},{7,5},{8,10},{10,8},{9,1... | collective-permute-start | bytes 196616 | tf_op jit(solution)/shard_map/ppermute | solution.py:183
  30.9 0.0 collective-permute-done.2.refs_3_
  30.9 0.9 %shard_map.57.base_ref = f32[512,512]{1,0:T(8,128)S(1)} custom-call(s32[8]{0:T(128)S(1)} %stack.37.info_ref, bf16[512,512]{1,0:T(8,128)(2,1)S(1)} %get-tuple-element.17.refs_0_, bf16[512,512]{1,0:T(8,128)(2,1)S(1)} %shard_map.56.refs_1_, bf16[512,512]{1,0:T(8,128)(2,1)S(1)} %collective-permute-done.1.refs_2_, bf16[512,512]{1,0:T(8,128)(2,1)S(1)} %collective-permute-done.2.refs_3_), custom_call_target="tpu_custom_call" | custom-call | flops 1048576 | bytes 2097184 | tf_op jit(solution)/shard_map/pallas_call | solution.py:21
  31.8 2.7 %collective-permute-done.12.refs_0_ = bf16[64,512]{1,0:T(8,128)(2,1)S(1)} collective-permute-done((bf16[64,512]{1,0:T(8,128)(2,1)S(1)}, bf16[64,512]{1,0:T(8,128)(2,1)S(1)}, u32[]{:S(2)}, u32[]{:S(2)}) %collective-permute-start.12) | collective-permute-done | bytes 65568 | tf_op jit(solution)/shard_map/ppermute | solution.py:183
  34.5 1.7 %shard_map.60 = bf16[512,512]{1,0:T(8,128)(2,1)} custom-call(s32[8]{0:T(128)S(1)} %stack.37.info_ref, s32[1,512]{1,0:T(1,128)S(1)} %bitcast.16, f32[512,512]{1,0:T(8,128)S(1)} %shard_map.57.base_ref, bf16[256,512]{1,0:T(8,128)(2,1)S(1)} %get-tuple-element.22.up_ref, f32[64,512]{1,0:T(8,128)S(1)} %get-tuple-element.23.low_ref, ...), custom_call_target="tpu_custom_call" | custom-call | flops 134217728 | bytes 1509408 | tf_op jit(solution)/shard_map/pallas_call | solution.py:21
  (1 shorter events, 0.0 us)
Async XLA Ops:
  0.0 16.2 %collective-permute-start = (bf16[4096,512]{1,0:T(8,128)(2,1)}, bf16[4096,512]{1,0:T(8,128)(2,1)}, u32[]{:S(2)}, u32[]{:S(2)}) collective-permute-start(bf16[4096,512]{1,0:T(8,128)(2,1)} %v_ref.1), channel_id=1, source_target_pairs={{0,1},{1,0},{2,3},{3,2},{4,5},{5,4},{6,7},{7,6},{8,9},{9,8},{10,11... | collective-permute-start | bytes 12582920 | tf_op jit(solution)/shard_map/ppermute | solution.py:183
  1.4 9.4 %collective-permute-start.3 = (bf16[16,4608]{1,0:T(8,128)(2,1)S(1)}, bf16[16,4608]{1,0:T(8,128)(2,1)S(1)}, u32[]{:S(2)}, u32[]{:S(2)}) collective-permute-start(bf16[16,4608]{1,0:T(8,128)(2,1)S(1)} %fusion), channel_id=1, source_target_pairs={{0,4},{4,0},{8,12},{12,8},{1,5},{5,1},{9,13},{13,9},{2,6},{6,2},{1... | collective-permute-start | bytes 442376 | tf_op jit(solution)/shard_map/ppermute | solution.py:189
  4.0 10.0 %collective-permute-start.4 = (bf16[16,4608]{1,0:T(8,128)(2,1)S(1)}, bf16[16,4608]{1,0:T(8,128)(2,1)S(1)}, u32[]{:S(2)}, u32[]{:S(2)}) collective-permute-start(bf16[16,4608]{1,0:T(8,128)(2,1)S(1)} %fusion), channel_id=1, source_target_pairs={{0,12},{4,8},{8,4},{12,0},{1,13},{5,9},{9,5},{13,1},{2,14},{6,10},... | collective-permute-start | bytes 442376 | tf_op jit(solution)/shard_map/ppermute | solution.py:189
  10.8 15.9 %collective-permute-start.1 = (bf16[512,512]{1,0:T(8,128)(2,1)S(1)}, bf16[512,512]{1,0:T(8,128)(2,1)S(1)}, u32[]{:S(2)}, u32[]{:S(2)}) collective-permute-start(bf16[512,512]{1,0:T(8,128)(2,1)S(1)} %get-tuple-element.17.refs_0_), channel_id=1, source_target_pairs={{0,1},{1,3},{2,0},{3,2},{4,5},{5,7},{6,4},{7,6},{8,9},{9,11},{10,8... | collective-permute-start | bytes 1572872 | tf_op jit(solution)/shard_map/ppermute | solution.py:247
  14.0 8.6 %collective-permute-start.6 = (bf16[32,4608]{1,0:T(8,128)(2,1)S(1)}, bf16[32,4608]{1,0:T(8,128)(2,1)S(1)}, u32[]{:S(2)}, u32[]{:S(2)}) collective-permute-start(bf16[32,4608]{1,0:T(8,128)(2,1)S(1)} %shard_map.58.refs_1_), channel_id=1, source_target_pairs={{0,16},{16,0},{1,17},{17,1},{2,18},{18,2},{3,19},{19,3},{4,20},{20... | collective-permute-start | bytes 884744 | tf_op jit(solution)/shard_map/ppermute | solution.py:183
  15.6 5.9 %collective-permute-start.8 = (bf16[16,4608]{1,0:T(8,128)(2,1)S(1)}, bf16[16,4608]{1,0:T(8,128)(2,1)S(1)}, u32[]{:S(2)}, u32[]{:S(2)}) collective-permute-start(bf16[16,4608]{1,0:T(8,128)(2,1)S(1)} %collective-permute-done.4.refs_1_), channel_id=1, source_target_pairs={{0,4},{4,0},{8,12},{12,8},{1,5},{5,1},{9,13},{13,9},{2,6},{6,2},{1... | collective-permute-start | bytes 442376 | tf_op jit(solution)/shard_map/ppermute | solution.py:189
  16.2 12.1 %copy-start = (bf16[1,4096,64]{1,2,0:T(8,128)(2,1)S(1)}, bf16[1,4096,64]{1,2,0:T(8,128)(2,1)}, u32[]{:S(2)}) copy-start(bf16[1,4096,64]{1,2,0:T(8,128)(2,1)} %param.7) | copy-start | bytes 1572868
  16.2 12.1 %copy-start.1 = (bf16[1,64,512]{2,1,0:T(8,128)(2,1)S(1)}, bf16[1,64,512]{2,1,0:T(8,128)(2,1)}, u32[]{:S(2)}) copy-start(bf16[1,64,512]{2,1,0:T(8,128)(2,1)} %param.8) | copy-start | bytes 196612
  16.2 12.1 %copy-start.2 = (s32[512,1]{0,1:T(1,128)S(1)}, s32[512,1]{0,1:T(1,128)}, u32[]{:S(2)}) copy-start(s32[512,1]{0,1:T(1,128)} %param.9) | copy-start | bytes 6148
  20.0 10.9 %collective-permute-start.2 = (bf16[512,512]{1,0:T(8,128)(2,1)S(1)}, bf16[512,512]{1,0:T(8,128)(2,1)S(1)}, u32[]{:S(2)}, u32[]{:S(2)}) collective-permute-start(bf16[512,512]{1,0:T(8,128)(2,1)S(1)} %shard_map.56.refs_1_), channel_id=1, source_target_pairs={{0,2},{1,0},{2,3},{3,1},{4,6},{5,4},{6,7},{7,5},{8,10},{9,8},{10,1... | collective-permute-start | bytes 1572872 | tf_op jit(solution)/shard_map/ppermute | solution.py:247
  21.5 5.1 %collective-permute-start.10 = (bf16[16,4608]{1,0:T(8,128)(2,1)S(1)}, bf16[16,4608]{1,0:T(8,128)(2,1)S(1)}, u32[]{:S(2)}, u32[]{:S(2)}) collective-permute-start(bf16[16,4608]{1,0:T(8,128)(2,1)S(1)} %collective-permute-done.8.refs_5_), channel_id=1, source_target_pairs={{0,16},{16,0},{1,17},{17,1},{2,18},{18,2},{3,19},{19,3},{4,20},{20... | collective-permute-start | bytes 442376 | tf_op jit(solution)/shard_map/ppermute | solution.py:183
  22.0 5.2 %collective-permute-start.5 = (bf16[32,4608]{1,0:T(8,128)(2,1)S(1)}, bf16[32,4608]{1,0:T(8,128)(2,1)S(1)}, u32[]{:S(2)}, u32[]{:S(2)}) collective-permute-start(bf16[32,4608]{1,0:T(8,128)(2,1)S(1)} %shard_map.58.refs_1_), channel_id=1, source_target_pairs={{0,1},{1,0},{2,3},{3,2},{4,5},{5,4},{6,7},{7,6},{8,9},{9,8},{10,11... | collective-permute-start | bytes 884744 | tf_op jit(solution)/shard_map/ppermute | solution.py:183
  22.7 5.6 %collective-permute-start.7 = (bf16[32,4608]{1,0:T(8,128)(2,1)S(1)}, bf16[32,4608]{1,0:T(8,128)(2,1)S(1)}, u32[]{:S(2)}, u32[]{:S(2)}) collective-permute-start(bf16[32,4608]{1,0:T(8,128)(2,1)S(1)} %collective-permute-done.6.refs_3_), channel_id=1, source_target_pairs={{0,1},{1,0},{2,3},{3,2},{4,5},{5,4},{6,7},{7,6},{8,9},{9,8},{10,11... | collective-permute-start | bytes 884744 | tf_op jit(solution)/shard_map/ppermute | solution.py:183
  26.7 1.4 %collective-permute-start.9 = (bf16[16,4608]{1,0:T(8,128)(2,1)S(1)}, bf16[16,4608]{1,0:T(8,128)(2,1)S(1)}, u32[]{:S(2)}, u32[]{:S(2)}) collective-permute-start(bf16[16,4608]{1,0:T(8,128)(2,1)S(1)} %collective-permute-done.8.refs_5_), channel_id=1, source_target_pairs={{0,1},{1,0},{2,3},{3,2},{4,5},{5,4},{6,7},{7,6},{8,9},{9,8},{10,11... | collective-permute-start | bytes 442376 | tf_op jit(solution)/shard_map/ppermute | solution.py:183
  26.7 1.6 %collective-permute-start.11 = (bf16[16,4608]{1,0:T(8,128)(2,1)S(1)}, bf16[16,4608]{1,0:T(8,128)(2,1)S(1)}, u32[]{:S(2)}, u32[]{:S(2)}) collective-permute-start(bf16[16,4608]{1,0:T(8,128)(2,1)S(1)} %collective-permute-done.10.refs_7_), channel_id=1, source_target_pairs={{0,1},{1,0},{2,3},{3,2},{4,5},{5,4},{6,7},{7,6},{8,9},{9,8},{10,11... | collective-permute-start | bytes 442376 | tf_op jit(solution)/shard_map/ppermute | solution.py:183
  30.1 4.4 %collective-permute-start.12 = (bf16[64,512]{1,0:T(8,128)(2,1)S(1)}, bf16[64,512]{1,0:T(8,128)(2,1)S(1)}, u32[]{:S(2)}, u32[]{:S(2)}) collective-permute-start(bf16[64,512]{1,0:T(8,128)(2,1)S(1)} %get-tuple-element.24), channel_id=1, source_target_pairs={{0,2},{2,0},{1,3},{3,1},{4,6},{6,4},{5,7},{7,5},{8,10},{10,8},{9,1... | collective-permute-start | bytes 196616 | tf_op jit(solution)/shard_map/ppermute | solution.py:183

commit v9 on v8

--- a/solution.py
+++ b/solution.py
@@ -213,7 +213,7 @@
         cols = u.shape[2]
         row = idx.reshape(1, tokens)
 
-        order = [*range(1, adapters, 2), *range(2, adapters, 2)]
+        order = [*range(3, adapters, 2), *range(2, adapters, 2), 1][: adapters - 1]
         halves = [lax.rem(r - h + replicas, replicas) * per_half for h in range(replicas)]
         here = [((t >= n) & (t < n + per_half)).astype(jnp.int32) for n in halves]
         info = [a] + [lax.bitwise_xor(a, jnp.int32(p)) for p in order]
@@ -224,8 +224,13 @@
         down = d[0].T
         share = rank // (groups * replicas)
         own = jnp.concatenate([down, u[0]], axis=1)
-        mine = lax.dynamic_slice_in_dim(own, (g * replicas + r) * share, share, 0)
-        near = [p for p in order if p % 2]
+        mine, *rest = [
+            lax.dynamic_slice_in_dim(
+                own, (r * groups + lax.rem(g + n, groups)) * share, share, 0
+            )
+            for n in range(groups)
+        ]
+        near = [p for p in order if p % 2 and p > 1]
         pieces = {p: flip(mine, p) for p in near}
 
         blocks, recvs = [], []
@@ -248,35 +253,34 @@
             return terms, cuts
 
         xs = None
-        x, info = lax.optimization_barrier((x, info, mine))[:2]
+        x, info = lax.optimization_barrier((x, info, mine, *rest))[:2]
         first, xs = base(0, [])
         for p, piece in zip(near, lax.optimization_barrier((*[pieces[p] for p in near], first))):
             pieces[p] = piece
-        for p in order[len(near) :]:
-            pieces[p] = flip(pieces[p + 1], 1)
+        for p in order:
+            if p % 2 == 0:
+                pieces[p] = flip(pieces[p + 1], 1)
+        beside = [flip(after(mine, first), 1)]
+        second = first
         for h in range(1, replicas):
-            base(h, [])
+            second, _ = base(h, [])
+        beside += [flip(after(piece, second), 1) for piece in rest]
 
         arrays, layout = [down], [[(0, 0, rank)]] + [[] for _ in order]
 
-        def keep(array, pair):
+        def keep(array, p):
             arrays.append(array)
-            for n, p in enumerate(pair):
-                layout[1 + order.index(p)].append((len(arrays) - 1, n * share, share))
-
-        for n in range(0, len(order), 2):
-            pair = order[n : n + 2]
-            packed = pieces[pair[0]]
-            if len(pair) > 1:
-                packed = call(
-                    pack_kernel,
-                    jax.ShapeDtypeStruct((share * len(pair), wide + cols), BF16),
-                    tuple(pieces[p] for p in pair),
-                )
-            for member in [packed] + others(packed, "groups"):
-                keep(member, pair)
+            layout[1 + order.index(p)].append((len(arrays) - 1, 0, array.shape[0]))
+
+        for p in order:
+            members = beside if p == 1 else [pieces[p]] + others(pieces[p], "groups")
+            if p in [*near, 1] and len(members) > 1:
+                shape = (share * groups, wide + cols)
+                members = [call(pack_kernel, jax.ShapeDtypeStruct(shape, BF16), tuple(members))]
+            for member in members:
+                keep(member, p)
                 for other in others(member, "replica"):
-                    keep(other, pair)
+                    keep(other, p)
 
         low, sent, every = call(
             functools.partial(down_kernel, layout),

time: 36.3 us -> 35.8 us (0.986)
  waiting for transfers between devices: 11.5 us -> 8.46 us
  starting transfers between devices: 11.1 us -> 13.5 us
    ppermute x8, waiting for transfers between devices: 8.36 us -> 5.97 us  [shift(): return lax.ppermute(x, axis, [(i, (i + by) % size) for i in range(size)])]
    ppermute x3 -> x4, starting transfers between devices: 5.69 us -> 7.52 us  [flip(): return lax.ppermute(x, 'adapter', [(i, i ^ bits) for i in range(adapters)])]
    ppermute x3 -> x4, waiting for transfers between devices: 3.17 us -> 2.49 us  [flip(): return lax.ppermute(x, 'adapter', [(i, i ^ bits) for i in range(adapters)])]
    ppermute x8, starting transfers between devices: 3.85 us -> 4.26 us  [shift(): return lax.ppermute(x, axis, [(i, (i + by) % size) for i in range(size)])]
    pallas_call x6 -> x7, Pallas kernels: 12.5 us -> 12.5 us  [call(): pl.pallas_call(kernel, out_shape=outs, in_specs=specs or [VMEM] * len(arg...]
  transfers between devices with their start and end apart: 13 -> 14, of which waited for: 6 -> 6; matrix products, arithmetic and copies ran while one was open for 3% -> 3% of each run, Pallas kernels for 30% -> 30%
where the time goes in v9:
time: 35.8 us; the launch traced here: 35.7 us
  starting transfers between devices  13.5 us (38%)
  Pallas kernels  12.5 us (35%)
  waiting for transfers between devices  8.46 us (24%)
  other arithmetic  0.99 us (3%)
    pallas_call x7, Pallas kernels, call(): pl.pallas_call(kernel, out_shape=outs, in_specs=specs or [VMEM] * len(arg...  12.5 us
    ppermute x4, starting transfers between devices, flip(): return lax.ppermute(x, 'adapter', [(i, i ^ bits) for i in range(adapters)])  7.52 us
    ppermute x8, waiting for transfers between devices, shift(): return lax.ppermute(x, axis, [(i, (i + by) % size) for i in range(size)])  5.97 us
    ppermute x8, starting transfers between devices, shift(): return lax.ppermute(x, axis, [(i, (i + by) % size) for i in range(size)])  4.26 us
    ppermute x4, waiting for transfers between devices, flip(): return lax.ppermute(x, 'adapter', [(i, i ^ bits) for i in range(adapters)])  2.49 us
    ppermute x2, starting transfers between devices, base(): recvs.append(lax.ppermute(block, ('tensor', 'replica'), base_pairs(h, by)))  1.75 us
    concatenate x1, other arithmetic, shards(): own = jnp.concatenate([down, u[0]], axis=1)  0.99 us
  transfers between devices with their start and end apart: 14, of which 6 were waited for; matrix products, arithmetic and copies ran while one was open for 3% of the time, Pallas kernels for 30%

profile of v9, /device:TPU:0, one launch (start us, length us, event | category | flops | bytes accessed | tf_op | source)
XLA Modules:
  0.0 35.7 jit_solution(19500547765629386)
XLA Ops:
  0.0 0.5 %collective-permute-start = (bf16[4096,512]{1,0:T(8,128)(2,1)}, bf16[4096,512]{1,0:T(8,128)(2,1)}, u32[]{:S(2)}, u32[]{:S(2)}) collective-permute-start(bf16[4096,512]{1,0:T(8,128)(2,1)} %v_ref.1), channel_id=1, source_target_pairs={{0,1},{1,0},{2,3},{3,2},{4,5},{5,4},{6,7},{7,6},{8,9},{9,8},{10,11... | collective-permute-start | bytes 12582920 | tf_op jit(solution)/shard_map/ppermute | solution.py:183
  0.5 1.0 %fusion = (bf16[16,4608]{1,0:T(8,128)(2,1)S(1)}, bf16[16,4608]{1,0:T(8,128)(2,1)S(1)}) fusion(s32[]{:T(128)S(6)} %select_n.7, bf16[64,4096]{1,0:T(8,128)(2,1)} %bitcast.11, bf16[64,512]{1,0:T(8,128)(2,1)} %bitcast.13, s32[]{:T(128)S(6)} %select_n.6), kind=kLoop, calls=%fused_computation.4 | loop fusion | flops 589824 | bytes 884744 | tf_op jit(solution)/shard_map/concatenate | solution.py:226
  1.4 4.7 %collective-permute-start.3 = (bf16[16,4608]{1,0:T(8,128)(2,1)S(1)}, bf16[16,4608]{1,0:T(8,128)(2,1)S(1)}, u32[]{:S(2)}, u32[]{:S(2)}) collective-permute-start(bf16[16,4608]{1,0:T(8,128)(2,1)S(1)} %get-tuple-element.22), channel_id=1, source_target_pairs={{0,12},{4,8},{8,4},{12,0},{1,13},{5,9},{9,5},{13,1},{2,14},{6,10},... | collective-permute-start | bytes 442376 | tf_op jit(solution)/shard_map/ppermute | solution.py:189
  6.1 0.1 stack.37.info_ref
  6.2 4.2 %shard_map.55 = (bf16[512,512]{1,0:T(8,128)(2,1)S(1)}, bf16[4,512,1024]{2,1,0:T(8,128)(2,1)S(1)}) custom-call(bf16[512,4096]{1,0:T(8,128)(2,1)} %x_ref, bf16[4096,512]{1,0:T(8,128)(2,1)} %v_ref.1), custom_call_target="tpu_custom_call" | custom-call | flops 2147483648 | bytes 8388608 | tf_op jit(solution)/shard_map/pallas_call | solution.py:21
  10.4 0.2 collective-permute-start.1
  10.6 0.0 collective-permute-start.10
  10.6 0.1 collective-permute-done.3.refs_0_
  10.7 1.5 %collective-permute-start.4 = (bf16[16,4608]{1,0:T(8,128)(2,1)S(1)}, bf16[16,4608]{1,0:T(8,128)(2,1)S(1)}, u32[]{:S(2)}, u32[]{:S(2)}) collective-permute-start(bf16[16,4608]{1,0:T(8,128)(2,1)S(1)} %collective-permute-done.3.refs_0_), channel_id=1, source_target_pairs={{0,16},{16,0},{1,17},{17,1},{2,18},{18,2},{3,19},{19,3},{4,20},{20... | collective-permute-start | bytes 442376 | tf_op jit(solution)/shard_map/ppermute | solution.py:183
  12.3 2.8 %collective-permute-start.6 = (bf16[16,4608]{1,0:T(8,128)(2,1)S(1)}, bf16[16,4608]{1,0:T(8,128)(2,1)S(1)}, u32[]{:S(2)}, u32[]{:S(2)}) collective-permute-start(bf16[16,4608]{1,0:T(8,128)(2,1)S(1)} %collective-permute-done.3.refs_0_), channel_id=1, source_target_pairs={{0,4},{4,0},{8,12},{12,8},{1,5},{5,1},{9,13},{13,9},{2,6},{6,2},{1... | collective-permute-start | bytes 442376 | tf_op jit(solution)/shard_map/ppermute | solution.py:189
  15.0 0.0 collective-permute-done.v_ref
  15.0 0.0 copy-start
  15.0 0.0 copy-start.1
  15.0 0.0 copy-start.2
  15.0 3.8 %shard_map.56.refs_1_ = bf16[512,512]{1,0:T(8,128)(2,1)S(1)} custom-call(bf16[4,512,1024]{2,1,0:T(8,128)(2,1)S(1)} %get-tuple-element.20.x_ref, bf16[4096,512]{1,0:T(8,128)(2,1)} %collective-permute-done.v_ref), custom_call_target="tpu_custom_call" | custom-call | flops 2147483648 | bytes 8388608 | tf_op jit(solution)/shard_map/pallas_call | solution.py:21
  18.9 0.1 collective-permute-start.11
  18.9 0.0 collective-permute-done.4.refs_1_
  18.9 1.5 %collective-permute-start.2 = (bf16[512,512]{1,0:T(8,128)(2,1)S(1)}, bf16[512,512]{1,0:T(8,128)(2,1)S(1)}, u32[]{:S(2)}, u32[]{:S(2)}) collective-permute-start(bf16[512,512]{1,0:T(8,128)(2,1)S(1)} %shard_map.56.refs_1_), channel_id=1, source_target_pairs={{0,2},{1,0},{2,3},{3,1},{4,6},{5,4},{6,7},{7,5},{8,10},{9,8},{10,1... | collective-permute-start | bytes 1572872 | tf_op jit(solution)/shard_map/ppermute | solution.py:252
  20.5 0.0 collective-permute-done.6.refs_3_
  20.5 1.3 %collective-permute-start.8 = (bf16[16,4608]{1,0:T(8,128)(2,1)S(1)}, bf16[16,4608]{1,0:T(8,128)(2,1)S(1)}, u32[]{:S(2)}, u32[]{:S(2)}) collective-permute-start(bf16[16,4608]{1,0:T(8,128)(2,1)S(1)} %collective-permute-done.6.refs_3_), channel_id=1, source_target_pairs={{0,16},{16,0},{1,17},{17,1},{2,18},{18,2},{3,19},{19,3},{4,20},{20... | collective-permute-start | bytes 442376 | tf_op jit(solution)/shard_map/ppermute | solution.py:183
  21.8 0.0 collective-permute-done.10.refs_0_
  21.8 0.0 collective-permute-start.5
  21.8 2.4 %collective-permute-done.11.refs_1_ = bf16[16,4608]{1,0:T(8,128)(2,1)S(1)} collective-permute-done((bf16[16,4608]{1,0:T(8,128)(2,1)S(1)}, bf16[16,4608]{1,0:T(8,128)(2,1)S(1)}, u32[]{:S(2)}, u32[]{:S(2)}) %collective-permute-start.11) | collective-permute-done | bytes 147488 | tf_op jit(solution)/shard_map/ppermute | solution.py:189
  24.2 0.1 collective-permute-start.12
  24.3 1.8 %collective-permute-done.8.refs_5_ = bf16[16,4608]{1,0:T(8,128)(2,1)S(1)} collective-permute-done((bf16[16,4608]{1,0:T(8,128)(2,1)S(1)}, bf16[16,4608]{1,0:T(8,128)(2,1)S(1)}, u32[]{:S(2)}, u32[]{:S(2)}) %collective-permute-start.8) | collective-permute-done | bytes 147488 | tf_op jit(solution)/shard_map/ppermute | solution.py:183
  26.2 0.0 collective-permute-start.7
  26.2 0.0 collective-permute-done.1.refs_2_
  26.2 0.5 %collective-permute-start.9 = (bf16[16,4608]{1,0:T(8,128)(2,1)S(1)}, bf16[16,4608]{1,0:T(8,128)(2,1)S(1)}, u32[]{:S(2)}, u32[]{:S(2)}) collective-permute-start(bf16[16,4608]{1,0:T(8,128)(2,1)S(1)} %collective-permute-done.8.refs_5_), channel_id=1, source_target_pairs={{0,1},{1,0},{2,3},{3,2},{4,5},{5,4},{6,7},{7,6},{8,9},{9,8},{10,11... | collective-permute-start | bytes 442376 | tf_op jit(solution)/shard_map/ppermute | solution.py:183
  26.7 0.9 %collective-permute-done.7.refs_4_ = bf16[16,4608]{1,0:T(8,128)(2,1)S(1)} collective-permute-done((bf16[16,4608]{1,0:T(8,128)(2,1)S(1)}, bf16[16,4608]{1,0:T(8,128)(2,1)S(1)}, u32[]{:S(2)}, u32[]{:S(2)}) %collective-permute-start.7) | collective-permute-done | bytes 147488 | tf_op jit(solution)/shard_map/ppermute | solution.py:183
  27.5 0.0 collective-permute-done.5.refs_2_
  27.5 0.2 collective-permute-done.9.refs_6_
  27.7 0.0 collective-permute-done.12.refs_8_
  27.7 0.0 copy-done
  27.7 0.0 copy-done.1
  27.8 0.0 copy-done.2
  27.8 1.8 %shard_map.60 = (f32[64,512]{1,0:T(8,128)S(1)}, bf16[64,512]{1,0:T(8,128)(2,1)S(1)}, bf16[256,512]{1,0:T(8,128)(2,1)S(1)}) custom-call(s32[8]{0:T(128)S(1)} %stack.37.info_ref, s32[1,512]{1,0:T(1,128)S(1)} %bitcast.15, bf16[4,512,1024]{2,1,0:T(8,128)(2,1)S(1)} %get-tuple-element.20.x_ref, bf16[64,512]{1,0:T(8,128)(2,1)S(1)} %bitcast.14, ...), custom_call_target="tpu_custom_call" | custom-call | flops 1073741824 | bytes 6555680 | tf_op jit(solution)/shard_map/pallas_call | solution.py:21
  29.6 0.4 %collective-permute-start.13 = (bf16[64,512]{1,0:T(8,128)(2,1)S(1)}, bf16[64,512]{1,0:T(8,128)(2,1)S(1)}, u32[]{:S(2)}, u32[]{:S(2)}) collective-permute-start(bf16[64,512]{1,0:T(8,128)(2,1)S(1)} %get-tuple-element.26), channel_id=1, source_target_pairs={{0,2},{2,0},{1,3},{3,1},{4,6},{6,4},{5,7},{7,5},{8,10},{10,8},{9,1... | collective-permute-start | bytes 196616 | tf_op jit(solution)/shard_map/ppermute | solution.py:183
  30.0 0.0 collective-permute-done.2.refs_3_
  30.0 0.9 %shard_map.57.base_ref = f32[512,512]{1,0:T(8,128)S(1)} custom-call(s32[8]{0:T(128)S(1)} %stack.37.info_ref, bf16[512,512]{1,0:T(8,128)(2,1)S(1)} %get-tuple-element.18.refs_0_, bf16[512,512]{1,0:T(8,128)(2,1)S(1)} %shard_map.56.refs_1_, bf16[512,512]{1,0:T(8,128)(2,1)S(1)} %collective-permute-done.1.refs_2_, bf16[512,512]{1,0:T(8,128)(2,1)S(1)} %collective-permute-done.2.refs_3_), custom_call_target="tpu_custom_call" | custom-call | flops 1048576 | bytes 2097184 | tf_op jit(solution)/shard_map/pallas_call | solution.py:21
  30.9 3.1 %collective-permute-done.13.refs_0_ = bf16[64,512]{1,0:T(8,128)(2,1)S(1)} collective-permute-done((bf16[64,512]{1,0:T(8,128)(2,1)S(1)}, bf16[64,512]{1,0:T(8,128)(2,1)S(1)}, u32[]{:S(2)}, u32[]{:S(2)}) %collective-permute-start.13) | collective-permute-done | bytes 65568 | tf_op jit(solution)/shard_map/ppermute | solution.py:183
  34.0 1.7 %shard_map.61 = bf16[512,512]{1,0:T(8,128)(2,1)} custom-call(s32[8]{0:T(128)S(1)} %stack.37.info_ref, s32[1,512]{1,0:T(1,128)S(1)} %bitcast.16, f32[512,512]{1,0:T(8,128)S(1)} %shard_map.57.base_ref, bf16[256,512]{1,0:T(8,128)(2,1)S(1)} %get-tuple-element.24.up_ref, f32[64,512]{1,0:T(8,128)S(1)} %get-tuple-element.25.low_ref, ...), custom_call_target="tpu_custom_call" | custom-call | flops 134217728 | bytes 1509408 | tf_op jit(solution)/shard_map/pallas_call | solution.py:21
  (2 shorter events, 0.0 us)
Async XLA Ops:
  0.0 15.0 %collective-permute-start = (bf16[4096,512]{1,0:T(8,128)(2,1)}, bf16[4096,512]{1,0:T(8,128)(2,1)}, u32[]{:S(2)}, u32[]{:S(2)}) collective-permute-start(bf16[4096,512]{1,0:T(8,128)(2,1)} %v_ref.1), channel_id=1, source_target_pairs={{0,1},{1,0},{2,3},{3,2},{4,5},{5,4},{6,7},{7,6},{8,9},{9,8},{10,11... | collective-permute-start | bytes 12582920 | tf_op jit(solution)/shard_map/ppermute | solution.py:183
  1.4 9.3 %collective-permute-start.3 = (bf16[16,4608]{1,0:T(8,128)(2,1)S(1)}, bf16[16,4608]{1,0:T(8,128)(2,1)S(1)}, u32[]{:S(2)}, u32[]{:S(2)}) collective-permute-start(bf16[16,4608]{1,0:T(8,128)(2,1)S(1)} %get-tuple-element.22), channel_id=1, source_target_pairs={{0,12},{4,8},{8,4},{12,0},{1,13},{5,9},{9,5},{13,1},{2,14},{6,10},... | collective-permute-start | bytes 442376 | tf_op jit(solution)/shard_map/ppermute | solution.py:189
  10.4 15.8 %collective-permute-start.1 = (bf16[512,512]{1,0:T(8,128)(2,1)S(1)}, bf16[512,512]{1,0:T(8,128)(2,1)S(1)}, u32[]{:S(2)}, u32[]{:S(2)}) collective-permute-start(bf16[512,512]{1,0:T(8,128)(2,1)S(1)} %get-tuple-element.18.refs_0_), channel_id=1, source_target_pairs={{0,1},{1,3},{2,0},{3,2},{4,5},{5,7},{6,4},{7,6},{8,9},{9,11},{10,8... | collective-permute-start | bytes 1572872 | tf_op jit(solution)/shard_map/ppermute | solution.py:252
  10.6 11.2 %collective-permute-start.10 = (bf16[16,4608]{1,0:T(8,128)(2,1)S(1)}, bf16[16,4608]{1,0:T(8,128)(2,1)S(1)}, u32[]{:S(2)}, u32[]{:S(2)}) collective-permute-start(bf16[16,4608]{1,0:T(8,128)(2,1)S(1)} %get-tuple-element.22), channel_id=1, source_target_pairs={{0,4},{4,0},{8,12},{12,8},{1,5},{5,1},{9,13},{13,9},{2,6},{6,2},{1... | collective-permute-start | bytes 442376 | tf_op jit(solution)/shard_map/ppermute | solution.py:189
  10.7 8.2 %collective-permute-start.4 = (bf16[16,4608]{1,0:T(8,128)(2,1)S(1)}, bf16[16,4608]{1,0:T(8,128)(2,1)S(1)}, u32[]{:S(2)}, u32[]{:S(2)}) collective-permute-start(bf16[16,4608]{1,0:T(8,128)(2,1)S(1)} %collective-permute-done.3.refs_0_), channel_id=1, source_target_pairs={{0,16},{16,0},{1,17},{17,1},{2,18},{18,2},{3,19},{19,3},{4,20},{20... | collective-permute-start | bytes 442376 | tf_op jit(solution)/shard_map/ppermute | solution.py:183
  12.3 8.2 %collective-permute-start.6 = (bf16[16,4608]{1,0:T(8,128)(2,1)S(1)}, bf16[16,4608]{1,0:T(8,128)(2,1)S(1)}, u32[]{:S(2)}, u32[]{:S(2)}) collective-permute-start(bf16[16,4608]{1,0:T(8,128)(2,1)S(1)} %collective-permute-done.3.refs_0_), channel_id=1, source_target_pairs={{0,4},{4,0},{8,12},{12,8},{1,5},{5,1},{9,13},{13,9},{2,6},{6,2},{1... | collective-permute-start | bytes 442376 | tf_op jit(solution)/shard_map/ppermute | solution.py:189
  15.0 12.7 %copy-start = (bf16[1,4096,64]{1,2,0:T(8,128)(2,1)S(1)}, bf16[1,4096,64]{1,2,0:T(8,128)(2,1)}, u32[]{:S(2)}) copy-start(bf16[1,4096,64]{1,2,0:T(8,128)(2,1)} %param.7) | copy-start | bytes 1572868
  15.0 12.7 %copy-start.1 = (bf16[1,64,512]{2,1,0:T(8,128)(2,1)S(1)}, bf16[1,64,512]{2,1,0:T(8,128)(2,1)}, u32[]{:S(2)}) copy-start(bf16[1,64,512]{2,1,0:T(8,128)(2,1)} %param.8) | copy-start | bytes 196612
  15.0 12.7 %copy-start.2 = (s32[512,1]{0,1:T(1,128)S(1)}, s32[512,1]{0,1:T(1,128)}, u32[]{:S(2)}) copy-start(s32[512,1]{0,1:T(1,128)} %param.9) | copy-start | bytes 6148
  18.9 5.4 %collective-permute-start.11 = (bf16[16,4608]{1,0:T(8,128)(2,1)S(1)}, bf16[16,4608]{1,0:T(8,128)(2,1)S(1)}, u32[]{:S(2)}, u32[]{:S(2)}) collective-permute-start(bf16[16,4608]{1,0:T(8,128)(2,1)S(1)} %get-tuple-element.23), channel_id=1, source_target_pairs={{0,4},{4,0},{8,12},{12,8},{1,5},{5,1},{9,13},{13,9},{2,6},{6,2},{1... | collective-permute-start | bytes 442376 | tf_op jit(solution)/shard_map/ppermute | solution.py:189
  18.9 11.1 %collective-permute-start.2 = (bf16[512,512]{1,0:T(8,128)(2,1)S(1)}, bf16[512,512]{1,0:T(8,128)(2,1)S(1)}, u32[]{:S(2)}, u32[]{:S(2)}) collective-permute-start(bf16[512,512]{1,0:T(8,128)(2,1)S(1)} %shard_map.56.refs_1_), channel_id=1, source_target_pairs={{0,2},{1,0},{2,3},{3,1},{4,6},{5,4},{6,7},{7,5},{8,10},{9,8},{10,1... | collective-permute-start | bytes 1572872 | tf_op jit(solution)/shard_map/ppermute | solution.py:252
  20.5 5.7 %collective-permute-start.8 = (bf16[16,4608]{1,0:T(8,128)(2,1)S(1)}, bf16[16,4608]{1,0:T(8,128)(2,1)S(1)}, u32[]{:S(2)}, u32[]{:S(2)}) collective-permute-start(bf16[16,4608]{1,0:T(8,128)(2,1)S(1)} %collective-permute-done.6.refs_3_), channel_id=1, source_target_pairs={{0,16},{16,0},{1,17},{17,1},{2,18},{18,2},{3,19},{19,3},{4,20},{20... | collective-permute-start | bytes 442376 | tf_op jit(solution)/shard_map/ppermute | solution.py:183
  21.8 5.7 %collective-permute-start.5 = (bf16[32,4608]{1,0:T(8,128)(2,1)S(1)}, bf16[32,4608]{1,0:T(8,128)(2,1)S(1)}, u32[]{:S(2)}, u32[]{:S(2)}) collective-permute-start(bf16[32,4608]{1,0:T(8,128)(2,1)S(1)} %shard_map.58.refs_1_), channel_id=1, source_target_pairs={{0,1},{1,0},{2,3},{3,2},{4,5},{5,4},{6,7},{7,6},{8,9},{9,8},{10,11... | collective-permute-start | bytes 884744 | tf_op jit(solution)/shard_map/ppermute | solution.py:183
  24.2 3.5 %collective-permute-start.12 = (bf16[32,4608]{1,0:T(8,128)(2,1)S(1)}, bf16[32,4608]{1,0:T(8,128)(2,1)S(1)}, u32[]{:S(2)}, u32[]{:S(2)}) collective-permute-start(bf16[32,4608]{1,0:T(8,128)(2,1)S(1)} %shard_map.59.refs_7_), channel_id=1, source_target_pairs={{0,1},{1,0},{2,3},{3,2},{4,5},{5,4},{6,7},{7,6},{8,9},{9,8},{10,11... | collective-permute-start | bytes 884744 | tf_op jit(solution)/shard_map/ppermute | solution.py:183
  26.2 1.4 %collective-permute-start.7 = (bf16[16,4608]{1,0:T(8,128)(2,1)S(1)}, bf16[16,4608]{1,0:T(8,128)(2,1)S(1)}, u32[]{:S(2)}, u32[]{:S(2)}) collective-permute-start(bf16[16,4608]{1,0:T(8,128)(2,1)S(1)} %collective-permute-done.6.refs_3_), channel_id=1, source_target_pairs={{0,1},{1,0},{2,3},{3,2},{4,5},{5,4},{6,7},{7,6},{8,9},{9,8},{10,11... | collective-permute-start | bytes 442376 | tf_op jit(solution)/shard_map/ppermute | solution.py:183
  26.2 1.6 %collective-permute-start.9 = (bf16[16,4608]{1,0:T(8,128)(2,1)S(1)}, bf16[16,4608]{1,0:T(8,128)(2,1)S(1)}, u32[]{:S(2)}, u32[]{:S(2)}) collective-permute-start(bf16[16,4608]{1,0:T(8,128)(2,1)S(1)} %collective-permute-done.8.refs_5_), channel_id=1, source_target_pairs={{0,1},{1,0},{2,3},{3,2},{4,5},{5,4},{6,7},{7,6},{8,9},{9,8},{10,11... | collective-permute-start | bytes 442376 | tf_op jit(solution)/shard_map/ppermute | solution.py:183
  29.6 4.4 %collective-permute-start.13 = (bf16[64,512]{1,0:T(8,128)(2,1)S(1)}, bf16[64,512]{1,0:T(8,128)(2,1)S(1)}, u32[]{:S(2)}, u32[]{:S(2)}) collective-permute-start(bf16[64,512]{1,0:T(8,128)(2,1)S(1)} %get-tuple-element.26), channel_id=1, source_target_pairs={{0,2},{2,0},{1,3},{3,1},{4,6},{6,4},{5,7},{7,5},{8,10},{10,8},{9,1... | collective-permute-start | bytes 196616 | tf_op jit(solution)/shard_map/ppermute | solution.py:183

commit v10 on v9

--- a/solution.py
+++ b/solution.py
@@ -264,7 +264,7 @@
         second = first
         for h in range(1, replicas):
             second, _ = base(h, [])
-        beside += [flip(after(piece, second), 1) for piece in rest]
+        beside += [flip(after(piece, pieces[order[-2]]), 1) for piece in rest]
 
         arrays, layout = [down], [[(0, 0, rank)]] + [[] for _ in order]
 
@@ -274,7 +274,7 @@
 
         for p in order:
             members = beside if p == 1 else [pieces[p]] + others(pieces[p], "groups")
-            if p in [*near, 1] and len(members) > 1:
+            if p in order and len(members) > 1:
                 shape = (share * groups, wide + cols)
                 members = [call(pack_kernel, jax.ShapeDtypeStruct(shape, BF16), tuple(members))]
             for member in members:

time: 35.8 us -> 37.7 us (1.053)
  starting transfers between devices: 13.5 us -> 16 us
  waiting for transfers between devices: 8.46 us -> 7.81 us
    ppermute x8 -> x7, waiting for transfers between devices: 5.97 us -> 2.11 us  [shift(): return lax.ppermute(x, axis, [(i, (i + by) % size) for i in range(size)])]
    ppermute x2, waiting for transfers between devices: 0.01 us -> 2.65 us  [base(): recvs.append(lax.ppermute(block, ('tensor', 'replica'), base_pairs(h, by)))]
    ppermute x4, starting transfers between devices: 7.52 us -> 9.94 us  [flip(): return lax.ppermute(x, 'adapter', [(i, i ^ bits) for i in range(adapters)])]
    ppermute x4, waiting for transfers between devices: 2.49 us -> 3.06 us  [flip(): return lax.ppermute(x, 'adapter', [(i, i ^ bits) for i in range(adapters)])]
    ppermute x8 -> x7, starting transfers between devices: 4.26 us -> 4.57 us  [shift(): return lax.ppermute(x, axis, [(i, (i + by) % size) for i in range(size)])]
    pallas_call x7 -> x8, Pallas kernels: 12.5 us -> 12.5 us  [call(): pl.pallas_call(kernel, out_shape=outs, in_specs=specs or [VMEM] * len(arg...]
  transfers between devices with their start and end apart: 14 -> 13, of which waited for: 6 -> 7; matrix products, arithmetic and copies ran while one was open for 3% -> 3% of each run, Pallas kernels for 30% -> 29%
where the time goes in v10:
time: 37.7 us; the launch traced here: 37.5 us
  starting transfers between devices  16 us (42%)
  Pallas kernels  12.5 us (33%)
  waiting for transfers between devices  7.81 us (21%)
  other arithmetic  0.99 us (3%)
    pallas_call x8, Pallas kernels, call(): pl.pallas_call(kernel, out_shape=outs, in_specs=specs or [VMEM] * len(arg...  12.5 us
    ppermute x4, starting transfers between devices, flip(): return lax.ppermute(x, 'adapter', [(i, i ^ bits) for i in range(adapters)])  9.94 us
    ppermute x7, starting transfers between devices, shift(): return lax.ppermute(x, axis, [(i, (i + by) % size) for i in range(size)])  4.57 us
    ppermute x4, waiting for transfers between devices, flip(): return lax.ppermute(x, 'adapter', [(i, i ^ bits) for i in range(adapters)])  3.06 us
    ppermute x2, waiting for transfers between devices, base(): recvs.append(lax.ppermute(block, ('tensor', 'replica'), base_pairs(h, by)))  2.65 us
    ppermute x7, waiting for transfers between devices, shift(): return lax.ppermute(x, axis, [(i, (i + by) % size) for i in range(size)])  2.11 us
    ppermute x2, starting transfers between devices, base(): recvs.append(lax.ppermute(block, ('tensor', 'replica'), base_pairs(h, by)))  1.51 us
    concatenate x1, other arithmetic, shards(): own = jnp.concatenate([down, u[0]], axis=1)  0.99 us
  transfers between devices with their start and end apart: 13, of which 7 were waited for; matrix products, arithmetic and copies ran while one was open for 3% of the time, Pallas kernels for 29%

profile of v10, /device:TPU:0, one launch (start us, length us, event | category | flops | bytes accessed | tf_op | source)
XLA Modules:
  0.0 37.5 jit_solution(2985325236902356047)
XLA Ops:
  0.0 0.5 %collective-permute-start = (bf16[4096,512]{1,0:T(8,128)(2,1)}, bf16[4096,512]{1,0:T(8,128)(2,1)}, u32[]{:S(2)}, u32[]{:S(2)}) collective-permute-start(bf16[4096,512]{1,0:T(8,128)(2,1)} %v_ref.1), channel_id=1, source_target_pairs={{0,1},{1,0},{2,3},{3,2},{4,5},{5,4},{6,7},{7,6},{8,9},{9,8},{10,11... | collective-permute-start | bytes 12582920 | tf_op jit(solution)/shard_map/ppermute | solution.py:183
  0.5 1.0 %fusion = (bf16[16,4608]{1,0:T(8,128)(2,1)S(1)}, bf16[16,4608]{1,0:T(8,128)(2,1)S(1)}) fusion(s32[]{:T(128)S(6)} %select_n.7, bf16[64,4096]{1,0:T(8,128)(2,1)} %bitcast.11, bf16[64,512]{1,0:T(8,128)(2,1)} %bitcast.13, s32[]{:T(128)S(6)} %select_n.6), kind=kLoop, calls=%fused_computation.4 | loop fusion | flops 589824 | bytes 884744 | tf_op jit(solution)/shard_map/concatenate | solution.py:226
  1.4 4.7 %collective-permute-start.3 = (bf16[16,4608]{1,0:T(8,128)(2,1)S(1)}, bf16[16,4608]{1,0:T(8,128)(2,1)S(1)}, u32[]{:S(2)}, u32[]{:S(2)}) collective-permute-start(bf16[16,4608]{1,0:T(8,128)(2,1)S(1)} %get-tuple-element.22), channel_id=1, source_target_pairs={{0,12},{4,8},{8,4},{12,0},{1,13},{5,9},{9,5},{13,1},{2,14},{6,10},... | collective-permute-start | bytes 442376 | tf_op jit(solution)/shard_map/ppermute | solution.py:189
  6.1 0.1 stack.37.info_ref
  6.2 4.2 %shard_map.55 = (bf16[512,512]{1,0:T(8,128)(2,1)S(1)}, bf16[4,512,1024]{2,1,0:T(8,128)(2,1)S(1)}) custom-call(bf16[512,4096]{1,0:T(8,128)(2,1)} %x_ref, bf16[4096,512]{1,0:T(8,128)(2,1)} %v_ref.1), custom_call_target="tpu_custom_call" | custom-call | flops 2147483648 | bytes 8388608 | tf_op jit(solution)/shard_map/pallas_call | solution.py:21
  10.4 0.3 collective-permute-done.3.refs_0_
  10.7 2.8 %collective-permute-start.6 = (bf16[16,4608]{1,0:T(8,128)(2,1)S(1)}, bf16[16,4608]{1,0:T(8,128)(2,1)S(1)}, u32[]{:S(2)}, u32[]{:S(2)}) collective-permute-start(bf16[16,4608]{1,0:T(8,128)(2,1)S(1)} %collective-permute-done.3.refs_0_), channel_id=1, source_target_pairs={{0,4},{4,0},{8,12},{12,8},{1,5},{5,1},{9,13},{13,9},{2,6},{6,2},{1... | collective-permute-start | bytes 442376 | tf_op jit(solution)/shard_map/ppermute | solution.py:189
  13.5 0.0 collective-permute-start.1
  13.5 0.0 collective-permute-start.9
  13.5 1.5 %collective-permute-start.4 = (bf16[16,4608]{1,0:T(8,128)(2,1)S(1)}, bf16[16,4608]{1,0:T(8,128)(2,1)S(1)}, u32[]{:S(2)}, u32[]{:S(2)}) collective-permute-start(bf16[16,4608]{1,0:T(8,128)(2,1)S(1)} %collective-permute-done.3.refs_0_), channel_id=1, source_target_pairs={{0,16},{16,0},{1,17},{17,1},{2,18},{18,2},{3,19},{19,3},{4,20},{20... | collective-permute-start | bytes 442376 | tf_op jit(solution)/shard_map/ppermute | solution.py:183
  15.1 2.7 %collective-permute-done.6.refs_0_ = bf16[16,4608]{1,0:T(8,128)(2,1)S(1)} collective-permute-done((bf16[16,4608]{1,0:T(8,128)(2,1)S(1)}, bf16[16,4608]{1,0:T(8,128)(2,1)S(1)}, u32[]{:S(2)}, u32[]{:S(2)}) %collective-permute-start.6) | collective-permute-done | bytes 147488 | tf_op jit(solution)/shard_map/ppermute | solution.py:189
  17.8 2.5 %collective-permute-start.10 = (bf16[16,4608]{1,0:T(8,128)(2,1)S(1)}, bf16[16,4608]{1,0:T(8,128)(2,1)S(1)}, u32[]{:S(2)}, u32[]{:S(2)}) collective-permute-start(bf16[16,4608]{1,0:T(8,128)(2,1)S(1)} %get-tuple-element.23), channel_id=1, source_target_pairs={{0,4},{4,0},{8,12},{12,8},{1,5},{5,1},{9,13},{13,9},{2,6},{6,2},{1... | collective-permute-start | bytes 442376 | tf_op jit(solution)/shard_map/ppermute | solution.py:189
  20.3 0.0 collective-permute-done.v_ref
  20.3 1.5 %collective-permute-start.7 = (bf16[16,4608]{1,0:T(8,128)(2,1)S(1)}, bf16[16,4608]{1,0:T(8,128)(2,1)S(1)}, u32[]{:S(2)}, u32[]{:S(2)}) collective-permute-start(bf16[16,4608]{1,0:T(8,128)(2,1)S(1)} %collective-permute-done.6.refs_0_), channel_id=1, source_target_pairs={{0,16},{16,0},{1,17},{17,1},{2,18},{18,2},{3,19},{19,3},{4,20},{20... | collective-permute-start | bytes 442376 | tf_op jit(solution)/shard_map/ppermute | solution.py:183
  21.8 0.0 copy-start
  21.8 0.0 copy-start.1
  21.8 0.0 copy-start.2
  21.8 3.8 %shard_map.56.refs_1_ = bf16[512,512]{1,0:T(8,128)(2,1)S(1)} custom-call(bf16[4,512,1024]{2,1,0:T(8,128)(2,1)S(1)} %get-tuple-element.20.x_ref, bf16[4096,512]{1,0:T(8,128)(2,1)} %collective-permute-done.v_ref), custom_call_target="tpu_custom_call" | custom-call | flops 2147483648 | bytes 8388608 | tf_op jit(solution)/shard_map/pallas_call | solution.py:21
  25.6 0.0 collective-permute-done.4.refs_1_
  25.6 1.5 %collective-permute-start.2 = (bf16[512,512]{1,0:T(8,128)(2,1)S(1)}, bf16[512,512]{1,0:T(8,128)(2,1)S(1)}, u32[]{:S(2)}, u32[]{:S(2)}) collective-permute-start(bf16[512,512]{1,0:T(8,128)(2,1)S(1)} %shard_map.56.refs_1_), channel_id=1, source_target_pairs={{0,2},{1,0},{2,3},{3,1},{4,6},{5,4},{6,7},{7,5},{8,10},{9,8},{10,1... | collective-permute-start | bytes 1572872 | tf_op jit(solution)/shard_map/ppermute | solution.py:252
  27.1 0.0 collective-permute-done.7.refs_1_
  27.2 0.1 collective-permute-start.5
  27.3 0.0 collective-permute-done.9.refs_0_
  27.3 0.6 %collective-permute-start.8 = (bf16[32,4608]{1,0:T(8,128)(2,1)S(1)}, bf16[32,4608]{1,0:T(8,128)(2,1)S(1)}, u32[]{:S(2)}, u32[]{:S(2)}) collective-permute-start(bf16[32,4608]{1,0:T(8,128)(2,1)S(1)} %shard_map.59.refs_3_), channel_id=1, source_target_pairs={{0,1},{1,0},{2,3},{3,2},{4,5},{5,4},{6,7},{7,6},{8,9},{9,8},{10,11... | collective-permute-start | bytes 884744 | tf_op jit(solution)/shard_map/ppermute | solution.py:183
  27.8 0.0 collective-permute-done.10.refs_1_
  27.9 0.1 collective-permute-start.11
  27.9 0.0 collective-permute-done.1.refs_2_
  27.9 0.9 %collective-permute-done.5.refs_2_ = bf16[32,4608]{1,0:T(8,128)(2,1)S(1)} collective-permute-done((bf16[32,4608]{1,0:T(8,128)(2,1)S(1)}, bf16[32,4608]{1,0:T(8,128)(2,1)S(1)}, u32[]{:S(2)}, u32[]{:S(2)}) %collective-permute-start.5) | collective-permute-done | bytes 294944 | tf_op jit(solution)/shard_map/ppermute | solution.py:183
  28.8 0.4 %collective-permute-done.8.refs_4_ = bf16[32,4608]{1,0:T(8,128)(2,1)S(1)} collective-permute-done((bf16[32,4608]{1,0:T(8,128)(2,1)S(1)}, bf16[32,4608]{1,0:T(8,128)(2,1)S(1)}, u32[]{:S(2)}, u32[]{:S(2)}) %collective-permute-start.8) | collective-permute-done | bytes 294944 | tf_op jit(solution)/shard_map/ppermute | solution.py:183
  29.2 0.4 %collective-permute-done.11.refs_6_ = bf16[32,4608]{1,0:T(8,128)(2,1)S(1)} collective-permute-done((bf16[32,4608]{1,0:T(8,128)(2,1)S(1)}, bf16[32,4608]{1,0:T(8,128)(2,1)S(1)}, u32[]{:S(2)}, u32[]{:S(2)}) %collective-permute-start.11) | collective-permute-done | bytes 294944 | tf_op jit(solution)/shard_map/ppermute | solution.py:183
  29.6 0.0 copy-done
  29.6 0.0 copy-done.1
  29.6 0.0 copy-done.2
  29.7 1.9 %shard_map.61 = (f32[64,512]{1,0:T(8,128)S(1)}, bf16[64,512]{1,0:T(8,128)(2,1)S(1)}, bf16[256,512]{1,0:T(8,128)(2,1)S(1)}) custom-call(s32[8]{0:T(128)S(1)} %stack.37.info_ref, s32[1,512]{1,0:T(1,128)S(1)} %bitcast.15, bf16[4,512,1024]{2,1,0:T(8,128)(2,1)S(1)} %get-tuple-element.20.x_ref, bf16[64,512]{1,0:T(8,128)(2,1)S(1)} %bitcast.14, ...), custom_call_target="tpu_custom_call" | custom-call | flops 1073741824 | bytes 6555680 | tf_op jit(solution)/shard_map/pallas_call | solution.py:21
  31.5 0.4 collective-permute-start.12
  31.9 2.6 %collective-permute-done.2.refs_3_ = bf16[512,512]{1,0:T(8,128)(2,1)S(1)} collective-permute-done((bf16[512,512]{1,0:T(8,128)(2,1)S(1)}, bf16[512,512]{1,0:T(8,128)(2,1)S(1)}, u32[]{:S(2)}, u32[]{:S(2)}) %collective-permute-start.2) | collective-permute-done | bytes 524320 | tf_op jit(solution)/shard_map/ppermute | solution.py:252
  34.5 0.9 %shard_map.57.base_ref = f32[512,512]{1,0:T(8,128)S(1)} custom-call(s32[8]{0:T(128)S(1)} %stack.37.info_ref, bf16[512,512]{1,0:T(8,128)(2,1)S(1)} %get-tuple-element.18.refs_0_, bf16[512,512]{1,0:T(8,128)(2,1)S(1)} %shard_map.56.refs_1_, bf16[512,512]{1,0:T(8,128)(2,1)S(1)} %collective-permute-done.1.refs_2_, bf16[512,512]{1,0:T(8,128)(2,1)S(1)} %collective-permute-done.2.refs_3_), custom_call_target="tpu_custom_call" | custom-call | flops 1048576 | bytes 2097184 | tf_op jit(solution)/shard_map/pallas_call | solution.py:21
  35.4 0.4 %collective-permute-done.12.refs_0_ = bf16[64,512]{1,0:T(8,128)(2,1)S(1)} collective-permute-done((bf16[64,512]{1,0:T(8,128)(2,1)S(1)}, bf16[64,512]{1,0:T(8,128)(2,1)S(1)}, u32[]{:S(2)}, u32[]{:S(2)}) %collective-permute-start.12) | collective-permute-done | bytes 65568 | tf_op jit(solution)/shard_map/ppermute | solution.py:183
  35.8 1.7 %shard_map.62 = bf16[512,512]{1,0:T(8,128)(2,1)} custom-call(s32[8]{0:T(128)S(1)} %stack.37.info_ref, s32[1,512]{1,0:T(1,128)S(1)} %bitcast.16, f32[512,512]{1,0:T(8,128)S(1)} %shard_map.57.base_ref, bf16[256,512]{1,0:T(8,128)(2,1)S(1)} %get-tuple-element.24.up_ref, f32[64,512]{1,0:T(8,128)S(1)} %get-tuple-element.25.low_ref, ...), custom_call_target="tpu_custom_call" | custom-call | flops 134217728 | bytes 1509408 | tf_op jit(solution)/shard_map/pallas_call | solution.py:21
  (3 shorter events, 0.1 us)
Async XLA Ops:
  0.0 20.3 %collective-permute-start = (bf16[4096,512]{1,0:T(8,128)(2,1)}, bf16[4096,512]{1,0:T(8,128)(2,1)}, u32[]{:S(2)}, u32[]{:S(2)}) collective-permute-start(bf16[4096,512]{1,0:T(8,128)(2,1)} %v_ref.1), channel_id=1, source_target_pairs={{0,1},{1,0},{2,3},{3,2},{4,5},{5,4},{6,7},{7,6},{8,9},{9,8},{10,11... | collective-permute-start | bytes 12582920 | tf_op jit(solution)/shard_map/ppermute | solution.py:183
  1.4 9.3 %collective-permute-start.3 = (bf16[16,4608]{1,0:T(8,128)(2,1)S(1)}, bf16[16,4608]{1,0:T(8,128)(2,1)S(1)}, u32[]{:S(2)}, u32[]{:S(2)}) collective-permute-start(bf16[16,4608]{1,0:T(8,128)(2,1)S(1)} %get-tuple-element.22), channel_id=1, source_target_pairs={{0,12},{4,8},{8,4},{12,0},{1,13},{5,9},{9,5},{13,1},{2,14},{6,10},... | collective-permute-start | bytes 442376 | tf_op jit(solution)/shard_map/ppermute | solution.py:189
  10.7 7.0 %collective-permute-start.6 = (bf16[16,4608]{1,0:T(8,128)(2,1)S(1)}, bf16[16,4608]{1,0:T(8,128)(2,1)S(1)}, u32[]{:S(2)}, u32[]{:S(2)}) collective-permute-start(bf16[16,4608]{1,0:T(8,128)(2,1)S(1)} %collective-permute-done.3.refs_0_), channel_id=1, source_target_pairs={{0,4},{4,0},{8,12},{12,8},{1,5},{5,1},{9,13},{13,9},{2,6},{6,2},{1... | collective-permute-start | bytes 442376 | tf_op jit(solution)/shard_map/ppermute | solution.py:189
  13.5 14.4 %collective-permute-start.1 = (bf16[512,512]{1,0:T(8,128)(2,1)S(1)}, bf16[512,512]{1,0:T(8,128)(2,1)S(1)}, u32[]{:S(2)}, u32[]{:S(2)}) collective-permute-start(bf16[512,512]{1,0:T(8,128)(2,1)S(1)} %get-tuple-element.18.refs_0_), channel_id=1, source_target_pairs={{0,1},{1,3},{2,0},{3,2},{4,5},{5,7},{6,4},{7,6},{8,9},{9,11},{10,8... | collective-permute-start | bytes 1572872 | tf_op jit(solution)/shard_map/ppermute | solution.py:252
  13.5 13.8 %collective-permute-start.9 = (bf16[16,4608]{1,0:T(8,128)(2,1)S(1)}, bf16[16,4608]{1,0:T(8,128)(2,1)S(1)}, u32[]{:S(2)}, u32[]{:S(2)}) collective-permute-start(bf16[16,4608]{1,0:T(8,128)(2,1)S(1)} %get-tuple-element.22), channel_id=1, source_target_pairs={{0,4},{4,0},{8,12},{12,8},{1,5},{5,1},{9,13},{13,9},{2,6},{6,2},{1... | collective-permute-start | bytes 442376 | tf_op jit(solution)/shard_map/ppermute | solution.py:189
  13.5 12.1 %collective-permute-start.4 = (bf16[16,4608]{1,0:T(8,128)(2,1)S(1)}, bf16[16,4608]{1,0:T(8,128)(2,1)S(1)}, u32[]{:S(2)}, u32[]{:S(2)}) collective-permute-start(bf16[16,4608]{1,0:T(8,128)(2,1)S(1)} %collective-permute-done.3.refs_0_), channel_id=1, source_target_pairs={{0,16},{16,0},{1,17},{17,1},{2,18},{18,2},{3,19},{19,3},{4,20},{20... | collective-permute-start | bytes 442376 | tf_op jit(solution)/shard_map/ppermute | solution.py:183
  17.8 10.1 %collective-permute-start.10 = (bf16[16,4608]{1,0:T(8,128)(2,1)S(1)}, bf16[16,4608]{1,0:T(8,128)(2,1)S(1)}, u32[]{:S(2)}, u32[]{:S(2)}) collective-permute-start(bf16[16,4608]{1,0:T(8,128)(2,1)S(1)} %get-tuple-element.23), channel_id=1, source_target_pairs={{0,4},{4,0},{8,12},{12,8},{1,5},{5,1},{9,13},{13,9},{2,6},{6,2},{1... | collective-permute-start | bytes 442376 | tf_op jit(solution)/shard_map/ppermute | solution.py:189
  20.3 6.9 %collective-permute-start.7 = (bf16[16,4608]{1,0:T(8,128)(2,1)S(1)}, bf16[16,4608]{1,0:T(8,128)(2,1)S(1)}, u32[]{:S(2)}, u32[]{:S(2)}) collective-permute-start(bf16[16,4608]{1,0:T(8,128)(2,1)S(1)} %collective-permute-done.6.refs_0_), channel_id=1, source_target_pairs={{0,16},{16,0},{1,17},{17,1},{2,18},{18,2},{3,19},{19,3},{4,20},{20... | collective-permute-start | bytes 442376 | tf_op jit(solution)/shard_map/ppermute | solution.py:183
  21.8 7.9 %copy-start = (bf16[1,4096,64]{1,2,0:T(8,128)(2,1)S(1)}, bf16[1,4096,64]{1,2,0:T(8,128)(2,1)}, u32[]{:S(2)}) copy-start(bf16[1,4096,64]{1,2,0:T(8,128)(2,1)} %param.7) | copy-start | bytes 1572868
  21.8 7.9 %copy-start.1 = (bf16[1,64,512]{2,1,0:T(8,128)(2,1)S(1)}, bf16[1,64,512]{2,1,0:T(8,128)(2,1)}, u32[]{:S(2)}) copy-start(bf16[1,64,512]{2,1,0:T(8,128)(2,1)} %param.8) | copy-start | bytes 196612
  21.8 7.9 %copy-start.2 = (s32[512,1]{0,1:T(1,128)S(1)}, s32[512,1]{0,1:T(1,128)}, u32[]{:S(2)}) copy-start(s32[512,1]{0,1:T(1,128)} %param.9) | copy-start | bytes 6148
  25.6 8.9 %collective-permute-start.2 = (bf16[512,512]{1,0:T(8,128)(2,1)S(1)}, bf16[512,512]{1,0:T(8,128)(2,1)S(1)}, u32[]{:S(2)}, u32[]{:S(2)}) collective-permute-start(bf16[512,512]{1,0:T(8,128)(2,1)S(1)} %shard_map.56.refs_1_), channel_id=1, source_target_pairs={{0,2},{1,0},{2,3},{3,1},{4,6},{5,4},{6,7},{7,5},{8,10},{9,8},{10,1... | collective-permute-start | bytes 1572872 | tf_op jit(solution)/shard_map/ppermute | solution.py:252
  27.2 1.6 %collective-permute-start.5 = (bf16[32,4608]{1,0:T(8,128)(2,1)S(1)}, bf16[32,4608]{1,0:T(8,128)(2,1)S(1)}, u32[]{:S(2)}, u32[]{:S(2)}) collective-permute-start(bf16[32,4608]{1,0:T(8,128)(2,1)S(1)} %shard_map.58.refs_1_), channel_id=1, source_target_pairs={{0,1},{1,0},{2,3},{3,2},{4,5},{5,4},{6,7},{7,6},{8,9},{9,8},{10,11... | collective-permute-start | bytes 884744 | tf_op jit(solution)/shard_map/ppermute | solution.py:183
  27.3 2.0 %collective-permute-start.8 = (bf16[32,4608]{1,0:T(8,128)(2,1)S(1)}, bf16[32,4608]{1,0:T(8,128)(2,1)S(1)}, u32[]{:S(2)}, u32[]{:S(2)}) collective-permute-start(bf16[32,4608]{1,0:T(8,128)(2,1)S(1)} %shard_map.59.refs_3_), channel_id=1, source_target_pairs={{0,1},{1,0},{2,3},{3,2},{4,5},{5,4},{6,7},{7,6},{8,9},{9,8},{10,11... | collective-permute-start | bytes 884744 | tf_op jit(solution)/shard_map/ppermute | solution.py:183
  27.9 1.8 %collective-permute-start.11 = (bf16[32,4608]{1,0:T(8,128)(2,1)S(1)}, bf16[32,4608]{1,0:T(8,128)(2,1)S(1)}, u32[]{:S(2)}, u32[]{:S(2)}) collective-permute-start(bf16[32,4608]{1,0:T(8,128)(2,1)S(1)} %shard_map.60.refs_5_), channel_id=1, source_target_pairs={{0,1},{1,0},{2,3},{3,2},{4,5},{5,4},{6,7},{7,6},{8,9},{9,8},{10,11... | collective-permute-start | bytes 884744 | tf_op jit(solution)/shard_map/ppermute | solution.py:183
  31.5 4.3 %collective-permute-start.12 = (bf16[64,512]{1,0:T(8,128)(2,1)S(1)}, bf16[64,512]{1,0:T(8,128)(2,1)S(1)}, u32[]{:S(2)}, u32[]{:S(2)}) collective-permute-start(bf16[64,512]{1,0:T(8,128)(2,1)S(1)} %get-tuple-element.26), channel_id=1, source_target_pairs={{0,2},{2,0},{1,3},{3,1},{4,6},{6,4},{5,7},{7,5},{8,10},{10,8},{9,1... | collective-permute-start | bytes 196616 | tf_op jit(solution)/shard_map/ppermute | solution.py:183

commit v11 on v9

--- a/solution.py
+++ b/solution.py
@@ -120,7 +120,7 @@
         row += rows
 
 
-def down_kernel(layout, info_ref, idx_ref, x_ref, own_ref, *refs):
+def down_kernel(layout, slots, slot_ref, x_ref, own_ref, *refs):
     parts, (low_ref, sent_ref, up_ref, scratch) = refs[:-4], refs[-4:]
     rank, size, cols = low_ref.shape[0], x_ref.shape[2], own_ref.shape[1]
     up_ref[:rank, :] = own_ref[...]
@@ -140,21 +140,21 @@
                 preferred_element_type=F32,
             )
         for k in range(len(group)):
-            match = idx_ref[...] == info_ref[first + k]
+            match = slot_ref[...] == slots[first + k]
             low = low + jnp.where(match, prod[k * rank : (k + 1) * rank, :], 0.0)
     low_ref[...] = low
     sent_ref[...] = low.astype(BF16)
 
 
-def sum_kernel(adapters, info_ref, *refs):
+def sum_kernel(flag_ref, *refs):
     terms, out_ref = refs[:-1], refs[-1]
     total = jnp.zeros(out_ref.shape, F32)
     for n, term in enumerate(terms):
-        total = total + jnp.where(info_ref[adapters + n] == 1, term[...].astype(F32), 0.0)
+        total = total + jnp.where(flag_ref[n] == 1, term[...].astype(F32), 0.0)
     out_ref[...] = total
 
 
-def last_kernel(info_ref, idx_ref, base_ref, up_ref, low_ref, *refs):
+def last_kernel(slots, slot_ref, base_ref, up_ref, low_ref, *refs):
     others, (out_ref, spread) = refs[:-2], refs[-2:]
     rank = low_ref.shape[0]
     low = low_ref[...]
@@ -162,7 +162,7 @@
         low = low + other[...].astype(F32)
     low = low.astype(BF16).astype(F32)
     for k in range(up_ref.shape[0] // rank):
-        match = idx_ref[...] == info_ref[k]
+        match = slot_ref[...] == slots[k]
         spread[k * rank : (k + 1) * rank, :] = jnp.where(match, low, 0.0).astype(BF16)
     lora = lax.dot_general(
         spread[...], up_ref[...], (((0,), (0,)), ((), ())), preferred_element_type=F32
@@ -216,8 +216,9 @@
         order = [*range(3, adapters, 2), *range(2, adapters, 2), 1][: adapters - 1]
         halves = [lax.rem(r - h + replicas, replicas) * per_half for h in range(replicas)]
         here = [((t >= n) & (t < n + per_half)).astype(jnp.int32) for n in halves]
-        info = [a] + [lax.bitwise_xor(a, jnp.int32(p)) for p in order]
-        info = jnp.stack(info + here + [f for f in here for _ in range(1, tensors)])
+        flags = jnp.stack(here + [f for f in here for _ in range(1, tensors)])
+        slots = [0, *order]
+        slot = lax.bitwise_xor(row, jnp.broadcast_to(a, row.shape))
 
         held = [v] + others(v, "replica")
 
@@ -253,7 +254,7 @@
             return terms, cuts
 
         xs = None
-        x, info = lax.optimization_barrier((x, info, mine, *rest))[:2]
+        x, flags, slot = lax.optimization_barrier((x, flags, slot, mine, *rest))[:3]
         first, xs = base(0, [])
         for p, piece in zip(near, lax.optimization_barrier((*[pieces[p] for p in near], first))):
             pieces[p] = piece
@@ -283,32 +284,32 @@
                     keep(other, p)
 
         low, sent, every = call(
-            functools.partial(down_kernel, layout),
+            functools.partial(down_kernel, layout, slots),
             (jax.ShapeDtypeStruct((rank, tokens), F32), jax.ShapeDtypeStruct((rank, tokens), BF16),
                 jax.ShapeDtypeStruct((adapters * rank, cols), BF16)),
-            (info, row, after(xs, *recvs[: tensors - 1]), u[0], *arrays),
+            (slot, after(xs, *recvs[: tensors - 1]), u[0], *arrays),
             scratch=[
                 pltpu.VMEM((CHUNKS, min(BATCH, adapters) * rank, wide // CHUNKS), BF16),
             ],
             flops=2 * x.size * rank * adapters,
-            specs=[SMEM] + [VMEM] * (3 + len(arrays)),
+            specs=[VMEM] * (3 + len(arrays)),
         )
         lows = others(sent, "tensor")
         terms = blocks + recvs
         total = call(
-            functools.partial(sum_kernel, adapters),
+            sum_kernel,
             jax.ShapeDtypeStruct((tokens, cols), F32),
-            (info, *terms),
+            (flags, *terms),
             flops=len(terms) * tokens * cols,
             specs=[SMEM] + [VMEM] * len(terms),
         )
         return call(
-            last_kernel,
+            functools.partial(last_kernel, slots),
             jax.ShapeDtypeStruct((tokens, cols), BF16),
-            (info, row, total, every, low, *lows),
+            (slot, total, every, low, *lows),
             scratch=[pltpu.VMEM((adapters * rank, tokens), BF16)],
             flops=2 * tokens * rank * adapters * cols,
-            specs=[SMEM] + [VMEM] * (4 + len(lows)),
+            specs=[VMEM] * (4 + len(lows)),
         )
 
     return shards

time: 35.8 us -> 35.4 us (0.989)
  Pallas kernels: 12.5 us -> 11.4 us
  other arithmetic: 0.99 us -> 1.75 us
    pallas_call x7, Pallas kernels: 12.5 us -> 11.4 us  [call(): pl.pallas_call(kernel, out_shape=outs, in_specs=specs or [VMEM] * len(arg...]
    xor x0 -> x1, other arithmetic: none -> 0.69 us  [shards(): slot = lax.bitwise_xor(row, jnp.broadcast_to(a, row.shape))]
    ppermute x4, starting transfers between devices: 7.52 us -> 6.92 us  [flip(): return lax.ppermute(x, 'adapter', [(i, i ^ bits) for i in range(adapters)])]
    ppermute x8, starting transfers between devices: 4.26 us -> 4.64 us  [shift(): return lax.ppermute(x, axis, [(i, (i + by) % size) for i in range(size)])]
  transfers between devices with their start and end apart: 14 -> 14, of which waited for: 6 -> 6; matrix products, arithmetic and copies ran while one was open for 3% -> 5% of each run, Pallas kernels for 30% -> 29%
where the time goes in v11:
time: 35.4 us; the launch traced here: 35.2 us
  starting transfers between devices  13.5 us (38%)
  Pallas kernels  11.4 us (32%)
  waiting for transfers between devices  8.54 us (24%)
  other arithmetic  1.75 us (5%)
    pallas_call x7, Pallas kernels, call(): pl.pallas_call(kernel, out_shape=outs, in_specs=specs or [VMEM] * len(arg...  11.4 us
    ppermute x4, starting transfers between devices, flip(): return lax.ppermute(x, 'adapter', [(i, i ^ bits) for i in range(adapters)])  6.92 us
    ppermute x8, waiting for transfers between devices, shift(): return lax.ppermute(x, axis, [(i, (i + by) % size) for i in range(size)])  5.8 us
    ppermute x8, starting transfers between devices, shift(): return lax.ppermute(x, axis, [(i, (i + by) % size) for i in range(size)])  4.64 us
    ppermute x4, waiting for transfers between devices, flip(): return lax.ppermute(x, 'adapter', [(i, i ^ bits) for i in range(adapters)])  2.74 us
    ppermute x2, starting transfers between devices, base(): recvs.append(lax.ppermute(block, ('tensor', 'replica'), base_pairs(h, by)))  1.9 us
    concatenate x1, other arithmetic, shards(): own = jnp.concatenate([down, u[0]], axis=1)  0.99 us
  transfers between devices with their start and end apart: 14, of which 6 were waited for; matrix products, arithmetic and copies ran while one was open for 5% of the time, Pallas kernels for 29%

profile of v11, /device:TPU:0, one launch (start us, length us, event | category | flops | bytes accessed | tf_op | source)
XLA Modules:
  0.0 35.2 jit_solution(2709437196594859210)
XLA Ops:
  0.0 0.5 %collective-permute-start = (bf16[4096,512]{1,0:T(8,128)(2,1)}, bf16[4096,512]{1,0:T(8,128)(2,1)}, u32[]{:S(2)}, u32[]{:S(2)}) collective-permute-start(bf16[4096,512]{1,0:T(8,128)(2,1)} %v_ref.1), channel_id=1, source_target_pairs={{0,1},{1,0},{2,3},{3,2},{4,5},{5,4},{6,7},{7,6},{8,9},{9,8},{10,11... | collective-permute-start | bytes 12582920 | tf_op jit(solution)/shard_map/ppermute | solution.py:183
  0.5 1.0 %fusion = (bf16[16,4608]{1,0:T(8,128)(2,1)S(1)}, bf16[16,4608]{1,0:T(8,128)(2,1)S(1)}) fusion(s32[]{:T(128)S(6)} %select_n.7, bf16[64,4096]{1,0:T(8,128)(2,1)} %bitcast.8, bf16[64,512]{1,0:T(8,128)(2,1)} %bitcast.10, s32[]{:T(128)S(6)} %select_n.6), kind=kLoop, calls=%fused_computation.4 | loop fusion | flops 589824 | bytes 884744 | tf_op jit(solution)/shard_map/concatenate | solution.py:227
  1.4 4.7 %collective-permute-start.3 = (bf16[16,4608]{1,0:T(8,128)(2,1)S(1)}, bf16[16,4608]{1,0:T(8,128)(2,1)S(1)}, u32[]{:S(2)}, u32[]{:S(2)}) collective-permute-start(bf16[16,4608]{1,0:T(8,128)(2,1)S(1)} %get-tuple-element.24), channel_id=1, source_target_pairs={{0,12},{4,8},{8,4},{12,0},{1,13},{5,9},{9,5},{13,1},{2,14},{6,10},... | collective-permute-start | bytes 442376 | tf_op jit(solution)/shard_map/ppermute | solution.py:189
  6.1 0.1 add_convert_fusion.flag_ref
  6.2 0.7 %xor_bitcast_fusion.slot_ref = s32[1,512]{1,0:T(1,128)S(1)} fusion(s32[512,1]{0,1:T(1,128)} %param.9, s32[]{:T(128)S(6)} %axis_index.48), kind=kLoop, calls=%fused_computation.6 | loop fusion | flops 512 | bytes 4100 | tf_op jit(solution)/shard_map/xor | solution.py:221
  6.9 4.2 %shard_map.55 = (bf16[512,512]{1,0:T(8,128)(2,1)S(1)}, bf16[4,512,1024]{2,1,0:T(8,128)(2,1)S(1)}) custom-call(bf16[512,4096]{1,0:T(8,128)(2,1)} %x_ref, bf16[4096,512]{1,0:T(8,128)(2,1)} %v_ref.1), custom_call_target="tpu_custom_call" | custom-call | flops 2147483648 | bytes 8388608 | tf_op jit(solution)/shard_map/pallas_call | solution.py:21
  11.1 0.2 collective-permute-start.1
  11.3 0.0 collective-permute-start.10
  11.3 0.0 collective-permute-done.3.refs_0_
  11.3 1.5 %collective-permute-start.4 = (bf16[16,4608]{1,0:T(8,128)(2,1)S(1)}, bf16[16,4608]{1,0:T(8,128)(2,1)S(1)}, u32[]{:S(2)}, u32[]{:S(2)}) collective-permute-start(bf16[16,4608]{1,0:T(8,128)(2,1)S(1)} %collective-permute-done.3.refs_0_), channel_id=1, source_target_pairs={{0,16},{16,0},{1,17},{17,1},{2,18},{18,2},{3,19},{19,3},{4,20},{20... | collective-permute-start | bytes 442376 | tf_op jit(solution)/shard_map/ppermute | solution.py:183
  12.8 2.2 %collective-permute-start.6 = (bf16[16,4608]{1,0:T(8,128)(2,1)S(1)}, bf16[16,4608]{1,0:T(8,128)(2,1)S(1)}, u32[]{:S(2)}, u32[]{:S(2)}) collective-permute-start(bf16[16,4608]{1,0:T(8,128)(2,1)S(1)} %collective-permute-done.3.refs_0_), channel_id=1, source_target_pairs={{0,4},{4,0},{8,12},{12,8},{1,5},{5,1},{9,13},{13,9},{2,6},{6,2},{1... | collective-permute-start | bytes 442376 | tf_op jit(solution)/shard_map/ppermute | solution.py:189
  15.0 0.0 collective-permute-done.v_ref
  15.0 0.0 copy-start
  15.0 0.0 copy-start.1
  15.0 3.8 %shard_map.56.refs_1_ = bf16[512,512]{1,0:T(8,128)(2,1)S(1)} custom-call(bf16[4,512,1024]{2,1,0:T(8,128)(2,1)S(1)} %get-tuple-element.22.x_ref, bf16[4096,512]{1,0:T(8,128)(2,1)} %collective-permute-done.v_ref), custom_call_target="tpu_custom_call" | custom-call | flops 2147483648 | bytes 8388608 | tf_op jit(solution)/shard_map/pallas_call | solution.py:21
  18.8 0.1 collective-permute-start.11
  18.9 0.0 collective-permute-done.4.refs_1_
  18.9 1.7 %collective-permute-start.2 = (bf16[512,512]{1,0:T(8,128)(2,1)S(1)}, bf16[512,512]{1,0:T(8,128)(2,1)S(1)}, u32[]{:S(2)}, u32[]{:S(2)}) collective-permute-start(bf16[512,512]{1,0:T(8,128)(2,1)S(1)} %shard_map.56.refs_1_), channel_id=1, source_target_pairs={{0,2},{1,0},{2,3},{3,1},{4,6},{5,4},{6,7},{7,5},{8,10},{9,8},{10,1... | collective-permute-start | bytes 1572872 | tf_op jit(solution)/shard_map/ppermute | solution.py:253
  20.6 0.3 collective-permute-done.6.refs_3_
  21.0 1.5 %collective-permute-start.8 = (bf16[16,4608]{1,0:T(8,128)(2,1)S(1)}, bf16[16,4608]{1,0:T(8,128)(2,1)S(1)}, u32[]{:S(2)}, u32[]{:S(2)}) collective-permute-start(bf16[16,4608]{1,0:T(8,128)(2,1)S(1)} %collective-permute-done.6.refs_3_), channel_id=1, source_target_pairs={{0,16},{16,0},{1,17},{17,1},{2,18},{18,2},{3,19},{19,3},{4,20},{20... | collective-permute-start | bytes 442376 | tf_op jit(solution)/shard_map/ppermute | solution.py:183
  22.5 0.0 collective-permute-done.10.refs_0_
  22.5 0.0 collective-permute-start.5
  22.5 2.4 %collective-permute-done.11.refs_1_ = bf16[16,4608]{1,0:T(8,128)(2,1)S(1)} collective-permute-done((bf16[16,4608]{1,0:T(8,128)(2,1)S(1)}, bf16[16,4608]{1,0:T(8,128)(2,1)S(1)}, u32[]{:S(2)}, u32[]{:S(2)}) %collective-permute-start.11) | collective-permute-done | bytes 147488 | tf_op jit(solution)/shard_map/ppermute | solution.py:189
  24.9 0.1 collective-permute-start.12
  25.0 1.8 %collective-permute-done.8.refs_5_ = bf16[16,4608]{1,0:T(8,128)(2,1)S(1)} collective-permute-done((bf16[16,4608]{1,0:T(8,128)(2,1)S(1)}, bf16[16,4608]{1,0:T(8,128)(2,1)S(1)}, u32[]{:S(2)}, u32[]{:S(2)}) %collective-permute-start.8) | collective-permute-done | bytes 147488 | tf_op jit(solution)/shard_map/ppermute | solution.py:183
  26.8 0.0 collective-permute-start.7
  26.8 0.0 collective-permute-done.1.refs_2_
  26.8 0.5 %collective-permute-start.9 = (bf16[16,4608]{1,0:T(8,128)(2,1)S(1)}, bf16[16,4608]{1,0:T(8,128)(2,1)S(1)}, u32[]{:S(2)}, u32[]{:S(2)}) collective-permute-start(bf16[16,4608]{1,0:T(8,128)(2,1)S(1)} %collective-permute-done.8.refs_5_), channel_id=1, source_target_pairs={{0,1},{1,0},{2,3},{3,2},{4,5},{5,4},{6,7},{7,6},{8,9},{9,8},{10,11... | collective-permute-start | bytes 442376 | tf_op jit(solution)/shard_map/ppermute | solution.py:183
  27.3 0.9 %collective-permute-done.7.refs_4_ = bf16[16,4608]{1,0:T(8,128)(2,1)S(1)} collective-permute-done((bf16[16,4608]{1,0:T(8,128)(2,1)S(1)}, bf16[16,4608]{1,0:T(8,128)(2,1)S(1)}, u32[]{:S(2)}, u32[]{:S(2)}) %collective-permute-start.7) | collective-permute-done | bytes 147488 | tf_op jit(solution)/shard_map/ppermute | solution.py:183
  28.2 0.0 collective-permute-done.5.refs_2_
  28.2 0.2 collective-permute-done.9.refs_6_
  28.4 0.0 collective-permute-done.12.refs_8_
  28.4 0.0 copy-done
  28.4 0.0 copy-done.1
  28.4 1.3 %shard_map.60 = (f32[64,512]{1,0:T(8,128)S(1)}, bf16[64,512]{1,0:T(8,128)(2,1)S(1)}, bf16[256,512]{1,0:T(8,128)(2,1)S(1)}) custom-call(s32[1,512]{1,0:T(1,128)S(1)} %xor_bitcast_fusion.slot_ref, bf16[4,512,1024]{2,1,0:T(8,128)(2,1)S(1)} %get-tuple-element.22.x_ref, bf16[64,512]{1,0:T(8,128)(2,1)S(1)} %bitcast.11, bf16[64,4096]{1,0:T(8,128)(2,1)S(1)} %bitcast.9, ...), custom_call_target="tpu_custom_call" | custom-call | flops 1073741824 | bytes 6555648 | tf_op jit(solution)/shard_map/pallas_call | solution.py:21
  29.7 0.6 %collective-permute-start.13 = (bf16[64,512]{1,0:T(8,128)(2,1)S(1)}, bf16[64,512]{1,0:T(8,128)(2,1)S(1)}, u32[]{:S(2)}, u32[]{:S(2)}) collective-permute-start(bf16[64,512]{1,0:T(8,128)(2,1)S(1)} %get-tuple-element.28), channel_id=1, source_target_pairs={{0,2},{2,0},{1,3},{3,1},{4,6},{6,4},{5,7},{7,5},{8,10},{10,8},{9,1... | collective-permute-start | bytes 196616 | tf_op jit(solution)/shard_map/ppermute | solution.py:183
  30.3 0.0 collective-permute-done.2.refs_3_
  30.3 0.9 %shard_map.57.base_ref = f32[512,512]{1,0:T(8,128)S(1)} custom-call(s32[4]{0:T(128)S(1)} %add_convert_fusion.flag_ref, bf16[512,512]{1,0:T(8,128)(2,1)S(1)} %get-tuple-element.20.refs_0_, bf16[512,512]{1,0:T(8,128)(2,1)S(1)} %shard_map.56.refs_1_, bf16[512,512]{1,0:T(8,128)(2,1)S(1)} %collective-permute-done.1.refs_2_, ...), custom_call_target="tpu_custom_call" | custom-call | flops 1048576 | bytes 2097168 | tf_op jit(solution)/shard_map/pallas_call | solution.py:21
  31.2 2.9 %collective-permute-done.13.refs_0_ = bf16[64,512]{1,0:T(8,128)(2,1)S(1)} collective-permute-done((bf16[64,512]{1,0:T(8,128)(2,1)S(1)}, bf16[64,512]{1,0:T(8,128)(2,1)S(1)}, u32[]{:S(2)}, u32[]{:S(2)}) %collective-permute-start.13) | collective-permute-done | bytes 65568 | tf_op jit(solution)/shard_map/ppermute | solution.py:183
  34.1 1.1 %shard_map.61 = bf16[512,512]{1,0:T(8,128)(2,1)} custom-call(s32[1,512]{1,0:T(1,128)S(1)} %xor_bitcast_fusion.slot_ref, f32[512,512]{1,0:T(8,128)S(1)} %shard_map.57.base_ref, bf16[256,512]{1,0:T(8,128)(2,1)S(1)} %get-tuple-element.26.up_ref, f32[64,512]{1,0:T(8,128)S(1)} %get-tuple-element.27.low_ref, bf16[64,512]{1,0:T(8,128)(2,1)S(1)} %collective-permute-done.13.refs_0_), custom_call_target="tpu_custom_call" | custom-call | flops 134217728 | bytes 1509376 | tf_op jit(solution)/shard_map/pallas_call | solution.py:21
  (2 shorter events, 0.0 us)
Async XLA Ops:
  0.0 15.0 %collective-permute-start = (bf16[4096,512]{1,0:T(8,128)(2,1)}, bf16[4096,512]{1,0:T(8,128)(2,1)}, u32[]{:S(2)}, u32[]{:S(2)}) collective-permute-start(bf16[4096,512]{1,0:T(8,128)(2,1)} %v_ref.1), channel_id=1, source_target_pairs={{0,1},{1,0},{2,3},{3,2},{4,5},{5,4},{6,7},{7,6},{8,9},{9,8},{10,11... | collective-permute-start | bytes 12582920 | tf_op jit(solution)/shard_map/ppermute | solution.py:183
  1.4 9.9 %collective-permute-start.3 = (bf16[16,4608]{1,0:T(8,128)(2,1)S(1)}, bf16[16,4608]{1,0:T(8,128)(2,1)S(1)}, u32[]{:S(2)}, u32[]{:S(2)}) collective-permute-start(bf16[16,4608]{1,0:T(8,128)(2,1)S(1)} %get-tuple-element.24), channel_id=1, source_target_pairs={{0,12},{4,8},{8,4},{12,0},{1,13},{5,9},{9,5},{13,1},{2,14},{6,10},... | collective-permute-start | bytes 442376 | tf_op jit(solution)/shard_map/ppermute | solution.py:189
  11.1 15.8 %collective-permute-start.1 = (bf16[512,512]{1,0:T(8,128)(2,1)S(1)}, bf16[512,512]{1,0:T(8,128)(2,1)S(1)}, u32[]{:S(2)}, u32[]{:S(2)}) collective-permute-start(bf16[512,512]{1,0:T(8,128)(2,1)S(1)} %get-tuple-element.20.refs_0_), channel_id=1, source_target_pairs={{0,1},{1,3},{2,0},{3,2},{4,5},{5,7},{6,4},{7,6},{8,9},{9,11},{10,8... | collective-permute-start | bytes 1572872 | tf_op jit(solution)/shard_map/ppermute | solution.py:253
  11.3 11.2 %collective-permute-start.10 = (bf16[16,4608]{1,0:T(8,128)(2,1)S(1)}, bf16[16,4608]{1,0:T(8,128)(2,1)S(1)}, u32[]{:S(2)}, u32[]{:S(2)}) collective-permute-start(bf16[16,4608]{1,0:T(8,128)(2,1)S(1)} %get-tuple-element.24), channel_id=1, source_target_pairs={{0,4},{4,0},{8,12},{12,8},{1,5},{5,1},{9,13},{13,9},{2,6},{6,2},{1... | collective-permute-start | bytes 442376 | tf_op jit(solution)/shard_map/ppermute | solution.py:189
  11.3 7.6 %collective-permute-start.4 = (bf16[16,4608]{1,0:T(8,128)(2,1)S(1)}, bf16[16,4608]{1,0:T(8,128)(2,1)S(1)}, u32[]{:S(2)}, u32[]{:S(2)}) collective-permute-start(bf16[16,4608]{1,0:T(8,128)(2,1)S(1)} %collective-permute-done.3.refs_0_), channel_id=1, source_target_pairs={{0,16},{16,0},{1,17},{17,1},{2,18},{18,2},{3,19},{19,3},{4,20},{20... | collective-permute-start | bytes 442376 | tf_op jit(solution)/shard_map/ppermute | solution.py:183
  12.8 8.1 %collective-permute-start.6 = (bf16[16,4608]{1,0:T(8,128)(2,1)S(1)}, bf16[16,4608]{1,0:T(8,128)(2,1)S(1)}, u32[]{:S(2)}, u32[]{:S(2)}) collective-permute-start(bf16[16,4608]{1,0:T(8,128)(2,1)S(1)} %collective-permute-done.3.refs_0_), channel_id=1, source_target_pairs={{0,4},{4,0},{8,12},{12,8},{1,5},{5,1},{9,13},{13,9},{2,6},{6,2},{1... | collective-permute-start | bytes 442376 | tf_op jit(solution)/shard_map/ppermute | solution.py:189
  15.0 13.4 %copy-start = (bf16[1,4096,64]{1,2,0:T(8,128)(2,1)S(1)}, bf16[1,4096,64]{1,2,0:T(8,128)(2,1)}, u32[]{:S(2)}) copy-start(bf16[1,4096,64]{1,2,0:T(8,128)(2,1)} %param.7) | copy-start | bytes 1572868
  15.0 13.4 %copy-start.1 = (bf16[1,64,512]{2,1,0:T(8,128)(2,1)S(1)}, bf16[1,64,512]{2,1,0:T(8,128)(2,1)}, u32[]{:S(2)}) copy-start(bf16[1,64,512]{2,1,0:T(8,128)(2,1)} %param.8) | copy-start | bytes 196612
  18.8 6.0 %collective-permute-start.11 = (bf16[16,4608]{1,0:T(8,128)(2,1)S(1)}, bf16[16,4608]{1,0:T(8,128)(2,1)S(1)}, u32[]{:S(2)}, u32[]{:S(2)}) collective-permute-start(bf16[16,4608]{1,0:T(8,128)(2,1)S(1)} %get-tuple-element.25), channel_id=1, source_target_pairs={{0,4},{4,0},{8,12},{12,8},{1,5},{5,1},{9,13},{13,9},{2,6},{6,2},{1... | collective-permute-start | bytes 442376 | tf_op jit(solution)/shard_map/ppermute | solution.py:189
  18.9 11.3 %collective-permute-start.2 = (bf16[512,512]{1,0:T(8,128)(2,1)S(1)}, bf16[512,512]{1,0:T(8,128)(2,1)S(1)}, u32[]{:S(2)}, u32[]{:S(2)}) collective-permute-start(bf16[512,512]{1,0:T(8,128)(2,1)S(1)} %shard_map.56.refs_1_), channel_id=1, source_target_pairs={{0,2},{1,0},{2,3},{3,1},{4,6},{5,4},{6,7},{7,5},{8,10},{9,8},{10,1... | collective-permute-start | bytes 1572872 | tf_op jit(solution)/shard_map/ppermute | solution.py:253
  21.0 5.9 %collective-permute-start.8 = (bf16[16,4608]{1,0:T(8,128)(2,1)S(1)}, bf16[16,4608]{1,0:T(8,128)(2,1)S(1)}, u32[]{:S(2)}, u32[]{:S(2)}) collective-permute-start(bf16[16,4608]{1,0:T(8,128)(2,1)S(1)} %collective-permute-done.6.refs_3_), channel_id=1, source_target_pairs={{0,16},{16,0},{1,17},{17,1},{2,18},{18,2},{3,19},{19,3},{4,20},{20... | collective-permute-start | bytes 442376 | tf_op jit(solution)/shard_map/ppermute | solution.py:183
  22.5 5.7 %collective-permute-start.5 = (bf16[32,4608]{1,0:T(8,128)(2,1)S(1)}, bf16[32,4608]{1,0:T(8,128)(2,1)S(1)}, u32[]{:S(2)}, u32[]{:S(2)}) collective-permute-start(bf16[32,4608]{1,0:T(8,128)(2,1)S(1)} %shard_map.58.refs_1_), channel_id=1, source_target_pairs={{0,1},{1,0},{2,3},{3,2},{4,5},{5,4},{6,7},{7,6},{8,9},{9,8},{10,11... | collective-permute-start | bytes 884744 | tf_op jit(solution)/shard_map/ppermute | solution.py:183
  24.9 3.5 %collective-permute-start.12 = (bf16[32,4608]{1,0:T(8,128)(2,1)S(1)}, bf16[32,4608]{1,0:T(8,128)(2,1)S(1)}, u32[]{:S(2)}, u32[]{:S(2)}) collective-permute-start(bf16[32,4608]{1,0:T(8,128)(2,1)S(1)} %shard_map.59.refs_7_), channel_id=1, source_target_pairs={{0,1},{1,0},{2,3},{3,2},{4,5},{5,4},{6,7},{7,6},{8,9},{9,8},{10,11... | collective-permute-start | bytes 884744 | tf_op jit(solution)/shard_map/ppermute | solution.py:183
  26.8 1.4 %collective-permute-start.7 = (bf16[16,4608]{1,0:T(8,128)(2,1)S(1)}, bf16[16,4608]{1,0:T(8,128)(2,1)S(1)}, u32[]{:S(2)}, u32[]{:S(2)}) collective-permute-start(bf16[16,4608]{1,0:T(8,128)(2,1)S(1)} %collective-permute-done.6.refs_3_), channel_id=1, source_target_pairs={{0,1},{1,0},{2,3},{3,2},{4,5},{5,4},{6,7},{7,6},{8,9},{9,8},{10,11... | collective-permute-start | bytes 442376 | tf_op jit(solution)/shard_map/ppermute | solution.py:183
  26.8 1.6 %collective-permute-start.9 = (bf16[16,4608]{1,0:T(8,128)(2,1)S(1)}, bf16[16,4608]{1,0:T(8,128)(2,1)S(1)}, u32[]{:S(2)}, u32[]{:S(2)}) collective-permute-start(bf16[16,4608]{1,0:T(8,128)(2,1)S(1)} %collective-permute-done.8.refs_5_), channel_id=1, source_target_pairs={{0,1},{1,0},{2,3},{3,2},{4,5},{5,4},{6,7},{7,6},{8,9},{9,8},{10,11... | collective-permute-start | bytes 442376 | tf_op jit(solution)/shard_map/ppermute | solution.py:183
  29.7 4.4 %collective-permute-start.13 = (bf16[64,512]{1,0:T(8,128)(2,1)S(1)}, bf16[64,512]{1,0:T(8,128)(2,1)S(1)}, u32[]{:S(2)}, u32[]{:S(2)}) collective-permute-start(bf16[64,512]{1,0:T(8,128)(2,1)S(1)} %get-tuple-element.28), channel_id=1, source_target_pairs={{0,2},{2,0},{1,3},{3,1},{4,6},{6,4},{5,7},{7,5},{8,10},{10,8},{9,1... | collective-permute-start | bytes 196616 | tf_op jit(solution)/shard_map/ppermute | solution.py:183

commit v12 on v11

--- a/solution.py
+++ b/solution.py
@@ -120,12 +120,13 @@
         row += rows
 
 
-def down_kernel(layout, slots, slot_ref, x_ref, own_ref, *refs):
+def down_kernel(layout, slots, idx_ref, own_idx_ref, x_ref, own_ref, *refs):
     parts, (low_ref, sent_ref, up_ref, scratch) = refs[:-4], refs[-4:]
     rank, size, cols = low_ref.shape[0], x_ref.shape[2], own_ref.shape[1]
     up_ref[:rank, :] = own_ref[...]
     pieces = [p for pieces in layout[1:] for p in pieces]
     fill(up_ref.at[rank:], parts, pieces, slice(CHUNKS * size, CHUNKS * size + cols))
+    slot = idx_ref[...] ^ own_idx_ref[...]
     low = jnp.zeros(low_ref.shape, F32)
     for first in range(0, len(layout), BATCH):
         group = layout[first : first + BATCH]
@@ -140,7 +141,7 @@
                 preferred_element_type=F32,
             )
         for k in range(len(group)):
-            match = slot_ref[...] == slots[first + k]
+            match = slot == slots[first + k]
             low = low + jnp.where(match, prod[k * rank : (k + 1) * rank, :], 0.0)
     low_ref[...] = low
     sent_ref[...] = low.astype(BF16)
@@ -154,15 +155,16 @@
     out_ref[...] = total
 
 
-def last_kernel(slots, slot_ref, base_ref, up_ref, low_ref, *refs):
+def last_kernel(slots, idx_ref, own_idx_ref, base_ref, up_ref, low_ref, *refs):
     others, (out_ref, spread) = refs[:-2], refs[-2:]
     rank = low_ref.shape[0]
     low = low_ref[...]
     for other in others:
         low = low + other[...].astype(F32)
     low = low.astype(BF16).astype(F32)
+    slot = idx_ref[...] ^ own_idx_ref[...]
     for k in range(up_ref.shape[0] // rank):
-        match = slot_ref[...] == slots[k]
+        match = slot == slots[k]
         spread[k * rank : (k + 1) * rank, :] = jnp.where(match, low, 0.0).astype(BF16)
     lora = lax.dot_general(
         spread[...], up_ref[...], (((0,), (0,)), ((), ())), preferred_element_type=F32
@@ -218,7 +220,7 @@
         here = [((t >= n) & (t < n + per_half)).astype(jnp.int32) for n in halves]
         flags = jnp.stack(here + [f for f in here for _ in range(1, tensors)])
         slots = [0, *order]
-        slot = lax.bitwise_xor(row, jnp.broadcast_to(a, row.shape))
+        own_idx = jnp.broadcast_to(a, row.shape)
 
         held = [v] + others(v, "replica")
 
@@ -254,7 +256,7 @@
             return terms, cuts
 
         xs = None
-        x, flags, slot = lax.optimization_barrier((x, flags, slot, mine, *rest))[:3]
+        x, flags, own_idx = lax.optimization_barrier((x, flags, own_idx, mine, *rest))[:3]
         first, xs = base(0, [])
         for p, piece in zip(near, lax.optimization_barrier((*[pieces[p] for p in near], first))):
             pieces[p] = piece
@@ -287,12 +289,12 @@
             functools.partial(down_kernel, layout, slots),
             (jax.ShapeDtypeStruct((rank, tokens), F32), jax.ShapeDtypeStruct((rank, tokens), BF16),
                 jax.ShapeDtypeStruct((adapters * rank, cols), BF16)),
-            (slot, after(xs, *recvs[: tensors - 1]), u[0], *arrays),
+            (row, own_idx, after(xs, *recvs[: tensors - 1]), u[0], *arrays),
             scratch=[
                 pltpu.VMEM((CHUNKS, min(BATCH, adapters) * rank, wide // CHUNKS), BF16),
             ],
             flops=2 * x.size * rank * adapters,
-            specs=[VMEM] * (3 + len(arrays)),
+            specs=[VMEM] * (4 + len(arrays)),
         )
         lows = others(sent, "tensor")
         terms = blocks + recvs
@@ -306,10 +308,10 @@
         return call(
             functools.partial(last_kernel, slots),
             jax.ShapeDtypeStruct((tokens, cols), BF16),
-            (slot, total, every, low, *lows),
+            (row, own_idx, total, every, low, *lows),
             scratch=[pltpu.VMEM((adapters * rank, tokens), BF16)],
             flops=2 * tokens * rank * adapters * cols,
-            specs=[VMEM] * (4 + len(lows)),
+            specs=[VMEM] * (5 + len(lows)),
         )
 
     return shards

time: 35.4 us -> 34.7 us (0.980)
  other arithmetic: 1.75 us -> 1.07 us
    xor x1 -> x0, other arithmetic: 0.69 us -> none  [shards(): slot = lax.bitwise_xor(row, jnp.broadcast_to(a, row.shape))]
    ppermute x4, starting transfers between devices: 6.92 us -> 7.52 us  [flip(): return lax.ppermute(x, 'adapter', [(i, i ^ bits) for i in range(adapters)])]
    ppermute x8, starting transfers between devices: 4.64 us -> 4.26 us  [shift(): return lax.ppermute(x, axis, [(i, (i + by) % size) for i in range(size)])]
  transfers between devices with their start and end apart: 14 -> 14, of which waited for: 6 -> 6; matrix products, arithmetic and copies ran while one was open for 5% -> 3% of each run, Pallas kernels for 29% -> 30%
where the time goes in v12:
time: 34.7 us; the launch traced here: 34.5 us
  starting transfers between devices  13.5 us (39%)
  Pallas kernels  11.4 us (33%)
  waiting for transfers between devices  8.46 us (24%)
  other arithmetic  1.07 us (3%)
    pallas_call x7, Pallas kernels, call(): pl.pallas_call(kernel, out_shape=outs, in_specs=specs or [VMEM] * len(arg...  11.4 us
    ppermute x4, starting transfers between devices, flip(): return lax.ppermute(x, 'adapter', [(i, i ^ bits) for i in range(adapters)])  7.52 us
    ppermute x8, waiting for transfers between devices, shift(): return lax.ppermute(x, axis, [(i, (i + by) % size) for i in range(size)])  5.96 us
    ppermute x8, starting transfers between devices, shift(): return lax.ppermute(x, axis, [(i, (i + by) % size) for i in range(size)])  4.26 us
    ppermute x4, waiting for transfers between devices, flip(): return lax.ppermute(x, 'adapter', [(i, i ^ bits) for i in range(adapters)])  2.5 us
    ppermute x2, starting transfers between devices, base(): recvs.append(lax.ppermute(block, ('tensor', 'replica'), base_pairs(h, by)))  1.75 us
    concatenate x1, other arithmetic, shards(): own = jnp.concatenate([down, u[0]], axis=1)  0.99 us
  transfers between devices with their start and end apart: 14, of which 6 were waited for; matrix products, arithmetic and copies ran while one was open for 3% of the time, Pallas kernels for 30%

profile of v12, /device:TPU:0, one launch (start us, length us, event | category | flops | bytes accessed | tf_op | source)
XLA Modules:
  0.0 34.5 jit_solution(7763445111421093134)
XLA Ops:
  0.0 0.5 %collective-permute-start = (bf16[4096,512]{1,0:T(8,128)(2,1)}, bf16[4096,512]{1,0:T(8,128)(2,1)}, u32[]{:S(2)}, u32[]{:S(2)}) collective-permute-start(bf16[4096,512]{1,0:T(8,128)(2,1)} %v_ref.1), channel_id=1, source_target_pairs={{0,1},{1,0},{2,3},{3,2},{4,5},{5,4},{6,7},{7,6},{8,9},{9,8},{10,11... | collective-permute-start | bytes 12582920 | tf_op jit(solution)/shard_map/ppermute | solution.py:185
  0.5 1.0 %fusion = (bf16[16,4608]{1,0:T(8,128)(2,1)S(1)}, bf16[16,4608]{1,0:T(8,128)(2,1)S(1)}) fusion(s32[]{:T(128)S(6)} %select_n.7, bf16[64,4096]{1,0:T(8,128)(2,1)} %bitcast.7, bf16[64,512]{1,0:T(8,128)(2,1)} %bitcast.9, s32[]{:T(128)S(6)} %select_n.6), kind=kLoop, calls=%fused_computation.4 | loop fusion | flops 589824 | bytes 884744 | tf_op jit(solution)/shard_map/concatenate | solution.py:229
  1.4 4.7 %collective-permute-start.3 = (bf16[16,4608]{1,0:T(8,128)(2,1)S(1)}, bf16[16,4608]{1,0:T(8,128)(2,1)S(1)}, u32[]{:S(2)}, u32[]{:S(2)}) collective-permute-start(bf16[16,4608]{1,0:T(8,128)(2,1)S(1)} %get-tuple-element.24), channel_id=1, source_target_pairs={{0,12},{4,8},{8,4},{12,0},{1,13},{5,9},{9,5},{13,1},{2,14},{6,10},... | collective-permute-start | bytes 442376 | tf_op jit(solution)/shard_map/ppermute | solution.py:191
  6.1 0.1 add_convert_fusion.flag_ref
  6.2 4.2 %shard_map.55 = (bf16[512,512]{1,0:T(8,128)(2,1)S(1)}, bf16[4,512,1024]{2,1,0:T(8,128)(2,1)S(1)}) custom-call(bf16[512,4096]{1,0:T(8,128)(2,1)} %x_ref, bf16[4096,512]{1,0:T(8,128)(2,1)} %v_ref.1), custom_call_target="tpu_custom_call" | custom-call | flops 2147483648 | bytes 8388608 | tf_op jit(solution)/shard_map/pallas_call | solution.py:21
  10.4 0.2 collective-permute-start.1
  10.6 0.0 collective-permute-start.10
  10.6 0.1 collective-permute-done.3.refs_0_
  10.7 1.5 %collective-permute-start.4 = (bf16[16,4608]{1,0:T(8,128)(2,1)S(1)}, bf16[16,4608]{1,0:T(8,128)(2,1)S(1)}, u32[]{:S(2)}, u32[]{:S(2)}) collective-permute-start(bf16[16,4608]{1,0:T(8,128)(2,1)S(1)} %collective-permute-done.3.refs_0_), channel_id=1, source_target_pairs={{0,16},{16,0},{1,17},{17,1},{2,18},{18,2},{3,19},{19,3},{4,20},{20... | collective-permute-start | bytes 442376 | tf_op jit(solution)/shard_map/ppermute | solution.py:185
  12.3 2.8 %collective-permute-start.6 = (bf16[16,4608]{1,0:T(8,128)(2,1)S(1)}, bf16[16,4608]{1,0:T(8,128)(2,1)S(1)}, u32[]{:S(2)}, u32[]{:S(2)}) collective-permute-start(bf16[16,4608]{1,0:T(8,128)(2,1)S(1)} %collective-permute-done.3.refs_0_), channel_id=1, source_target_pairs={{0,4},{4,0},{8,12},{12,8},{1,5},{5,1},{9,13},{13,9},{2,6},{6,2},{1... | collective-permute-start | bytes 442376 | tf_op jit(solution)/shard_map/ppermute | solution.py:191
  15.0 0.0 collective-permute-done.v_ref
  15.0 0.0 copy-start
  15.0 0.0 copy-start.1
  15.0 0.0 copy-start.2
  15.0 3.8 %shard_map.56.refs_1_ = bf16[512,512]{1,0:T(8,128)(2,1)S(1)} custom-call(bf16[4,512,1024]{2,1,0:T(8,128)(2,1)S(1)} %get-tuple-element.22.x_ref, bf16[4096,512]{1,0:T(8,128)(2,1)} %collective-permute-done.v_ref), custom_call_target="tpu_custom_call" | custom-call | flops 2147483648 | bytes 8388608 | tf_op jit(solution)/shard_map/pallas_call | solution.py:21
  18.9 0.1 collective-permute-start.11
  18.9 0.0 collective-permute-done.4.refs_1_
  18.9 1.5 %collective-permute-start.2 = (bf16[512,512]{1,0:T(8,128)(2,1)S(1)}, bf16[512,512]{1,0:T(8,128)(2,1)S(1)}, u32[]{:S(2)}, u32[]{:S(2)}) collective-permute-start(bf16[512,512]{1,0:T(8,128)(2,1)S(1)} %shard_map.56.refs_1_), channel_id=1, source_target_pairs={{0,2},{1,0},{2,3},{3,1},{4,6},{5,4},{6,7},{7,5},{8,10},{9,8},{10,1... | collective-permute-start | bytes 1572872 | tf_op jit(solution)/shard_map/ppermute | solution.py:255
  20.5 0.0 collective-permute-done.6.refs_3_
  20.5 1.3 %collective-permute-start.8 = (bf16[16,4608]{1,0:T(8,128)(2,1)S(1)}, bf16[16,4608]{1,0:T(8,128)(2,1)S(1)}, u32[]{:S(2)}, u32[]{:S(2)}) collective-permute-start(bf16[16,4608]{1,0:T(8,128)(2,1)S(1)} %collective-permute-done.6.refs_3_), channel_id=1, source_target_pairs={{0,16},{16,0},{1,17},{17,1},{2,18},{18,2},{3,19},{19,3},{4,20},{20... | collective-permute-start | bytes 442376 | tf_op jit(solution)/shard_map/ppermute | solution.py:185
  21.8 0.0 collective-permute-done.10.refs_0_
  21.8 0.0 collective-permute-start.5
  21.8 2.4 %collective-permute-done.11.refs_1_ = bf16[16,4608]{1,0:T(8,128)(2,1)S(1)} collective-permute-done((bf16[16,4608]{1,0:T(8,128)(2,1)S(1)}, bf16[16,4608]{1,0:T(8,128)(2,1)S(1)}, u32[]{:S(2)}, u32[]{:S(2)}) %collective-permute-start.11) | collective-permute-done | bytes 147488 | tf_op jit(solution)/shard_map/ppermute | solution.py:191
  24.2 0.1 collective-permute-start.12
  24.3 1.8 %collective-permute-done.8.refs_5_ = bf16[16,4608]{1,0:T(8,128)(2,1)S(1)} collective-permute-done((bf16[16,4608]{1,0:T(8,128)(2,1)S(1)}, bf16[16,4608]{1,0:T(8,128)(2,1)S(1)}, u32[]{:S(2)}, u32[]{:S(2)}) %collective-permute-start.8) | collective-permute-done | bytes 147488 | tf_op jit(solution)/shard_map/ppermute | solution.py:185
  26.1 0.0 collective-permute-start.7
  26.1 0.0 collective-permute-done.1.refs_2_
  26.2 0.5 %collective-permute-start.9 = (bf16[16,4608]{1,0:T(8,128)(2,1)S(1)}, bf16[16,4608]{1,0:T(8,128)(2,1)S(1)}, u32[]{:S(2)}, u32[]{:S(2)}) collective-permute-start(bf16[16,4608]{1,0:T(8,128)(2,1)S(1)} %collective-permute-done.8.refs_5_), channel_id=1, source_target_pairs={{0,1},{1,0},{2,3},{3,2},{4,5},{5,4},{6,7},{7,6},{8,9},{9,8},{10,11... | collective-permute-start | bytes 442376 | tf_op jit(solution)/shard_map/ppermute | solution.py:185
  26.7 0.9 %collective-permute-done.7.refs_4_ = bf16[16,4608]{1,0:T(8,128)(2,1)S(1)} collective-permute-done((bf16[16,4608]{1,0:T(8,128)(2,1)S(1)}, bf16[16,4608]{1,0:T(8,128)(2,1)S(1)}, u32[]{:S(2)}, u32[]{:S(2)}) %collective-permute-start.7) | collective-permute-done | bytes 147488 | tf_op jit(solution)/shard_map/ppermute | solution.py:185
  27.5 0.0 collective-permute-done.5.refs_2_
  27.5 0.2 collective-permute-done.9.refs_6_
  27.7 0.0 collective-permute-done.12.refs_8_
  27.7 0.0 copy-done
  27.7 0.0 copy-done.1
  27.7 0.0 copy-done.2
  27.7 1.3 %shard_map.60 = (f32[64,512]{1,0:T(8,128)S(1)}, bf16[64,512]{1,0:T(8,128)(2,1)S(1)}, bf16[256,512]{1,0:T(8,128)(2,1)S(1)}) custom-call(s32[1,512]{1,0:T(1,128)S(1)} %bitcast.11, s32[1,512]{1,0:T(1,128)S(1)} %broadcast_in_dim.3.own_idx_ref, bf16[4,512,1024]{2,1,0:T(8,128)(2,1)S(1)} %get-tuple-element.22.x_ref, bf16[64,512]{1,0:T(8,128)(2,1)S(1)} %bitcast.10, ...), custom_call_target="tpu_custom_call" | custom-call | flops 1073741824 | bytes 6557696 | tf_op jit(solution)/shard_map/pallas_call | solution.py:21
  29.0 0.4 %collective-permute-start.13 = (bf16[64,512]{1,0:T(8,128)(2,1)S(1)}, bf16[64,512]{1,0:T(8,128)(2,1)S(1)}, u32[]{:S(2)}, u32[]{:S(2)}) collective-permute-start(bf16[64,512]{1,0:T(8,128)(2,1)S(1)} %get-tuple-element.28), channel_id=1, source_target_pairs={{0,2},{2,0},{1,3},{3,1},{4,6},{6,4},{5,7},{7,5},{8,10},{10,8},{9,1... | collective-permute-start | bytes 196616 | tf_op jit(solution)/shard_map/ppermute | solution.py:185
  29.4 0.0 collective-permute-done.2.refs_3_
  29.4 0.9 %shard_map.57.base_ref = f32[512,512]{1,0:T(8,128)S(1)} custom-call(s32[4]{0:T(128)S(1)} %add_convert_fusion.flag_ref, bf16[512,512]{1,0:T(8,128)(2,1)S(1)} %get-tuple-element.20.refs_0_, bf16[512,512]{1,0:T(8,128)(2,1)S(1)} %shard_map.56.refs_1_, bf16[512,512]{1,0:T(8,128)(2,1)S(1)} %collective-permute-done.1.refs_2_, ...), custom_call_target="tpu_custom_call" | custom-call | flops 1048576 | bytes 2097168 | tf_op jit(solution)/shard_map/pallas_call | solution.py:21
  30.4 3.0 %collective-permute-done.13.refs_0_ = bf16[64,512]{1,0:T(8,128)(2,1)S(1)} collective-permute-done((bf16[64,512]{1,0:T(8,128)(2,1)S(1)}, bf16[64,512]{1,0:T(8,128)(2,1)S(1)}, u32[]{:S(2)}, u32[]{:S(2)}) %collective-permute-start.13) | collective-permute-done | bytes 65568 | tf_op jit(solution)/shard_map/ppermute | solution.py:185
  33.4 1.1 %shard_map.61 = bf16[512,512]{1,0:T(8,128)(2,1)} custom-call(s32[1,512]{1,0:T(1,128)S(1)} %bitcast.12, s32[1,512]{1,0:T(1,128)S(1)} %broadcast_in_dim.3.own_idx_ref, f32[512,512]{1,0:T(8,128)S(1)} %shard_map.57.base_ref, bf16[256,512]{1,0:T(8,128)(2,1)S(1)} %get-tuple-element.26.up_ref, f32[64,512]{1,0:T(8,128)S(1)} %get-tuple-element.27.low_ref, ...), custom_call_target="tpu_custom_call" | custom-call | flops 134217728 | bytes 1511424 | tf_op jit(solution)/shard_map/pallas_call | solution.py:21
  (3 shorter events, 0.0 us)
Async XLA Ops:
  0.0 15.0 %collective-permute-start = (bf16[4096,512]{1,0:T(8,128)(2,1)}, bf16[4096,512]{1,0:T(8,128)(2,1)}, u32[]{:S(2)}, u32[]{:S(2)}) collective-permute-start(bf16[4096,512]{1,0:T(8,128)(2,1)} %v_ref.1), channel_id=1, source_target_pairs={{0,1},{1,0},{2,3},{3,2},{4,5},{5,4},{6,7},{7,6},{8,9},{9,8},{10,11... | collective-permute-start | bytes 12582920 | tf_op jit(solution)/shard_map/ppermute | solution.py:185
  1.4 9.3 %collective-permute-start.3 = (bf16[16,4608]{1,0:T(8,128)(2,1)S(1)}, bf16[16,4608]{1,0:T(8,128)(2,1)S(1)}, u32[]{:S(2)}, u32[]{:S(2)}) collective-permute-start(bf16[16,4608]{1,0:T(8,128)(2,1)S(1)} %get-tuple-element.24), channel_id=1, source_target_pairs={{0,12},{4,8},{8,4},{12,0},{1,13},{5,9},{9,5},{13,1},{2,14},{6,10},... | collective-permute-start | bytes 442376 | tf_op jit(solution)/shard_map/ppermute | solution.py:191
  10.4 15.8 %collective-permute-start.1 = (bf16[512,512]{1,0:T(8,128)(2,1)S(1)}, bf16[512,512]{1,0:T(8,128)(2,1)S(1)}, u32[]{:S(2)}, u32[]{:S(2)}) collective-permute-start(bf16[512,512]{1,0:T(8,128)(2,1)S(1)} %get-tuple-element.20.refs_0_), channel_id=1, source_target_pairs={{0,1},{1,3},{2,0},{3,2},{4,5},{5,7},{6,4},{7,6},{8,9},{9,11},{10,8... | collective-permute-start | bytes 1572872 | tf_op jit(solution)/shard_map/ppermute | solution.py:255
  10.6 11.2 %collective-permute-start.10 = (bf16[16,4608]{1,0:T(8,128)(2,1)S(1)}, bf16[16,4608]{1,0:T(8,128)(2,1)S(1)}, u32[]{:S(2)}, u32[]{:S(2)}) collective-permute-start(bf16[16,4608]{1,0:T(8,128)(2,1)S(1)} %get-tuple-element.24), channel_id=1, source_target_pairs={{0,4},{4,0},{8,12},{12,8},{1,5},{5,1},{9,13},{13,9},{2,6},{6,2},{1... | collective-permute-start | bytes 442376 | tf_op jit(solution)/shard_map/ppermute | solution.py:191
  10.7 8.2 %collective-permute-start.4 = (bf16[16,4608]{1,0:T(8,128)(2,1)S(1)}, bf16[16,4608]{1,0:T(8,128)(2,1)S(1)}, u32[]{:S(2)}, u32[]{:S(2)}) collective-permute-start(bf16[16,4608]{1,0:T(8,128)(2,1)S(1)} %collective-permute-done.3.refs_0_), channel_id=1, source_target_pairs={{0,16},{16,0},{1,17},{17,1},{2,18},{18,2},{3,19},{19,3},{4,20},{20... | collective-permute-start | bytes 442376 | tf_op jit(solution)/shard_map/ppermute | solution.py:185
  12.3 8.2 %collective-permute-start.6 = (bf16[16,4608]{1,0:T(8,128)(2,1)S(1)}, bf16[16,4608]{1,0:T(8,128)(2,1)S(1)}, u32[]{:S(2)}, u32[]{:S(2)}) collective-permute-start(bf16[16,4608]{1,0:T(8,128)(2,1)S(1)} %collective-permute-done.3.refs_0_), channel_id=1, source_target_pairs={{0,4},{4,0},{8,12},{12,8},{1,5},{5,1},{9,13},{13,9},{2,6},{6,2},{1... | collective-permute-start | bytes 442376 | tf_op jit(solution)/shard_map/ppermute | solution.py:191
  15.0 12.7 %copy-start = (bf16[1,4096,64]{1,2,0:T(8,128)(2,1)S(1)}, bf16[1,4096,64]{1,2,0:T(8,128)(2,1)}, u32[]{:S(2)}) copy-start(bf16[1,4096,64]{1,2,0:T(8,128)(2,1)} %param.7) | copy-start | bytes 1572868
  15.0 12.7 %copy-start.1 = (bf16[1,64,512]{2,1,0:T(8,128)(2,1)S(1)}, bf16[1,64,512]{2,1,0:T(8,128)(2,1)}, u32[]{:S(2)}) copy-start(bf16[1,64,512]{2,1,0:T(8,128)(2,1)} %param.8) | copy-start | bytes 196612
  15.0 12.7 %copy-start.2 = (s32[512,1]{0,1:T(1,128)S(1)}, s32[512,1]{0,1:T(1,128)}, u32[]{:S(2)}) copy-start(s32[512,1]{0,1:T(1,128)} %param.9) | copy-start | bytes 6148
  18.9 5.4 %collective-permute-start.11 = (bf16[16,4608]{1,0:T(8,128)(2,1)S(1)}, bf16[16,4608]{1,0:T(8,128)(2,1)S(1)}, u32[]{:S(2)}, u32[]{:S(2)}) collective-permute-start(bf16[16,4608]{1,0:T(8,128)(2,1)S(1)} %get-tuple-element.25), channel_id=1, source_target_pairs={{0,4},{4,0},{8,12},{12,8},{1,5},{5,1},{9,13},{13,9},{2,6},{6,2},{1... | collective-permute-start | bytes 442376 | tf_op jit(solution)/shard_map/ppermute | solution.py:191
  18.9 10.5 %collective-permute-start.2 = (bf16[512,512]{1,0:T(8,128)(2,1)S(1)}, bf16[512,512]{1,0:T(8,128)(2,1)S(1)}, u32[]{:S(2)}, u32[]{:S(2)}) collective-permute-start(bf16[512,512]{1,0:T(8,128)(2,1)S(1)} %shard_map.56.refs_1_), channel_id=1, source_target_pairs={{0,2},{1,0},{2,3},{3,1},{4,6},{5,4},{6,7},{7,5},{8,10},{9,8},{10,1... | collective-permute-start | bytes 1572872 | tf_op jit(solution)/shard_map/ppermute | solution.py:255
  20.5 5.7 %collective-permute-start.8 = (bf16[16,4608]{1,0:T(8,128)(2,1)S(1)}, bf16[16,4608]{1,0:T(8,128)(2,1)S(1)}, u32[]{:S(2)}, u32[]{:S(2)}) collective-permute-start(bf16[16,4608]{1,0:T(8,128)(2,1)S(1)} %collective-permute-done.6.refs_3_), channel_id=1, source_target_pairs={{0,16},{16,0},{1,17},{17,1},{2,18},{18,2},{3,19},{19,3},{4,20},{20... | collective-permute-start | bytes 442376 | tf_op jit(solution)/shard_map/ppermute | solution.py:185
  21.8 5.7 %collective-permute-start.5 = (bf16[32,4608]{1,0:T(8,128)(2,1)S(1)}, bf16[32,4608]{1,0:T(8,128)(2,1)S(1)}, u32[]{:S(2)}, u32[]{:S(2)}) collective-permute-start(bf16[32,4608]{1,0:T(8,128)(2,1)S(1)} %shard_map.58.refs_1_), channel_id=1, source_target_pairs={{0,1},{1,0},{2,3},{3,2},{4,5},{5,4},{6,7},{7,6},{8,9},{9,8},{10,11... | collective-permute-start | bytes 884744 | tf_op jit(solution)/shard_map/ppermute | solution.py:185
  24.2 3.5 %collective-permute-start.12 = (bf16[32,4608]{1,0:T(8,128)(2,1)S(1)}, bf16[32,4608]{1,0:T(8,128)(2,1)S(1)}, u32[]{:S(2)}, u32[]{:S(2)}) collective-permute-start(bf16[32,4608]{1,0:T(8,128)(2,1)S(1)} %shard_map.59.refs_7_), channel_id=1, source_target_pairs={{0,1},{1,0},{2,3},{3,2},{4,5},{5,4},{6,7},{7,6},{8,9},{9,8},{10,11... | collective-permute-start | bytes 884744 | tf_op jit(solution)/shard_map/ppermute | solution.py:185
  26.1 1.4 %collective-permute-start.7 = (bf16[16,4608]{1,0:T(8,128)(2,1)S(1)}, bf16[16,4608]{1,0:T(8,128)(2,1)S(1)}, u32[]{:S(2)}, u32[]{:S(2)}) collective-permute-start(bf16[16,4608]{1,0:T(8,128)(2,1)S(1)} %collective-permute-done.6.refs_3_), channel_id=1, source_target_pairs={{0,1},{1,0},{2,3},{3,2},{4,5},{5,4},{6,7},{7,6},{8,9},{9,8},{10,11... | collective-permute-start | bytes 442376 | tf_op jit(solution)/shard_map/ppermute | solution.py:185
  26.2 1.6 %collective-permute-start.9 = (bf16[16,4608]{1,0:T(8,128)(2,1)S(1)}, bf16[16,4608]{1,0:T(8,128)(2,1)S(1)}, u32[]{:S(2)}, u32[]{:S(2)}) collective-permute-start(bf16[16,4608]{1,0:T(8,128)(2,1)S(1)} %collective-permute-done.8.refs_5_), channel_id=1, source_target_pairs={{0,1},{1,0},{2,3},{3,2},{4,5},{5,4},{6,7},{7,6},{8,9},{9,8},{10,11... | collective-permute-start | bytes 442376 | tf_op jit(solution)/shard_map/ppermute | solution.py:185
  29.0 4.4 %collective-permute-start.13 = (bf16[64,512]{1,0:T(8,128)(2,1)S(1)}, bf16[64,512]{1,0:T(8,128)(2,1)S(1)}, u32[]{:S(2)}, u32[]{:S(2)}) collective-permute-start(bf16[64,512]{1,0:T(8,128)(2,1)S(1)} %get-tuple-element.28), channel_id=1, source_target_pairs={{0,2},{2,0},{1,3},{3,1},{4,6},{6,4},{5,7},{7,5},{8,10},{10,8},{9,1... | collective-permute-start | bytes 196616 | tf_op jit(solution)/shard_map/ppermute | solution.py:185

commit v13 on v12

--- a/solution.py
+++ b/solution.py
@@ -266,7 +266,7 @@
         beside = [flip(after(mine, first), 1)]
         second = first
         for h in range(1, replicas):
-            second, _ = base(h, [])
+            second, _ = base(h, [beside[0], *pieces.values()])
         beside += [flip(after(piece, second), 1) for piece in rest]
 
         arrays, layout = [down], [[(0, 0, rank)]] + [[] for _ in order]

time: 34.7 us -> 35.1 us (1.012)
  starting transfers between devices: 13.5 us -> 14.5 us
  waiting for transfers between devices: 8.46 us -> 7.92 us
    ppermute x8, starting transfers between devices: 4.26 us -> 5.66 us  [shift(): return lax.ppermute(x, axis, [(i, (i + by) % size) for i in range(size)])]
    ppermute x8, waiting for transfers between devices: 5.96 us -> 5.33 us  [shift(): return lax.ppermute(x, axis, [(i, (i + by) % size) for i in range(size)])]
    ppermute x2, starting transfers between devices: 1.75 us -> 1.29 us  [base(): recvs.append(lax.ppermute(block, ('tensor', 'replica'), base_pairs(h, by)))]
  transfers between devices with their start and end apart: 14 -> 14, of which waited for: 6 -> 7; matrix products, arithmetic and copies ran while one was open for 3% -> 3% of each run, Pallas kernels for 30% -> 29%
where the time goes in v13:
time: 35.1 us; the launch traced here: 34.9 us
  starting transfers between devices  14.5 us (41%)
  Pallas kernels  11.4 us (32%)
  waiting for transfers between devices  7.92 us (23%)
  other arithmetic  1.07 us (3%)
    pallas_call x7, Pallas kernels, call(): pl.pallas_call(kernel, out_shape=outs, in_specs=specs or [VMEM] * len(arg...  11.4 us
    ppermute x4, starting transfers between devices, flip(): return lax.ppermute(x, 'adapter', [(i, i ^ bits) for i in range(adapters)])  7.51 us
    ppermute x8, starting transfers between devices, shift(): return lax.ppermute(x, axis, [(i, (i + by) % size) for i in range(size)])  5.66 us
    ppermute x8, waiting for transfers between devices, shift(): return lax.ppermute(x, axis, [(i, (i + by) % size) for i in range(size)])  5.33 us
    ppermute x4, waiting for transfers between devices, flip(): return lax.ppermute(x, 'adapter', [(i, i ^ bits) for i in range(adapters)])  2.58 us
    ppermute x2, starting transfers between devices, base(): recvs.append(lax.ppermute(block, ('tensor', 'replica'), base_pairs(h, by)))  1.29 us
    concatenate x1, other arithmetic, shards(): own = jnp.concatenate([down, u[0]], axis=1)  0.99 us
  transfers between devices with their start and end apart: 14, of which 7 were waited for; matrix products, arithmetic and copies ran while one was open for 3% of the time, Pallas kernels for 29%

profile of v13, /device:TPU:0, one launch (start us, length us, event | category | flops | bytes accessed | tf_op | source)
XLA Modules:
  0.0 34.9 jit_solution(17025190532437853873)
XLA Ops:
  0.0 0.5 %collective-permute-start = (bf16[4096,512]{1,0:T(8,128)(2,1)}, bf16[4096,512]{1,0:T(8,128)(2,1)}, u32[]{:S(2)}, u32[]{:S(2)}) collective-permute-start(bf16[4096,512]{1,0:T(8,128)(2,1)} %v_ref.1), channel_id=1, source_target_pairs={{0,1},{1,0},{2,3},{3,2},{4,5},{5,4},{6,7},{7,6},{8,9},{9,8},{10,11... | collective-permute-start | bytes 12582920 | tf_op jit(solution)/shard_map/ppermute | solution.py:185
  0.5 1.0 %fusion = (bf16[16,4608]{1,0:T(8,128)(2,1)S(1)}, bf16[16,4608]{1,0:T(8,128)(2,1)S(1)}) fusion(s32[]{:T(128)S(6)} %select_n.7, bf16[64,4096]{1,0:T(8,128)(2,1)} %bitcast.7, bf16[64,512]{1,0:T(8,128)(2,1)} %bitcast.9, s32[]{:T(128)S(6)} %select_n.6), kind=kLoop, calls=%fused_computation.4 | loop fusion | flops 589824 | bytes 884744 | tf_op jit(solution)/shard_map/concatenate | solution.py:229
  1.4 4.7 %collective-permute-start.3 = (bf16[16,4608]{1,0:T(8,128)(2,1)S(1)}, bf16[16,4608]{1,0:T(8,128)(2,1)S(1)}, u32[]{:S(2)}, u32[]{:S(2)}) collective-permute-start(bf16[16,4608]{1,0:T(8,128)(2,1)S(1)} %get-tuple-element.23), channel_id=1, source_target_pairs={{0,12},{4,8},{8,4},{12,0},{1,13},{5,9},{9,5},{13,1},{2,14},{6,10},... | collective-permute-start | bytes 442376 | tf_op jit(solution)/shard_map/ppermute | solution.py:191
  6.1 0.1 add_convert_fusion.flag_ref
  6.2 4.2 %shard_map.55 = (bf16[512,512]{1,0:T(8,128)(2,1)S(1)}, bf16[4,512,1024]{2,1,0:T(8,128)(2,1)S(1)}) custom-call(bf16[512,4096]{1,0:T(8,128)(2,1)} %x_ref, bf16[4096,512]{1,0:T(8,128)(2,1)} %v_ref.1), custom_call_target="tpu_custom_call" | custom-call | flops 2147483648 | bytes 8388608 | tf_op jit(solution)/shard_map/pallas_call | solution.py:21
  10.4 0.2 collective-permute-start.1
  10.6 0.0 collective-permute-start.2
  10.6 0.1 collective-permute-done.3.refs_0_
  10.7 2.8 %collective-permute-start.4 = (bf16[16,4608]{1,0:T(8,128)(2,1)S(1)}, bf16[16,4608]{1,0:T(8,128)(2,1)S(1)}, u32[]{:S(2)}, u32[]{:S(2)}) collective-permute-start(bf16[16,4608]{1,0:T(8,128)(2,1)S(1)} %collective-permute-done.3.refs_0_), channel_id=1, source_target_pairs={{0,4},{4,0},{8,12},{12,8},{1,5},{5,1},{9,13},{13,9},{2,6},{6,2},{1... | collective-permute-start | bytes 442376 | tf_op jit(solution)/shard_map/ppermute | solution.py:191
  13.5 1.5 %collective-permute-start.6 = (bf16[16,4608]{1,0:T(8,128)(2,1)S(1)}, bf16[16,4608]{1,0:T(8,128)(2,1)S(1)}, u32[]{:S(2)}, u32[]{:S(2)}) collective-permute-start(bf16[16,4608]{1,0:T(8,128)(2,1)S(1)} %collective-permute-done.3.refs_0_), channel_id=1, source_target_pairs={{0,16},{16,0},{1,17},{17,1},{2,18},{18,2},{3,19},{19,3},{4,20},{20... | collective-permute-start | bytes 442376 | tf_op jit(solution)/shard_map/ppermute | solution.py:185
  15.0 0.0 collective-permute-done.v_ref
  15.0 0.0 copy-start
  15.0 0.0 copy-start.1
  15.0 0.0 copy-start.2
  15.0 3.8 %shard_map.56.refs_1_ = bf16[512,512]{1,0:T(8,128)(2,1)S(1)} custom-call(bf16[4,512,1024]{2,1,0:T(8,128)(2,1)S(1)} %get-tuple-element.26.x_ref, bf16[4096,512]{1,0:T(8,128)(2,1)} %collective-permute-done.v_ref), custom_call_target="tpu_custom_call" | custom-call | flops 2147483648 | bytes 8388608 | tf_op jit(solution)/shard_map/pallas_call | solution.py:21
  18.9 0.1 collective-permute-start.11
  18.9 0.0 collective-permute-done.2.refs_0_
  18.9 1.3 %collective-permute-done.4.refs_3_ = bf16[16,4608]{1,0:T(8,128)(2,1)S(1)} collective-permute-done((bf16[16,4608]{1,0:T(8,128)(2,1)S(1)}, bf16[16,4608]{1,0:T(8,128)(2,1)S(1)}, u32[]{:S(2)}, u32[]{:S(2)}) %collective-permute-start.4) | collective-permute-done | bytes 147488 | tf_op jit(solution)/shard_map/ppermute | solution.py:191
  20.3 1.1 %collective-permute-start.5 = (bf16[512,512]{1,0:T(8,128)(2,1)S(1)}, bf16[512,512]{1,0:T(8,128)(2,1)S(1)}, u32[]{:S(2)}, u32[]{:S(2)}) collective-permute-start(bf16[512,512]{1,0:T(8,128)(2,1)S(1)} %shard_map.56.refs_1_), channel_id=1, source_target_pairs={{0,2},{1,0},{2,3},{3,1},{4,6},{5,4},{6,7},{7,5},{8,10},{9,8},{10,1... | collective-permute-start | bytes 1572872 | tf_op jit(solution)/shard_map/ppermute | solution.py:255
  21.3 1.6 %collective-permute-start.9 = (bf16[16,4608]{1,0:T(8,128)(2,1)S(1)}, bf16[16,4608]{1,0:T(8,128)(2,1)S(1)}, u32[]{:S(2)}, u32[]{:S(2)}) collective-permute-start(bf16[16,4608]{1,0:T(8,128)(2,1)S(1)} %collective-permute-done.4.refs_3_), channel_id=1, source_target_pairs={{0,16},{16,0},{1,17},{17,1},{2,18},{18,2},{3,19},{19,3},{4,20},{20... | collective-permute-start | bytes 442376 | tf_op jit(solution)/shard_map/ppermute | solution.py:185
  22.9 0.0 collective-permute-done.6.refs_1_
  23.0 0.1 collective-permute-start.7
  23.1 1.2 %collective-permute-done.11.refs_1_ = bf16[16,4608]{1,0:T(8,128)(2,1)S(1)} collective-permute-done((bf16[16,4608]{1,0:T(8,128)(2,1)S(1)}, bf16[16,4608]{1,0:T(8,128)(2,1)S(1)}, u32[]{:S(2)}, u32[]{:S(2)}) %collective-permute-start.11) | collective-permute-done | bytes 147488 | tf_op jit(solution)/shard_map/ppermute | solution.py:191
  24.2 0.1 collective-permute-start.12
  24.3 2.2 %collective-permute-done.9.refs_5_ = bf16[16,4608]{1,0:T(8,128)(2,1)S(1)} collective-permute-done((bf16[16,4608]{1,0:T(8,128)(2,1)S(1)}, bf16[16,4608]{1,0:T(8,128)(2,1)S(1)}, u32[]{:S(2)}, u32[]{:S(2)}) %collective-permute-start.9) | collective-permute-done | bytes 147488 | tf_op jit(solution)/shard_map/ppermute | solution.py:185
  26.5 0.0 collective-permute-start.8
  26.5 0.0 collective-permute-done.1.refs_2_
  26.5 0.5 %collective-permute-start.10 = (bf16[16,4608]{1,0:T(8,128)(2,1)S(1)}, bf16[16,4608]{1,0:T(8,128)(2,1)S(1)}, u32[]{:S(2)}, u32[]{:S(2)}) collective-permute-start(bf16[16,4608]{1,0:T(8,128)(2,1)S(1)} %collective-permute-done.9.refs_5_), channel_id=1, source_target_pairs={{0,1},{1,0},{2,3},{3,2},{4,5},{5,4},{6,7},{7,6},{8,9},{9,8},{10,11... | collective-permute-start | bytes 442376 | tf_op jit(solution)/shard_map/ppermute | solution.py:185
  27.1 0.9 %collective-permute-done.8.refs_4_ = bf16[16,4608]{1,0:T(8,128)(2,1)S(1)} collective-permute-done((bf16[16,4608]{1,0:T(8,128)(2,1)S(1)}, bf16[16,4608]{1,0:T(8,128)(2,1)S(1)}, u32[]{:S(2)}, u32[]{:S(2)}) %collective-permute-start.8) | collective-permute-done | bytes 147488 | tf_op jit(solution)/shard_map/ppermute | solution.py:185
  27.9 0.0 collective-permute-done.7.refs_2_
  27.9 0.2 collective-permute-done.10.refs_6_
  28.1 0.0 collective-permute-done.12.refs_8_
  28.1 0.0 copy-done
  28.1 0.0 copy-done.1
  28.1 0.0 copy-done.2
  28.1 1.3 %shard_map.60 = (f32[64,512]{1,0:T(8,128)S(1)}, bf16[64,512]{1,0:T(8,128)(2,1)S(1)}, bf16[256,512]{1,0:T(8,128)(2,1)S(1)}) custom-call(s32[1,512]{1,0:T(1,128)S(1)} %bitcast.11, s32[1,512]{1,0:T(1,128)S(1)} %broadcast_in_dim.3.own_idx_ref, bf16[4,512,1024]{2,1,0:T(8,128)(2,1)S(1)} %get-tuple-element.26.x_ref, bf16[64,512]{1,0:T(8,128)(2,1)S(1)} %bitcast.10, ...), custom_call_target="tpu_custom_call" | custom-call | flops 1073741824 | bytes 6557696 | tf_op jit(solution)/shard_map/pallas_call | solution.py:21
  29.4 1.4 %collective-permute-start.13 = (bf16[64,512]{1,0:T(8,128)(2,1)S(1)}, bf16[64,512]{1,0:T(8,128)(2,1)S(1)}, u32[]{:S(2)}, u32[]{:S(2)}) collective-permute-start(bf16[64,512]{1,0:T(8,128)(2,1)S(1)} %get-tuple-element.30), channel_id=1, source_target_pairs={{0,2},{2,0},{1,3},{3,1},{4,6},{6,4},{5,7},{7,5},{8,10},{10,8},{9,1... | collective-permute-start | bytes 196616 | tf_op jit(solution)/shard_map/ppermute | solution.py:185
  30.9 0.0 collective-permute-done.5.refs_3_
  30.9 0.9 %shard_map.57.base_ref = f32[512,512]{1,0:T(8,128)S(1)} custom-call(s32[4]{0:T(128)S(1)} %add_convert_fusion.flag_ref, bf16[512,512]{1,0:T(8,128)(2,1)S(1)} %get-tuple-element.21.refs_0_, bf16[512,512]{1,0:T(8,128)(2,1)S(1)} %shard_map.56.refs_1_, bf16[512,512]{1,0:T(8,128)(2,1)S(1)} %collective-permute-done.1.refs_2_, ...), custom_call_target="tpu_custom_call" | custom-call | flops 1048576 | bytes 2097168 | tf_op jit(solution)/shard_map/pallas_call | solution.py:21
  31.8 2.0 %collective-permute-done.13.refs_0_ = bf16[64,512]{1,0:T(8,128)(2,1)S(1)} collective-permute-done((bf16[64,512]{1,0:T(8,128)(2,1)S(1)}, bf16[64,512]{1,0:T(8,128)(2,1)S(1)}, u32[]{:S(2)}, u32[]{:S(2)}) %collective-permute-start.13) | collective-permute-done | bytes 65568 | tf_op jit(solution)/shard_map/ppermute | solution.py:185
  33.8 1.1 %shard_map.61 = bf16[512,512]{1,0:T(8,128)(2,1)} custom-call(s32[1,512]{1,0:T(1,128)S(1)} %bitcast.12, s32[1,512]{1,0:T(1,128)S(1)} %broadcast_in_dim.3.own_idx_ref, f32[512,512]{1,0:T(8,128)S(1)} %shard_map.57.base_ref, bf16[256,512]{1,0:T(8,128)(2,1)S(1)} %get-tuple-element.28.up_ref, f32[64,512]{1,0:T(8,128)S(1)} %get-tuple-element.29.low_ref, ...), custom_call_target="tpu_custom_call" | custom-call | flops 134217728 | bytes 1511424 | tf_op jit(solution)/shard_map/pallas_call | solution.py:21
  (3 shorter events, 0.0 us)
Async XLA Ops:
  0.0 15.0 %collective-permute-start = (bf16[4096,512]{1,0:T(8,128)(2,1)}, bf16[4096,512]{1,0:T(8,128)(2,1)}, u32[]{:S(2)}, u32[]{:S(2)}) collective-permute-start(bf16[4096,512]{1,0:T(8,128)(2,1)} %v_ref.1), channel_id=1, source_target_pairs={{0,1},{1,0},{2,3},{3,2},{4,5},{5,4},{6,7},{7,6},{8,9},{9,8},{10,11... | collective-permute-start | bytes 12582920 | tf_op jit(solution)/shard_map/ppermute | solution.py:185
  1.4 9.3 %collective-permute-start.3 = (bf16[16,4608]{1,0:T(8,128)(2,1)S(1)}, bf16[16,4608]{1,0:T(8,128)(2,1)S(1)}, u32[]{:S(2)}, u32[]{:S(2)}) collective-permute-start(bf16[16,4608]{1,0:T(8,128)(2,1)S(1)} %get-tuple-element.23), channel_id=1, source_target_pairs={{0,12},{4,8},{8,4},{12,0},{1,13},{5,9},{9,5},{13,1},{2,14},{6,10},... | collective-permute-start | bytes 442376 | tf_op jit(solution)/shard_map/ppermute | solution.py:191
  10.4 16.1 %collective-permute-start.1 = (bf16[512,512]{1,0:T(8,128)(2,1)S(1)}, bf16[512,512]{1,0:T(8,128)(2,1)S(1)}, u32[]{:S(2)}, u32[]{:S(2)}) collective-permute-start(bf16[512,512]{1,0:T(8,128)(2,1)S(1)} %get-tuple-element.21.refs_0_), channel_id=1, source_target_pairs={{0,1},{1,3},{2,0},{3,2},{4,5},{5,7},{6,4},{7,6},{8,9},{9,11},{10,8... | collective-permute-start | bytes 1572872 | tf_op jit(solution)/shard_map/ppermute | solution.py:255
  10.6 8.3 %collective-permute-start.2 = (bf16[16,4608]{1,0:T(8,128)(2,1)S(1)}, bf16[16,4608]{1,0:T(8,128)(2,1)S(1)}, u32[]{:S(2)}, u32[]{:S(2)}) collective-permute-start(bf16[16,4608]{1,0:T(8,128)(2,1)S(1)} %get-tuple-element.23), channel_id=1, source_target_pairs={{0,4},{4,0},{8,12},{12,8},{1,5},{5,1},{9,13},{13,9},{2,6},{6,2},{1... | collective-permute-start | bytes 442376 | tf_op jit(solution)/shard_map/ppermute | solution.py:191
  10.7 9.5 %collective-permute-start.4 = (bf16[16,4608]{1,0:T(8,128)(2,1)S(1)}, bf16[16,4608]{1,0:T(8,128)(2,1)S(1)}, u32[]{:S(2)}, u32[]{:S(2)}) collective-permute-start(bf16[16,4608]{1,0:T(8,128)(2,1)S(1)} %collective-permute-done.3.refs_0_), channel_id=1, source_target_pairs={{0,4},{4,0},{8,12},{12,8},{1,5},{5,1},{9,13},{13,9},{2,6},{6,2},{1... | collective-permute-start | bytes 442376 | tf_op jit(solution)/shard_map/ppermute | solution.py:191
  13.5 9.4 %collective-permute-start.6 = (bf16[16,4608]{1,0:T(8,128)(2,1)S(1)}, bf16[16,4608]{1,0:T(8,128)(2,1)S(1)}, u32[]{:S(2)}, u32[]{:S(2)}) collective-permute-start(bf16[16,4608]{1,0:T(8,128)(2,1)S(1)} %collective-permute-done.3.refs_0_), channel_id=1, source_target_pairs={{0,16},{16,0},{1,17},{17,1},{2,18},{18,2},{3,19},{19,3},{4,20},{20... | collective-permute-start | bytes 442376 | tf_op jit(solution)/shard_map/ppermute | solution.py:185
  15.0 13.1 %copy-start = (bf16[1,4096,64]{1,2,0:T(8,128)(2,1)S(1)}, bf16[1,4096,64]{1,2,0:T(8,128)(2,1)}, u32[]{:S(2)}) copy-start(bf16[1,4096,64]{1,2,0:T(8,128)(2,1)} %param.7) | copy-start | bytes 1572868
  15.0 13.1 %copy-start.1 = (bf16[1,64,512]{2,1,0:T(8,128)(2,1)S(1)}, bf16[1,64,512]{2,1,0:T(8,128)(2,1)}, u32[]{:S(2)}) copy-start(bf16[1,64,512]{2,1,0:T(8,128)(2,1)} %param.8) | copy-start | bytes 196612
  15.0 13.1 %copy-start.2 = (s32[512,1]{0,1:T(1,128)S(1)}, s32[512,1]{0,1:T(1,128)}, u32[]{:S(2)}) copy-start(s32[512,1]{0,1:T(1,128)} %param.9) | copy-start | bytes 6148
  18.9 5.4 %collective-permute-start.11 = (bf16[16,4608]{1,0:T(8,128)(2,1)S(1)}, bf16[16,4608]{1,0:T(8,128)(2,1)S(1)}, u32[]{:S(2)}, u32[]{:S(2)}) collective-permute-start(bf16[16,4608]{1,0:T(8,128)(2,1)S(1)} %get-tuple-element.27), channel_id=1, source_target_pairs={{0,4},{4,0},{8,12},{12,8},{1,5},{5,1},{9,13},{13,9},{2,6},{6,2},{1... | collective-permute-start | bytes 442376 | tf_op jit(solution)/shard_map/ppermute | solution.py:191
  20.3 10.6 %collective-permute-start.5 = (bf16[512,512]{1,0:T(8,128)(2,1)S(1)}, bf16[512,512]{1,0:T(8,128)(2,1)S(1)}, u32[]{:S(2)}, u32[]{:S(2)}) collective-permute-start(bf16[512,512]{1,0:T(8,128)(2,1)S(1)} %shard_map.56.refs_1_), channel_id=1, source_target_pairs={{0,2},{1,0},{2,3},{3,1},{4,6},{5,4},{6,7},{7,5},{8,10},{9,8},{10,1... | collective-permute-start | bytes 1572872 | tf_op jit(solution)/shard_map/ppermute | solution.py:255
  21.3 5.2 %collective-permute-start.9 = (bf16[16,4608]{1,0:T(8,128)(2,1)S(1)}, bf16[16,4608]{1,0:T(8,128)(2,1)S(1)}, u32[]{:S(2)}, u32[]{:S(2)}) collective-permute-start(bf16[16,4608]{1,0:T(8,128)(2,1)S(1)} %collective-permute-done.4.refs_3_), channel_id=1, source_target_pairs={{0,16},{16,0},{1,17},{17,1},{2,18},{18,2},{3,19},{19,3},{4,20},{20... | collective-permute-start | bytes 442376 | tf_op jit(solution)/shard_map/ppermute | solution.py:185
  23.0 4.9 %collective-permute-start.7 = (bf16[32,4608]{1,0:T(8,128)(2,1)S(1)}, bf16[32,4608]{1,0:T(8,128)(2,1)S(1)}, u32[]{:S(2)}, u32[]{:S(2)}) collective-permute-start(bf16[32,4608]{1,0:T(8,128)(2,1)S(1)} %shard_map.58.refs_1_), channel_id=1, source_target_pairs={{0,1},{1,0},{2,3},{3,2},{4,5},{5,4},{6,7},{7,6},{8,9},{9,8},{10,11... | collective-permute-start | bytes 884744 | tf_op jit(solution)/shard_map/ppermute | solution.py:185
  24.2 3.9 %collective-permute-start.12 = (bf16[32,4608]{1,0:T(8,128)(2,1)S(1)}, bf16[32,4608]{1,0:T(8,128)(2,1)S(1)}, u32[]{:S(2)}, u32[]{:S(2)}) collective-permute-start(bf16[32,4608]{1,0:T(8,128)(2,1)S(1)} %shard_map.59.refs_7_), channel_id=1, source_target_pairs={{0,1},{1,0},{2,3},{3,2},{4,5},{5,4},{6,7},{7,6},{8,9},{9,8},{10,11... | collective-permute-start | bytes 884744 | tf_op jit(solution)/shard_map/ppermute | solution.py:185
  26.5 1.4 %collective-permute-start.8 = (bf16[16,4608]{1,0:T(8,128)(2,1)S(1)}, bf16[16,4608]{1,0:T(8,128)(2,1)S(1)}, u32[]{:S(2)}, u32[]{:S(2)}) collective-permute-start(bf16[16,4608]{1,0:T(8,128)(2,1)S(1)} %collective-permute-done.4.refs_3_), channel_id=1, source_target_pairs={{0,1},{1,0},{2,3},{3,2},{4,5},{5,4},{6,7},{7,6},{8,9},{9,8},{10,11... | collective-permute-start | bytes 442376 | tf_op jit(solution)/shard_map/ppermute | solution.py:185
  26.5 1.6 %collective-permute-start.10 = (bf16[16,4608]{1,0:T(8,128)(2,1)S(1)}, bf16[16,4608]{1,0:T(8,128)(2,1)S(1)}, u32[]{:S(2)}, u32[]{:S(2)}) collective-permute-start(bf16[16,4608]{1,0:T(8,128)(2,1)S(1)} %collective-permute-done.9.refs_5_), channel_id=1, source_target_pairs={{0,1},{1,0},{2,3},{3,2},{4,5},{5,4},{6,7},{7,6},{8,9},{9,8},{10,11... | collective-permute-start | bytes 442376 | tf_op jit(solution)/shard_map/ppermute | solution.py:185
  29.4 4.4 %collective-permute-start.13 = (bf16[64,512]{1,0:T(8,128)(2,1)S(1)}, bf16[64,512]{1,0:T(8,128)(2,1)S(1)}, u32[]{:S(2)}, u32[]{:S(2)}) collective-permute-start(bf16[64,512]{1,0:T(8,128)(2,1)S(1)} %get-tuple-element.30), channel_id=1, source_target_pairs={{0,2},{2,0},{1,3},{3,1},{4,6},{6,4},{5,7},{7,5},{8,10},{10,8},{9,1... | collective-permute-start | bytes 196616 | tf_op jit(solution)/shard_map/ppermute | solution.py:185

commit v14 on v12

--- a/solution.py
+++ b/solution.py
@@ -277,6 +277,8 @@
 
         for p in order:
             members = beside if p == 1 else [pieces[p]] + others(pieces[p], "groups")
+            if p == 1:
+                members = [after(member, *recvs[: tensors - 1]) for member in members]
             if p in [*near, 1] and len(members) > 1:
                 shape = (share * groups, wide + cols)
                 members = [call(pack_kernel, jax.ShapeDtypeStruct(shape, BF16), tuple(members))]

time: 34.7 us -> 39.5 us (1.14)
  waiting for transfers between devices: 8.46 us -> 14 us
  starting transfers between devices: 13.5 us -> 12.8 us
    ppermute x4, waiting for transfers between devices: 2.5 us -> 8.41 us  [flip(): return lax.ppermute(x, 'adapter', [(i, i ^ bits) for i in range(adapters)])]
    ppermute x2, starting transfers between devices: 1.75 us -> 0.91 us  [base(): recvs.append(lax.ppermute(block, ('tensor', 'replica'), base_pairs(h, by)))]
    ppermute x4, starting transfers between devices: 7.52 us -> 7.95 us  [flip(): return lax.ppermute(x, 'adapter', [(i, i ^ bits) for i in range(adapters)])]
    ppermute x8, waiting for transfers between devices: 5.96 us -> 5.56 us  [shift(): return lax.ppermute(x, axis, [(i, (i + by) % size) for i in range(size)])]
  transfers between devices with their start and end apart: 14 -> 14, of which waited for: 6 -> 6; matrix products, arithmetic and copies ran while one was open for 3% -> 3% of each run, Pallas kernels for 30% -> 26%
where the time goes in v14:
time: 39.5 us; the launch traced here: 39.3 us
  waiting for transfers between devices  14 us (35%)
  starting transfers between devices  12.8 us (32%)
  Pallas kernels  11.4 us (29%)
  other arithmetic  1.07 us (3%)
    pallas_call x7, Pallas kernels, call(): pl.pallas_call(kernel, out_shape=outs, in_specs=specs or [VMEM] * len(arg...  11.4 us
    ppermute x4, waiting for transfers between devices, flip(): return lax.ppermute(x, 'adapter', [(i, i ^ bits) for i in range(adapters)])  8.41 us
    ppermute x4, starting transfers between devices, flip(): return lax.ppermute(x, 'adapter', [(i, i ^ bits) for i in range(adapters)])  7.95 us
    ppermute x8, waiting for transfers between devices, shift(): return lax.ppermute(x, axis, [(i, (i + by) % size) for i in range(size)])  5.56 us
    ppermute x8, starting transfers between devices, shift(): return lax.ppermute(x, axis, [(i, (i + by) % size) for i in range(size)])  3.89 us
    concatenate x1, other arithmetic, shards(): own = jnp.concatenate([down, u[0]], axis=1)  0.99 us
    ppermute x2, starting transfers between devices, base(): recvs.append(lax.ppermute(block, ('tensor', 'replica'), base_pairs(h, by)))  0.91 us
  transfers between devices with their start and end apart: 14, of which 6 were waited for; matrix products, arithmetic and copies ran while one was open for 3% of the time, Pallas kernels for 26%

profile of v14, /device:TPU:0, one launch (start us, length us, event | category | flops | bytes accessed | tf_op | source)
XLA Modules:
  0.0 39.3 jit_solution(16137214004835300621)
XLA Ops:
  0.0 0.5 %collective-permute-start = (bf16[4096,512]{1,0:T(8,128)(2,1)}, bf16[4096,512]{1,0:T(8,128)(2,1)}, u32[]{:S(2)}, u32[]{:S(2)}) collective-permute-start(bf16[4096,512]{1,0:T(8,128)(2,1)} %v_ref.1), channel_id=1, source_target_pairs={{0,1},{1,0},{2,3},{3,2},{4,5},{5,4},{6,7},{7,6},{8,9},{9,8},{10,11... | collective-permute-start | bytes 12582920 | tf_op jit(solution)/shard_map/ppermute | solution.py:185
  0.5 0.1 add_convert_fusion.flag_ref
  0.5 1.0 %fusion = (bf16[16,4608]{1,0:T(8,128)(2,1)S(1)}, bf16[16,4608]{1,0:T(8,128)(2,1)S(1)}) fusion(s32[]{:T(128)S(6)} %select_n.7, bf16[64,4096]{1,0:T(8,128)(2,1)} %bitcast.7, bf16[64,512]{1,0:T(8,128)(2,1)} %bitcast.9, s32[]{:T(128)S(6)} %select_n.6), kind=kLoop, calls=%fused_computation.4 | loop fusion | flops 589824 | bytes 884744 | tf_op jit(solution)/shard_map/concatenate | solution.py:229
  1.5 4.2 %shard_map.55 = (bf16[512,512]{1,0:T(8,128)(2,1)S(1)}, bf16[4,512,1024]{2,1,0:T(8,128)(2,1)S(1)}) custom-call(bf16[512,4096]{1,0:T(8,128)(2,1)} %x_ref, bf16[4096,512]{1,0:T(8,128)(2,1)} %v_ref.1), custom_call_target="tpu_custom_call" | custom-call | flops 2147483648 | bytes 8388608 | tf_op jit(solution)/shard_map/pallas_call | solution.py:21
  5.8 0.1 collective-permute-start.1
  5.8 5.1 %collective-permute-start.3 = (bf16[16,4608]{1,0:T(8,128)(2,1)S(1)}, bf16[16,4608]{1,0:T(8,128)(2,1)S(1)}, u32[]{:S(2)}, u32[]{:S(2)}) collective-permute-start(bf16[16,4608]{1,0:T(8,128)(2,1)S(1)} %get-tuple-element.26), channel_id=1, source_target_pairs={{0,12},{4,8},{8,4},{12,0},{1,13},{5,9},{9,5},{13,1},{2,14},{6,10},... | collective-permute-start | bytes 442376 | tf_op jit(solution)/shard_map/ppermute | solution.py:191
  10.9 0.0 collective-permute-start.10
  10.9 4.4 %collective-permute-done.3.refs_0_ = bf16[16,4608]{1,0:T(8,128)(2,1)S(1)} collective-permute-done((bf16[16,4608]{1,0:T(8,128)(2,1)S(1)}, bf16[16,4608]{1,0:T(8,128)(2,1)S(1)}, u32[]{:S(2)}, u32[]{:S(2)}) %collective-permute-start.3) | collective-permute-done | bytes 147488 | tf_op jit(solution)/shard_map/ppermute | solution.py:191
  15.3 1.9 %collective-permute-start.4 = (bf16[16,4608]{1,0:T(8,128)(2,1)S(1)}, bf16[16,4608]{1,0:T(8,128)(2,1)S(1)}, u32[]{:S(2)}, u32[]{:S(2)}) collective-permute-start(bf16[16,4608]{1,0:T(8,128)(2,1)S(1)} %collective-permute-done.3.refs_0_), channel_id=1, source_target_pairs={{0,16},{16,0},{1,17},{17,1},{2,18},{18,2},{3,19},{19,3},{4,20},{20... | collective-permute-start | bytes 442376 | tf_op jit(solution)/shard_map/ppermute | solution.py:185
  17.2 2.8 %collective-permute-start.6 = (bf16[16,4608]{1,0:T(8,128)(2,1)S(1)}, bf16[16,4608]{1,0:T(8,128)(2,1)S(1)}, u32[]{:S(2)}, u32[]{:S(2)}) collective-permute-start(bf16[16,4608]{1,0:T(8,128)(2,1)S(1)} %collective-permute-done.3.refs_0_), channel_id=1, source_target_pairs={{0,4},{4,0},{8,12},{12,8},{1,5},{5,1},{9,13},{13,9},{2,6},{6,2},{1... | collective-permute-start | bytes 442376 | tf_op jit(solution)/shard_map/ppermute | solution.py:191
  20.0 0.0 collective-permute-done.v_ref
  20.0 0.0 copy-start
  20.0 0.0 copy-start.1
  20.0 0.0 copy-start.2
  20.0 3.8 %shard_map.56.refs_1_ = bf16[512,512]{1,0:T(8,128)(2,1)S(1)} custom-call(bf16[4,512,1024]{2,1,0:T(8,128)(2,1)S(1)} %get-tuple-element.24.x_ref, bf16[4096,512]{1,0:T(8,128)(2,1)} %collective-permute-done.v_ref), custom_call_target="tpu_custom_call" | custom-call | flops 2147483648 | bytes 8388608 | tf_op jit(solution)/shard_map/pallas_call | solution.py:21
  23.9 0.1 collective-permute-start.11
  23.9 0.0 collective-permute-done.4.refs_1_
  23.9 0.8 %collective-permute-start.2 = (bf16[512,512]{1,0:T(8,128)(2,1)S(1)}, bf16[512,512]{1,0:T(8,128)(2,1)S(1)}, u32[]{:S(2)}, u32[]{:S(2)}) collective-permute-start(bf16[512,512]{1,0:T(8,128)(2,1)S(1)} %shard_map.56.refs_1_), channel_id=1, source_target_pairs={{0,2},{1,0},{2,3},{3,1},{4,6},{5,4},{6,7},{7,5},{8,10},{9,8},{10,1... | collective-permute-start | bytes 1572872 | tf_op jit(solution)/shard_map/ppermute | solution.py:255
  24.8 0.0 collective-permute-done.10.refs_0_
  24.8 0.1 collective-permute-start.5
  24.9 0.0 collective-permute-done.6.refs_3_
  24.9 0.6 %collective-permute-start.8 = (bf16[16,4608]{1,0:T(8,128)(2,1)S(1)}, bf16[16,4608]{1,0:T(8,128)(2,1)S(1)}, u32[]{:S(2)}, u32[]{:S(2)}) collective-permute-start(bf16[16,4608]{1,0:T(8,128)(2,1)S(1)} %collective-permute-done.6.refs_3_), channel_id=1, source_target_pairs={{0,16},{16,0},{1,17},{17,1},{2,18},{18,2},{3,19},{19,3},{4,20},{20... | collective-permute-start | bytes 442376 | tf_op jit(solution)/shard_map/ppermute | solution.py:185
  25.5 0.0 collective-permute-done.1.refs_2_
  25.5 4.0 %collective-permute-done.11.refs_1_ = bf16[16,4608]{1,0:T(8,128)(2,1)S(1)} collective-permute-done((bf16[16,4608]{1,0:T(8,128)(2,1)S(1)}, bf16[16,4608]{1,0:T(8,128)(2,1)S(1)}, u32[]{:S(2)}, u32[]{:S(2)}) %collective-permute-start.11) | collective-permute-done | bytes 147488 | tf_op jit(solution)/shard_map/ppermute | solution.py:191
  29.5 0.1 collective-permute-start.12
  29.6 0.5 %collective-permute-start.7 = (bf16[16,4608]{1,0:T(8,128)(2,1)S(1)}, bf16[16,4608]{1,0:T(8,128)(2,1)S(1)}, u32[]{:S(2)}, u32[]{:S(2)}) collective-permute-start(bf16[16,4608]{1,0:T(8,128)(2,1)S(1)} %collective-permute-done.6.refs_3_), channel_id=1, source_target_pairs={{0,1},{1,0},{2,3},{3,2},{4,5},{5,4},{6,7},{7,6},{8,9},{9,8},{10,11... | collective-permute-start | bytes 442376 | tf_op jit(solution)/shard_map/ppermute | solution.py:185
  30.1 1.1 %collective-permute-done.8.refs_5_ = bf16[16,4608]{1,0:T(8,128)(2,1)S(1)} collective-permute-done((bf16[16,4608]{1,0:T(8,128)(2,1)S(1)}, bf16[16,4608]{1,0:T(8,128)(2,1)S(1)}, u32[]{:S(2)}, u32[]{:S(2)}) %collective-permute-start.8) | collective-permute-done | bytes 147488 | tf_op jit(solution)/shard_map/ppermute | solution.py:185
  31.2 0.0 collective-permute-start.9
  31.2 0.2 collective-permute-done.7.refs_4_
  31.3 0.0 collective-permute-done.5.refs_2_
  31.3 1.2 %collective-permute-done.9.refs_6_ = bf16[16,4608]{1,0:T(8,128)(2,1)S(1)} collective-permute-done((bf16[16,4608]{1,0:T(8,128)(2,1)S(1)}, bf16[16,4608]{1,0:T(8,128)(2,1)S(1)}, u32[]{:S(2)}, u32[]{:S(2)}) %collective-permute-start.9) | collective-permute-done | bytes 147488 | tf_op jit(solution)/shard_map/ppermute | solution.py:185
  32.5 0.0 collective-permute-done.12.refs_8_
  32.5 0.0 copy-done
  32.5 0.0 copy-done.1
  32.5 0.0 copy-done.2
  32.6 1.3 %shard_map.60 = (f32[64,512]{1,0:T(8,128)S(1)}, bf16[64,512]{1,0:T(8,128)(2,1)S(1)}, bf16[256,512]{1,0:T(8,128)(2,1)S(1)}) custom-call(s32[1,512]{1,0:T(1,128)S(1)} %bitcast.11, s32[1,512]{1,0:T(1,128)S(1)} %broadcast_in_dim.3.own_idx_ref, bf16[4,512,1024]{2,1,0:T(8,128)(2,1)S(1)} %get-tuple-element.24.x_ref, bf16[64,512]{1,0:T(8,128)(2,1)S(1)} %bitcast.10, ...), custom_call_target="tpu_custom_call" | custom-call | flops 1073741824 | bytes 6557696 | tf_op jit(solution)/shard_map/pallas_call | solution.py:21
  33.9 0.3 collective-permute-start.13
  34.2 0.0 collective-permute-done.2.refs_3_
  34.2 0.9 %shard_map.57.base_ref = f32[512,512]{1,0:T(8,128)S(1)} custom-call(s32[4]{0:T(128)S(1)} %add_convert_fusion.flag_ref, bf16[512,512]{1,0:T(8,128)(2,1)S(1)} %get-tuple-element.22.refs_0_, bf16[512,512]{1,0:T(8,128)(2,1)S(1)} %shard_map.56.refs_1_, bf16[512,512]{1,0:T(8,128)(2,1)S(1)} %collective-permute-done.1.refs_2_, ...), custom_call_target="tpu_custom_call" | custom-call | flops 1048576 | bytes 2097168 | tf_op jit(solution)/shard_map/pallas_call | solution.py:21
  35.1 3.1 %collective-permute-done.13.refs_0_ = bf16[64,512]{1,0:T(8,128)(2,1)S(1)} collective-permute-done((bf16[64,512]{1,0:T(8,128)(2,1)S(1)}, bf16[64,512]{1,0:T(8,128)(2,1)S(1)}, u32[]{:S(2)}, u32[]{:S(2)}) %collective-permute-start.13) | collective-permute-done | bytes 65568 | tf_op jit(solution)/shard_map/ppermute | solution.py:185
  38.2 1.1 %shard_map.61 = bf16[512,512]{1,0:T(8,128)(2,1)} custom-call(s32[1,512]{1,0:T(1,128)S(1)} %bitcast.12, s32[1,512]{1,0:T(1,128)S(1)} %broadcast_in_dim.3.own_idx_ref, f32[512,512]{1,0:T(8,128)S(1)} %shard_map.57.base_ref, bf16[256,512]{1,0:T(8,128)(2,1)S(1)} %get-tuple-element.30.up_ref, f32[64,512]{1,0:T(8,128)S(1)} %get-tuple-element.31.low_ref, ...), custom_call_target="tpu_custom_call" | custom-call | flops 134217728 | bytes 1511424 | tf_op jit(solution)/shard_map/pallas_call | solution.py:21
  (3 shorter events, 0.0 us)
Async XLA Ops:
  0.0 20.0 %collective-permute-start = (bf16[4096,512]{1,0:T(8,128)(2,1)}, bf16[4096,512]{1,0:T(8,128)(2,1)}, u32[]{:S(2)}, u32[]{:S(2)}) collective-permute-start(bf16[4096,512]{1,0:T(8,128)(2,1)} %v_ref.1), channel_id=1, source_target_pairs={{0,1},{1,0},{2,3},{3,2},{4,5},{5,4},{6,7},{7,6},{8,9},{9,8},{10,11... | collective-permute-start | bytes 12582920 | tf_op jit(solution)/shard_map/ppermute | solution.py:185
  5.8 19.7 %collective-permute-start.1 = (bf16[512,512]{1,0:T(8,128)(2,1)S(1)}, bf16[512,512]{1,0:T(8,128)(2,1)S(1)}, u32[]{:S(2)}, u32[]{:S(2)}) collective-permute-start(bf16[512,512]{1,0:T(8,128)(2,1)S(1)} %get-tuple-element.22.refs_0_), channel_id=1, source_target_pairs={{0,1},{1,3},{2,0},{3,2},{4,5},{5,7},{6,4},{7,6},{8,9},{9,11},{10,8... | collective-permute-start | bytes 1572872 | tf_op jit(solution)/shard_map/ppermute | solution.py:255
  5.8 9.5 %collective-permute-start.3 = (bf16[16,4608]{1,0:T(8,128)(2,1)S(1)}, bf16[16,4608]{1,0:T(8,128)(2,1)S(1)}, u32[]{:S(2)}, u32[]{:S(2)}) collective-permute-start(bf16[16,4608]{1,0:T(8,128)(2,1)S(1)} %get-tuple-element.26), channel_id=1, source_target_pairs={{0,12},{4,8},{8,4},{12,0},{1,13},{5,9},{9,5},{13,1},{2,14},{6,10},... | collective-permute-start | bytes 442376 | tf_op jit(solution)/shard_map/ppermute | solution.py:191
  10.9 13.9 %collective-permute-start.10 = (bf16[16,4608]{1,0:T(8,128)(2,1)S(1)}, bf16[16,4608]{1,0:T(8,128)(2,1)S(1)}, u32[]{:S(2)}, u32[]{:S(2)}) collective-permute-start(bf16[16,4608]{1,0:T(8,128)(2,1)S(1)} %get-tuple-element.26), channel_id=1, source_target_pairs={{0,4},{4,0},{8,12},{12,8},{1,5},{5,1},{9,13},{13,9},{2,6},{6,2},{1... | collective-permute-start | bytes 442376 | tf_op jit(solution)/shard_map/ppermute | solution.py:191
  15.3 8.6 %collective-permute-start.4 = (bf16[16,4608]{1,0:T(8,128)(2,1)S(1)}, bf16[16,4608]{1,0:T(8,128)(2,1)S(1)}, u32[]{:S(2)}, u32[]{:S(2)}) collective-permute-start(bf16[16,4608]{1,0:T(8,128)(2,1)S(1)} %collective-permute-done.3.refs_0_), channel_id=1, source_target_pairs={{0,16},{16,0},{1,17},{17,1},{2,18},{18,2},{3,19},{19,3},{4,20},{20... | collective-permute-start | bytes 442376 | tf_op jit(solution)/shard_map/ppermute | solution.py:185
  17.2 7.7 %collective-permute-start.6 = (bf16[16,4608]{1,0:T(8,128)(2,1)S(1)}, bf16[16,4608]{1,0:T(8,128)(2,1)S(1)}, u32[]{:S(2)}, u32[]{:S(2)}) collective-permute-start(bf16[16,4608]{1,0:T(8,128)(2,1)S(1)} %collective-permute-done.3.refs_0_), channel_id=1, source_target_pairs={{0,4},{4,0},{8,12},{12,8},{1,5},{5,1},{9,13},{13,9},{2,6},{6,2},{1... | collective-permute-start | bytes 442376 | tf_op jit(solution)/shard_map/ppermute | solution.py:191
  20.0 12.5 %copy-start = (bf16[1,4096,64]{1,2,0:T(8,128)(2,1)S(1)}, bf16[1,4096,64]{1,2,0:T(8,128)(2,1)}, u32[]{:S(2)}) copy-start(bf16[1,4096,64]{1,2,0:T(8,128)(2,1)} %param.7) | copy-start | bytes 1572868
  20.0 12.5 %copy-start.1 = (bf16[1,64,512]{2,1,0:T(8,128)(2,1)S(1)}, bf16[1,64,512]{2,1,0:T(8,128)(2,1)}, u32[]{:S(2)}) copy-start(bf16[1,64,512]{2,1,0:T(8,128)(2,1)} %param.8) | copy-start | bytes 196612
  20.0 12.5 %copy-start.2 = (s32[512,1]{0,1:T(1,128)S(1)}, s32[512,1]{0,1:T(1,128)}, u32[]{:S(2)}) copy-start(s32[512,1]{0,1:T(1,128)} %param.9) | copy-start | bytes 6148
  23.9 5.6 %collective-permute-start.11 = (bf16[16,4608]{1,0:T(8,128)(2,1)S(1)}, bf16[16,4608]{1,0:T(8,128)(2,1)S(1)}, u32[]{:S(2)}, u32[]{:S(2)}) collective-permute-start(bf16[16,4608]{1,0:T(8,128)(2,1)S(1)} %get-tuple-element.28), channel_id=1, source_target_pairs={{0,4},{4,0},{8,12},{12,8},{1,5},{5,1},{9,13},{13,9},{2,6},{6,2},{1... | collective-permute-start | bytes 442376 | tf_op jit(solution)/shard_map/ppermute | solution.py:191
  23.9 10.2 %collective-permute-start.2 = (bf16[512,512]{1,0:T(8,128)(2,1)S(1)}, bf16[512,512]{1,0:T(8,128)(2,1)S(1)}, u32[]{:S(2)}, u32[]{:S(2)}) collective-permute-start(bf16[512,512]{1,0:T(8,128)(2,1)S(1)} %shard_map.56.refs_1_), channel_id=1, source_target_pairs={{0,2},{1,0},{2,3},{3,1},{4,6},{5,4},{6,7},{7,5},{8,10},{9,8},{10,1... | collective-permute-start | bytes 1572872 | tf_op jit(solution)/shard_map/ppermute | solution.py:255
  24.8 6.5 %collective-permute-start.5 = (bf16[32,4608]{1,0:T(8,128)(2,1)S(1)}, bf16[32,4608]{1,0:T(8,128)(2,1)S(1)}, u32[]{:S(2)}, u32[]{:S(2)}) collective-permute-start(bf16[32,4608]{1,0:T(8,128)(2,1)S(1)} %shard_map.58.refs_1_), channel_id=1, source_target_pairs={{0,1},{1,0},{2,3},{3,2},{4,5},{5,4},{6,7},{7,6},{8,9},{9,8},{10,11... | collective-permute-start | bytes 884744 | tf_op jit(solution)/shard_map/ppermute | solution.py:185
  24.9 6.3 %collective-permute-start.8 = (bf16[16,4608]{1,0:T(8,128)(2,1)S(1)}, bf16[16,4608]{1,0:T(8,128)(2,1)S(1)}, u32[]{:S(2)}, u32[]{:S(2)}) collective-permute-start(bf16[16,4608]{1,0:T(8,128)(2,1)S(1)} %collective-permute-done.6.refs_3_), channel_id=1, source_target_pairs={{0,16},{16,0},{1,17},{17,1},{2,18},{18,2},{3,19},{19,3},{4,20},{20... | collective-permute-start | bytes 442376 | tf_op jit(solution)/shard_map/ppermute | solution.py:185
  29.5 3.1 %collective-permute-start.12 = (bf16[32,4608]{1,0:T(8,128)(2,1)S(1)}, bf16[32,4608]{1,0:T(8,128)(2,1)S(1)}, u32[]{:S(2)}, u32[]{:S(2)}) collective-permute-start(bf16[32,4608]{1,0:T(8,128)(2,1)S(1)} %shard_map.59.refs_7_), channel_id=1, source_target_pairs={{0,1},{1,0},{2,3},{3,2},{4,5},{5,4},{6,7},{7,6},{8,9},{9,8},{10,11... | collective-permute-start | bytes 884744 | tf_op jit(solution)/shard_map/ppermute | solution.py:185
  29.6 1.8 %collective-permute-start.7 = (bf16[16,4608]{1,0:T(8,128)(2,1)S(1)}, bf16[16,4608]{1,0:T(8,128)(2,1)S(1)}, u32[]{:S(2)}, u32[]{:S(2)}) collective-permute-start(bf16[16,4608]{1,0:T(8,128)(2,1)S(1)} %collective-permute-done.6.refs_3_), channel_id=1, source_target_pairs={{0,1},{1,0},{2,3},{3,2},{4,5},{5,4},{6,7},{7,6},{8,9},{9,8},{10,11... | collective-permute-start | bytes 442376 | tf_op jit(solution)/shard_map/ppermute | solution.py:185
  31.2 1.4 %collective-permute-start.9 = (bf16[16,4608]{1,0:T(8,128)(2,1)S(1)}, bf16[16,4608]{1,0:T(8,128)(2,1)S(1)}, u32[]{:S(2)}, u32[]{:S(2)}) collective-permute-start(bf16[16,4608]{1,0:T(8,128)(2,1)S(1)} %collective-permute-done.8.refs_5_), channel_id=1, source_target_pairs={{0,1},{1,0},{2,3},{3,2},{4,5},{5,4},{6,7},{7,6},{8,9},{9,8},{10,11... | collective-permute-start | bytes 442376 | tf_op jit(solution)/shard_map/ppermute | solution.py:185
  33.9 4.3 %collective-permute-start.13 = (bf16[64,512]{1,0:T(8,128)(2,1)S(1)}, bf16[64,512]{1,0:T(8,128)(2,1)S(1)}, u32[]{:S(2)}, u32[]{:S(2)}) collective-permute-start(bf16[64,512]{1,0:T(8,128)(2,1)S(1)} %get-tuple-element.32), channel_id=1, source_target_pairs={{0,2},{2,0},{1,3},{3,1},{4,6},{6,4},{5,7},{7,5},{8,10},{10,8},{9,1... | collective-permute-start | bytes 196616 | tf_op jit(solution)/shard_map/ppermute | solution.py:185

commit v15 on v12

--- a/solution.py
+++ b/solution.py
@@ -267,7 +267,7 @@
         second = first
         for h in range(1, replicas):
             second, _ = base(h, [])
-        beside += [flip(after(piece, second), 1) for piece in rest]
+        beside += [flip(after(piece, *[pieces[p] for p in near]), 1) for piece in rest]
 
         arrays, layout = [down], [[(0, 0, rank)]] + [[] for _ in order]
 

time: 34.7 us -> 35.2 us (1.014)
  starting transfers between devices: 13.5 us -> 14.5 us
  waiting for transfers between devices: 8.46 us -> 8.04 us
    ppermute x4, waiting for transfers between devices: 2.5 us -> 1.42 us  [flip(): return lax.ppermute(x, 'adapter', [(i, i ^ bits) for i in range(adapters)])]
    ppermute x8, starting transfers between devices: 4.26 us -> 5.24 us  [shift(): return lax.ppermute(x, axis, [(i, (i + by) % size) for i in range(size)])]
    ppermute x8, waiting for transfers between devices: 5.96 us -> 6.61 us  [shift(): return lax.ppermute(x, axis, [(i, (i + by) % size) for i in range(size)])]
  transfers between devices with their start and end apart: 14 -> 14, of which waited for: 6 -> 6; matrix products, arithmetic and copies ran while one was open for 3% -> 3% of each run, Pallas kernels for 30% -> 29%
where the time goes in v15:
time: 35.2 us; the launch traced here: 35 us
  starting transfers between devices  14.5 us (41%)
  Pallas kernels  11.4 us (32%)
  waiting for transfers between devices  8.04 us (23%)
  other arithmetic  1.07 us (3%)
    pallas_call x7, Pallas kernels, call(): pl.pallas_call(kernel, out_shape=outs, in_specs=specs or [VMEM] * len(arg...  11.4 us
    ppermute x4, starting transfers between devices, flip(): return lax.ppermute(x, 'adapter', [(i, i ^ bits) for i in range(adapters)])  7.47 us
    ppermute x8, waiting for transfers between devices, shift(): return lax.ppermute(x, axis, [(i, (i + by) % size) for i in range(size)])  6.61 us
    ppermute x8, starting transfers between devices, shift(): return lax.ppermute(x, axis, [(i, (i + by) % size) for i in range(size)])  5.24 us
    ppermute x2, starting transfers between devices, base(): recvs.append(lax.ppermute(block, ('tensor', 'replica'), base_pairs(h, by)))  1.75 us
    ppermute x4, waiting for transfers between devices, flip(): return lax.ppermute(x, 'adapter', [(i, i ^ bits) for i in range(adapters)])  1.42 us
    concatenate x1, other arithmetic, shards(): own = jnp.concatenate([down, u[0]], axis=1)  0.99 us
  transfers between devices with their start and end apart: 14, of which 6 were waited for; matrix products, arithmetic and copies ran while one was open for 3% of the time, Pallas kernels for 29%

profile of v15, /device:TPU:0, one launch (start us, length us, event | category | flops | bytes accessed | tf_op | source)
XLA Modules:
  0.0 35.0 jit_solution(8434267857387145142)
XLA Ops:
  0.0 0.5 %collective-permute-start = (bf16[4096,512]{1,0:T(8,128)(2,1)}, bf16[4096,512]{1,0:T(8,128)(2,1)}, u32[]{:S(2)}, u32[]{:S(2)}) collective-permute-start(bf16[4096,512]{1,0:T(8,128)(2,1)} %v_ref.1), channel_id=1, source_target_pairs={{0,1},{1,0},{2,3},{3,2},{4,5},{5,4},{6,7},{7,6},{8,9},{9,8},{10,11... | collective-permute-start | bytes 12582920 | tf_op jit(solution)/shard_map/ppermute | solution.py:185
  0.5 1.0 %fusion = (bf16[16,4608]{1,0:T(8,128)(2,1)S(1)}, bf16[16,4608]{1,0:T(8,128)(2,1)S(1)}) fusion(s32[]{:T(128)S(6)} %select_n.7, bf16[64,4096]{1,0:T(8,128)(2,1)} %bitcast.7, bf16[64,512]{1,0:T(8,128)(2,1)} %bitcast.9, s32[]{:T(128)S(6)} %select_n.6), kind=kLoop, calls=%fused_computation.4 | loop fusion | flops 589824 | bytes 884744 | tf_op jit(solution)/shard_map/concatenate | solution.py:229
  1.4 4.7 %collective-permute-start.3 = (bf16[16,4608]{1,0:T(8,128)(2,1)S(1)}, bf16[16,4608]{1,0:T(8,128)(2,1)S(1)}, u32[]{:S(2)}, u32[]{:S(2)}) collective-permute-start(bf16[16,4608]{1,0:T(8,128)(2,1)S(1)} %get-tuple-element.24), channel_id=1, source_target_pairs={{0,12},{4,8},{8,4},{12,0},{1,13},{5,9},{9,5},{13,1},{2,14},{6,10},... | collective-permute-start | bytes 442376 | tf_op jit(solution)/shard_map/ppermute | solution.py:191
  6.1 0.1 add_convert_fusion.flag_ref
  6.2 4.2 %shard_map.55 = (bf16[512,512]{1,0:T(8,128)(2,1)S(1)}, bf16[4,512,1024]{2,1,0:T(8,128)(2,1)S(1)}) custom-call(bf16[512,4096]{1,0:T(8,128)(2,1)} %x_ref, bf16[4096,512]{1,0:T(8,128)(2,1)} %v_ref.1), custom_call_target="tpu_custom_call" | custom-call | flops 2147483648 | bytes 8388608 | tf_op jit(solution)/shard_map/pallas_call | solution.py:21
  10.4 0.2 collective-permute-start.1
  10.6 0.0 collective-permute-start.10
  10.6 0.1 collective-permute-done.3.refs_0_
  10.7 1.5 %collective-permute-start.4 = (bf16[16,4608]{1,0:T(8,128)(2,1)S(1)}, bf16[16,4608]{1,0:T(8,128)(2,1)S(1)}, u32[]{:S(2)}, u32[]{:S(2)}) collective-permute-start(bf16[16,4608]{1,0:T(8,128)(2,1)S(1)} %collective-permute-done.3.refs_0_), channel_id=1, source_target_pairs={{0,16},{16,0},{1,17},{17,1},{2,18},{18,2},{3,19},{19,3},{4,20},{20... | collective-permute-start | bytes 442376 | tf_op jit(solution)/shard_map/ppermute | solution.py:185
  12.3 2.8 %collective-permute-start.6 = (bf16[16,4608]{1,0:T(8,128)(2,1)S(1)}, bf16[16,4608]{1,0:T(8,128)(2,1)S(1)}, u32[]{:S(2)}, u32[]{:S(2)}) collective-permute-start(bf16[16,4608]{1,0:T(8,128)(2,1)S(1)} %collective-permute-done.3.refs_0_), channel_id=1, source_target_pairs={{0,4},{4,0},{8,12},{12,8},{1,5},{5,1},{9,13},{13,9},{2,6},{6,2},{1... | collective-permute-start | bytes 442376 | tf_op jit(solution)/shard_map/ppermute | solution.py:191
  15.0 0.0 collective-permute-done.v_ref
  15.0 0.0 collective-permute-start.11
  15.1 0.0 copy-start
  15.1 0.0 copy-start.1
  15.1 0.0 copy-start.2
  15.1 3.8 %shard_map.56.refs_1_ = bf16[512,512]{1,0:T(8,128)(2,1)S(1)} custom-call(bf16[4,512,1024]{2,1,0:T(8,128)(2,1)S(1)} %get-tuple-element.22.x_ref, bf16[4096,512]{1,0:T(8,128)(2,1)} %collective-permute-done.v_ref), custom_call_target="tpu_custom_call" | custom-call | flops 2147483648 | bytes 8388608 | tf_op jit(solution)/shard_map/pallas_call | solution.py:21
  18.9 0.0 collective-permute-done.4.refs_1_
  18.9 1.5 %collective-permute-start.2 = (bf16[512,512]{1,0:T(8,128)(2,1)S(1)}, bf16[512,512]{1,0:T(8,128)(2,1)S(1)}, u32[]{:S(2)}, u32[]{:S(2)}) collective-permute-start(bf16[512,512]{1,0:T(8,128)(2,1)S(1)} %shard_map.56.refs_1_), channel_id=1, source_target_pairs={{0,2},{1,0},{2,3},{3,1},{4,6},{5,4},{6,7},{7,5},{8,10},{9,8},{10,1... | collective-permute-start | bytes 1572872 | tf_op jit(solution)/shard_map/ppermute | solution.py:255
  20.4 0.0 collective-permute-done.6.refs_3_
  20.4 1.4 %collective-permute-start.8 = (bf16[16,4608]{1,0:T(8,128)(2,1)S(1)}, bf16[16,4608]{1,0:T(8,128)(2,1)S(1)}, u32[]{:S(2)}, u32[]{:S(2)}) collective-permute-start(bf16[16,4608]{1,0:T(8,128)(2,1)S(1)} %collective-permute-done.6.refs_3_), channel_id=1, source_target_pairs={{0,16},{16,0},{1,17},{17,1},{2,18},{18,2},{3,19},{19,3},{4,20},{20... | collective-permute-start | bytes 442376 | tf_op jit(solution)/shard_map/ppermute | solution.py:185
  21.8 0.0 collective-permute-done.10.refs_0_
  21.8 0.3 collective-permute-start.5
  22.1 1.3 %collective-permute-done.11.refs_1_ = bf16[16,4608]{1,0:T(8,128)(2,1)S(1)} collective-permute-done((bf16[16,4608]{1,0:T(8,128)(2,1)S(1)}, bf16[16,4608]{1,0:T(8,128)(2,1)S(1)}, u32[]{:S(2)}, u32[]{:S(2)}) %collective-permute-start.11) | collective-permute-done | bytes 147488 | tf_op jit(solution)/shard_map/ppermute | solution.py:191
  23.5 0.2 collective-permute-start.12
  23.6 3.0 %collective-permute-done.8.refs_5_ = bf16[16,4608]{1,0:T(8,128)(2,1)S(1)} collective-permute-done((bf16[16,4608]{1,0:T(8,128)(2,1)S(1)}, bf16[16,4608]{1,0:T(8,128)(2,1)S(1)}, u32[]{:S(2)}, u32[]{:S(2)}) %collective-permute-start.8) | collective-permute-done | bytes 147488 | tf_op jit(solution)/shard_map/ppermute | solution.py:185
  26.6 0.0 collective-permute-start.7
  26.6 0.0 collective-permute-done.1.refs_2_
  26.6 0.5 %collective-permute-start.9 = (bf16[16,4608]{1,0:T(8,128)(2,1)S(1)}, bf16[16,4608]{1,0:T(8,128)(2,1)S(1)}, u32[]{:S(2)}, u32[]{:S(2)}) collective-permute-start(bf16[16,4608]{1,0:T(8,128)(2,1)S(1)} %collective-permute-done.8.refs_5_), channel_id=1, source_target_pairs={{0,1},{1,0},{2,3},{3,2},{4,5},{5,4},{6,7},{7,6},{8,9},{9,8},{10,11... | collective-permute-start | bytes 442376 | tf_op jit(solution)/shard_map/ppermute | solution.py:185
  27.1 0.9 %collective-permute-done.7.refs_4_ = bf16[16,4608]{1,0:T(8,128)(2,1)S(1)} collective-permute-done((bf16[16,4608]{1,0:T(8,128)(2,1)S(1)}, bf16[16,4608]{1,0:T(8,128)(2,1)S(1)}, u32[]{:S(2)}, u32[]{:S(2)}) %collective-permute-start.7) | collective-permute-done | bytes 147488 | tf_op jit(solution)/shard_map/ppermute | solution.py:185
  28.0 0.0 collective-permute-done.5.refs_2_
  28.0 0.2 collective-permute-done.9.refs_6_
  28.2 0.0 collective-permute-done.12.refs_8_
  28.2 0.0 copy-done
  28.2 0.0 copy-done.1
  28.2 0.0 copy-done.2
  28.2 1.3 %shard_map.60 = (f32[64,512]{1,0:T(8,128)S(1)}, bf16[64,512]{1,0:T(8,128)(2,1)S(1)}, bf16[256,512]{1,0:T(8,128)(2,1)S(1)}) custom-call(s32[1,512]{1,0:T(1,128)S(1)} %bitcast.11, s32[1,512]{1,0:T(1,128)S(1)} %broadcast_in_dim.3.own_idx_ref, bf16[4,512,1024]{2,1,0:T(8,128)(2,1)S(1)} %get-tuple-element.22.x_ref, bf16[64,512]{1,0:T(8,128)(2,1)S(1)} %bitcast.10, ...), custom_call_target="tpu_custom_call" | custom-call | flops 1073741824 | bytes 6557696 | tf_op jit(solution)/shard_map/pallas_call | solution.py:21
  29.5 0.9 %collective-permute-start.13 = (bf16[64,512]{1,0:T(8,128)(2,1)S(1)}, bf16[64,512]{1,0:T(8,128)(2,1)S(1)}, u32[]{:S(2)}, u32[]{:S(2)}) collective-permute-start(bf16[64,512]{1,0:T(8,128)(2,1)S(1)} %get-tuple-element.28), channel_id=1, source_target_pairs={{0,2},{2,0},{1,3},{3,1},{4,6},{6,4},{5,7},{7,5},{8,10},{10,8},{9,1... | collective-permute-start | bytes 196616 | tf_op jit(solution)/shard_map/ppermute | solution.py:185
  30.4 0.0 collective-permute-done.2.refs_3_
  30.4 0.9 %shard_map.57.base_ref = f32[512,512]{1,0:T(8,128)S(1)} custom-call(s32[4]{0:T(128)S(1)} %add_convert_fusion.flag_ref, bf16[512,512]{1,0:T(8,128)(2,1)S(1)} %get-tuple-element.20.refs_0_, bf16[512,512]{1,0:T(8,128)(2,1)S(1)} %shard_map.56.refs_1_, bf16[512,512]{1,0:T(8,128)(2,1)S(1)} %collective-permute-done.1.refs_2_, ...), custom_call_target="tpu_custom_call" | custom-call | flops 1048576 | bytes 2097168 | tf_op jit(solution)/shard_map/pallas_call | solution.py:21
  31.4 2.5 %collective-permute-done.13.refs_0_ = bf16[64,512]{1,0:T(8,128)(2,1)S(1)} collective-permute-done((bf16[64,512]{1,0:T(8,128)(2,1)S(1)}, bf16[64,512]{1,0:T(8,128)(2,1)S(1)}, u32[]{:S(2)}, u32[]{:S(2)}) %collective-permute-start.13) | collective-permute-done | bytes 65568 | tf_op jit(solution)/shard_map/ppermute | solution.py:185
  33.9 1.1 %shard_map.61 = bf16[512,512]{1,0:T(8,128)(2,1)} custom-call(s32[1,512]{1,0:T(1,128)S(1)} %bitcast.12, s32[1,512]{1,0:T(1,128)S(1)} %broadcast_in_dim.3.own_idx_ref, f32[512,512]{1,0:T(8,128)S(1)} %shard_map.57.base_ref, bf16[256,512]{1,0:T(8,128)(2,1)S(1)} %get-tuple-element.26.up_ref, f32[64,512]{1,0:T(8,128)S(1)} %get-tuple-element.27.low_ref, ...), custom_call_target="tpu_custom_call" | custom-call | flops 134217728 | bytes 1511424 | tf_op jit(solution)/shard_map/pallas_call | solution.py:21
  (3 shorter events, 0.0 us)
Async XLA Ops:
  0.0 15.0 %collective-permute-start = (bf16[4096,512]{1,0:T(8,128)(2,1)}, bf16[4096,512]{1,0:T(8,128)(2,1)}, u32[]{:S(2)}, u32[]{:S(2)}) collective-permute-start(bf16[4096,512]{1,0:T(8,128)(2,1)} %v_ref.1), channel_id=1, source_target_pairs={{0,1},{1,0},{2,3},{3,2},{4,5},{5,4},{6,7},{7,6},{8,9},{9,8},{10,11... | collective-permute-start | bytes 12582920 | tf_op jit(solution)/shard_map/ppermute | solution.py:185
  1.4 9.3 %collective-permute-start.3 = (bf16[16,4608]{1,0:T(8,128)(2,1)S(1)}, bf16[16,4608]{1,0:T(8,128)(2,1)S(1)}, u32[]{:S(2)}, u32[]{:S(2)}) collective-permute-start(bf16[16,4608]{1,0:T(8,128)(2,1)S(1)} %get-tuple-element.24), channel_id=1, source_target_pairs={{0,12},{4,8},{8,4},{12,0},{1,13},{5,9},{9,5},{13,1},{2,14},{6,10},... | collective-permute-start | bytes 442376 | tf_op jit(solution)/shard_map/ppermute | solution.py:191
  10.4 16.2 %collective-permute-start.1 = (bf16[512,512]{1,0:T(8,128)(2,1)S(1)}, bf16[512,512]{1,0:T(8,128)(2,1)S(1)}, u32[]{:S(2)}, u32[]{:S(2)}) collective-permute-start(bf16[512,512]{1,0:T(8,128)(2,1)S(1)} %get-tuple-element.20.refs_0_), channel_id=1, source_target_pairs={{0,1},{1,3},{2,0},{3,2},{4,5},{5,7},{6,4},{7,6},{8,9},{9,11},{10,8... | collective-permute-start | bytes 1572872 | tf_op jit(solution)/shard_map/ppermute | solution.py:255
  10.6 11.2 %collective-permute-start.10 = (bf16[16,4608]{1,0:T(8,128)(2,1)S(1)}, bf16[16,4608]{1,0:T(8,128)(2,1)S(1)}, u32[]{:S(2)}, u32[]{:S(2)}) collective-permute-start(bf16[16,4608]{1,0:T(8,128)(2,1)S(1)} %get-tuple-element.24), channel_id=1, source_target_pairs={{0,4},{4,0},{8,12},{12,8},{1,5},{5,1},{9,13},{13,9},{2,6},{6,2},{1... | collective-permute-start | bytes 442376 | tf_op jit(solution)/shard_map/ppermute | solution.py:191
  10.7 8.1 %collective-permute-start.4 = (bf16[16,4608]{1,0:T(8,128)(2,1)S(1)}, bf16[16,4608]{1,0:T(8,128)(2,1)S(1)}, u32[]{:S(2)}, u32[]{:S(2)}) collective-permute-start(bf16[16,4608]{1,0:T(8,128)(2,1)S(1)} %collective-permute-done.3.refs_0_), channel_id=1, source_target_pairs={{0,16},{16,0},{1,17},{17,1},{2,18},{18,2},{3,19},{19,3},{4,20},{20... | collective-permute-start | bytes 442376 | tf_op jit(solution)/shard_map/ppermute | solution.py:185
  12.3 8.2 %collective-permute-start.6 = (bf16[16,4608]{1,0:T(8,128)(2,1)S(1)}, bf16[16,4608]{1,0:T(8,128)(2,1)S(1)}, u32[]{:S(2)}, u32[]{:S(2)}) collective-permute-start(bf16[16,4608]{1,0:T(8,128)(2,1)S(1)} %collective-permute-done.3.refs_0_), channel_id=1, source_target_pairs={{0,4},{4,0},{8,12},{12,8},{1,5},{5,1},{9,13},{13,9},{2,6},{6,2},{1... | collective-permute-start | bytes 442376 | tf_op jit(solution)/shard_map/ppermute | solution.py:191
  15.0 8.4 %collective-permute-start.11 = (bf16[16,4608]{1,0:T(8,128)(2,1)S(1)}, bf16[16,4608]{1,0:T(8,128)(2,1)S(1)}, u32[]{:S(2)}, u32[]{:S(2)}) collective-permute-start(bf16[16,4608]{1,0:T(8,128)(2,1)S(1)} %get-tuple-element.25), channel_id=1, source_target_pairs={{0,4},{4,0},{8,12},{12,8},{1,5},{5,1},{9,13},{13,9},{2,6},{6,2},{1... | collective-permute-start | bytes 442376 | tf_op jit(solution)/shard_map/ppermute | solution.py:191
  15.1 13.2 %copy-start = (bf16[1,4096,64]{1,2,0:T(8,128)(2,1)S(1)}, bf16[1,4096,64]{1,2,0:T(8,128)(2,1)}, u32[]{:S(2)}) copy-start(bf16[1,4096,64]{1,2,0:T(8,128)(2,1)} %param.7) | copy-start | bytes 1572868
  15.1 13.2 %copy-start.1 = (bf16[1,64,512]{2,1,0:T(8,128)(2,1)S(1)}, bf16[1,64,512]{2,1,0:T(8,128)(2,1)}, u32[]{:S(2)}) copy-start(bf16[1,64,512]{2,1,0:T(8,128)(2,1)} %param.8) | copy-start | bytes 196612
  15.1 13.2 %copy-start.2 = (s32[512,1]{0,1:T(1,128)S(1)}, s32[512,1]{0,1:T(1,128)}, u32[]{:S(2)}) copy-start(s32[512,1]{0,1:T(1,128)} %param.9) | copy-start | bytes 6148
  18.9 11.5 %collective-permute-start.2 = (bf16[512,512]{1,0:T(8,128)(2,1)S(1)}, bf16[512,512]{1,0:T(8,128)(2,1)S(1)}, u32[]{:S(2)}, u32[]{:S(2)}) collective-permute-start(bf16[512,512]{1,0:T(8,128)(2,1)S(1)} %shard_map.56.refs_1_), channel_id=1, source_target_pairs={{0,2},{1,0},{2,3},{3,1},{4,6},{5,4},{6,7},{7,5},{8,10},{9,8},{10,1... | collective-permute-start | bytes 1572872 | tf_op jit(solution)/shard_map/ppermute | solution.py:255
  20.4 6.2 %collective-permute-start.8 = (bf16[16,4608]{1,0:T(8,128)(2,1)S(1)}, bf16[16,4608]{1,0:T(8,128)(2,1)S(1)}, u32[]{:S(2)}, u32[]{:S(2)}) collective-permute-start(bf16[16,4608]{1,0:T(8,128)(2,1)S(1)} %collective-permute-done.6.refs_3_), channel_id=1, source_target_pairs={{0,16},{16,0},{1,17},{17,1},{2,18},{18,2},{3,19},{19,3},{4,20},{20... | collective-permute-start | bytes 442376 | tf_op jit(solution)/shard_map/ppermute | solution.py:185
  21.8 6.2 %collective-permute-start.5 = (bf16[32,4608]{1,0:T(8,128)(2,1)S(1)}, bf16[32,4608]{1,0:T(8,128)(2,1)S(1)}, u32[]{:S(2)}, u32[]{:S(2)}) collective-permute-start(bf16[32,4608]{1,0:T(8,128)(2,1)S(1)} %shard_map.58.refs_1_), channel_id=1, source_target_pairs={{0,1},{1,0},{2,3},{3,2},{4,5},{5,4},{6,7},{7,6},{8,9},{9,8},{10,11... | collective-permute-start | bytes 884744 | tf_op jit(solution)/shard_map/ppermute | solution.py:185
  23.5 4.8 %collective-permute-start.12 = (bf16[32,4608]{1,0:T(8,128)(2,1)S(1)}, bf16[32,4608]{1,0:T(8,128)(2,1)S(1)}, u32[]{:S(2)}, u32[]{:S(2)}) collective-permute-start(bf16[32,4608]{1,0:T(8,128)(2,1)S(1)} %shard_map.59.refs_7_), channel_id=1, source_target_pairs={{0,1},{1,0},{2,3},{3,2},{4,5},{5,4},{6,7},{7,6},{8,9},{9,8},{10,11... | collective-permute-start | bytes 884744 | tf_op jit(solution)/shard_map/ppermute | solution.py:185
  26.6 1.4 %collective-permute-start.7 = (bf16[16,4608]{1,0:T(8,128)(2,1)S(1)}, bf16[16,4608]{1,0:T(8,128)(2,1)S(1)}, u32[]{:S(2)}, u32[]{:S(2)}) collective-permute-start(bf16[16,4608]{1,0:T(8,128)(2,1)S(1)} %collective-permute-done.6.refs_3_), channel_id=1, source_target_pairs={{0,1},{1,0},{2,3},{3,2},{4,5},{5,4},{6,7},{7,6},{8,9},{9,8},{10,11... | collective-permute-start | bytes 442376 | tf_op jit(solution)/shard_map/ppermute | solution.py:185
  26.6 1.6 %collective-permute-start.9 = (bf16[16,4608]{1,0:T(8,128)(2,1)S(1)}, bf16[16,4608]{1,0:T(8,128)(2,1)S(1)}, u32[]{:S(2)}, u32[]{:S(2)}) collective-permute-start(bf16[16,4608]{1,0:T(8,128)(2,1)S(1)} %collective-permute-done.8.refs_5_), channel_id=1, source_target_pairs={{0,1},{1,0},{2,3},{3,2},{4,5},{5,4},{6,7},{7,6},{8,9},{9,8},{10,11... | collective-permute-start | bytes 442376 | tf_op jit(solution)/shard_map/ppermute | solution.py:185
  29.5 4.4 %collective-permute-start.13 = (bf16[64,512]{1,0:T(8,128)(2,1)S(1)}, bf16[64,512]{1,0:T(8,128)(2,1)S(1)}, u32[]{:S(2)}, u32[]{:S(2)}) collective-permute-start(bf16[64,512]{1,0:T(8,128)(2,1)S(1)} %get-tuple-element.28), channel_id=1, source_target_pairs={{0,2},{2,0},{1,3},{3,1},{4,6},{6,4},{5,7},{7,5},{8,10},{10,8},{9,1... | collective-permute-start | bytes 196616 | tf_op jit(solution)/shard_map/ppermute | solution.py:185
